TPU v7x, 32 devices: a whole 2x2x4 slice. The times are simulated.
32 devices in a mesh: blk: 16 (over z, x, core), pair: 2 (over y).
Axes of the slice: x: 2, y: 2, z: 4, core: 2. Of those that a mesh axis runs over, the one named last changes fastest.
Arguments:
- mps: float32 [64, 32, 2048], P('pair', None, 'blk'), may hold values from -0.75 to 0.75
Outputs:
- kernel: float32 [32, 26], P(('blk', 'pair'))
All inputs are finite; a program needn't handle non-finite values.
Results may differ from a plain program's by a relative error of at most 0.0002.
Values sent between devices are 32-bit elements; how exact they have to be, the bound alone decides.
No kernel may reach another device: no remote copies, remote signals or barrier semaphores. Data moves between devices by JAX's collectives and lax.ppermute only.
A program may use at most 64 MiB of HBM per device.

v0:
```python
import jax
import jax.numpy as jnp
from jax import lax
from jax.sharding import PartitionSpec as P

REACH = 6


def shifted(array, axis, by):
    peers = lax.axis_size(axis)
    return lax.ppermute(array, axis, [(i, (i + by) % peers) for i in range(peers)])


def from_partner(array, axis, apart):
    return lax.ppermute(array, axis, [(i, i ^ 1 << apart) for i in range(lax.axis_size(axis))])


def contract(left, right, chi, samp):
    sites = left.shape[0]
    own_tensors = left.reshape(sites, chi, samp, 2, chi)
    far_tensors = right.reshape(sites, chi, samp, 2, chi)
    start = jnp.zeros((samp, samp, chi, chi), jnp.float32).at[:, :, 0, 0].set(1.0)

    def advance(state, pieces):
        own_site, far_site = pieces
        inner = jnp.einsum("nmxy,ympq->nmxpq", state, far_site, precision=lax.Precision.HIGHEST)
        return (
            jnp.einsum("xnpz,nmxpq->nmzq", own_site, inner, precision=lax.Precision.HIGHEST),
            None,
        )

    final, _ = lax.scan(advance, start, (own_tensors, far_tensors), unroll=8)
    return final


def body(mps):
    chi = mps.shape[1]
    samp = mps.shape[2] // (2 * chi)
    blocks = lax.axis_size("blk")
    band = min(REACH, (blocks - 1) // 2)
    core = lax.axis_index("pair")
    shaped = mps.reshape(mps.shape[0], chi, samp, 2, chi)
    flipped = jnp.flip(jnp.swapaxes(shaped, 1, 4), 0).reshape(mps.shape)
    working = jnp.where(core == 1, flipped, mps)
    first = contract(working, working, chi, samp)
    states = jnp.zeros((band + 1,) + first.shape, jnp.float32).at[0].set(first)
    selves = jnp.zeros((band,) + first.shape, jnp.float32)

    def advance_sites(offset, carry):
        moving, gathered, passing = carry
        moving = shifted(moving, "blk", 1)
        gathered = gathered.at[offset].set(contract(working, moving, chi, samp))
        passing = passing.at[offset - 1].set(contract(moving, moving, chi, samp))
        return (moving, gathered, passing)

    _, states, selves = lax.fori_loop(1, band + 1, advance_sites, (working, states, selves))
    partner, partner_selves = from_partner((states, selves), "pair", 0)
    correlations = jnp.sum(states * partner, axis=(3, 4))
    lower_norm = jnp.diagonal(jnp.sum(selves * partner_selves, axis=(3, 4)), axis1=1, axis2=2)
    own_norm = jnp.diagonal(correlations[0])

    def bring(step_index, carry):
        travel, mirrored, upper = carry
        travel = shifted(travel, "blk", -1)
        mirrored = mirrored.at[step_index - 1].set(travel[step_index].T)
        upper = upper.at[step_index - 1].set(jnp.diagonal(travel[0]))
        return (travel, mirrored, upper)

    empty = jnp.zeros((band, samp, samp), jnp.float32)
    empty_norm = jnp.zeros((band, samp), jnp.float32)
    _, mirrored, upper_norm = lax.fori_loop(1, band + 1, bring, (correlations, empty, empty_norm))
    remote_norm = jnp.concatenate([lower_norm[::-1], own_norm[None], upper_norm], 0)
    tiles = jnp.concatenate([correlations[1:][::-1], correlations[:1], mirrored], 0)
    kernel = tiles * tiles / (own_norm[None, :, None] * remote_norm[:, None, :])
    result = jnp.swapaxes(kernel, 0, 1).reshape(samp, (2 * band + 1) * samp)
    half = samp // 2
    return lax.dynamic_slice_in_dim(result, core * half, half, 0)


def solution(mesh):
    in_specs = (P("pair", None, "blk"),)
    out_specs = P(("blk", "pair"), None)
    return jax.shard_map(body, mesh=mesh, in_specs=in_specs, out_specs=out_specs, check_vma=False)
```

profile of v0, /device:TPU:0, one launch (start us, length us, event | category | flops | bytes accessed | tf_op | source)
XLA Modules:
  0.0 436.2 jit_solution(10770523665075883671)
XLA Ops:
  3.0 4.1 copy.228
  13.3 17.7 %while.147 = (s32[]{:T(128)}, f32[2,2,32,32]{2,3,1,0:T(8,128)S(1)}, f32[4,8,32,2,2,32]{2,5,4,3,1,0:T(8,128)S(1)}, s32[]{:T(128)}, s32[]{:T(128)}, /*index=5*/s32[]{}, s32[]{}, s32[]{}, s32[]{}, s32[]{}, /*index=10*/s32[]{}, s32[]{}) while((s32[]{:T(128)}, f32[2,2,32,32]{2,3,1,0:T(8,128)S(1)}, f32[4,8,32,2,2,32]{2,5,4,3,1,0:T(8,128)S(1)}, ...), condition=%wide.region_1.2_spmd, body=%wide.region_0.1_spmd.sunk | while | flops 50331652 | bytes 3014977 | solution.py:32
  32.7 340.3 %while.150 = (s32[]{:T(128)}, f32[32,32,128]{2,1,0:T(8,128)}, f32[7,2,2,32,32]{3,4,2,1,0:T(8,128)}, f32[6,2,2,32,32]{3,4,2,1,0:T(8,128)}, f32[32,32,128]{2,1,0:T...) while((s32[]{:T(128)}, f32[32,32,128]{2,1,0:T(8,128)}, ...), condition=%wide.region_9.10_spmd, body=%wide.region_2.9_spmd.sunk | while | flops 100671536 | bytes 10693951 | solution.py:56
  37.5 7.6 %collective-permute-done.1 = f32[32,32,128]{2,1,0:T(8,128)S(1)} collective-permute-done((f32[32,32,128]{2,1,0:T(8,128)}, f32[32,32,128]{2,1,0:T(8,128)S(1)}, u32[]{:S(2)}, u32[]{:S(2)}) %collective-permute-start.1) | collective-permute-done | bytes 524320 | tf_op jit(solution)/shard_map/while/body/eval_jaxpr/ppermute | solution.py:11
  45.8 23.2 %while.153 = (s32[]{:T(128)}, f32[2,2,32,32]{2,3,1,0:T(8,128)S(1)}, f32[4,8,32,2,2,32]{2,5,4,3,1,0:T(8,128)S(1)}, f32[4,8,32,2,2,32]{5,4,3,2,1,0:T(2,128)}, s32[...) while((s32[]{:T(128)}, f32[2,2,32,32]{2,3,1,0:T(8,128)S(1)}, ...), condition=%wide.region_5.5_spmd, body=%wide.region_4.4_spmd.sunk | while | flops 50331656 | bytes 2097453 | solution.py:32
  69.0 17.7 %while.152 = (s32[]{:T(128)}, f32[2,2,32,32]{2,3,1,0:T(8,128)S(1)}, f32[4,8,32,2,2,32]{2,5,4,3,1,0:T(8,128)S(1)}, s32[]{:T(128)}, s32[]{:T(128)}, /*index=5*/s32[]{}, s32[]{}, s32[]{}, s32[]{}, s32[]{}, /*index=10*/s32[]{}, s32[]{}) while((s32[]{:T(128)}, f32[2,2,32,32]{2,3,1,0:T(8,128)S(1)}, f32[4,8,32,2,2,32]{2,5,4,3,1,0:T(8,128)S(1)}, ...), condition=%wide.region_8.8_spmd, body=%wide.region_7.7_spmd.sunk | while | flops 50331652 | bytes 3014977 | solution.py:32
  90.4 3.0 reshape.700
  94.6 7.1 %collective-permute-done.1 = f32[32,32,128]{2,1,0:T(8,128)S(1)} collective-permute-done((f32[32,32,128]{2,1,0:T(8,128)}, f32[32,32,128]{2,1,0:T(8,128)S(1)}, u32[]{:S(2)}, u32[]{:S(2)}) %collective-permute-start.1) | collective-permute-done | bytes 524320 | tf_op jit(solution)/shard_map/while/body/eval_jaxpr/ppermute | solution.py:11
  102.3 23.2 %while.153 = (s32[]{:T(128)}, f32[2,2,32,32]{2,3,1,0:T(8,128)S(1)}, f32[4,8,32,2,2,32]{2,5,4,3,1,0:T(8,128)S(1)}, f32[4,8,32,2,2,32]{5,4,3,2,1,0:T(2,128)}, s32[...) while((s32[]{:T(128)}, f32[2,2,32,32]{2,3,1,0:T(8,128)S(1)}, ...), condition=%wide.region_5.5_spmd, body=%wide.region_4.4_spmd.sunk | while | flops 50331656 | bytes 2097453 | solution.py:32
  125.5 17.7 %while.152 = (s32[]{:T(128)}, f32[2,2,32,32]{2,3,1,0:T(8,128)S(1)}, f32[4,8,32,2,2,32]{2,5,4,3,1,0:T(8,128)S(1)}, s32[]{:T(128)}, s32[]{:T(128)}, /*index=5*/s32[]{}, s32[]{}, s32[]{}, s32[]{}, s32[]{}, /*index=10*/s32[]{}, s32[]{}) while((s32[]{:T(128)}, f32[2,2,32,32]{2,3,1,0:T(8,128)S(1)}, f32[4,8,32,2,2,32]{2,5,4,3,1,0:T(8,128)S(1)}, ...), condition=%wide.region_8.8_spmd, body=%wide.region_7.7_spmd.sunk | while | flops 50331652 | bytes 3014977 | solution.py:32
  146.9 3.0 reshape.700
  151.1 7.1 %collective-permute-done.1 = f32[32,32,128]{2,1,0:T(8,128)S(1)} collective-permute-done((f32[32,32,128]{2,1,0:T(8,128)}, f32[32,32,128]{2,1,0:T(8,128)S(1)}, u32[]{:S(2)}, u32[]{:S(2)}) %collective-permute-start.1) | collective-permute-done | bytes 524320 | tf_op jit(solution)/shard_map/while/body/eval_jaxpr/ppermute | solution.py:11
  158.9 23.2 %while.153 = (s32[]{:T(128)}, f32[2,2,32,32]{2,3,1,0:T(8,128)S(1)}, f32[4,8,32,2,2,32]{2,5,4,3,1,0:T(8,128)S(1)}, f32[4,8,32,2,2,32]{5,4,3,2,1,0:T(2,128)}, s32[...) while((s32[]{:T(128)}, f32[2,2,32,32]{2,3,1,0:T(8,128)S(1)}, ...), condition=%wide.region_5.5_spmd, body=%wide.region_4.4_spmd.sunk | while | flops 50331656 | bytes 2097453 | solution.py:32
  182.1 17.7 %while.152 = (s32[]{:T(128)}, f32[2,2,32,32]{2,3,1,0:T(8,128)S(1)}, f32[4,8,32,2,2,32]{2,5,4,3,1,0:T(8,128)S(1)}, s32[]{:T(128)}, s32[]{:T(128)}, /*index=5*/s32[]{}, s32[]{}, s32[]{}, s32[]{}, s32[]{}, /*index=10*/s32[]{}, s32[]{}) while((s32[]{:T(128)}, f32[2,2,32,32]{2,3,1,0:T(8,128)S(1)}, f32[4,8,32,2,2,32]{2,5,4,3,1,0:T(8,128)S(1)}, ...), condition=%wide.region_8.8_spmd, body=%wide.region_7.7_spmd.sunk | while | flops 50331652 | bytes 3014977 | solution.py:32
  203.5 3.0 reshape.700
  207.7 7.1 %collective-permute-done.1 = f32[32,32,128]{2,1,0:T(8,128)S(1)} collective-permute-done((f32[32,32,128]{2,1,0:T(8,128)}, f32[32,32,128]{2,1,0:T(8,128)S(1)}, u32[]{:S(2)}, u32[]{:S(2)}) %collective-permute-start.1) | collective-permute-done | bytes 524320 | tf_op jit(solution)/shard_map/while/body/eval_jaxpr/ppermute | solution.py:11
  215.4 23.2 %while.153 = (s32[]{:T(128)}, f32[2,2,32,32]{2,3,1,0:T(8,128)S(1)}, f32[4,8,32,2,2,32]{2,5,4,3,1,0:T(8,128)S(1)}, f32[4,8,32,2,2,32]{5,4,3,2,1,0:T(2,128)}, s32[...) while((s32[]{:T(128)}, f32[2,2,32,32]{2,3,1,0:T(8,128)S(1)}, ...), condition=%wide.region_5.5_spmd, body=%wide.region_4.4_spmd.sunk | while | flops 50331656 | bytes 2097453 | solution.py:32
  238.6 17.7 %while.152 = (s32[]{:T(128)}, f32[2,2,32,32]{2,3,1,0:T(8,128)S(1)}, f32[4,8,32,2,2,32]{2,5,4,3,1,0:T(8,128)S(1)}, s32[]{:T(128)}, s32[]{:T(128)}, /*index=5*/s32[]{}, s32[]{}, s32[]{}, s32[]{}, s32[]{}, /*index=10*/s32[]{}, s32[]{}) while((s32[]{:T(128)}, f32[2,2,32,32]{2,3,1,0:T(8,128)S(1)}, f32[4,8,32,2,2,32]{2,5,4,3,1,0:T(8,128)S(1)}, ...), condition=%wide.region_8.8_spmd, body=%wide.region_7.7_spmd.sunk | while | flops 50331652 | bytes 3014977 | solution.py:32
  264.2 7.1 %collective-permute-done.1 = f32[32,32,128]{2,1,0:T(8,128)S(1)} collective-permute-done((f32[32,32,128]{2,1,0:T(8,128)}, f32[32,32,128]{2,1,0:T(8,128)S(1)}, u32[]{:S(2)}, u32[]{:S(2)}) %collective-permute-start.1) | collective-permute-done | bytes 524320 | tf_op jit(solution)/shard_map/while/body/eval_jaxpr/ppermute | solution.py:11
  271.9 23.2 %while.153 = (s32[]{:T(128)}, f32[2,2,32,32]{2,3,1,0:T(8,128)S(1)}, f32[4,8,32,2,2,32]{2,5,4,3,1,0:T(8,128)S(1)}, f32[4,8,32,2,2,32]{5,4,3,2,1,0:T(2,128)}, s32[...) while((s32[]{:T(128)}, f32[2,2,32,32]{2,3,1,0:T(8,128)S(1)}, ...), condition=%wide.region_5.5_spmd, body=%wide.region_4.4_spmd.sunk | while | flops 50331656 | bytes 2097453 | solution.py:32
  295.1 17.8 %while.152 = (s32[]{:T(128)}, f32[2,2,32,32]{2,3,1,0:T(8,128)S(1)}, f32[4,8,32,2,2,32]{2,5,4,3,1,0:T(8,128)S(1)}, s32[]{:T(128)}, s32[]{:T(128)}, /*index=5*/s32[]{}, s32[]{}, s32[]{}, s32[]{}, s32[]{}, /*index=10*/s32[]{}, s32[]{}) while((s32[]{:T(128)}, f32[2,2,32,32]{2,3,1,0:T(8,128)S(1)}, f32[4,8,32,2,2,32]{2,5,4,3,1,0:T(8,128)S(1)}, ...), condition=%wide.region_8.8_spmd, body=%wide.region_7.7_spmd.sunk | while | flops 50331652 | bytes 3014977 | solution.py:32
  316.5 3.0 reshape.700
  320.8 7.1 %collective-permute-done.1 = f32[32,32,128]{2,1,0:T(8,128)S(1)} collective-permute-done((f32[32,32,128]{2,1,0:T(8,128)}, f32[32,32,128]{2,1,0:T(8,128)S(1)}, u32[]{:S(2)}, u32[]{:S(2)}) %collective-permute-start.1) | collective-permute-done | bytes 524320 | tf_op jit(solution)/shard_map/while/body/eval_jaxpr/ppermute | solution.py:11
  328.5 23.2 %while.153 = (s32[]{:T(128)}, f32[2,2,32,32]{2,3,1,0:T(8,128)S(1)}, f32[4,8,32,2,2,32]{2,5,4,3,1,0:T(8,128)S(1)}, f32[4,8,32,2,2,32]{5,4,3,2,1,0:T(2,128)}, s32[...) while((s32[]{:T(128)}, f32[2,2,32,32]{2,3,1,0:T(8,128)S(1)}, ...), condition=%wide.region_5.5_spmd, body=%wide.region_4.4_spmd.sunk | while | flops 50331656 | bytes 2097453 | solution.py:32
  351.7 17.8 %while.152 = (s32[]{:T(128)}, f32[2,2,32,32]{2,3,1,0:T(8,128)S(1)}, f32[4,8,32,2,2,32]{2,5,4,3,1,0:T(8,128)S(1)}, s32[]{:T(128)}, s32[]{:T(128)}, /*index=5*/s32[]{}, s32[]{}, s32[]{}, s32[]{}, s32[]{}, /*index=10*/s32[]{}, s32[]{}) while((s32[]{:T(128)}, f32[2,2,32,32]{2,3,1,0:T(8,128)S(1)}, f32[4,8,32,2,2,32]{2,5,4,3,1,0:T(8,128)S(1)}, ...), condition=%wide.region_8.8_spmd, body=%wide.region_7.7_spmd.sunk | while | flops 50331652 | bytes 3014977 | solution.py:32
  376.0 10.8 %collective-permute-done.3 = f32[6,2,2,32,32]{3,4,2,1,0:T(8,128)S(1)} collective-permute-done((f32[6,2,2,32,32]{3,4,2,1,0:T(8,128)}, f32[6,2,2,32,32]{3,4,2,1,0:T(8,128)S(1)}, u32[]{:S(2)}, u32[]{:S(2)}) %collective-permute-start.3) | collective-permute-done | bytes 98336 | tf_op jit(solution)/shard_map/ppermute | solution.py:15
  390.7 44.3 %while.151 = (s32[]{:T(128)}, f32[7,2,2]{2,1,0:T(2,128)S(1)}, f32[6,2,2]{2,1,0:T(2,128)S(1)}, f32[6,2]{1,0:T(8,128)S(1)}, s32[]{:T(128)}, /*index=5*/s32[]{:T(12...) while((s32[]{:T(128)}, f32[7,2,2]{2,1,0:T(2,128)S(1)}, f32[6,2,2]{2,1,0:T(2,128)S(1)}, ...), condition=%wide.region_14.15_spmd, body=%wide.region_11.0_spmd.sunk | while | flops 45 | bytes 4159 | solution.py:71
  395.5 4.3 collective-permute-start
  403.4 4.3 collective-permute-start
  411.3 4.3 collective-permute-start
  419.2 4.3 collective-permute-start
  427.1 4.3 collective-permute-start
  (1031 shorter events, 337.6 us)
Async XLA Ops:
  9.4 2.4 copy-start
  11.8 1.4 copy-start.1
  13.3 19.4 %copy-start.4 = (s32[5]{0:T(128)S(1)}, s32[5]{0:T(128)}, u32[]{:S(2)}) copy-start(s32[5]{0:T(128)} %constant.491.clone.1) | copy-start | bytes 64
  13.3 19.4 %copy-start.5 = (s32[5]{0:T(128)S(1)}, s32[5]{0:T(128)}, u32[]{:S(2)}) copy-start(s32[5]{0:T(128)} %constant.495.clone.1) | copy-start | bytes 64
  32.7 12.5 %collective-permute-start.1 = (f32[32,32,128]{2,1,0:T(8,128)}, f32[32,32,128]{2,1,0:T(8,128)S(1)}, u32[]{:S(2)}, u32[]{:S(2)}) collective-permute-start(f32[32,32,128]{2,1,0:T(8,128)} %get-tuple-element.939), channel_id=1, source_target_pairs={{0,2},{2,4},{4,6},{6,8},{8,10},{10,12},{12,14},{14,16},{16,18},{18... | collective-permute-start | bytes 1572872 | tf_op jit(solution)/shard_map/while/body/eval_jaxpr/ppermute | solution.py:11
  90.2 11.5 %collective-permute-start.1 = (f32[32,32,128]{2,1,0:T(8,128)}, f32[32,32,128]{2,1,0:T(8,128)S(1)}, u32[]{:S(2)}, u32[]{:S(2)}) collective-permute-start(f32[32,32,128]{2,1,0:T(8,128)} %get-tuple-element.939), channel_id=1, source_target_pairs={{0,2},{2,4},{4,6},{6,8},{8,10},{10,12},{12,14},{14,16},{16,18},{18... | collective-permute-start | bytes 1572872 | tf_op jit(solution)/shard_map/while/body/eval_jaxpr/ppermute | solution.py:11
  146.7 11.5 %collective-permute-start.1 = (f32[32,32,128]{2,1,0:T(8,128)}, f32[32,32,128]{2,1,0:T(8,128)S(1)}, u32[]{:S(2)}, u32[]{:S(2)}) collective-permute-start(f32[32,32,128]{2,1,0:T(8,128)} %get-tuple-element.939), channel_id=1, source_target_pairs={{0,2},{2,4},{4,6},{6,8},{8,10},{10,12},{12,14},{14,16},{16,18},{18... | collective-permute-start | bytes 1572872 | tf_op jit(solution)/shard_map/while/body/eval_jaxpr/ppermute | solution.py:11
  203.3 11.5 %collective-permute-start.1 = (f32[32,32,128]{2,1,0:T(8,128)}, f32[32,32,128]{2,1,0:T(8,128)S(1)}, u32[]{:S(2)}, u32[]{:S(2)}) collective-permute-start(f32[32,32,128]{2,1,0:T(8,128)} %get-tuple-element.939), channel_id=1, source_target_pairs={{0,2},{2,4},{4,6},{6,8},{8,10},{10,12},{12,14},{14,16},{16,18},{18... | collective-permute-start | bytes 1572872 | tf_op jit(solution)/shard_map/while/body/eval_jaxpr/ppermute | solution.py:11
  259.8 11.5 %collective-permute-start.1 = (f32[32,32,128]{2,1,0:T(8,128)}, f32[32,32,128]{2,1,0:T(8,128)S(1)}, u32[]{:S(2)}, u32[]{:S(2)}) collective-permute-start(f32[32,32,128]{2,1,0:T(8,128)} %get-tuple-element.939), channel_id=1, source_target_pairs={{0,2},{2,4},{4,6},{6,8},{8,10},{10,12},{12,14},{14,16},{16,18},{18... | collective-permute-start | bytes 1572872 | tf_op jit(solution)/shard_map/while/body/eval_jaxpr/ppermute | solution.py:11
  316.4 11.5 %collective-permute-start.1 = (f32[32,32,128]{2,1,0:T(8,128)}, f32[32,32,128]{2,1,0:T(8,128)S(1)}, u32[]{:S(2)}, u32[]{:S(2)}) collective-permute-start(f32[32,32,128]{2,1,0:T(8,128)} %get-tuple-element.939), channel_id=1, source_target_pairs={{0,2},{2,4},{4,6},{6,8},{8,10},{10,12},{12,14},{14,16},{16,18},{18... | collective-permute-start | bytes 1572872 | tf_op jit(solution)/shard_map/while/body/eval_jaxpr/ppermute | solution.py:11
  372.9 17.7 %copy-start.2 = (s32[3]{0:T(128)S(1)}, s32[3]{0:T(128)}, u32[]{:S(2)}) copy-start(s32[3]{0:T(128)} %constant.500.clone.1) | copy-start | bytes 40
  372.9 17.7 %copy-start.3 = (s32[2]{0:T(128)S(1)}, s32[2]{0:T(128)}, u32[]{:S(2)}) copy-start(s32[2]{0:T(128)} %constant.503.clone.1) | copy-start | bytes 28
  372.9 15.8 %collective-permute-start.2 = (f32[7,2,2,32,32]{3,4,2,1,0:T(8,128)}, f32[7,2,2,32,32]{3,4,2,1,0:T(8,128)S(1)}, u32[]{:S(2)}, u32[]{:S(2)}) collective-permute-start(f32[7,2,2,32,32]{3,4,2,1,0:T(8,128)} %get-tuple-element.527), channel_id=1, source_target_pairs={{0,1},{1,0},{2,3},{3,2},{4,5},{5,4},{6,7},{7,6},{8,9},{9,8},{10,11... | collective-permute-start | bytes 344072 | tf_op jit(solution)/shard_map/ppermute | solution.py:15
  375.9 10.9 %collective-permute-start.3 = (f32[6,2,2,32,32]{3,4,2,1,0:T(8,128)}, f32[6,2,2,32,32]{3,4,2,1,0:T(8,128)S(1)}, u32[]{:S(2)}, u32[]{:S(2)}) collective-permute-start(f32[6,2,2,32,32]{3,4,2,1,0:T(8,128)} %get-tuple-element.529), channel_id=1, source_target_pairs={{0,1},{1,0},{2,3},{3,2},{4,5},{5,4},{6,7},{7,6},{8,9},{9,8},{10,11... | collective-permute-start | bytes 294920 | tf_op jit(solution)/shard_map/ppermute | solution.py:15
  390.7 2.8 collective-permute-start
  395.5 5.8 %collective-permute-start = (f32[7,2,2]{2,1,0:T(2,128)S(1)}, f32[7,2,2]{2,1,0:T(2,128)S(1)}, u32[]{:S(2)}, u32[]{:S(2)}) collective-permute-start(f32[7,2,2]{2,1,0:T(2,128)S(1)} %get-tuple-element.1009), channel_id=1, source_target_pairs={{0,30},{2,0},{4,2},{6,4},{8,6},{10,8},{12,10},{14,12},{16,14},{18,... | collective-permute-start | bytes 344 | tf_op jit(solution)/shard_map/while/body/eval_jaxpr/ppermute | solution.py:11
  403.4 5.8 %collective-permute-start = (f32[7,2,2]{2,1,0:T(2,128)S(1)}, f32[7,2,2]{2,1,0:T(2,128)S(1)}, u32[]{:S(2)}, u32[]{:S(2)}) collective-permute-start(f32[7,2,2]{2,1,0:T(2,128)S(1)} %get-tuple-element.1009), channel_id=1, source_target_pairs={{0,30},{2,0},{4,2},{6,4},{8,6},{10,8},{12,10},{14,12},{16,14},{18,... | collective-permute-start | bytes 344 | tf_op jit(solution)/shard_map/while/body/eval_jaxpr/ppermute | solution.py:11
  411.3 5.8 %collective-permute-start = (f32[7,2,2]{2,1,0:T(2,128)S(1)}, f32[7,2,2]{2,1,0:T(2,128)S(1)}, u32[]{:S(2)}, u32[]{:S(2)}) collective-permute-start(f32[7,2,2]{2,1,0:T(2,128)S(1)} %get-tuple-element.1009), channel_id=1, source_target_pairs={{0,30},{2,0},{4,2},{6,4},{8,6},{10,8},{12,10},{14,12},{16,14},{18,... | collective-permute-start | bytes 344 | tf_op jit(solution)/shard_map/while/body/eval_jaxpr/ppermute | solution.py:11
  419.2 5.8 %collective-permute-start = (f32[7,2,2]{2,1,0:T(2,128)S(1)}, f32[7,2,2]{2,1,0:T(2,128)S(1)}, u32[]{:S(2)}, u32[]{:S(2)}) collective-permute-start(f32[7,2,2]{2,1,0:T(2,128)S(1)} %get-tuple-element.1009), channel_id=1, source_target_pairs={{0,30},{2,0},{4,2},{6,4},{8,6},{10,8},{12,10},{14,12},{16,14},{18,... | collective-permute-start | bytes 344 | tf_op jit(solution)/shard_map/while/body/eval_jaxpr/ppermute | solution.py:11
  427.1 5.8 %collective-permute-start = (f32[7,2,2]{2,1,0:T(2,128)S(1)}, f32[7,2,2]{2,1,0:T(2,128)S(1)}, u32[]{:S(2)}, u32[]{:S(2)}) collective-permute-start(f32[7,2,2]{2,1,0:T(2,128)S(1)} %get-tuple-element.1009), channel_id=1, source_target_pairs={{0,30},{2,0},{4,2},{6,4},{8,6},{10,8},{12,10},{14,12},{16,14},{18,... | collective-permute-start | bytes 344 | tf_op jit(solution)/shard_map/while/body/eval_jaxpr/ppermute | solution.py:11
where the time goes:
time: 438 us; the launch traced here: 436 us
  matrix products  226 us (52%)
  local copies, waits for them, and re-layouts  79.7 us (18%)
  waiting for transfers between devices  54 us (12%)
  other arithmetic  42.6 us (10%)
  starting transfers between devices  26.2 us (6%)
  loops' own time  6.97 us (2%)
    dot_general x416, matrix products, advance(): jnp.einsum('xnpz,nmxpq->nmzq', own_site, inner, precision=lax.Precision.H...  118 us
    dot_general x416, matrix products, advance(): jnp.einsum('nmxy,ympq->nmxpq', state, far_site, precision=lax.Precision.H...  108 us
    ppermute x12, waiting for transfers between devices, shifted(): lax.ppermute(array, axis, [(i, (i + by) % peers) for i in range(peers)])  43.2 us
    slice x24, local copies, waits for them, and re-layouts, contract(): final, _ = lax.scan(advance, start, (own_tensors, far_tensors), unroll=8)  30.3 us
    ppermute x12, starting transfers between devices, shifted(): lax.ppermute(array, axis, [(i, (i + by) % peers) for i in range(peers)])  23.2 us
    another operation x30, other arithmetic  20.1 us
    reshape x6, local copies, waits for them, and re-layouts, contract(): final, _ = lax.scan(advance, start, (own_tensors, far_tensors), unroll=8)  18 us
    scatter x6, other arithmetic, advance_sites(): passing = passing.at[offset - 1].set(contract(moving, moving, chi, samp))  16 us
  transfers between devices with their start and end apart: 14, of which 7 were waited for; matrix products, arithmetic and copies ran while one was open for 9% of the time, Pallas kernels for 0%

commit v1 on v0

v1 whole, which is shorter than its diff:
```python
import jax
import jax.numpy as jnp
from jax import lax
from jax.experimental import pallas as pl
from jax.experimental.pallas import tpu as pltpu
from jax.sharding import PartitionSpec as P

REACH = 6
MARKS = (0, 1, 4, 6)
HOME = 1
BF16, F32 = jnp.bfloat16, jnp.float32


def shifted(array, axis, by):
    peers = lax.axis_size(axis)
    return lax.ppermute(array, axis, [(i, (i + by) % peers) for i in range(peers)])


def split(x):
    high = x.astype(BF16)
    return high, (x - high.astype(F32)).astype(BF16)


def product(left, right, across):
    dims = (((1,), (1 if across else 0,)), ((), ()))
    return lax.dot_general(left, right, dims, preferred_element_type=F32)


def lane_slot(shape):
    return lax.broadcasted_iota(jnp.int32, shape, 1) // 32


def interleave(first, second):
    even = lane_slot(first.shape) % 2 == 0
    return (
        jnp.where(even, first, pltpu.roll(second, 32, 1)),
        jnp.where(even, pltpu.roll(first, 96, 1), second),
    )


def far_weights(tiles, flip):
    parts = []
    for half in zip(*[split(t) for t in tiles]):
        slot = lane_slot(half[0].shape)
        zero = jnp.zeros_like(half[0])
        placed = [[jnp.where(slot == k, h, zero) for h in half] for k in range(4)]
        if flip:
            parts.append(jnp.concatenate([placed[k][p] for p in range(2) for k in range(4)], 0))
        else:
            parts.append(jnp.concatenate([jnp.concatenate(placed[k], 1) for k in range(4)], 0))
    high, low = parts
    return jnp.concatenate([high, high], 1 if flip else 0), low


def near_turned(tiles):
    stack = jnp.concatenate([tiles[0], tiles[1], tiles[0], tiles[1]], 0).T
    return [stack[32 * k : 32 * k + 32] for k in range(4)]


def near_plain(tile):
    twice = pltpu.roll(tile, 64, 1)
    lower = lane_slot(tile.shape) < 2
    return [jnp.where(lower, tile, twice), jnp.where(lower, twice, tile)]


def near_operand(tile):
    high, low = split(tile)
    return jnp.concatenate([high, low], 1)


def spread(states, weights, flip):
    double, low = weights
    high, rest = split(states)
    return product(jnp.concatenate([high, rest], 1), double, flip) + product(high, low, flip)


def stacked(inner):
    h0, l0 = split(inner[:, :128])
    h1, l1 = split(inner[:, 128:])
    return jnp.concatenate([h0, h1, l0, l1] * 2, 0)


def site_step(wide, narrow, tiles, flip):
    t0, t1, t4, t6 = tiles
    low_pair, high_pair = interleave(t0, t1), interleave(t4, t6)
    if flip:
        near = near_plain(t0) + near_plain(t1) + near_plain(t4)
    else:
        turned, other = near_turned(low_pair), near_turned(high_pair)
        near = [turned[0], turned[2], turned[1], turned[3], other[0], other[2]]
    wide_inner = spread(wide, far_weights(high_pair, flip), flip)
    narrow_inner = spread(narrow, far_weights(low_pair, flip), flip)
    wide_out, narrow_out = [], []
    for k, tile in enumerate(near):
        rows = slice(32 * k, 32 * k + 32)
        operand = near_operand(tile)
        if k < 2:
            both = jnp.concatenate([stacked(wide_inner[rows]), stacked(narrow_inner[rows])], 1)
            result = product(operand, both, False)
            wide_out.append(result[:, :128])
            narrow_out.append(result[:, 128:])
        else:
            wide_out.append(product(operand, stacked(wide_inner[rows]), False))
    return jnp.concatenate(wide_out, 0), jnp.concatenate(narrow_out, 0)


def chain_kernel(core_ref, b0, b1, b4, b6, out):
    sites = b0.shape[0]
    row = lax.broadcasted_iota(jnp.int32, out.shape, 0) % 32
    lane = lax.broadcasted_iota(jnp.int32, out.shape, 1) % 32
    out[...] = jnp.where((row == 0) & (lane == 0), 1.0, 0.0)

    def run(flip):
        def step(index, carry):
            site = sites - 1 - index if flip else index
            return site_step(*carry, [b[site] for b in (b0, b1, b4, b6)], flip)

        wide, narrow = lax.fori_loop(0, sites, step, (out[:192], out[192:]), unroll=2)
        out[:192] = wide
        out[192:] = narrow

    @pl.when(core_ref[0] == 0)
    def _():
        run(False)

    @pl.when(core_ref[0] == 1)
    def _():
        run(True)


def meet_kernel(mine, theirs, out):
    pairs = (mine[...] * theirs[...]).reshape(8, 32, 128).sum(1)
    row = lax.broadcasted_iota(jnp.int32, (128, 128), 0) // 32
    lane = lax.broadcasted_iota(jnp.int32, (128, 128), 1)
    chosen = jnp.where(row == lane, 1.0, 0.0)
    out[...] = jnp.dot(pairs, chosen, precision=lax.Precision.HIGHEST, preferred_element_type=F32)


def tables(samp, band):
    at = {m: k for k, m in enumerate(MARKS)}

    def tile(low, high, near, far):
        if (low, high) in ((0, 0), (0, 1)):
            return 6 + near, (0 if high == 0 else 1) + 2 * far
        return 2 * at[low] + near, (0 if high == 4 else 1) + 2 * far

    which = {}
    for low in MARKS:
        for high in MARKS:
            if low < high:
                which[high - low] = (low, high)
    which[0] = (0, 0)
    rows = []
    for n in range(samp):
        entries = []
        for o in range(-band, band + 1):
            low, high = which[abs(o)]
            for m in range(samp):
                if o >= 0:
                    entries.append((MARKS[HOME] - low, *tile(low, high, n, m)))
                else:
                    entries.append((MARKS[HOME] - high, *tile(low, high, m, n)))
        norms = [(o + MARKS[HOME], *tile(0, 0, m, m)) for o in range(-band, band + 1) for m in range(samp)]
        rows.append(entries + norms + [(MARKS[HOME], *tile(0, 0, n, n))])
    return rows


def body(mps):
    chi = mps.shape[1]
    samp = mps.shape[2] // (2 * chi)
    blocks = lax.axis_size("blk")
    band = min(REACH, (blocks - 1) // 2)
    core = lax.axis_index("pair")
    home = MARKS[HOME]
    held = [mps if m == home else shifted(mps, "blk", home - m) for m in MARKS]
    vmem = pl.BlockSpec(memory_space=pltpu.VMEM)
    states = pl.pallas_call(
        chain_kernel,
        out_shape=jax.ShapeDtypeStruct((256, 128), F32),
        in_specs=[pl.BlockSpec(memory_space=pltpu.SMEM)] + [vmem] * 4,
        out_specs=vmem,
        compiler_params=pltpu.CompilerParams(vmem_limit_bytes=32 * 2**20),
        name="half_chains",
    )(core[None].astype(jnp.int32), *held)
    partner = lax.ppermute(states, "pair", [(0, 1), (1, 0)])
    correlations = pl.pallas_call(
        meet_kernel,
        out_shape=jax.ShapeDtypeStruct((8, 128), F32),
        in_specs=[vmem] * 2,
        out_specs=vmem,
        name="meet",
    )(states, partner)[:, :4]
    everywhere = lax.all_gather(correlations.reshape(32), "blk")
    spots = jnp.asarray(tables(samp, band), jnp.int32)[core]
    source = (lax.axis_index("blk") + spots[:, 0]) % blocks
    values = everywhere.reshape(-1)[source * 32 + spots[:, 1] * 4 + spots[:, 2]]
    width = (2 * band + 1) * samp
    tile, remote, own = values[:width], values[width : 2 * width], values[2 * width]
    return (tile * tile / (own * remote))[None]


def solution(mesh):
    in_specs = (P("pair", None, "blk"),)
    out_specs = P(("blk", "pair"), None)
    return jax.shard_map(body, mesh=mesh, in_specs=in_specs, out_specs=out_specs, check_vma=False)
```

time: 438 us -> 78.6 us (0.18)
  matrix products: 226 us -> 0 us
  local copies, waits for them, and re-layouts: 79.7 us -> 5.1 us
  other arithmetic: 42.6 us -> 1.84 us
  waiting for transfers between devices: 54 us -> 26.3 us
  blocking collectives: 0 us -> 21.5 us
  starting transfers between devices: 26.2 us -> 8.48 us
  Pallas kernels: 0 us -> 15.1 us
  loops' own time: 6.97 us -> 0 us
    dot_general x832 -> x0, matrix products: 226 us -> none  [the longest x416 118 us: advance(): jnp.einsum('xnpz,nmxpq->nmzq', own_site, inner, precision=lax.Precision.H...]
    slice x26 -> x1, local copies, waits for them, and re-layouts: 30.4 us -> 0.58 us  [body(): values[2 * width]]
    reshape x10 -> x1, local copies, waits for them, and re-layouts: 27.5 us -> 0.08 us  [body(): values = everywhere.reshape(-1)[source * 32 + spots[:, 1] * 4 + spots[:, 2]]]
    all_gather x0 -> x1, blocking collectives: none -> 21.5 us  [body(): everywhere = lax.all_gather(correlations.reshape(32), 'blk')]
    ppermute x12 -> x3, waiting for transfers between devices: 43.2 us -> 22.4 us  [shifted(): lax.ppermute(array, axis, [(i, (i + by) % peers) for i in range(peers)])]
    another operation x30 -> x0, other arithmetic: 20.1 us -> none
    scatter x12 -> x0, other arithmetic: 19.9 us -> none  [the longest x6 16 us: advance_sites(): passing = passing.at[offset - 1].set(contract(moving, moving, chi, samp))]
    ppermute x12 -> x3, starting transfers between devices: 23.2 us -> 6.26 us  [shifted(): lax.ppermute(array, axis, [(i, (i + by) % peers) for i in range(peers)])]
  transfers between devices with their start and end apart: 14 -> 4, of which waited for: 7 -> 4; matrix products, arithmetic and copies ran while one was open for 9% -> 0% of each run, Pallas kernels for 0% -> 0%
where the time goes in v1:
time: 78.6 us; the launch traced here: 78.4 us
  waiting for transfers between devices  26.3 us (33%)
  blocking collectives  21.5 us (27%)
  Pallas kernels  15.1 us (19%)
  starting transfers between devices  8.48 us (11%)
  local copies, waits for them, and re-layouts  5.1 us (6%)
  other arithmetic  1.84 us (2%)
    ppermute x3, waiting for transfers between devices, shifted(): lax.ppermute(array, axis, [(i, (i + by) % peers) for i in range(peers)])  22.4 us
    all_gather x1, blocking collectives, body(): everywhere = lax.all_gather(correlations.reshape(32), 'blk')  21.5 us
    pallas_call x1, Pallas kernels, body(): pl.pallas_call(chain_kernel, out_shape=jax.ShapeDtypeStruct((256, 128), F...  13.4 us
    ppermute x3, starting transfers between devices, shifted(): lax.ppermute(array, axis, [(i, (i + by) % peers) for i in range(peers)])  6.26 us
    ppermute x1, waiting for transfers between devices, body(): partner = lax.ppermute(states, 'pair', [(0, 1), (1, 0)])  3.95 us
    unnamed x9, local copies, waits for them, and re-layouts  3.13 us
    ppermute x1, starting transfers between devices, body(): partner = lax.ppermute(states, 'pair', [(0, 1), (1, 0)])  2.22 us
    pallas_call x1, Pallas kernels, body(): pl.pallas_call(meet_kernel, out_shape=jax.ShapeDtypeStruct((8, 128), F32)...  1.74 us
  transfers between devices with their start and end apart: 4, of which 4 were waited for; matrix products, arithmetic and copies ran while one was open for 0% of the time, Pallas kernels for 0%

profile of v1, /device:TPU:0, one launch (start us, length us, event | category | flops | bytes accessed | tf_op | source)
XLA Modules:
  0.0 78.4 jit_solution(1771493885708263254)
XLA Ops:
  0.0 0.5 collective-permute-start
  0.5 5.8 %collective-permute-start.1 = (f32[32,32,128]{2,1,0:T(8,128)}, f32[32,32,128]{2,1,0:T(8,128)S(1)}, u32[]{:S(2)}, u32[]{:S(2)}) collective-permute-start(f32[32,32,128]{2,1,0:T(8,128)} %b1.1), channel_id=1, source_target_pairs={{0,26},{2,28},{4,30},{6,0},{8,2},{10,4},{12,6},{14,8},{16,10},{18,... | collective-permute-start | bytes 1572872 | tf_op jit(solution)/shard_map/ppermute | solution.py:16
  6.3 0.0 collective-permute-start.2
  6.3 0.0 copy-start.3
  6.3 0.7 copy-done.3
  7.0 8.5 %collective-permute-done.b0 = f32[32,32,128]{2,1,0:T(8,128)S(1)} collective-permute-done((f32[32,32,128]{2,1,0:T(8,128)}, f32[32,32,128]{2,1,0:T(8,128)S(1)}, u32[]{:S(2)}, u32[]{:S(2)}) %collective-permute-start) | collective-permute-done | bytes 524320 | tf_op jit(solution)/shard_map/ppermute | solution.py:16
  15.5 3.4 %collective-permute-done.1.b4 = f32[32,32,128]{2,1,0:T(8,128)S(1)} collective-permute-done((f32[32,32,128]{2,1,0:T(8,128)}, f32[32,32,128]{2,1,0:T(8,128)S(1)}, u32[]{:S(2)}, u32[]{:S(2)}) %collective-permute-start.1) | collective-permute-done | bytes 524320 | tf_op jit(solution)/shard_map/ppermute | solution.py:16
  18.9 10.4 %collective-permute-done.2.b6 = f32[32,32,128]{2,1,0:T(8,128)S(1)} collective-permute-done((f32[32,32,128]{2,1,0:T(8,128)}, f32[32,32,128]{2,1,0:T(8,128)S(1)}, u32[]{:S(2)}, u32[]{:S(2)}) %collective-permute-start.2) | collective-permute-done | bytes 524320 | tf_op jit(solution)/shard_map/ppermute | solution.py:16
  29.3 0.0 copy-start
  29.3 1.0 %copy-done = f32[32,32,128]{2,1,0:T(8,128)S(1)} copy-done((f32[32,32,128]{2,1,0:T(8,128)S(1)}, f32[32,32,128]{2,1,0:T(8,128)}, u32[]{:S(2)}) %copy-start) | copy-done | bytes 524312
  30.4 13.4 %half_chains.1.mine = f32[256,128]{1,0:T(8,128)S(1)} custom-call(s32[1]{0:T(128)} %bitcast.core_ref, f32[32,32,128]{2,1,0:T(8,128)S(1)} %collective-permute-done.b0, f32[32,32,128]{2,1,0:T(8,128)S(1)} %copy-done, f32[32,32,128]{2,1,0:T(8,128)S(1)} %collective-permute-done.1.b4, f32[32,32,128]{2,1,0:T(8,128)S(1)} %collective-permute-done.2.b6), custom_call_target="tpu_custom_call" | custom-call | tf_op jit(solution)/shard_map/half_chains/pallas_call | solution.py:177
  43.7 0.0 copy-start.1
  43.7 2.2 %collective-permute-start.3 = (f32[256,128]{1,0:T(8,128)S(1)}, f32[256,128]{1,0:T(8,128)S(1)}, u32[]{:S(2)}, u32[]{:S(2)}) collective-permute-start(f32[256,128]{1,0:T(8,128)S(1)} %half_chains.1.mine), channel_id=1, source_target_pairs={{0,1},{1,0},{2,3},{3,2},{4,5},{5,4},{6,7},{7,6},{8,9},{9,8},{10,11... | collective-permute-start | bytes 393224 | tf_op jit(solution)/shard_map/ppermute | solution.py:185
  46.0 4.0 %collective-permute-done.3.theirs = f32[256,128]{1,0:T(8,128)S(1)} collective-permute-done((f32[256,128]{1,0:T(8,128)S(1)}, f32[256,128]{1,0:T(8,128)S(1)}, u32[]{:S(2)}, u32[]{:S(2)}) %collective-permute-start.3) | collective-permute-done | bytes 131104 | tf_op jit(solution)/shard_map/ppermute | solution.py:185
  49.9 0.0 copy-done.1
  49.9 0.0 copy-start.2
  49.9 0.6 copy-done.2
  50.6 1.7 %meet.1 = f32[8,128]{1,0:T(8,128)} custom-call(f32[256,128]{1,0:T(8,128)} %copy-done.1, f32[256,128]{1,0:T(8,128)} %copy-done.2), custom_call_target="tpu_custom_call" | custom-call | tf_op jit(solution)/shard_map/meet/pallas_call | solution.py:186
  52.3 0.7 reshape.12
  53.1 21.5 %all-gather = f32[16,1,32]{2,1,0:T(1,128)S(1)} all-gather(f32[1,1,32]{2,1,0:T(1,128)S(1)} %reshape.12), channel_id=1, replica_groups=mesh['blk'=16,'pair'=2] {'blk'}, dimensions={0}, use_global_device_ids=true | all-gather | bytes 2176 | tf_op jit(solution)/shard_map/all_gather | solution.py:193
  74.6 0.5 broadcast.24
  75.1 0.7 reduce.3
  75.8 0.1 reshape.3
  75.8 0.8 %gather_fusion = f32[53]{0:T(128)S(1)} fusion(f32[512]{0:T(512)S(1)} %reshape.3, s32[1024]{0:T(1024)S(1)} %pad_clamp_fusion), kind=kCustom, calls=%fused_computation | custom fusion | bytes 636 | tf_op jit(solution)/shard_map/gather | solution.py:196
  76.6 0.6 slice.26
  77.2 1.1 %fusion.5 = f32[1,26]{1,0:T(1,128)} fusion(f32[53]{0:T(128)S(1)} %gather_fusion, f32[]{:T(128)} %bitcast.3), kind=kLoop, calls=%fused_computation.13 | loop fusion | flops 78 | bytes 316 | tf_op jit(solution)/shard_map/broadcast_in_dim | solution.py:199
  (3 shorter events, 0.0 us)
Async XLA Ops:
  0.0 15.5 %collective-permute-start = (f32[32,32,128]{2,1,0:T(8,128)}, f32[32,32,128]{2,1,0:T(8,128)S(1)}, u32[]{:S(2)}, u32[]{:S(2)}) collective-permute-start(f32[32,32,128]{2,1,0:T(8,128)} %b1.1), channel_id=1, source_target_pairs={{0,2},{2,4},{4,6},{6,8},{8,10},{10,12},{12,14},{14,16},{16,18},{18... | collective-permute-start | bytes 1572872 | tf_op jit(solution)/shard_map/ppermute | solution.py:16
  0.5 18.5 %collective-permute-start.1 = (f32[32,32,128]{2,1,0:T(8,128)}, f32[32,32,128]{2,1,0:T(8,128)S(1)}, u32[]{:S(2)}, u32[]{:S(2)}) collective-permute-start(f32[32,32,128]{2,1,0:T(8,128)} %b1.1), channel_id=1, source_target_pairs={{0,26},{2,28},{4,30},{6,0},{8,2},{10,4},{12,6},{14,8},{16,10},{18,... | collective-permute-start | bytes 1572872 | tf_op jit(solution)/shard_map/ppermute | solution.py:16
  6.3 23.1 %collective-permute-start.2 = (f32[32,32,128]{2,1,0:T(8,128)}, f32[32,32,128]{2,1,0:T(8,128)S(1)}, u32[]{:S(2)}, u32[]{:S(2)}) collective-permute-start(f32[32,32,128]{2,1,0:T(8,128)} %b1.1), channel_id=1, source_target_pairs={{0,22},{2,24},{4,26},{6,28},{8,30},{10,0},{12,2},{14,4},{16,6},{18... | collective-permute-start | bytes 1572872 | tf_op jit(solution)/shard_map/ppermute | solution.py:16
  6.3 0.7 copy-start.3
  29.3 1.0 %copy-start = (f32[32,32,128]{2,1,0:T(8,128)S(1)}, f32[32,32,128]{2,1,0:T(8,128)}, u32[]{:S(2)}) copy-start(f32[32,32,128]{2,1,0:T(8,128)} %b1.1) | copy-start | bytes 1572868
  43.7 6.2 %copy-start.1 = (f32[256,128]{1,0:T(8,128)}, f32[256,128]{1,0:T(8,128)S(1)}, u32[]{:S(2)}) copy-start(f32[256,128]{1,0:T(8,128)S(1)} %half_chains.1.mine) | copy-start | bytes 393220
  43.7 6.2 %collective-permute-start.3 = (f32[256,128]{1,0:T(8,128)S(1)}, f32[256,128]{1,0:T(8,128)S(1)}, u32[]{:S(2)}, u32[]{:S(2)}) collective-permute-start(f32[256,128]{1,0:T(8,128)S(1)} %half_chains.1.mine), channel_id=1, source_target_pairs={{0,1},{1,0},{2,3},{3,2},{4,5},{5,4},{6,7},{7,6},{8,9},{9,8},{10,11... | collective-permute-start | bytes 393224 | tf_op jit(solution)/shard_map/ppermute | solution.py:185
  49.9 0.7 copy-start.2

commit v2 on v0

v2 whole, which is shorter than its diff:
```python
import functools

import jax
import jax.numpy as jnp
from jax import lax
from jax.experimental import pallas as pl
from jax.experimental.pallas import tpu as pltpu
from jax.sharding import PartitionSpec as P

REACH = 6
CHUNKS = (12, 12, 8)
BF16, F32 = jnp.bfloat16, jnp.float32
VMEM = pl.BlockSpec(memory_space=pltpu.VMEM)
SMEM = pl.BlockSpec(memory_space=pltpu.SMEM)


def move(array, source):
    peers = lax.axis_size("blk")
    chips = peers // 2
    pairs = []
    for d in range(peers):
        chip, core = source(d // 2, d % 2)
        pairs.append(((chip % chips) * 2 + core, d))
    return lax.ppermute(array, "blk", pairs)


def split(x):
    high = x.astype(BF16)
    return high, (x - high.astype(F32)).astype(BF16)


def product(left, right, across=False):
    dims = (((1,), (1 if across else 0,)), ((), ()))
    return lax.dot_general(left, right, dims, preferred_element_type=F32)


def lane_slot(shape):
    return lax.broadcasted_iota(jnp.int32, shape, 1) // 32


def interleave(first, second):
    even = lane_slot(first.shape) % 2 == 0
    return (
        jnp.where(even, first, pltpu.roll(second, 32, 1)),
        jnp.where(even, pltpu.roll(first, 96, 1), second),
    )


def far_weights(tiles, flip):
    parts = []
    for half in zip(*[split(t) for t in tiles]):
        slot = lane_slot(half[0].shape)
        zero = jnp.zeros_like(half[0])
        placed = [[jnp.where(slot == k, h, zero) for h in half] for k in range(4)]
        if flip:
            parts.append(jnp.concatenate([placed[k][p] for p in range(2) for k in range(4)], 0))
        else:
            parts.append(jnp.concatenate([jnp.concatenate(placed[k], 1) for k in range(4)], 0))
    high, low = parts
    return jnp.concatenate([high, high], 1 if flip else 0), low


def near_turned(tiles):
    stack = jnp.concatenate([tiles[0], tiles[1], tiles[0], tiles[1]], 0).T
    return [stack[32 * k : 32 * k + 32] for k in (0, 2, 1, 3)]


def near_plain(tile):
    twice = pltpu.roll(tile, 64, 1)
    lower = lane_slot(tile.shape) < 2
    return [jnp.where(lower, tile, twice), jnp.where(lower, twice, tile)]


def advance(state, near, far, flip):
    double, low = far_weights(far, flip)
    high, rest = split(state)
    inner = product(jnp.concatenate([high, rest], 1), double, flip) + product(high, low, flip)
    h0, l0 = split(inner[:, :128])
    h1, l1 = split(inner[:, 128:])
    results = []
    for k, tile in enumerate(near):
        rows = slice(32 * k, 32 * k + 32)
        weights = jnp.concatenate([h0[rows], h1[rows], l0[rows], l1[rows]], 0)
        both = product(jnp.concatenate(split(tile), 0), weights)
        results.append(both[:32] + both[32:])
    return jnp.concatenate(results, 0)


def corner(shape):
    row = lax.broadcasted_iota(jnp.int32, shape, 0) % 32
    lane = lax.broadcasted_iota(jnp.int32, shape, 1) % 32
    return jnp.where((row == 0) & (lane == 0), 1.0, 0.0)


def on_each_side(side_ref, run):
    for side in range(2):
        pl.when(side_ref[0] == side)(functools.partial(run, side == 1))


def wide_kernel(start, side_ref, own, sibling, first, second, other, *rest):
    out = rest[-1]
    sites, count = own.shape[0], first.shape[0]

    def run(flip):
        def step(index, state):
            whole = sites - 1 - start - index if flip else start + index
            part = count - 1 - index if flip else index
            far = interleave(first[part], second[part])
            if flip:
                near = [n for t in (own[whole], sibling[whole], other[part], first[part], second[part])
                        for n in near_plain(t)]
            else:
                extra = other[part]
                near = (
                    near_turned(interleave(own[whole], sibling[whole]))
                    + near_turned(interleave(extra, extra))[:2]
                    + near_turned(far)
                )
            return advance(state, near, far, flip)

        begin = corner(out.shape) if start == 0 else rest[0][...]
        out[...] = lax.fori_loop(0, count, step, begin, unroll=2)

    on_each_side(side_ref, run)


def narrow_kernel(side_ref, own, sibling, out):
    sites = own.shape[0]

    def run(flip):
        def step(index, state):
            site = sites - 1 - index if flip else index
            far = interleave(own[site], sibling[site])
            near = near_plain(own[site]) if flip else near_turned(far)[:2]
            return advance(state, near, far, flip)

        out[...] = lax.fori_loop(0, sites, step, corner(out.shape), unroll=4)

    on_each_side(side_ref, run)


def meet_kernel(wide, narrow, far_wide, far_narrow, out):
    units = [
        jnp.sum((a[...] * b[...]).reshape(-1, 32, 128), 1)
        for a, b in ((wide, far_wide), (narrow, far_narrow))
    ]
    units = jnp.concatenate(units + [jnp.zeros((4, 128), F32)], 0)
    row = lax.broadcasted_iota(jnp.int32, (8, 128), 0)
    chosen = jnp.where(row == lane_slot((8, 128)), 1.0, 0.0)
    found = lax.dot_general(
        chosen, units, (((1,), (1,)), ((), ())), precision=lax.Precision.HIGHEST, preferred_element_type=F32
    )
    out[...] = jnp.concatenate([found, jnp.zeros((8, 112), F32)], 1)


def pick_kernel(spot_ref, *refs):
    *tiles, out = refs
    joined = tiles[0][...]
    for k, tile in enumerate(tiles[1:], 1):
        joined += pltpu.roll(tile[...], 16 * k, 1)
    unit = lax.broadcasted_iota(jnp.int32, (128, 128), 0)
    slot = lax.broadcasted_iota(jnp.int32, (8, 128), 0)
    values = []
    for k in range(3):
        spot = spot_ref[pl.ds(k, 1), :]
        chosen = jnp.where(unit == spot // 8, 1.0, 0.0)
        found = jnp.dot(joined, chosen, precision=lax.Precision.HIGHEST, preferred_element_type=F32)
        values.append(jnp.sum(jnp.where(slot == spot % 8, found, 0.0), 0, keepdims=True))
    tile, remote, own = values
    width = out.shape[1]
    out[...] = (tile * tile / (own * remote))[:, :width]


def rosters(core):
    mine, theirs = ("A0", "A1"), ("Z1", "Z0")
    if core == 1:
        mine, theirs = theirs, mine
    own, sibling = f"O{core}", f"O{1 - core}"
    wide = [own, sibling, theirs[1], mine[0], mine[1]]
    return (wide, mine), ([own], (own, sibling))


def find(core, near, far):
    base = 0
    for rows, lanes in rosters(core):
        for a in range(2):
            for left, right in ((near, far), (far, near)):
                if left in rows and right in lanes:
                    unit, slot = base + 2 * rows.index(left), lanes.index(right)
                    if left == near:
                        return lambda n, m: (unit + n, slot + 2 * m)
                    return lambda n, m: (unit + m, slot + 2 * n)
        base += 2 * len(rows)
    return None


def spot_table(core, samp, band):
    views = [(role, (k, k + 1) if core == 0 else (k + 1, k)) for k, role in ((0, "O"), (2, "A"), (4, "Z"))]
    shift = {"O": 0, "A": -1, "Z": 2}

    def place(offset):
        goal = core + offset
        chip, lane = goal // 2, goal % 2
        for role, messages in views:
            for name, gap in shift.items():
                if gap - shift[role] == chip:
                    for k, message in enumerate(messages):
                        got = find(k, f"{role}{core}", f"{name}{lane}")
                        if got:
                            return message, got
        raise ValueError(offset)

    def norm(offset):
        goal = core + offset
        chip, lane = goal // 2, goal % 2
        for role, messages in views:
            for name, gap in shift.items():
                if gap - shift[role] == chip:
                    for k, message in enumerate(messages):
                        got = find(k, f"{name}{lane}", f"{name}{lane}")
                        if got:
                            return message, got
        raise ValueError(offset)

    def code(where, n, m):
        message, got = where
        unit, slot = got(n, m)
        return 8 * (16 * message + unit) + slot

    offsets = range(-band, band + 1)
    table = []
    for n in range(samp):
        tile = [code(place(o), n, m) for o in offsets for m in range(samp)]
        remote = [code(norm(o), m, m) for o in offsets for m in range(samp)]
        own = [code(norm(0), n, n)] * len(tile)
        rows = [r + r[:1] * (128 - len(r)) for r in (tile, remote, own)]
        table.append(rows + rows[:1] * 5)
    return table


def call(kernel, shape, *args, name):
    return pl.pallas_call(
        kernel,
        out_shape=jax.ShapeDtypeStruct(shape, F32),
        in_specs=[SMEM if a.ndim == 1 else VMEM for a in args],
        out_specs=VMEM,
        compiler_params=pltpu.CompilerParams(vmem_limit_bytes=40 * 2**20),
        name=name,
    )(*args)


def body(mps):
    sites, chi = mps.shape[:2]
    samp = mps.shape[2] // (2 * chi)
    blocks = lax.axis_size("blk")
    band = min(REACH, (blocks - 1) // 2)
    side = lax.axis_index("pair")
    flag = side[None].astype(jnp.int32)

    starts = [sum(CHUNKS[:k]) for k in range(len(CHUNKS))]
    firsts, seconds = [], []
    for start, count in zip(starts, CHUNKS):
        piece = lax.dynamic_slice_in_dim(mps, jnp.where(side == 0, start, sites - start - count), count, 0)
        seconds.append(move(piece, lambda chip, core: (chip - 1, 1) if core == 0 else (chip + 2, 0)))
        firsts.append(move(piece, lambda chip, core: (chip - 1, 0) if core == 0 else (chip + 2, 1)))
    across = lambda chip, core: (chip, 1 - core)
    sibling = move(mps, across)
    narrow = call(narrow_kernel, (64, 128), flag, mps, sibling, name="own_chains")
    swap = [(0, 1), (1, 0)]
    far_narrow = lax.ppermute(narrow, "pair", swap)
    wide = ()
    for start, first, second in zip(starts, firsts, seconds):
        other = move(second, across)
        wide = (
            call(functools.partial(wide_kernel, start), (320, 128), flag, mps, sibling, first, second, other,
                 *wide, name="half_chains"),
        )
    (wide,) = wide
    far_wide = lax.ppermute(wide, "pair", swap)
    tile = call(meet_kernel, (8, 128), wide, narrow, far_wide, far_narrow, name="meet")
    tiles = [tile, move(tile, across)]
    for gap in (1, -2):
        straight = move(tile, lambda chip, core: (chip + gap, core))
        crossed = move(tile, lambda chip, core: (chip + gap, 1 - core))
        tiles += [straight, crossed]
    spots = jnp.asarray([spot_table(core, samp, band) for core in range(2)], jnp.int32)
    spot = spots[lax.axis_index("blk") % 2, side]
    return call(pick_kernel, (1, (2 * band + 1) * samp), spot, *tiles, name="pick")


def solution(mesh):
    in_specs = (P("pair", None, "blk"),)
    out_specs = P(("blk", "pair"), None)
    return jax.shard_map(body, mesh=mesh, in_specs=in_specs, out_specs=out_specs, check_vma=False)
```

time: 438 us -> 68 us (0.16)
  matrix products: 226 us -> 0 us
  local copies, waits for them, and re-layouts: 79.7 us -> 1.75 us
  other arithmetic: 42.6 us -> 0 us
  waiting for transfers between devices: 54 us -> 18.5 us
  Pallas kernels: 0 us -> 27.6 us
  loops' own time: 6.97 us -> 0 us
  starting transfers between devices: 26.2 us -> 19.9 us
    dot_general x832 -> x0, matrix products: 226 us -> none  [the longest x416 118 us: advance(): jnp.einsum('xnpz,nmxpq->nmzq', own_site, inner, precision=lax.Precision.H...]
    ppermute x14 -> x17, waiting for transfers between devices: 54 us -> 18.5 us  [the longest x15 16 us: move(): return lax.ppermute(array, 'blk', pairs)]
    slice x26 -> x0, local copies, waits for them, and re-layouts: 30.4 us -> none  [the longest x24 30.3 us: contract(): final, _ = lax.scan(advance, start, (own_tensors, far_tensors), unroll=8)]
    pallas_call x0 -> x6, Pallas kernels: none -> 27.6 us  [call(): pl.pallas_call(kernel, out_shape=jax.ShapeDtypeStruct(shape, F32), in_spe...]
    reshape x10 -> x0, local copies, waits for them, and re-layouts: 27.5 us -> none  [the longest x6 18 us: contract(): final, _ = lax.scan(advance, start, (own_tensors, far_tensors), unroll=8)]
    another operation x30 -> x0, other arithmetic: 20.1 us -> none
    scatter x12 -> x0, other arithmetic: 19.9 us -> none  [the longest x6 16 us: advance_sites(): passing = passing.at[offset - 1].set(contract(moving, moving, chi, samp))]
    while x21 -> x0, local copies, waits for them, and re-layouts: 9.18 us -> none
  transfers between devices with their start and end apart: 14 -> 17, of which waited for: 7 -> 6; matrix products, arithmetic and copies ran while one was open for 9% -> 3% of each run, Pallas kernels for 0% -> 33%
where the time goes in v2:
time: 68 us; the launch traced here: 67.8 us
  Pallas kernels  27.6 us (41%)
  starting transfers between devices  19.9 us (29%)
  waiting for transfers between devices  18.5 us (27%)
  local copies, waits for them, and re-layouts  1.75 us (3%)
    pallas_call x6, Pallas kernels, call(): pl.pallas_call(kernel, out_shape=jax.ShapeDtypeStruct(shape, F32), in_spe...  27.6 us
    ppermute x15, starting transfers between devices, move(): return lax.ppermute(array, 'blk', pairs)  16.5 us
    ppermute x15, waiting for transfers between devices, move(): return lax.ppermute(array, 'blk', pairs)  16 us
    ppermute x1, waiting for transfers between devices, body(): far_narrow = lax.ppermute(narrow, 'pair', swap)  2.48 us
    ppermute x1, starting transfers between devices, body(): far_wide = lax.ppermute(wide, 'pair', swap)  1.85 us
    ppermute x1, starting transfers between devices, body(): far_narrow = lax.ppermute(narrow, 'pair', swap)  1.46 us
  transfers between devices with their start and end apart: 17, of which 6 were waited for; matrix products, arithmetic and copies ran while one was open for 3% of the time, Pallas kernels for 33%

profile of v2, /device:TPU:0, one launch (start us, length us, event | category | flops | bytes accessed | tf_op | source)
XLA Modules:
  0.0 67.8 jit_solution(613593589656842277)
XLA Ops:
  0.0 0.5 collective-permute-start
  0.5 1.0 %constant_dynamic-slice_fusion = (f32[12,32,128]{2,1,0:T(8,128)S(1)}, f32[12,32,128]{2,1,0:T(8,128)S(1)}) fusion(f32[32,32,128]{2,1,0:T(8,128)} %own.7, s32[]{:T(128)S(6)} %select_n.31, s32[]{:T(128)S(6)} %select_n.30), kind=kLoop, calls=%fused_computation.1 | loop fusion | bytes 786440 | tf_op jit(solution)/shard_map/dynamic_slice | solution.py:263
  1.5 4.8 %collective-permute-start.8 = (f32[12,32,128]{2,1,0:T(8,128)S(1)}, f32[12,32,128]{2,1,0:T(8,128)S(1)}, u32[]{:S(2)}, u32[]{:S(2)}) collective-permute-start(f32[12,32,128]{2,1,0:T(8,128)S(1)} %get-tuple-element.5), channel_id=1, source_target_pairs={{30,0},{8,2},{2,4},{12,6},{6,8},{16,10},{10,12},{20,14},{14,16},{2... | collective-permute-start | bytes 589832 | tf_op jit(solution)/shard_map/ppermute | solution.py:24
  6.3 1.2 %collective-permute-start.5 = (f32[12,32,128]{2,1,0:T(8,128)S(1)}, f32[12,32,128]{2,1,0:T(8,128)S(1)}, u32[]{:S(2)}, u32[]{:S(2)}) collective-permute-start(f32[12,32,128]{2,1,0:T(8,128)S(1)} %get-tuple-element.6), channel_id=1, source_target_pairs={{30,0},{8,2},{2,4},{12,6},{6,8},{16,10},{10,12},{20,14},{14,16},{2... | collective-permute-start | bytes 589832 | tf_op jit(solution)/shard_map/ppermute | solution.py:24
  7.4 0.6 collective-permute-start.2
  8.0 3.3 %collective-permute-start.7 = (f32[12,32,128]{2,1,0:T(8,128)S(1)}, f32[12,32,128]{2,1,0:T(8,128)S(1)}, u32[]{:S(2)}, u32[]{:S(2)}) collective-permute-start(f32[12,32,128]{2,1,0:T(8,128)S(1)} %get-tuple-element.5), channel_id=1, source_target_pairs={{28,0},{10,2},{0,4},{14,6},{4,8},{18,10},{8,12},{22,14},{12,16},{2... | collective-permute-start | bytes 589832 | tf_op jit(solution)/shard_map/ppermute | solution.py:24
  11.3 0.6 collective-permute-done.8.second
  12.0 0.0 collective-permute-start.9
  12.0 7.0 %collective-permute-done.2.second = f32[8,32,128]{2,1,0:T(8,128)S(1)} collective-permute-done((f32[8,32,128]{2,1,0:T(8,128)S(1)}, f32[8,32,128]{2,1,0:T(8,128)S(1)}, u32[]{:S(2)}, u32[]{:S(2)}) %collective-permute-start.2) | collective-permute-done | bytes 131104 | tf_op jit(solution)/shard_map/ppermute | solution.py:24
  19.0 0.6 collective-permute-start.4
  19.6 0.0 collective-permute-done.5.second
  19.6 0.0 collective-permute-start.6
  19.6 4.3 %collective-permute-done.7.first = f32[12,32,128]{2,1,0:T(8,128)S(1)} collective-permute-done((f32[12,32,128]{2,1,0:T(8,128)S(1)}, f32[12,32,128]{2,1,0:T(8,128)S(1)}, u32[]{:S(2)}, u32[]{:S(2)}) %collective-permute-start.7) | collective-permute-done | bytes 196640 | tf_op jit(solution)/shard_map/ppermute | solution.py:24
  23.9 0.0 collective-permute-start.1
  23.9 0.0 collective-permute-done.9.other
  23.9 1.9 %collective-permute-start.3 = (f32[8,32,128]{2,1,0:T(8,128)S(1)}, f32[8,32,128]{2,1,0:T(8,128)S(1)}, u32[]{:S(2)}, u32[]{:S(2)}) collective-permute-start(f32[8,32,128]{2,1,0:T(8,128)S(1)} %collective-permute-done.2.second), channel_id=1, source_target_pairs={{2,0},{0,2},{6,4},{4,6},{10,8},{8,10},{14,12},{12,14},{18,16},{16,... | collective-permute-start | bytes 393224 | tf_op jit(solution)/shard_map/ppermute | solution.py:24
  25.8 6.1 %half_chains.3.rest_0_ = f32[320,128]{1,0:T(8,128)S(1)} custom-call(s32[1]{0:T(128)} %bitcast.1.side_ref, f32[32,32,128]{2,1,0:T(8,128)S(1)} %copy-done, f32[32,32,128]{2,1,0:T(8,128)S(1)} %collective-permute-done.sibling, f32[12,32,128]{2,1,0:T(8,128)S(1)} %collective-permute-done.7.first, f32[12,32,128]{2,1,0:T(8,128)S(1)} %collective-permute-done.8.second, ...), custom_call_target="tpu_custom_call" | custom-call | tf_op jit(solution)/shard_map/half_chains/pallas_call | solution.py:242
  32.0 6.2 %half_chains.4.rest_0_ = f32[320,128]{1,0:T(8,128)S(1)} custom-call(s32[1]{0:T(128)} %bitcast.1.side_ref, f32[32,32,128]{2,1,0:T(8,128)S(1)} %copy-done, f32[32,32,128]{2,1,0:T(8,128)S(1)} %collective-permute-done.sibling, f32[12,32,128]{2,1,0:T(8,128)S(1)} %collective-permute-done.4.first, f32[12,32,128]{2,1,0:T(8,128)S(1)} %collective-permute-done.5.second, ...), custom_call_target="tpu_custom_call" | custom-call | tf_op jit(solution)/shard_map/half_chains/pallas_call | solution.py:242
  38.2 4.1 %half_chains.5.wide = f32[320,128]{1,0:T(8,128)S(1)} custom-call(s32[1]{0:T(128)} %bitcast.1.side_ref, f32[32,32,128]{2,1,0:T(8,128)S(1)} %copy-done, f32[32,32,128]{2,1,0:T(8,128)S(1)} %collective-permute-done.sibling, f32[8,32,128]{2,1,0:T(8,128)S(1)} %collective-permute-done.1.first, f32[8,32,128]{2,1,0:T(8,128)S(1)} %collective-permute-done.2.second, ...), custom_call_target="tpu_custom_call" | custom-call | tf_op jit(solution)/shard_map/half_chains/pallas_call | solution.py:242
  42.3 1.8 %collective-permute-start.10 = (f32[320,128]{1,0:T(8,128)S(1)}, f32[320,128]{1,0:T(8,128)S(1)}, u32[]{:S(2)}, u32[]{:S(2)}) collective-permute-start(f32[320,128]{1,0:T(8,128)S(1)} %half_chains.5.wide), channel_id=1, source_target_pairs={{0,1},{1,0},{2,3},{3,2},{4,5},{5,4},{6,7},{7,6},{8,9},{9,8},{10,11... | collective-permute-start | bytes 491528 | tf_op jit(solution)/shard_map/ppermute | solution.py:279
  44.1 10.2 %own_chains.1.narrow = f32[64,128]{1,0:T(8,128)S(1)} custom-call(s32[1]{0:T(128)} %bitcast.1.side_ref, f32[32,32,128]{2,1,0:T(8,128)S(1)} %copy-done, f32[32,32,128]{2,1,0:T(8,128)S(1)} %collective-permute-done.sibling), custom_call_target="tpu_custom_call" | custom-call | tf_op jit(solution)/shard_map/own_chains/pallas_call | solution.py:242
  54.4 1.5 %collective-permute-start.11 = (f32[64,128]{1,0:T(8,128)S(1)}, f32[64,128]{1,0:T(8,128)S(1)}, u32[]{:S(2)}, u32[]{:S(2)}) collective-permute-start(f32[64,128]{1,0:T(8,128)S(1)} %own_chains.1.narrow), channel_id=1, source_target_pairs={{0,1},{1,0},{2,3},{3,2},{4,5},{5,4},{6,7},{7,6},{8,9},{9,8},{10,11... | collective-permute-start | bytes 98312 | tf_op jit(solution)/shard_map/ppermute | solution.py:270
  55.8 2.5 %collective-permute-done.11.far_narrow = f32[64,128]{1,0:T(8,128)S(1)} collective-permute-done((f32[64,128]{1,0:T(8,128)S(1)}, f32[64,128]{1,0:T(8,128)S(1)}, u32[]{:S(2)}, u32[]{:S(2)}) %collective-permute-start.11) | collective-permute-done | bytes 32800 | tf_op jit(solution)/shard_map/ppermute | solution.py:270
  58.3 0.2 meet.1.refs_0_
  58.5 2.9 %collective-permute-start.13 = (f32[8,128]{1,0:T(8,128)S(1)}, f32[8,128]{1,0:T(8,128)S(1)}, u32[]{:S(2)}, u32[]{:S(2)}) collective-permute-start(f32[8,128]{1,0:T(8,128)S(1)} %meet.1.refs_0_), channel_id=1, source_target_pairs={{4,0},{6,2},{8,4},{10,6},{12,8},{14,10},{16,12},{18,14},{20,16},{2... | collective-permute-start | bytes 12296 | tf_op jit(solution)/shard_map/ppermute | solution.py:24
  61.4 0.1 collective-permute-start.14
  61.5 0.3 collective-permute-start.15
  61.8 0.5 collective-permute-start.16
  62.3 0.7 %dynamic-slice_bitcast_fusion.spot_ref = s32[8,128]{1,0:T(8,128)S(1)} fusion(s32[2,2,8,128]{3,2,1,0:T(8,128)} %constant.36.clone, s32[]{:T(128)S(6)} %select_n.27, s32[]{:T(128)S(6)} %select_n.28), kind=kLoop, calls=%fused_computation | loop fusion | bytes 8200 | tf_op jit(solution)/shard_map/squeeze | solution.py:287
  62.9 1.5 %collective-permute-done.14.refs_3_ = f32[8,128]{1,0:T(8,128)S(1)} collective-permute-done((f32[8,128]{1,0:T(8,128)S(1)}, f32[8,128]{1,0:T(8,128)S(1)}, u32[]{:S(2)}, u32[]{:S(2)}) %collective-permute-start.14) | collective-permute-done | bytes 4128 | tf_op jit(solution)/shard_map/ppermute | solution.py:24
  64.4 2.5 %collective-permute-done.15.refs_4_ = f32[8,128]{1,0:T(8,128)S(1)} collective-permute-done((f32[8,128]{1,0:T(8,128)S(1)}, f32[8,128]{1,0:T(8,128)S(1)}, u32[]{:S(2)}, u32[]{:S(2)}) %collective-permute-start.15) | collective-permute-done | bytes 4128 | tf_op jit(solution)/shard_map/ppermute | solution.py:24
  66.9 0.9 %pick.1 = f32[1,26]{1,0:T(1,128)} custom-call(s32[8,128]{1,0:T(8,128)S(1)} %dynamic-slice_bitcast_fusion.spot_ref, f32[8,128]{1,0:T(8,128)S(1)} %meet.1.refs_0_, f32[8,128]{1,0:T(8,128)S(1)} %collective-permute-done.12.refs_1_, f32[8,128]{1,0:T(8,128)S(1)} %collective-permute-done.13.refs_2_, f32[8,128]{1,0:T(8,128)S(1)} %collective-permute-done.14.refs_3_, ...), custom_call_target="tpu_custom_call" | custom-call | tf_op jit(solution)/shard_map/pick/pallas_call | solution.py:242
  (13 shorter events, 0.0 us)
Async XLA Ops:
  0.0 7.4 %copy-start = (f32[32,32,128]{2,1,0:T(8,128)S(1)}, f32[32,32,128]{2,1,0:T(8,128)}, u32[]{:S(2)}) copy-start(f32[32,32,128]{2,1,0:T(8,128)} %own.7) | copy-start | bytes 1572868
  0.0 25.8 %collective-permute-start = (f32[32,32,128]{2,1,0:T(8,128)}, f32[32,32,128]{2,1,0:T(8,128)S(1)}, u32[]{:S(2)}, u32[]{:S(2)}) collective-permute-start(f32[32,32,128]{2,1,0:T(8,128)} %own.7), channel_id=1, source_target_pairs={{2,0},{0,2},{6,4},{4,6},{10,8},{8,10},{14,12},{12,14},{18,16},{16,... | collective-permute-start | bytes 1572872 | tf_op jit(solution)/shard_map/ppermute | solution.py:24
  1.5 10.5 %collective-permute-start.8 = (f32[12,32,128]{2,1,0:T(8,128)S(1)}, f32[12,32,128]{2,1,0:T(8,128)S(1)}, u32[]{:S(2)}, u32[]{:S(2)}) collective-permute-start(f32[12,32,128]{2,1,0:T(8,128)S(1)} %get-tuple-element.5), channel_id=1, source_target_pairs={{30,0},{8,2},{2,4},{12,6},{6,8},{16,10},{10,12},{20,14},{14,16},{2... | collective-permute-start | bytes 589832 | tf_op jit(solution)/shard_map/ppermute | solution.py:24
  6.3 13.3 %collective-permute-start.5 = (f32[12,32,128]{2,1,0:T(8,128)S(1)}, f32[12,32,128]{2,1,0:T(8,128)S(1)}, u32[]{:S(2)}, u32[]{:S(2)}) collective-permute-start(f32[12,32,128]{2,1,0:T(8,128)S(1)} %get-tuple-element.6), channel_id=1, source_target_pairs={{30,0},{8,2},{2,4},{12,6},{6,8},{16,10},{10,12},{20,14},{14,16},{2... | collective-permute-start | bytes 589832 | tf_op jit(solution)/shard_map/ppermute | solution.py:24
  7.4 11.5 %collective-permute-start.2 = (f32[8,32,128]{2,1,0:T(8,128)S(1)}, f32[8,32,128]{2,1,0:T(8,128)S(1)}, u32[]{:S(2)}, u32[]{:S(2)}) collective-permute-start(f32[8,32,128]{2,1,0:T(8,128)S(1)} %constant_dynamic-slice_fusion.2), channel_id=1, source_target_pairs={{30,0},{8,2},{2,4},{12,6},{6,8},{16,10},{10,12},{20,14},{14,16},{2... | collective-permute-start | bytes 393224 | tf_op jit(solution)/shard_map/ppermute | solution.py:24
  8.0 15.9 %collective-permute-start.7 = (f32[12,32,128]{2,1,0:T(8,128)S(1)}, f32[12,32,128]{2,1,0:T(8,128)S(1)}, u32[]{:S(2)}, u32[]{:S(2)}) collective-permute-start(f32[12,32,128]{2,1,0:T(8,128)S(1)} %get-tuple-element.5), channel_id=1, source_target_pairs={{28,0},{10,2},{0,4},{14,6},{4,8},{18,10},{8,12},{22,14},{12,16},{2... | collective-permute-start | bytes 589832 | tf_op jit(solution)/shard_map/ppermute | solution.py:24
  12.0 11.9 %collective-permute-start.9 = (f32[12,32,128]{2,1,0:T(8,128)S(1)}, f32[12,32,128]{2,1,0:T(8,128)S(1)}, u32[]{:S(2)}, u32[]{:S(2)}) collective-permute-start(f32[12,32,128]{2,1,0:T(8,128)S(1)} %collective-permute-done.8.second), channel_id=1, source_target_pairs={{2,0},{0,2},{6,4},{4,6},{10,8},{8,10},{14,12},{12,14},{18,16},{16,... | collective-permute-start | bytes 589832 | tf_op jit(solution)/shard_map/ppermute | solution.py:24
  19.0 13.0 %collective-permute-start.4 = (f32[12,32,128]{2,1,0:T(8,128)S(1)}, f32[12,32,128]{2,1,0:T(8,128)S(1)}, u32[]{:S(2)}, u32[]{:S(2)}) collective-permute-start(f32[12,32,128]{2,1,0:T(8,128)S(1)} %get-tuple-element.6), channel_id=1, source_target_pairs={{28,0},{10,2},{0,4},{14,6},{4,8},{18,10},{8,12},{22,14},{12,16},{2... | collective-permute-start | bytes 589832 | tf_op jit(solution)/shard_map/ppermute | solution.py:24
  19.6 12.4 %collective-permute-start.6 = (f32[12,32,128]{2,1,0:T(8,128)S(1)}, f32[12,32,128]{2,1,0:T(8,128)S(1)}, u32[]{:S(2)}, u32[]{:S(2)}) collective-permute-start(f32[12,32,128]{2,1,0:T(8,128)S(1)} %collective-permute-done.5.second), channel_id=1, source_target_pairs={{2,0},{0,2},{6,4},{4,6},{10,8},{8,10},{14,12},{12,14},{18,16},{16,... | collective-permute-start | bytes 589832 | tf_op jit(solution)/shard_map/ppermute | solution.py:24
  23.9 14.2 %collective-permute-start.1 = (f32[8,32,128]{2,1,0:T(8,128)S(1)}, f32[8,32,128]{2,1,0:T(8,128)S(1)}, u32[]{:S(2)}, u32[]{:S(2)}) collective-permute-start(f32[8,32,128]{2,1,0:T(8,128)S(1)} %constant_dynamic-slice_fusion.2), channel_id=1, source_target_pairs={{28,0},{10,2},{0,4},{14,6},{4,8},{18,10},{8,12},{22,14},{12,16},{2... | collective-permute-start | bytes 393224 | tf_op jit(solution)/shard_map/ppermute | solution.py:24
  23.9 14.3 %collective-permute-start.3 = (f32[8,32,128]{2,1,0:T(8,128)S(1)}, f32[8,32,128]{2,1,0:T(8,128)S(1)}, u32[]{:S(2)}, u32[]{:S(2)}) collective-permute-start(f32[8,32,128]{2,1,0:T(8,128)S(1)} %collective-permute-done.2.second), channel_id=1, source_target_pairs={{2,0},{0,2},{6,4},{4,6},{10,8},{8,10},{14,12},{12,14},{18,16},{16,... | collective-permute-start | bytes 393224 | tf_op jit(solution)/shard_map/ppermute | solution.py:24
  42.3 16.0 %collective-permute-start.10 = (f32[320,128]{1,0:T(8,128)S(1)}, f32[320,128]{1,0:T(8,128)S(1)}, u32[]{:S(2)}, u32[]{:S(2)}) collective-permute-start(f32[320,128]{1,0:T(8,128)S(1)} %half_chains.5.wide), channel_id=1, source_target_pairs={{0,1},{1,0},{2,3},{3,2},{4,5},{5,4},{6,7},{7,6},{8,9},{9,8},{10,11... | collective-permute-start | bytes 491528 | tf_op jit(solution)/shard_map/ppermute | solution.py:279
  54.4 3.9 %collective-permute-start.11 = (f32[64,128]{1,0:T(8,128)S(1)}, f32[64,128]{1,0:T(8,128)S(1)}, u32[]{:S(2)}, u32[]{:S(2)}) collective-permute-start(f32[64,128]{1,0:T(8,128)S(1)} %own_chains.1.narrow), channel_id=1, source_target_pairs={{0,1},{1,0},{2,3},{3,2},{4,5},{5,4},{6,7},{7,6},{8,9},{9,8},{10,11... | collective-permute-start | bytes 98312 | tf_op jit(solution)/shard_map/ppermute | solution.py:270
  58.4 4.5 %collective-permute-start.12 = (f32[8,128]{1,0:T(8,128)S(1)}, f32[8,128]{1,0:T(8,128)S(1)}, u32[]{:S(2)}, u32[]{:S(2)}) collective-permute-start(f32[8,128]{1,0:T(8,128)S(1)} %meet.1.refs_0_), channel_id=1, source_target_pairs={{2,0},{0,2},{6,4},{4,6},{10,8},{8,10},{14,12},{12,14},{18,16},{16,... | collective-permute-start | bytes 12296 | tf_op jit(solution)/shard_map/ppermute | solution.py:24
  58.5 4.5 %collective-permute-start.13 = (f32[8,128]{1,0:T(8,128)S(1)}, f32[8,128]{1,0:T(8,128)S(1)}, u32[]{:S(2)}, u32[]{:S(2)}) collective-permute-start(f32[8,128]{1,0:T(8,128)S(1)} %meet.1.refs_0_), channel_id=1, source_target_pairs={{4,0},{6,2},{8,4},{10,6},{12,8},{14,10},{16,12},{18,14},{20,16},{2... | collective-permute-start | bytes 12296 | tf_op jit(solution)/shard_map/ppermute | solution.py:24
  61.4 3.0 %collective-permute-start.14 = (f32[8,128]{1,0:T(8,128)S(1)}, f32[8,128]{1,0:T(8,128)S(1)}, u32[]{:S(2)}, u32[]{:S(2)}) collective-permute-start(f32[8,128]{1,0:T(8,128)S(1)} %meet.1.refs_0_), channel_id=1, source_target_pairs={{6,0},{4,2},{10,4},{8,6},{14,8},{12,10},{18,12},{16,14},{22,16},{2... | collective-permute-start | bytes 12296 | tf_op jit(solution)/shard_map/ppermute | solution.py:24
  61.5 5.4 %collective-permute-start.15 = (f32[8,128]{1,0:T(8,128)S(1)}, f32[8,128]{1,0:T(8,128)S(1)}, u32[]{:S(2)}, u32[]{:S(2)}) collective-permute-start(f32[8,128]{1,0:T(8,128)S(1)} %meet.1.refs_0_), channel_id=1, source_target_pairs={{24,0},{26,2},{28,4},{30,6},{0,8},{2,10},{4,12},{6,14},{8,16},{10,... | collective-permute-start | bytes 12296 | tf_op jit(solution)/shard_map/ppermute | solution.py:24
  61.8 5.2 %collective-permute-start.16 = (f32[8,128]{1,0:T(8,128)S(1)}, f32[8,128]{1,0:T(8,128)S(1)}, u32[]{:S(2)}, u32[]{:S(2)}) collective-permute-start(f32[8,128]{1,0:T(8,128)S(1)} %meet.1.refs_0_), channel_id=1, source_target_pairs={{26,0},{24,2},{30,4},{28,6},{2,8},{0,10},{6,12},{4,14},{10,16},{8,... | collective-permute-start | bytes 12296 | tf_op jit(solution)/shard_map/ppermute | solution.py:24

commit v3 on v2

--- a/solution.py
+++ b/solution.py
@@ -72,7 +72,7 @@
 
 
 def advance(state, near, far, flip):
-    double, low = far_weights(far, flip)
+    double, low = far
     high, rest = split(state)
     inner = product(jnp.concatenate([high, rest], 1), double, flip) + product(high, low, flip)
     h0, l0 = split(inner[:, :128])
@@ -97,54 +97,46 @@
         pl.when(side_ref[0] == side)(functools.partial(run, side == 1))
 
 
-def wide_kernel(start, side_ref, own, sibling, first, second, other, *rest):
+def norms_only(state):
+    slot = lane_slot((32, 128))
+    first = jnp.where(slot == 0, state[192:224], state[224:256])
+    second = jnp.where(slot == 1, state[256:288], state[288:320])
+    kept = jnp.where(slot % 2 == 0, first, second)
+    return jnp.concatenate([state[:192], kept, state[320:]], 0)
+
+
+def chain_kernel(start, side_ref, own, sibling, first, second, other, *rest):
     out = rest[-1]
     sites, count = own.shape[0], first.shape[0]
 
     def run(flip):
-        def step(index, state):
+        state = corner((384, 128)) if start == 0 else rest[0][...]
+        for index in range(count):
             whole = sites - 1 - start - index if flip else start + index
             part = count - 1 - index if flip else index
+            home = interleave(own[whole], sibling[whole])
             far = interleave(first[part], second[part])
             if flip:
                 near = [n for t in (own[whole], sibling[whole], other[part], first[part], second[part])
                         for n in near_plain(t)]
             else:
                 extra = other[part]
-                near = (
-                    near_turned(interleave(own[whole], sibling[whole]))
-                    + near_turned(interleave(extra, extra))[:2]
-                    + near_turned(far)
-                )
-            return advance(state, near, far, flip)
-
-        begin = corner(out.shape) if start == 0 else rest[0][...]
-        out[...] = lax.fori_loop(0, count, step, begin, unroll=2)
+                near = near_turned(home) + near_turned(interleave(extra, extra))[:2] + near_turned(far)
+            weights = far_weights(far, flip)
+            parts = [
+                advance(state[:192], near[:6], weights, flip),
+                advance(state[192:320], near[6:], weights, flip),
+                advance(state[320:], near[:2], far_weights(home, flip), flip),
+            ]
+            state = jnp.concatenate(parts, 0)
+        out[...] = norms_only(state) if start + count == sites else state
 
     on_each_side(side_ref, run)
 
 
-def narrow_kernel(side_ref, own, sibling, out):
-    sites = own.shape[0]
-
-    def run(flip):
-        def step(index, state):
-            site = sites - 1 - index if flip else index
-            far = interleave(own[site], sibling[site])
-            near = near_plain(own[site]) if flip else near_turned(far)[:2]
-            return advance(state, near, far, flip)
-
-        out[...] = lax.fori_loop(0, sites, step, corner(out.shape), unroll=4)
-
-    on_each_side(side_ref, run)
-
-
-def meet_kernel(wide, narrow, far_wide, far_narrow, out):
-    units = [
-        jnp.sum((a[...] * b[...]).reshape(-1, 32, 128), 1)
-        for a, b in ((wide, far_wide), (narrow, far_narrow))
-    ]
-    units = jnp.concatenate(units + [jnp.zeros((4, 128), F32)], 0)
+def meet_kernel(mine, theirs, out):
+    units = jnp.sum((mine[...] * theirs[...]).reshape(-1, 32, 128), 1)
+    units = jnp.concatenate([units, jnp.zeros((16 - units.shape[0], 128), F32)], 0)
     row = lax.broadcasted_iota(jnp.int32, (8, 128), 0)
     chosen = jnp.where(row == lane_slot((8, 128)), 1.0, 0.0)
     found = lax.dot_general(
@@ -171,26 +163,18 @@
     out[...] = (tile * tile / (own * remote))[:, :width]
 
 
-def rosters(core):
+def find(core, near, far):
     mine, theirs = ("A0", "A1"), ("Z1", "Z0")
     if core == 1:
         mine, theirs = theirs, mine
     own, sibling = f"O{core}", f"O{1 - core}"
-    wide = [own, sibling, theirs[1], mine[0], mine[1]]
-    return (wide, mine), ([own], (own, sibling))
-
-
-def find(core, near, far):
-    base = 0
-    for rows, lanes in rosters(core):
-        for a in range(2):
-            for left, right in ((near, far), (far, near)):
-                if left in rows and right in lanes:
-                    unit, slot = base + 2 * rows.index(left), lanes.index(right)
-                    if left == near:
-                        return lambda n, m: (unit + n, slot + 2 * m)
-                    return lambda n, m: (unit + m, slot + 2 * n)
-        base += 2 * len(rows)
+    if near == far and near in mine:
+        return lambda n, m: (6, mine.index(near) + 2 * m)
+    for base, rows, lanes in ((0, (own, sibling, theirs[1]), mine), (7, (own,), (own, sibling))):
+        if near in rows and far in lanes:
+            return lambda n, m: (base + 2 * rows.index(near) + n, lanes.index(far) + 2 * m)
+        if far in rows and near in lanes:
+            return lambda n, m: (base + 2 * rows.index(far) + m, lanes.index(near) + 2 * n)
     return None
 
 
@@ -198,26 +182,14 @@
     views = [(role, (k, k + 1) if core == 0 else (k + 1, k)) for k, role in ((0, "O"), (2, "A"), (4, "Z"))]
     shift = {"O": 0, "A": -1, "Z": 2}
 
-    def place(offset):
-        goal = core + offset
-        chip, lane = goal // 2, goal % 2
+    def place(offset, alone=False):
+        chip, lane = (core + offset) // 2, (core + offset) % 2
         for role, messages in views:
             for name, gap in shift.items():
                 if gap - shift[role] == chip:
+                    goal = f"{name}{lane}"
                     for k, message in enumerate(messages):
-                        got = find(k, f"{role}{core}", f"{name}{lane}")
-                        if got:
-                            return message, got
-        raise ValueError(offset)
-
-    def norm(offset):
-        goal = core + offset
-        chip, lane = goal // 2, goal % 2
-        for role, messages in views:
-            for name, gap in shift.items():
-                if gap - shift[role] == chip:
-                    for k, message in enumerate(messages):
-                        got = find(k, f"{name}{lane}", f"{name}{lane}")
+                        got = find(k, goal if alone else f"{role}{core}", goal)
                         if got:
                             return message, got
         raise ValueError(offset)
@@ -231,8 +203,8 @@
     table = []
     for n in range(samp):
         tile = [code(place(o), n, m) for o in offsets for m in range(samp)]
-        remote = [code(norm(o), m, m) for o in offsets for m in range(samp)]
-        own = [code(norm(0), n, n)] * len(tile)
+        remote = [code(place(o, True), m, m) for o in offsets for m in range(samp)]
+        own = [code(place(0, True), n, n)] * len(tile)
         rows = [r + r[:1] * (128 - len(r)) for r in (tile, remote, own)]
         table.append(rows + rows[:1] * 5)
     return table
@@ -265,19 +237,19 @@
         firsts.append(move(piece, lambda chip, core: (chip - 1, 0) if core == 0 else (chip + 2, 1)))
     across = lambda chip, core: (chip, 1 - core)
     sibling = move(mps, across)
-    narrow = call(narrow_kernel, (64, 128), flag, mps, sibling, name="own_chains")
-    swap = [(0, 1), (1, 0)]
-    far_narrow = lax.ppermute(narrow, "pair", swap)
-    wide = ()
+    state = ()
     for start, first, second in zip(starts, firsts, seconds):
+        if state:
+            second, *state = lax.optimization_barrier((second, *state))
         other = move(second, across)
-        wide = (
-            call(functools.partial(wide_kernel, start), (320, 128), flag, mps, sibling, first, second, other,
-                 *wide, name="half_chains"),
+        last = start == starts[-1]
+        state = (
+            call(functools.partial(chain_kernel, start), (288 if last else 384, 128), flag, mps, sibling, first,
+                 second, other, *state, name="half_chains"),
         )
-    (wide,) = wide
-    far_wide = lax.ppermute(wide, "pair", swap)
-    tile = call(meet_kernel, (8, 128), wide, narrow, far_wide, far_narrow, name="meet")
+    (state,) = state
+    partner = lax.ppermute(state, "pair", [(0, 1), (1, 0)])
+    tile = call(meet_kernel, (8, 128), state, partner, name="meet")
     tiles = [tile, move(tile, across)]
     for gap in (1, -2):
         straight = move(tile, lambda chip, core: (chip + gap, core))

time: 68 us -> 62.5 us (0.919)
  Pallas kernels: 27.6 us -> 14.8 us
  starting transfers between devices: 19.9 us -> 30.6 us
  waiting for transfers between devices: 18.5 us -> 15.1 us
    pallas_call x6 -> x5, Pallas kernels: 27.6 us -> 14.8 us  [call(): pl.pallas_call(kernel, out_shape=jax.ShapeDtypeStruct(shape, F32), in_spe...]
    ppermute x15, starting transfers between devices: 16.5 us -> 22.7 us  [move(): return lax.ppermute(array, 'blk', pairs)]
    ppermute x15, waiting for transfers between devices: 16 us -> 11 us  [move(): return lax.ppermute(array, 'blk', pairs)]
    ppermute x2 -> x1, starting transfers between devices: 3.3 us -> 7.86 us  [body(): partner = lax.ppermute(state, 'pair', [(0, 1), (1, 0)])]
    ppermute x2 -> x1, waiting for transfers between devices: 2.48 us -> 4.16 us  [body(): partner = lax.ppermute(state, 'pair', [(0, 1), (1, 0)])]
  transfers between devices with their start and end apart: 17 -> 16, of which waited for: 6 -> 6; matrix products, arithmetic and copies ran while one was open for 3% -> 3% of each run, Pallas kernels for 33% -> 16%
where the time goes in v3:
time: 62.5 us; the launch traced here: 62.4 us
  starting transfers between devices  30.6 us (49%)
  waiting for transfers between devices  15.1 us (24%)
  Pallas kernels  14.8 us (24%)
  local copies, waits for them, and re-layouts  1.75 us (3%)
    ppermute x15, starting transfers between devices, move(): return lax.ppermute(array, 'blk', pairs)  22.7 us
    pallas_call x5, Pallas kernels, call(): pl.pallas_call(kernel, out_shape=jax.ShapeDtypeStruct(shape, F32), in_spe...  14.8 us
    ppermute x15, waiting for transfers between devices, move(): return lax.ppermute(array, 'blk', pairs)  11 us
    ppermute x1, starting transfers between devices, body(): partner = lax.ppermute(state, 'pair', [(0, 1), (1, 0)])  7.86 us
    ppermute x1, waiting for transfers between devices, body(): partner = lax.ppermute(state, 'pair', [(0, 1), (1, 0)])  4.16 us
  transfers between devices with their start and end apart: 16, of which 6 were waited for; matrix products, arithmetic and copies ran while one was open for 3% of the time, Pallas kernels for 16%

profile of v3, /device:TPU:0, one launch (start us, length us, event | category | flops | bytes accessed | tf_op | source)
XLA Modules:
  0.0 62.4 jit_solution(16700059630501951340)
XLA Ops:
  0.0 0.5 collective-permute-start
  0.5 1.0 %constant_dynamic-slice_fusion = (f32[12,32,128]{2,1,0:T(8,128)S(1)}, f32[12,32,128]{2,1,0:T(8,128)S(1)}) fusion(f32[32,32,128]{2,1,0:T(8,128)} %own.5, s32[]{:T(128)S(6)} %select_n.31, s32[]{:T(128)S(6)} %select_n.30), kind=kLoop, calls=%fused_computation.1 | loop fusion | bytes 786440 | tf_op jit(solution)/shard_map/dynamic_slice | solution.py:235
  1.5 4.8 %collective-permute-start.6 = (f32[12,32,128]{2,1,0:T(8,128)S(1)}, f32[12,32,128]{2,1,0:T(8,128)S(1)}, u32[]{:S(2)}, u32[]{:S(2)}) collective-permute-start(f32[12,32,128]{2,1,0:T(8,128)S(1)} %get-tuple-element.13), channel_id=1, source_target_pairs={{30,0},{8,2},{2,4},{12,6},{6,8},{16,10},{10,12},{20,14},{14,16},{2... | collective-permute-start | bytes 589832 | tf_op jit(solution)/shard_map/ppermute | solution.py:24
  6.3 1.5 %collective-permute-start.5 = (f32[12,32,128]{2,1,0:T(8,128)S(1)}, f32[12,32,128]{2,1,0:T(8,128)S(1)}, u32[]{:S(2)}, u32[]{:S(2)}) collective-permute-start(f32[12,32,128]{2,1,0:T(8,128)S(1)} %get-tuple-element.13), channel_id=1, source_target_pairs={{28,0},{10,2},{0,4},{14,6},{4,8},{18,10},{8,12},{22,14},{12,16},{2... | collective-permute-start | bytes 589832 | tf_op jit(solution)/shard_map/ppermute | solution.py:24
  7.8 4.2 %collective-permute-done.6.second = f32[12,32,128]{2,1,0:T(8,128)S(1)} collective-permute-done((f32[12,32,128]{2,1,0:T(8,128)S(1)}, f32[12,32,128]{2,1,0:T(8,128)S(1)}, u32[]{:S(2)}, u32[]{:S(2)}) %collective-permute-start.6) | collective-permute-done | bytes 196640 | tf_op jit(solution)/shard_map/ppermute | solution.py:24
  12.0 0.0 collective-permute-start.7
  12.0 5.6 %collective-permute-start.4 = (f32[12,32,128]{2,1,0:T(8,128)S(1)}, f32[12,32,128]{2,1,0:T(8,128)S(1)}, u32[]{:S(2)}, u32[]{:S(2)}) collective-permute-start(f32[12,32,128]{2,1,0:T(8,128)S(1)} %get-tuple-element.14), channel_id=1, source_target_pairs={{30,0},{8,2},{2,4},{12,6},{6,8},{16,10},{10,12},{20,14},{14,16},{2... | collective-permute-start | bytes 589832 | tf_op jit(solution)/shard_map/ppermute | solution.py:24
  17.6 0.0 collective-permute-done.sibling
  17.6 5.0 %half_chains.3.rest_0_ = f32[384,128]{1,0:T(8,128)S(1)} custom-call(s32[1]{0:T(128)} %bitcast.1.side_ref, f32[32,32,128]{2,1,0:T(8,128)S(1)} %copy-done, f32[32,32,128]{2,1,0:T(8,128)S(1)} %collective-permute-done.sibling, f32[12,32,128]{2,1,0:T(8,128)S(1)} %collective-permute-done.5.first, f32[12,32,128]{2,1,0:T(8,128)S(1)} %collective-permute-done.6.second, ...), custom_call_target="tpu_custom_call" | custom-call | tf_op jit(solution)/shard_map/half_chains/pallas_call | solution.py:214
  22.6 0.0 collective-permute-done.4.second
  22.6 0.2 collective-permute-start.8
  22.8 6.9 %collective-permute-start.2 = (f32[8,32,128]{2,1,0:T(8,128)S(1)}, f32[8,32,128]{2,1,0:T(8,128)S(1)}, u32[]{:S(2)}, u32[]{:S(2)}) collective-permute-start(f32[8,32,128]{2,1,0:T(8,128)S(1)} %constant_dynamic-slice_fusion.2), channel_id=1, source_target_pairs={{30,0},{8,2},{2,4},{12,6},{6,8},{16,10},{10,12},{20,14},{14,16},{2... | collective-permute-start | bytes 393224 | tf_op jit(solution)/shard_map/ppermute | solution.py:24
  29.7 0.0 collective-permute-done.8.other
  29.7 5.2 %half_chains.4.rest_0_ = f32[384,128]{1,0:T(8,128)S(1)} custom-call(s32[1]{0:T(128)} %bitcast.1.side_ref, f32[32,32,128]{2,1,0:T(8,128)S(1)} %copy-done, f32[32,32,128]{2,1,0:T(8,128)S(1)} %collective-permute-done.sibling, f32[12,32,128]{2,1,0:T(8,128)S(1)} %collective-permute-done.3.first, f32[12,32,128]{2,1,0:T(8,128)S(1)} %collective-permute-done.4.second, ...), custom_call_target="tpu_custom_call" | custom-call | tf_op jit(solution)/shard_map/half_chains/pallas_call | solution.py:214
  34.9 0.1 collective-permute-start.9
  35.0 2.4 %collective-permute-done.1.first = f32[8,32,128]{2,1,0:T(8,128)S(1)} collective-permute-done((f32[8,32,128]{2,1,0:T(8,128)S(1)}, f32[8,32,128]{2,1,0:T(8,128)S(1)}, u32[]{:S(2)}, u32[]{:S(2)}) %collective-permute-start.1) | collective-permute-done | bytes 131104 | tf_op jit(solution)/shard_map/ppermute | solution.py:24
  37.3 3.6 %half_chains.5.mine = f32[288,128]{1,0:T(8,128)S(1)} custom-call(s32[1]{0:T(128)} %bitcast.1.side_ref, f32[32,32,128]{2,1,0:T(8,128)S(1)} %copy-done, f32[32,32,128]{2,1,0:T(8,128)S(1)} %collective-permute-done.sibling, f32[8,32,128]{2,1,0:T(8,128)S(1)} %collective-permute-done.1.first, f32[8,32,128]{2,1,0:T(8,128)S(1)} %collective-permute-done.2.second, ...), custom_call_target="tpu_custom_call" | custom-call | tf_op jit(solution)/shard_map/half_chains/pallas_call | solution.py:214
  40.9 7.9 %collective-permute-start.10 = (f32[288,128]{1,0:T(8,128)S(1)}, f32[288,128]{1,0:T(8,128)S(1)}, u32[]{:S(2)}, u32[]{:S(2)}) collective-permute-start(f32[288,128]{1,0:T(8,128)S(1)} %half_chains.5.mine), channel_id=1, source_target_pairs={{0,1},{1,0},{2,3},{3,2},{4,5},{5,4},{6,7},{7,6},{8,9},{9,8},{10,11... | collective-permute-start | bytes 442376 | tf_op jit(solution)/shard_map/ppermute | solution.py:251
  48.8 4.2 %collective-permute-done.10.theirs = f32[288,128]{1,0:T(8,128)S(1)} collective-permute-done((f32[288,128]{1,0:T(8,128)S(1)}, f32[288,128]{1,0:T(8,128)S(1)}, u32[]{:S(2)}, u32[]{:S(2)}) %collective-permute-start.10) | collective-permute-done | bytes 147488 | tf_op jit(solution)/shard_map/ppermute | solution.py:251
  53.0 0.1 meet.1.refs_0_
  53.1 0.0 collective-permute-start.11
  53.1 2.8 %collective-permute-start.12 = (f32[8,128]{1,0:T(8,128)S(1)}, f32[8,128]{1,0:T(8,128)S(1)}, u32[]{:S(2)}, u32[]{:S(2)}) collective-permute-start(f32[8,128]{1,0:T(8,128)S(1)} %meet.1.refs_0_), channel_id=1, source_target_pairs={{4,0},{6,2},{8,4},{10,6},{12,8},{14,10},{16,12},{18,14},{20,16},{2... | collective-permute-start | bytes 12296 | tf_op jit(solution)/shard_map/ppermute | solution.py:24
  55.9 0.1 collective-permute-start.13
  56.1 0.4 collective-permute-start.14
  56.4 0.0 collective-permute-start.15
  56.5 0.7 %dynamic-slice_bitcast_fusion.spot_ref = s32[8,128]{1,0:T(8,128)S(1)} fusion(s32[2,2,8,128]{3,2,1,0:T(8,128)} %constant.36.clone, s32[]{:T(128)S(6)} %select_n.27, s32[]{:T(128)S(6)} %select_n.28), kind=kLoop, calls=%fused_computation | loop fusion | bytes 8200 | tf_op jit(solution)/shard_map/squeeze | solution.py:259
  57.1 0.0 collective-permute-done.11.refs_1_
  57.1 0.1 collective-permute-done.12.refs_2_
  57.3 1.7 %collective-permute-done.13.refs_3_ = f32[8,128]{1,0:T(8,128)S(1)} collective-permute-done((f32[8,128]{1,0:T(8,128)S(1)}, f32[8,128]{1,0:T(8,128)S(1)}, u32[]{:S(2)}, u32[]{:S(2)}) %collective-permute-start.13) | collective-permute-done | bytes 4128 | tf_op jit(solution)/shard_map/ppermute | solution.py:24
  59.0 2.5 %collective-permute-done.14.refs_4_ = f32[8,128]{1,0:T(8,128)S(1)} collective-permute-done((f32[8,128]{1,0:T(8,128)S(1)}, f32[8,128]{1,0:T(8,128)S(1)}, u32[]{:S(2)}, u32[]{:S(2)}) %collective-permute-start.14) | collective-permute-done | bytes 4128 | tf_op jit(solution)/shard_map/ppermute | solution.py:24
  61.5 0.0 collective-permute-done.15.refs_5_
  61.5 0.9 %pick.1 = f32[1,26]{1,0:T(1,128)} custom-call(s32[8,128]{1,0:T(8,128)S(1)} %dynamic-slice_bitcast_fusion.spot_ref, f32[8,128]{1,0:T(8,128)S(1)} %meet.1.refs_0_, f32[8,128]{1,0:T(8,128)S(1)} %collective-permute-done.11.refs_1_, f32[8,128]{1,0:T(8,128)S(1)} %collective-permute-done.12.refs_2_, f32[8,128]{1,0:T(8,128)S(1)} %collective-permute-done.13.refs_3_, ...), custom_call_target="tpu_custom_call" | custom-call | tf_op jit(solution)/shard_map/pick/pallas_call | solution.py:214
  (10 shorter events, 0.0 us)
Async XLA Ops:
  0.0 17.6 %copy-start = (f32[32,32,128]{2,1,0:T(8,128)S(1)}, f32[32,32,128]{2,1,0:T(8,128)}, u32[]{:S(2)}) copy-start(f32[32,32,128]{2,1,0:T(8,128)} %own.5) | copy-start | bytes 1572868
  0.0 17.6 %collective-permute-start = (f32[32,32,128]{2,1,0:T(8,128)}, f32[32,32,128]{2,1,0:T(8,128)S(1)}, u32[]{:S(2)}, u32[]{:S(2)}) collective-permute-start(f32[32,32,128]{2,1,0:T(8,128)} %own.5), channel_id=1, source_target_pairs={{2,0},{0,2},{6,4},{4,6},{10,8},{8,10},{14,12},{12,14},{18,16},{16,... | collective-permute-start | bytes 1572872 | tf_op jit(solution)/shard_map/ppermute | solution.py:24
  1.5 10.5 %collective-permute-start.6 = (f32[12,32,128]{2,1,0:T(8,128)S(1)}, f32[12,32,128]{2,1,0:T(8,128)S(1)}, u32[]{:S(2)}, u32[]{:S(2)}) collective-permute-start(f32[12,32,128]{2,1,0:T(8,128)S(1)} %get-tuple-element.13), channel_id=1, source_target_pairs={{30,0},{8,2},{2,4},{12,6},{6,8},{16,10},{10,12},{20,14},{14,16},{2... | collective-permute-start | bytes 589832 | tf_op jit(solution)/shard_map/ppermute | solution.py:24
  6.3 11.3 %collective-permute-start.5 = (f32[12,32,128]{2,1,0:T(8,128)S(1)}, f32[12,32,128]{2,1,0:T(8,128)S(1)}, u32[]{:S(2)}, u32[]{:S(2)}) collective-permute-start(f32[12,32,128]{2,1,0:T(8,128)S(1)} %get-tuple-element.13), channel_id=1, source_target_pairs={{28,0},{10,2},{0,4},{14,6},{4,8},{18,10},{8,12},{22,14},{12,16},{2... | collective-permute-start | bytes 589832 | tf_op jit(solution)/shard_map/ppermute | solution.py:24
  12.0 5.6 %collective-permute-start.7 = (f32[12,32,128]{2,1,0:T(8,128)S(1)}, f32[12,32,128]{2,1,0:T(8,128)S(1)}, u32[]{:S(2)}, u32[]{:S(2)}) collective-permute-start(f32[12,32,128]{2,1,0:T(8,128)S(1)} %collective-permute-done.6.second), channel_id=1, source_target_pairs={{2,0},{0,2},{6,4},{4,6},{10,8},{8,10},{14,12},{12,14},{18,16},{16,... | collective-permute-start | bytes 589832 | tf_op jit(solution)/shard_map/ppermute | solution.py:24
  12.0 10.6 %collective-permute-start.4 = (f32[12,32,128]{2,1,0:T(8,128)S(1)}, f32[12,32,128]{2,1,0:T(8,128)S(1)}, u32[]{:S(2)}, u32[]{:S(2)}) collective-permute-start(f32[12,32,128]{2,1,0:T(8,128)S(1)} %get-tuple-element.14), channel_id=1, source_target_pairs={{30,0},{8,2},{2,4},{12,6},{6,8},{16,10},{10,12},{20,14},{14,16},{2... | collective-permute-start | bytes 589832 | tf_op jit(solution)/shard_map/ppermute | solution.py:24
  17.6 12.1 %collective-permute-start.3 = (f32[12,32,128]{2,1,0:T(8,128)S(1)}, f32[12,32,128]{2,1,0:T(8,128)S(1)}, u32[]{:S(2)}, u32[]{:S(2)}) collective-permute-start(f32[12,32,128]{2,1,0:T(8,128)S(1)} %get-tuple-element.14), channel_id=1, source_target_pairs={{28,0},{10,2},{0,4},{14,6},{4,8},{18,10},{8,12},{22,14},{12,16},{2... | collective-permute-start | bytes 589832 | tf_op jit(solution)/shard_map/ppermute | solution.py:24
  22.6 7.1 %collective-permute-start.8 = (f32[12,32,128]{2,1,0:T(8,128)S(1)}, f32[12,32,128]{2,1,0:T(8,128)S(1)}, u32[]{:S(2)}, u32[]{:S(2)}) collective-permute-start(f32[12,32,128]{2,1,0:T(8,128)S(1)} %collective-permute-done.4.second), channel_id=1, source_target_pairs={{2,0},{0,2},{6,4},{4,6},{10,8},{8,10},{14,12},{12,14},{18,16},{16,... | collective-permute-start | bytes 589832 | tf_op jit(solution)/shard_map/ppermute | solution.py:24
  22.8 12.1 %collective-permute-start.2 = (f32[8,32,128]{2,1,0:T(8,128)S(1)}, f32[8,32,128]{2,1,0:T(8,128)S(1)}, u32[]{:S(2)}, u32[]{:S(2)}) collective-permute-start(f32[8,32,128]{2,1,0:T(8,128)S(1)} %constant_dynamic-slice_fusion.2), channel_id=1, source_target_pairs={{30,0},{8,2},{2,4},{12,6},{6,8},{16,10},{10,12},{20,14},{14,16},{2... | collective-permute-start | bytes 393224 | tf_op jit(solution)/shard_map/ppermute | solution.py:24
  29.7 7.7 %collective-permute-start.1 = (f32[8,32,128]{2,1,0:T(8,128)S(1)}, f32[8,32,128]{2,1,0:T(8,128)S(1)}, u32[]{:S(2)}, u32[]{:S(2)}) collective-permute-start(f32[8,32,128]{2,1,0:T(8,128)S(1)} %constant_dynamic-slice_fusion.2), channel_id=1, source_target_pairs={{28,0},{10,2},{0,4},{14,6},{4,8},{18,10},{8,12},{22,14},{12,16},{2... | collective-permute-start | bytes 393224 | tf_op jit(solution)/shard_map/ppermute | solution.py:24
  34.9 2.5 %collective-permute-start.9 = (f32[8,32,128]{2,1,0:T(8,128)S(1)}, f32[8,32,128]{2,1,0:T(8,128)S(1)}, u32[]{:S(2)}, u32[]{:S(2)}) collective-permute-start(f32[8,32,128]{2,1,0:T(8,128)S(1)} %collective-permute-done.2.second), channel_id=1, source_target_pairs={{2,0},{0,2},{6,4},{4,6},{10,8},{8,10},{14,12},{12,14},{18,16},{16,... | collective-permute-start | bytes 393224 | tf_op jit(solution)/shard_map/ppermute | solution.py:24
  40.9 12.0 %collective-permute-start.10 = (f32[288,128]{1,0:T(8,128)S(1)}, f32[288,128]{1,0:T(8,128)S(1)}, u32[]{:S(2)}, u32[]{:S(2)}) collective-permute-start(f32[288,128]{1,0:T(8,128)S(1)} %half_chains.5.mine), channel_id=1, source_target_pairs={{0,1},{1,0},{2,3},{3,2},{4,5},{5,4},{6,7},{7,6},{8,9},{9,8},{10,11... | collective-permute-start | bytes 442376 | tf_op jit(solution)/shard_map/ppermute | solution.py:251
  53.1 4.0 %collective-permute-start.11 = (f32[8,128]{1,0:T(8,128)S(1)}, f32[8,128]{1,0:T(8,128)S(1)}, u32[]{:S(2)}, u32[]{:S(2)}) collective-permute-start(f32[8,128]{1,0:T(8,128)S(1)} %meet.1.refs_0_), channel_id=1, source_target_pairs={{2,0},{0,2},{6,4},{4,6},{10,8},{8,10},{14,12},{12,14},{18,16},{16,... | collective-permute-start | bytes 12296 | tf_op jit(solution)/shard_map/ppermute | solution.py:24
  53.1 4.1 %collective-permute-start.12 = (f32[8,128]{1,0:T(8,128)S(1)}, f32[8,128]{1,0:T(8,128)S(1)}, u32[]{:S(2)}, u32[]{:S(2)}) collective-permute-start(f32[8,128]{1,0:T(8,128)S(1)} %meet.1.refs_0_), channel_id=1, source_target_pairs={{4,0},{6,2},{8,4},{10,6},{12,8},{14,10},{16,12},{18,14},{20,16},{2... | collective-permute-start | bytes 12296 | tf_op jit(solution)/shard_map/ppermute | solution.py:24
  55.9 3.0 %collective-permute-start.13 = (f32[8,128]{1,0:T(8,128)S(1)}, f32[8,128]{1,0:T(8,128)S(1)}, u32[]{:S(2)}, u32[]{:S(2)}) collective-permute-start(f32[8,128]{1,0:T(8,128)S(1)} %meet.1.refs_0_), channel_id=1, source_target_pairs={{6,0},{4,2},{10,4},{8,6},{14,8},{12,10},{18,12},{16,14},{22,16},{2... | collective-permute-start | bytes 12296 | tf_op jit(solution)/shard_map/ppermute | solution.py:24
  56.1 5.4 %collective-permute-start.14 = (f32[8,128]{1,0:T(8,128)S(1)}, f32[8,128]{1,0:T(8,128)S(1)}, u32[]{:S(2)}, u32[]{:S(2)}) collective-permute-start(f32[8,128]{1,0:T(8,128)S(1)} %meet.1.refs_0_), channel_id=1, source_target_pairs={{24,0},{26,2},{28,4},{30,6},{0,8},{2,10},{4,12},{6,14},{8,16},{10,... | collective-permute-start | bytes 12296 | tf_op jit(solution)/shard_map/ppermute | solution.py:24
  56.4 5.1 %collective-permute-start.15 = (f32[8,128]{1,0:T(8,128)S(1)}, f32[8,128]{1,0:T(8,128)S(1)}, u32[]{:S(2)}, u32[]{:S(2)}) collective-permute-start(f32[8,128]{1,0:T(8,128)S(1)} %meet.1.refs_0_), channel_id=1, source_target_pairs={{26,0},{24,2},{30,4},{28,6},{2,8},{0,10},{6,12},{4,14},{10,16},{8,... | collective-permute-start | bytes 12296 | tf_op jit(solution)/shard_map/ppermute | solution.py:24

commit v4 on v3

--- a/solution.py
+++ b/solution.py
@@ -8,7 +8,7 @@
 from jax.sharding import PartitionSpec as P
 
 REACH = 6
-CHUNKS = (12, 12, 8)
+CHUNKS = (18, 14)
 BF16, F32 = jnp.bfloat16, jnp.float32
 VMEM = pl.BlockSpec(memory_space=pltpu.VMEM)
 SMEM = pl.BlockSpec(memory_space=pltpu.SMEM)
@@ -29,9 +29,8 @@
     return high, (x - high.astype(F32)).astype(BF16)
 
 
-def product(left, right, across=False):
-    dims = (((1,), (1 if across else 0,)), ((), ()))
-    return lax.dot_general(left, right, dims, preferred_element_type=F32)
+def product(left, right):
+    return jnp.dot(left, right, preferred_element_type=F32)
 
 
 def lane_slot(shape):
@@ -47,17 +46,15 @@
 
 
 def far_weights(tiles, flip):
-    parts = []
-    for half in zip(*[split(t) for t in tiles]):
-        slot = lane_slot(half[0].shape)
-        zero = jnp.zeros_like(half[0])
-        placed = [[jnp.where(slot == k, h, zero) for h in half] for k in range(4)]
-        if flip:
-            parts.append(jnp.concatenate([placed[k][p] for p in range(2) for k in range(4)], 0))
-        else:
-            parts.append(jnp.concatenate([jnp.concatenate(placed[k], 1) for k in range(4)], 0))
-    high, low = parts
-    return jnp.concatenate([high, high], 1 if flip else 0), low
+    if flip:
+        tiles = [jnp.concatenate([t] * 4, 0).T for t in tiles]
+        blocks = [[t[32 * k : 32 * k + 32] for t in tiles] for k in range(4)]
+    else:
+        blocks = [tiles] * 4
+    slot = lane_slot((32, 128))
+    rows = [jnp.concatenate([jnp.where(slot == k, t, 0.0) for t in blocks[k]], 1) for k in range(4)]
+    high, low = split(jnp.concatenate(rows, 0))
+    return jnp.concatenate([high, high], 0), low
 
 
 def near_turned(tiles):
@@ -71,10 +68,10 @@
     return [jnp.where(lower, tile, twice), jnp.where(lower, twice, tile)]
 
 
-def advance(state, near, far, flip):
+def advance(state, near, far):
     double, low = far
     high, rest = split(state)
-    inner = product(jnp.concatenate([high, rest], 1), double, flip) + product(high, low, flip)
+    inner = product(jnp.concatenate([high, rest], 1), double) + product(high, low)
     h0, l0 = split(inner[:, :128])
     h1, l1 = split(inner[:, 128:])
     results = []
@@ -102,15 +99,35 @@
     first = jnp.where(slot == 0, state[192:224], state[224:256])
     second = jnp.where(slot == 1, state[256:288], state[288:320])
     kept = jnp.where(slot % 2 == 0, first, second)
-    return jnp.concatenate([state[:192], kept, state[320:]], 0)
+    return jnp.concatenate([state[:192], kept], 0)
+
+
+def home_step(state, home, near, flip):
+    return advance(state, near[:2], far_weights(home, flip))
+
+
+def home_kernel(count, side_ref, own, sibling, out):
+    sites = own.shape[0]
+
+    def run(flip):
+        state = corner((64, 128))
+        for index in range(count):
+            site = sites - 1 - index if flip else index
+            home = interleave(own[site], sibling[site])
+            state = home_step(state, home, near_plain(own[site]) if flip else near_turned(home), flip)
+        out[...] = state
+
+    on_each_side(side_ref, run)
 
 
 def chain_kernel(start, side_ref, own, sibling, first, second, other, *rest):
     out = rest[-1]
     sites, count = own.shape[0], first.shape[0]
+    last = start + count == sites
 
     def run(flip):
-        state = corner((384, 128)) if start == 0 else rest[0][...]
+        state = rest[1][...] if start else corner((320, 128))
+        inner = rest[0][...] if last else None
         for index in range(count):
             whole = sites - 1 - start - index if flip else start + index
             part = count - 1 - index if flip else index
@@ -123,13 +140,11 @@
                 extra = other[part]
                 near = near_turned(home) + near_turned(interleave(extra, extra))[:2] + near_turned(far)
             weights = far_weights(far, flip)
-            parts = [
-                advance(state[:192], near[:6], weights, flip),
-                advance(state[192:320], near[6:], weights, flip),
-                advance(state[320:], near[:2], far_weights(home, flip), flip),
-            ]
+            parts = [advance(state[:192], near[:6], weights), advance(state[192:], near[6:], weights)]
             state = jnp.concatenate(parts, 0)
-        out[...] = norms_only(state) if start + count == sites else state
+            if last:
+                inner = home_step(inner, home, near, flip)
+        out[...] = jnp.concatenate([norms_only(state), inner], 0) if last else state
 
     on_each_side(side_ref, run)
 
@@ -230,24 +245,24 @@
     flag = side[None].astype(jnp.int32)
 
     starts = [sum(CHUNKS[:k]) for k in range(len(CHUNKS))]
-    firsts, seconds = [], []
-    for start, count in zip(starts, CHUNKS):
-        piece = lax.dynamic_slice_in_dim(mps, jnp.where(side == 0, start, sites - start - count), count, 0)
-        seconds.append(move(piece, lambda chip, core: (chip - 1, 1) if core == 0 else (chip + 2, 0)))
-        firsts.append(move(piece, lambda chip, core: (chip - 1, 0) if core == 0 else (chip + 2, 1)))
+    pieces = [
+        lax.dynamic_slice_in_dim(mps, jnp.where(side == 0, start, sites - start - count), count, 0)
+        for start, count in zip(starts, CHUNKS)
+    ]
+    pieces = lax.optimization_barrier(pieces)
+    seconds = [move(p, lambda chip, core: (chip - 1, 1) if core == 0 else (chip + 2, 0)) for p in pieces]
+    firsts = [move(p, lambda chip, core: (chip - 1, 0) if core == 0 else (chip + 2, 1)) for p in pieces]
     across = lambda chip, core: (chip, 1 - core)
     sibling = move(mps, across)
-    state = ()
+    inner = call(functools.partial(home_kernel, starts[-1]), (64, 128), flag, mps, sibling, name="own_chains")
+    carried = (inner,)
     for start, first, second in zip(starts, firsts, seconds):
-        if state:
-            second, *state = lax.optimization_barrier((second, *state))
+        second, *carried = lax.optimization_barrier((second, *carried))
         other = move(second, across)
-        last = start == starts[-1]
-        state = (
-            call(functools.partial(chain_kernel, start), (288 if last else 384, 128), flag, mps, sibling, first,
-                 second, other, *state, name="half_chains"),
-        )
-    (state,) = state
+        rows = 288 if start == starts[-1] else 320
+        state = call(functools.partial(chain_kernel, start), (rows, 128), flag, mps, sibling, first, second, other,
+                     *carried, name="half_chains")
+        carried = (carried[0], state)
     partner = lax.ppermute(state, "pair", [(0, 1), (1, 0)])
     tile = call(meet_kernel, (8, 128), state, partner, name="meet")
     tiles = [tile, move(tile, across)]

time: 62.5 us -> 53.4 us (0.85)
  starting transfers between devices: 30.6 us -> 22.7 us
  waiting for transfers between devices: 15.1 us -> 8.64 us
  Pallas kernels: 14.8 us -> 19.1 us
  local copies, waits for them, and re-layouts: 1.75 us -> 2.71 us
    ppermute x1, starting transfers between devices: 7.86 us -> 1.42 us  [body(): partner = lax.ppermute(state, 'pair', [(0, 1), (1, 0)])]
    ppermute x15 -> x12, waiting for transfers between devices: 11 us -> 4.85 us  [move(): return lax.ppermute(array, 'blk', pairs)]
    pallas_call x5, Pallas kernels: 14.8 us -> 19.1 us  [call(): pl.pallas_call(kernel, out_shape=jax.ShapeDtypeStruct(shape, F32), in_spe...]
    ppermute x15 -> x12, starting transfers between devices: 22.7 us -> 21.3 us  [move(): return lax.ppermute(array, 'blk', pairs)]
    dynamic_slice x2, local copies, waits for them, and re-layouts: 1.06 us -> 2.01 us  [body(): lax.dynamic_slice_in_dim(mps, jnp.where(side == 0, start, sites - start -...]
  transfers between devices with their start and end apart: 16 -> 13, of which waited for: 6 -> 6; matrix products, arithmetic and copies ran while one was open for 3% -> 5% of each run, Pallas kernels for 16% -> 23%
where the time goes in v4:
time: 53.4 us; the launch traced here: 53.3 us
  starting transfers between devices  22.7 us (43%)
  Pallas kernels  19.1 us (36%)
  waiting for transfers between devices  8.64 us (16%)
  local copies, waits for them, and re-layouts  2.71 us (5%)
    ppermute x12, starting transfers between devices, move(): return lax.ppermute(array, 'blk', pairs)  21.3 us
    pallas_call x5, Pallas kernels, call(): pl.pallas_call(kernel, out_shape=jax.ShapeDtypeStruct(shape, F32), in_spe...  19.1 us
    ppermute x12, waiting for transfers between devices, move(): return lax.ppermute(array, 'blk', pairs)  4.85 us
    ppermute x1, waiting for transfers between devices, body(): partner = lax.ppermute(state, 'pair', [(0, 1), (1, 0)])  3.79 us
    dynamic_slice x2, local copies, waits for them, and re-layouts, body(): lax.dynamic_slice_in_dim(mps, jnp.where(side == 0, start, sites - start -...  2.01 us
    ppermute x1, starting transfers between devices, body(): partner = lax.ppermute(state, 'pair', [(0, 1), (1, 0)])  1.42 us
  transfers between devices with their start and end apart: 13, of which 6 were waited for; matrix products, arithmetic and copies ran while one was open for 5% of the time, Pallas kernels for 23%

profile of v4, /device:TPU:0, one launch (start us, length us, event | category | flops | bytes accessed | tf_op | source)
XLA Modules:
  0.0 53.3 jit_solution(2986268081245826968)
XLA Ops:
  0.0 0.5 collective-permute-start
  0.5 1.0 %constant_dynamic-slice_fusion = f32[14,32,128]{2,1,0:T(8,128)S(1)} fusion(f32[32,32,128]{2,1,0:T(8,128)} %own.5, s32[]{:T(128)S(6)} %select_n.26), kind=kLoop, calls=%fused_computation.1 | loop fusion | bytes 458756 | tf_op jit(solution)/shard_map/dynamic_slice | solution.py:249
  1.5 1.0 %constant_dynamic-slice_fusion.1 = f32[18,32,128]{2,1,0:T(8,128)S(1)} fusion(f32[32,32,128]{2,1,0:T(8,128)} %own.5, s32[]{:T(128)S(6)} %select_n.25), kind=kLoop, calls=%fused_computation.2 | loop fusion | bytes 589828 | tf_op jit(solution)/shard_map/dynamic_slice | solution.py:249
  2.5 4.8 %collective-permute-start.3 = (f32[18,32,128]{2,1,0:T(8,128)S(1)}, f32[18,32,128]{2,1,0:T(8,128)S(1)}, u32[]{:S(2)}, u32[]{:S(2)}) collective-permute-start(f32[18,32,128]{2,1,0:T(8,128)S(1)} %constant_dynamic-slice_fusion.1), channel_id=1, source_target_pairs={{30,0},{8,2},{2,4},{12,6},{6,8},{16,10},{10,12},{20,14},{14,16},{2... | collective-permute-start | bytes 884744 | tf_op jit(solution)/shard_map/ppermute | solution.py:24
  7.2 1.5 %collective-permute-start.4 = (f32[18,32,128]{2,1,0:T(8,128)S(1)}, f32[18,32,128]{2,1,0:T(8,128)S(1)}, u32[]{:S(2)}, u32[]{:S(2)}) collective-permute-start(f32[18,32,128]{2,1,0:T(8,128)S(1)} %constant_dynamic-slice_fusion.1), channel_id=1, source_target_pairs={{28,0},{10,2},{0,4},{14,6},{4,8},{18,10},{8,12},{22,14},{12,16},{2... | collective-permute-start | bytes 884744 | tf_op jit(solution)/shard_map/ppermute | solution.py:24
  8.7 0.0 collective-permute-done.sibling
  8.7 5.3 %own_chains.1.rest_0_ = f32[64,128]{1,0:T(8,128)S(1)} custom-call(s32[1]{0:T(128)} %bitcast.1.side_ref, f32[32,32,128]{2,1,0:T(8,128)S(1)} %copy-done, f32[32,32,128]{2,1,0:T(8,128)S(1)} %collective-permute-done.sibling), custom_call_target="tpu_custom_call" | custom-call | tf_op jit(solution)/shard_map/own_chains/pallas_call | solution.py:229
  14.1 1.0 %collective-permute-done.3.second = f32[18,32,128]{2,1,0:T(8,128)S(1)} collective-permute-done((f32[18,32,128]{2,1,0:T(8,128)S(1)}, f32[18,32,128]{2,1,0:T(8,128)S(1)}, u32[]{:S(2)}, u32[]{:S(2)}) %collective-permute-start.3) | collective-permute-done | bytes 294944 | tf_op jit(solution)/shard_map/ppermute | solution.py:24
  15.0 0.0 collective-permute-start.5
  15.0 7.6 %collective-permute-start.2 = (f32[14,32,128]{2,1,0:T(8,128)S(1)}, f32[14,32,128]{2,1,0:T(8,128)S(1)}, u32[]{:S(2)}, u32[]{:S(2)}) collective-permute-start(f32[14,32,128]{2,1,0:T(8,128)S(1)} %constant_dynamic-slice_fusion), channel_id=1, source_target_pairs={{30,0},{8,2},{2,4},{12,6},{6,8},{16,10},{10,12},{20,14},{14,16},{2... | collective-permute-start | bytes 688136 | tf_op jit(solution)/shard_map/ppermute | solution.py:24
  22.6 0.0 collective-permute-start.1
  22.6 0.2 collective-permute-done.4.first
  22.8 6.7 %half_chains.2.rest_1_ = f32[320,128]{1,0:T(8,128)S(1)} custom-call(s32[1]{0:T(128)} %bitcast.1.side_ref, f32[32,32,128]{2,1,0:T(8,128)S(1)} %copy-done, f32[32,32,128]{2,1,0:T(8,128)S(1)} %collective-permute-done.sibling, f32[18,32,128]{2,1,0:T(8,128)S(1)} %collective-permute-done.4.first, f32[18,32,128]{2,1,0:T(8,128)S(1)} %collective-permute-done.3.second, ...), custom_call_target="tpu_custom_call" | custom-call | tf_op jit(solution)/shard_map/half_chains/pallas_call | solution.py:229
  29.6 0.0 collective-permute-done.2.second
  29.6 0.1 collective-permute-start.6
  29.7 2.2 %collective-permute-done.1.first = f32[14,32,128]{2,1,0:T(8,128)S(1)} collective-permute-done((f32[14,32,128]{2,1,0:T(8,128)S(1)}, f32[14,32,128]{2,1,0:T(8,128)S(1)}, u32[]{:S(2)}, u32[]{:S(2)}) %collective-permute-start.1) | collective-permute-done | bytes 229408 | tf_op jit(solution)/shard_map/ppermute | solution.py:24
  31.9 0.0 collective-permute-done.6.other
  31.9 6.0 %half_chains.3.mine = f32[288,128]{1,0:T(8,128)S(1)} custom-call(s32[1]{0:T(128)} %bitcast.1.side_ref, f32[32,32,128]{2,1,0:T(8,128)S(1)} %copy-done, f32[32,32,128]{2,1,0:T(8,128)S(1)} %collective-permute-done.sibling, f32[14,32,128]{2,1,0:T(8,128)S(1)} %collective-permute-done.1.first, f32[14,32,128]{2,1,0:T(8,128)S(1)} %collective-permute-done.2.second, ...), custom_call_target="tpu_custom_call" | custom-call | tf_op jit(solution)/shard_map/half_chains/pallas_call | solution.py:229
  37.9 1.4 %collective-permute-start.7 = (f32[288,128]{1,0:T(8,128)S(1)}, f32[288,128]{1,0:T(8,128)S(1)}, u32[]{:S(2)}, u32[]{:S(2)}) collective-permute-start(f32[288,128]{1,0:T(8,128)S(1)} %half_chains.3.mine), channel_id=1, source_target_pairs={{0,1},{1,0},{2,3},{3,2},{4,5},{5,4},{6,7},{7,6},{8,9},{9,8},{10,11... | collective-permute-start | bytes 442376 | tf_op jit(solution)/shard_map/ppermute | solution.py:266
  39.3 3.8 %collective-permute-done.7.theirs = f32[288,128]{1,0:T(8,128)S(1)} collective-permute-done((f32[288,128]{1,0:T(8,128)S(1)}, f32[288,128]{1,0:T(8,128)S(1)}, u32[]{:S(2)}, u32[]{:S(2)}) %collective-permute-start.7) | collective-permute-done | bytes 147488 | tf_op jit(solution)/shard_map/ppermute | solution.py:266
  43.1 0.1 meet.1.refs_0_
  43.3 3.4 %collective-permute-start.10 = (f32[8,128]{1,0:T(8,128)S(1)}, f32[8,128]{1,0:T(8,128)S(1)}, u32[]{:S(2)}, u32[]{:S(2)}) collective-permute-start(f32[8,128]{1,0:T(8,128)S(1)} %meet.1.refs_0_), channel_id=1, source_target_pairs={{6,0},{4,2},{10,4},{8,6},{14,8},{12,10},{18,12},{16,14},{22,16},{2... | collective-permute-start | bytes 12296 | tf_op jit(solution)/shard_map/ppermute | solution.py:24
  46.7 0.6 %collective-permute-start.12 = (f32[8,128]{1,0:T(8,128)S(1)}, f32[8,128]{1,0:T(8,128)S(1)}, u32[]{:S(2)}, u32[]{:S(2)}) collective-permute-start(f32[8,128]{1,0:T(8,128)S(1)} %meet.1.refs_0_), channel_id=1, source_target_pairs={{26,0},{24,2},{30,4},{28,6},{2,8},{0,10},{6,12},{4,14},{10,16},{8,... | collective-permute-start | bytes 12296 | tf_op jit(solution)/shard_map/ppermute | solution.py:24
  47.4 1.2 %collective-permute-start.8 = (f32[8,128]{1,0:T(8,128)S(1)}, f32[8,128]{1,0:T(8,128)S(1)}, u32[]{:S(2)}, u32[]{:S(2)}) collective-permute-start(f32[8,128]{1,0:T(8,128)S(1)} %meet.1.refs_0_), channel_id=1, source_target_pairs={{2,0},{0,2},{6,4},{4,6},{10,8},{8,10},{14,12},{12,14},{18,16},{16,... | collective-permute-start | bytes 12296 | tf_op jit(solution)/shard_map/ppermute | solution.py:24
  48.5 1.7 %collective-permute-start.9 = (f32[8,128]{1,0:T(8,128)S(1)}, f32[8,128]{1,0:T(8,128)S(1)}, u32[]{:S(2)}, u32[]{:S(2)}) collective-permute-start(f32[8,128]{1,0:T(8,128)S(1)} %meet.1.refs_0_), channel_id=1, source_target_pairs={{4,0},{6,2},{8,4},{10,6},{12,8},{14,10},{16,12},{18,14},{20,16},{2... | collective-permute-start | bytes 12296 | tf_op jit(solution)/shard_map/ppermute | solution.py:24
  50.3 0.7 %dynamic-slice_bitcast_fusion.spot_ref = s32[8,128]{1,0:T(8,128)S(1)} fusion(s32[2,2,8,128]{3,2,1,0:T(8,128)} %constant.31.clone, s32[]{:T(128)S(6)} %select_n.23, s32[]{:T(128)S(6)} %select_n.24), kind=kLoop, calls=%fused_computation | loop fusion | bytes 8200 | tf_op jit(solution)/shard_map/squeeze | solution.py:274
  51.0 0.0 collective-permute-done.10.refs_3_
  51.0 1.2 %collective-permute-done.11.refs_4_ = f32[8,128]{1,0:T(8,128)S(1)} collective-permute-done((f32[8,128]{1,0:T(8,128)S(1)}, f32[8,128]{1,0:T(8,128)S(1)}, u32[]{:S(2)}, u32[]{:S(2)}) %collective-permute-start.11) | collective-permute-done | bytes 4128 | tf_op jit(solution)/shard_map/ppermute | solution.py:24
  52.1 0.3 collective-permute-done.12.refs_5_
  52.4 0.0 collective-permute-done.8.refs_1_
  52.4 0.0 collective-permute-done.9.refs_2_
  52.4 0.9 %pick.1 = f32[1,26]{1,0:T(1,128)} custom-call(s32[8,128]{1,0:T(8,128)S(1)} %dynamic-slice_bitcast_fusion.spot_ref, f32[8,128]{1,0:T(8,128)S(1)} %meet.1.refs_0_, f32[8,128]{1,0:T(8,128)S(1)} %collective-permute-done.8.refs_1_, f32[8,128]{1,0:T(8,128)S(1)} %collective-permute-done.9.refs_2_, f32[8,128]{1,0:T(8,128)S(1)} %collective-permute-done.10.refs_3_, ...), custom_call_target="tpu_custom_call" | custom-call | tf_op jit(solution)/shard_map/pick/pallas_call | solution.py:229
  (4 shorter events, 0.0 us)
Async XLA Ops:
  0.0 8.7 %collective-permute-start = (f32[32,32,128]{2,1,0:T(8,128)}, f32[32,32,128]{2,1,0:T(8,128)S(1)}, u32[]{:S(2)}, u32[]{:S(2)}) collective-permute-start(f32[32,32,128]{2,1,0:T(8,128)} %own.5), channel_id=1, source_target_pairs={{2,0},{0,2},{6,4},{4,6},{10,8},{8,10},{14,12},{12,14},{18,16},{16,... | collective-permute-start | bytes 1572872 | tf_op jit(solution)/shard_map/ppermute | solution.py:24
  0.5 8.3 %copy-start = (f32[32,32,128]{2,1,0:T(8,128)S(1)}, f32[32,32,128]{2,1,0:T(8,128)}, u32[]{:S(2)}) copy-start(f32[32,32,128]{2,1,0:T(8,128)} %own.5) | copy-start | bytes 1572868
  2.5 12.6 %collective-permute-start.3 = (f32[18,32,128]{2,1,0:T(8,128)S(1)}, f32[18,32,128]{2,1,0:T(8,128)S(1)}, u32[]{:S(2)}, u32[]{:S(2)}) collective-permute-start(f32[18,32,128]{2,1,0:T(8,128)S(1)} %constant_dynamic-slice_fusion.1), channel_id=1, source_target_pairs={{30,0},{8,2},{2,4},{12,6},{6,8},{16,10},{10,12},{20,14},{14,16},{2... | collective-permute-start | bytes 884744 | tf_op jit(solution)/shard_map/ppermute | solution.py:24
  7.2 15.6 %collective-permute-start.4 = (f32[18,32,128]{2,1,0:T(8,128)S(1)}, f32[18,32,128]{2,1,0:T(8,128)S(1)}, u32[]{:S(2)}, u32[]{:S(2)}) collective-permute-start(f32[18,32,128]{2,1,0:T(8,128)S(1)} %constant_dynamic-slice_fusion.1), channel_id=1, source_target_pairs={{28,0},{10,2},{0,4},{14,6},{4,8},{18,10},{8,12},{22,14},{12,16},{2... | collective-permute-start | bytes 884744 | tf_op jit(solution)/shard_map/ppermute | solution.py:24
  15.0 7.8 %collective-permute-start.5 = (f32[18,32,128]{2,1,0:T(8,128)S(1)}, f32[18,32,128]{2,1,0:T(8,128)S(1)}, u32[]{:S(2)}, u32[]{:S(2)}) collective-permute-start(f32[18,32,128]{2,1,0:T(8,128)S(1)} %collective-permute-done.3.second), channel_id=1, source_target_pairs={{2,0},{0,2},{6,4},{4,6},{10,8},{8,10},{14,12},{12,14},{18,16},{16,... | collective-permute-start | bytes 884744 | tf_op jit(solution)/shard_map/ppermute | solution.py:24
  15.0 14.5 %collective-permute-start.2 = (f32[14,32,128]{2,1,0:T(8,128)S(1)}, f32[14,32,128]{2,1,0:T(8,128)S(1)}, u32[]{:S(2)}, u32[]{:S(2)}) collective-permute-start(f32[14,32,128]{2,1,0:T(8,128)S(1)} %constant_dynamic-slice_fusion), channel_id=1, source_target_pairs={{30,0},{8,2},{2,4},{12,6},{6,8},{16,10},{10,12},{20,14},{14,16},{2... | collective-permute-start | bytes 688136 | tf_op jit(solution)/shard_map/ppermute | solution.py:24
  22.6 9.3 %collective-permute-start.1 = (f32[14,32,128]{2,1,0:T(8,128)S(1)}, f32[14,32,128]{2,1,0:T(8,128)S(1)}, u32[]{:S(2)}, u32[]{:S(2)}) collective-permute-start(f32[14,32,128]{2,1,0:T(8,128)S(1)} %constant_dynamic-slice_fusion), channel_id=1, source_target_pairs={{28,0},{10,2},{0,4},{14,6},{4,8},{18,10},{8,12},{22,14},{12,16},{2... | collective-permute-start | bytes 688136 | tf_op jit(solution)/shard_map/ppermute | solution.py:24
  29.6 2.3 %collective-permute-start.6 = (f32[14,32,128]{2,1,0:T(8,128)S(1)}, f32[14,32,128]{2,1,0:T(8,128)S(1)}, u32[]{:S(2)}, u32[]{:S(2)}) collective-permute-start(f32[14,32,128]{2,1,0:T(8,128)S(1)} %collective-permute-done.2.second), channel_id=1, source_target_pairs={{2,0},{0,2},{6,4},{4,6},{10,8},{8,10},{14,12},{12,14},{18,16},{16,... | collective-permute-start | bytes 688136 | tf_op jit(solution)/shard_map/ppermute | solution.py:24
  37.9 5.2 %collective-permute-start.7 = (f32[288,128]{1,0:T(8,128)S(1)}, f32[288,128]{1,0:T(8,128)S(1)}, u32[]{:S(2)}, u32[]{:S(2)}) collective-permute-start(f32[288,128]{1,0:T(8,128)S(1)} %half_chains.3.mine), channel_id=1, source_target_pairs={{0,1},{1,0},{2,3},{3,2},{4,5},{5,4},{6,7},{7,6},{8,9},{9,8},{10,11... | collective-permute-start | bytes 442376 | tf_op jit(solution)/shard_map/ppermute | solution.py:266
  43.3 7.7 %collective-permute-start.10 = (f32[8,128]{1,0:T(8,128)S(1)}, f32[8,128]{1,0:T(8,128)S(1)}, u32[]{:S(2)}, u32[]{:S(2)}) collective-permute-start(f32[8,128]{1,0:T(8,128)S(1)} %meet.1.refs_0_), channel_id=1, source_target_pairs={{6,0},{4,2},{10,4},{8,6},{14,8},{12,10},{18,12},{16,14},{22,16},{2... | collective-permute-start | bytes 12296 | tf_op jit(solution)/shard_map/ppermute | solution.py:24
  46.7 5.4 %collective-permute-start.11 = (f32[8,128]{1,0:T(8,128)S(1)}, f32[8,128]{1,0:T(8,128)S(1)}, u32[]{:S(2)}, u32[]{:S(2)}) collective-permute-start(f32[8,128]{1,0:T(8,128)S(1)} %meet.1.refs_0_), channel_id=1, source_target_pairs={{24,0},{26,2},{28,4},{30,6},{0,8},{2,10},{4,12},{6,14},{8,16},{10,... | collective-permute-start | bytes 12296 | tf_op jit(solution)/shard_map/ppermute | solution.py:24
  46.7 5.7 %collective-permute-start.12 = (f32[8,128]{1,0:T(8,128)S(1)}, f32[8,128]{1,0:T(8,128)S(1)}, u32[]{:S(2)}, u32[]{:S(2)}) collective-permute-start(f32[8,128]{1,0:T(8,128)S(1)} %meet.1.refs_0_), channel_id=1, source_target_pairs={{26,0},{24,2},{30,4},{28,6},{2,8},{0,10},{6,12},{4,14},{10,16},{8,... | collective-permute-start | bytes 12296 | tf_op jit(solution)/shard_map/ppermute | solution.py:24
  47.4 5.0 %collective-permute-start.8 = (f32[8,128]{1,0:T(8,128)S(1)}, f32[8,128]{1,0:T(8,128)S(1)}, u32[]{:S(2)}, u32[]{:S(2)}) collective-permute-start(f32[8,128]{1,0:T(8,128)S(1)} %meet.1.refs_0_), channel_id=1, source_target_pairs={{2,0},{0,2},{6,4},{4,6},{10,8},{8,10},{14,12},{12,14},{18,16},{16,... | collective-permute-start | bytes 12296 | tf_op jit(solution)/shard_map/ppermute | solution.py:24
  48.5 3.9 %collective-permute-start.9 = (f32[8,128]{1,0:T(8,128)S(1)}, f32[8,128]{1,0:T(8,128)S(1)}, u32[]{:S(2)}, u32[]{:S(2)}) collective-permute-start(f32[8,128]{1,0:T(8,128)S(1)} %meet.1.refs_0_), channel_id=1, source_target_pairs={{4,0},{6,2},{8,4},{10,6},{12,8},{14,10},{16,12},{18,14},{20,16},{2... | collective-permute-start | bytes 12296 | tf_op jit(solution)/shard_map/ppermute | solution.py:24

commit v5 on v4

--- a/solution.py
+++ b/solution.py
@@ -8,7 +8,8 @@
 from jax.sharding import PartitionSpec as P
 
 REACH = 6
-CHUNKS = (18, 14)
+EDGE = 6
+SHARE = 0.63
 BF16, F32 = jnp.bfloat16, jnp.float32
 VMEM = pl.BlockSpec(memory_space=pltpu.VMEM)
 SMEM = pl.BlockSpec(memory_space=pltpu.SMEM)
@@ -83,15 +84,61 @@
     return jnp.concatenate(results, 0)
 
 
-def corner(shape):
-    row = lax.broadcasted_iota(jnp.int32, shape, 0) % 32
-    lane = lax.broadcasted_iota(jnp.int32, shape, 1) % 32
-    return jnp.where((row == 0) & (lane == 0), 1.0, 0.0)
+def identities(rows):
+    row = lax.broadcasted_iota(jnp.int32, (rows, 128), 0) % 32
+    lane = lax.broadcasted_iota(jnp.int32, (rows, 128), 1) % 32
+    return jnp.where(row == lane, 1.0, 0.0)
 
 
 def on_each_side(side_ref, run):
     for side in range(2):
         pl.when(side_ref[0] == side)(functools.partial(run, side == 1))
+
+
+def turned(tile):
+    stack = jnp.concatenate([tile] * 4, 0).T
+    slot = lane_slot(tile.shape)
+    result = stack[:32]
+    for k in range(1, 4):
+        result = jnp.where(slot == k, stack[32 * k : 32 * k + 32], result)
+    return result
+
+
+def edge_tile(tiles):
+    slot = lane_slot((32, 128))
+    row = lax.broadcasted_iota(jnp.int32, (32, 128), 0)
+    current = jnp.broadcast_to(tiles[0][:1], (32, 128))
+    for k, tile in enumerate(tiles[1:]):
+        chosen = jnp.where(slot % 2 == (row >> k) % 2, current, 0.0)
+        weights = [jnp.where(slot // 2 == n, tile, 0.0) for n in (0, 0, 1, 1)]
+        current = jnp.dot(
+            chosen,
+            jnp.concatenate(weights, 0),
+            precision=lax.Precision.HIGHEST,
+            preferred_element_type=F32,
+        )
+    return current
+
+
+def order_kernel(side_ref, sites_ref, whole, *pieces):
+    sites = sites_ref.shape[0]
+
+    def run(flip):
+        def tile(k):
+            return sites_ref[sites - 1 - k if flip else k]
+
+        edge = edge_tile([turned(tile(k)) if flip else tile(k) for k in range(EDGE)])
+        if flip:
+            edge = turned(edge)
+        at = 0
+        for piece in pieces:
+            for k in range(piece.shape[0]):
+                value = edge if at == 0 else tile(at + EDGE - 1)
+                piece[k] = value
+                whole[at] = value
+                at += 1
+
+    on_each_side(side_ref, run)
 
 
 def norms_only(state):
@@ -107,12 +154,9 @@
 
 
 def home_kernel(count, side_ref, own, sibling, out):
-    sites = own.shape[0]
-
     def run(flip):
-        state = corner((64, 128))
-        for index in range(count):
-            site = sites - 1 - index if flip else index
+        state = identities(64)
+        for site in range(count):
             home = interleave(own[site], sibling[site])
             state = home_step(state, home, near_plain(own[site]) if flip else near_turned(home), flip)
         out[...] = state
@@ -122,22 +166,21 @@
 
 def chain_kernel(start, side_ref, own, sibling, first, second, other, *rest):
     out = rest[-1]
-    sites, count = own.shape[0], first.shape[0]
-    last = start + count == sites
+    count = first.shape[0]
+    last = start + count == own.shape[0]
 
     def run(flip):
-        state = rest[1][...] if start else corner((320, 128))
+        state = rest[1][...] if start else identities(320)
         inner = rest[0][...] if last else None
         for index in range(count):
-            whole = sites - 1 - start - index if flip else start + index
-            part = count - 1 - index if flip else index
+            whole = start + index
             home = interleave(own[whole], sibling[whole])
-            far = interleave(first[part], second[part])
+            far = interleave(first[index], second[index])
             if flip:
-                near = [n for t in (own[whole], sibling[whole], other[part], first[part], second[part])
+                near = [n for t in (own[whole], sibling[whole], other[index], first[index], second[index])
                         for n in near_plain(t)]
             else:
-                extra = other[part]
+                extra = other[index]
                 near = near_turned(home) + near_turned(interleave(extra, extra))[:2] + near_turned(far)
             weights = far_weights(far, flip)
             parts = [advance(state[:192], near[:6], weights), advance(state[192:], near[6:], weights)]
@@ -160,11 +203,12 @@
     out[...] = jnp.concatenate([found, jnp.zeros((8, 112), F32)], 1)
 
 
-def pick_kernel(spot_ref, *refs):
-    *tiles, out = refs
-    joined = tiles[0][...]
-    for k, tile in enumerate(tiles[1:], 1):
-        joined += pltpu.roll(tile[...], 16 * k, 1)
+def join_kernel(mine, theirs, out):
+    out[...] = mine[...] + pltpu.roll(theirs[...], 16, 1)
+
+
+def pick_kernel(spot_ref, here, after, before, out):
+    joined = here[...] + pltpu.roll(after[...], 32, 1) + pltpu.roll(before[...], 64, 1)
     unit = lax.broadcasted_iota(jnp.int32, (128, 128), 0)
     slot = lax.broadcasted_iota(jnp.int32, (8, 128), 0)
     values = []
@@ -225,12 +269,14 @@
     return table
 
 
-def call(kernel, shape, *args, name):
+def call(kernel, shapes, *args, name):
+    many = isinstance(shapes, list)
+    shapes = [jax.ShapeDtypeStruct(shape, F32) for shape in (shapes if many else [shapes])]
     return pl.pallas_call(
         kernel,
-        out_shape=jax.ShapeDtypeStruct(shape, F32),
+        out_shape=shapes if many else shapes[0],
         in_specs=[SMEM if a.ndim == 1 else VMEM for a in args],
-        out_specs=VMEM,
+        out_specs=[VMEM] * len(shapes) if many else VMEM,
         compiler_params=pltpu.CompilerParams(vmem_limit_bytes=40 * 2**20),
         name=name,
     )(*args)
@@ -244,12 +290,11 @@
     side = lax.axis_index("pair")
     flag = side[None].astype(jnp.int32)
 
-    starts = [sum(CHUNKS[:k]) for k in range(len(CHUNKS))]
-    pieces = [
-        lax.dynamic_slice_in_dim(mps, jnp.where(side == 0, start, sites - start - count), count, 0)
-        for start, count in zip(starts, CHUNKS)
-    ]
-    pieces = lax.optimization_barrier(pieces)
+    steps = sites - EDGE + 1
+    starts = [0, round(SHARE * steps)]
+    counts = [starts[1], steps - starts[1]]
+    tile = mps.shape[1:]
+    mps, *pieces = call(order_kernel, [(n, *tile) for n in (steps, *counts)], flag, mps, name="order")
     seconds = [move(p, lambda chip, core: (chip - 1, 1) if core == 0 else (chip + 2, 0)) for p in pieces]
     firsts = [move(p, lambda chip, core: (chip - 1, 0) if core == 0 else (chip + 2, 1)) for p in pieces]
     across = lambda chip, core: (chip, 1 - core)
@@ -265,11 +310,8 @@
         carried = (carried[0], state)
     partner = lax.ppermute(state, "pair", [(0, 1), (1, 0)])
     tile = call(meet_kernel, (8, 128), state, partner, name="meet")
-    tiles = [tile, move(tile, across)]
-    for gap in (1, -2):
-        straight = move(tile, lambda chip, core: (chip + gap, core))
-        crossed = move(tile, lambda chip, core: (chip + gap, 1 - core))
-        tiles += [straight, crossed]
+    tile = call(join_kernel, (8, 128), tile, move(tile, across), name="join")
+    tiles = [tile] + [move(tile, lambda chip, core: (chip + gap, core)) for gap in (1, -2)]
     spots = jnp.asarray([spot_table(core, samp, band) for core in range(2)], jnp.int32)
     spot = spots[lax.axis_index("blk") % 2, side]
     return call(pick_kernel, (1, (2 * band + 1) * samp), spot, *tiles, name="pick")

time: 53.4 us -> 48.7 us (0.912)
  starting transfers between devices: 22.7 us -> 20.4 us
  Pallas kernels: 19.1 us -> 17.9 us
  local copies, waits for them, and re-layouts: 2.71 us -> 1.73 us
    ppermute x12 -> x10, starting transfers between devices: 21.3 us -> 18.6 us  [move(): return lax.ppermute(array, 'blk', pairs)]
    dynamic_slice x2 -> x0, local copies, waits for them, and re-layouts: 2.01 us -> none  [body(): lax.dynamic_slice_in_dim(mps, jnp.where(side == 0, start, sites - start -...]
    pallas_call x5 -> x7, Pallas kernels: 19.1 us -> 17.9 us  [call(): pl.pallas_call(kernel, out_shape=shapes if many else shapes[0], in_specs=...]
    unnamed x2, local copies, waits for them, and re-layouts: 0.01 us -> 1.04 us
    ppermute x12 -> x10, waiting for transfers between devices: 4.85 us -> 4.25 us  [move(): return lax.ppermute(array, 'blk', pairs)]
  transfers between devices with their start and end apart: 13 -> 11, of which waited for: 6 -> 7; matrix products, arithmetic and copies ran while one was open for 5% -> 1% of each run, Pallas kernels for 23% -> 24%
where the time goes in v5:
time: 48.7 us; the launch traced here: 48.5 us
  starting transfers between devices  20.4 us (42%)
  Pallas kernels  17.9 us (37%)
  waiting for transfers between devices  8.47 us (17%)
  local copies, waits for them, and re-layouts  1.73 us (4%)
    ppermute x10, starting transfers between devices, move(): return lax.ppermute(array, 'blk', pairs)  18.6 us
    pallas_call x7, Pallas kernels, call(): pl.pallas_call(kernel, out_shape=shapes if many else shapes[0], in_specs=...  17.9 us
    ppermute x10, waiting for transfers between devices, move(): return lax.ppermute(array, 'blk', pairs)  4.25 us
    ppermute x1, waiting for transfers between devices, body(): partner = lax.ppermute(state, 'pair', [(0, 1), (1, 0)])  4.22 us
    ppermute x1, starting transfers between devices, body(): partner = lax.ppermute(state, 'pair', [(0, 1), (1, 0)])  1.74 us
    unnamed x2, local copies, waits for them, and re-layouts  1.04 us
  transfers between devices with their start and end apart: 11, of which 7 were waited for; matrix products, arithmetic and copies ran while one was open for 1% of the time, Pallas kernels for 24%

profile of v5, /device:TPU:0, one launch (start us, length us, event | category | flops | bytes accessed | tf_op | source)
XLA Modules:
  0.0 48.5 jit_solution(15181555674526577128)
XLA Ops:
  0.0 0.0 copy-start
  0.0 1.0 %copy-done = f32[32,32,128]{2,1,0:T(8,128)S(1)} copy-done((f32[32,32,128]{2,1,0:T(8,128)S(1)}, f32[32,32,128]{2,1,0:T(8,128)}, u32[]{:S(2)}) %copy-start) | copy-done | bytes 524312
  1.0 1.0 %order.1 = (f32[27,32,128]{2,1,0:T(8,128)S(1)}, f32[17,32,128]{2,1,0:T(8,128)S(1)}, f32[10,32,128]{2,1,0:T(8,128)S(1)}) custom-call(s32[1]{0:T(128)} %bitcast.1.side_ref, f32[32,32,128]{2,1,0:T(8,128)S(1)} %copy-done), custom_call_target="tpu_custom_call" | custom-call | tf_op jit(solution)/shard_map/order/pallas_call | solution.py:275
  2.0 0.5 collective-permute-start
  2.5 4.7 %collective-permute-start.3 = (f32[17,32,128]{2,1,0:T(8,128)S(1)}, f32[17,32,128]{2,1,0:T(8,128)S(1)}, u32[]{:S(2)}, u32[]{:S(2)}) collective-permute-start(f32[17,32,128]{2,1,0:T(8,128)S(1)} %get-tuple-element.15), channel_id=1, source_target_pairs={{30,0},{8,2},{2,4},{12,6},{6,8},{16,10},{10,12},{20,14},{14,16},{2... | collective-permute-start | bytes 835592 | tf_op jit(solution)/shard_map/ppermute | solution.py:25
  7.2 1.5 %collective-permute-start.4 = (f32[17,32,128]{2,1,0:T(8,128)S(1)}, f32[17,32,128]{2,1,0:T(8,128)S(1)}, u32[]{:S(2)}, u32[]{:S(2)}) collective-permute-start(f32[17,32,128]{2,1,0:T(8,128)S(1)} %get-tuple-element.15), channel_id=1, source_target_pairs={{28,0},{10,2},{0,4},{14,6},{4,8},{18,10},{8,12},{22,14},{12,16},{2... | collective-permute-start | bytes 835592 | tf_op jit(solution)/shard_map/ppermute | solution.py:25
  8.7 0.0 collective-permute-done.sibling
  8.7 5.0 %own_chains.1.rest_0_ = f32[64,128]{1,0:T(8,128)S(1)} custom-call(s32[1]{0:T(128)} %bitcast.1.side_ref, f32[27,32,128]{2,1,0:T(8,128)S(1)} %get-tuple-element.13.own, f32[27,32,128]{2,1,0:T(8,128)S(1)} %collective-permute-done.sibling), custom_call_target="tpu_custom_call" | custom-call | tf_op jit(solution)/shard_map/own_chains/pallas_call | solution.py:275
  13.7 0.9 %collective-permute-done.3.second = f32[17,32,128]{2,1,0:T(8,128)S(1)} collective-permute-done((f32[17,32,128]{2,1,0:T(8,128)S(1)}, f32[17,32,128]{2,1,0:T(8,128)S(1)}, u32[]{:S(2)}, u32[]{:S(2)}) %collective-permute-start.3) | collective-permute-done | bytes 278560 | tf_op jit(solution)/shard_map/ppermute | solution.py:25
  14.6 0.0 collective-permute-start.5
  14.6 7.3 %collective-permute-start.2 = (f32[10,32,128]{2,1,0:T(8,128)S(1)}, f32[10,32,128]{2,1,0:T(8,128)S(1)}, u32[]{:S(2)}, u32[]{:S(2)}) collective-permute-start(f32[10,32,128]{2,1,0:T(8,128)S(1)} %get-tuple-element.14), channel_id=1, source_target_pairs={{30,0},{8,2},{2,4},{12,6},{6,8},{16,10},{10,12},{20,14},{14,16},{2... | collective-permute-start | bytes 491528 | tf_op jit(solution)/shard_map/ppermute | solution.py:25
  21.9 0.0 collective-permute-start.1
  21.9 0.1 collective-permute-done.4.first
  22.1 0.0 collective-permute-done.5.other
  22.1 6.4 %half_chains.2.rest_1_ = f32[320,128]{1,0:T(8,128)S(1)} custom-call(s32[1]{0:T(128)} %bitcast.1.side_ref, f32[27,32,128]{2,1,0:T(8,128)S(1)} %get-tuple-element.13.own, f32[27,32,128]{2,1,0:T(8,128)S(1)} %collective-permute-done.sibling, f32[17,32,128]{2,1,0:T(8,128)S(1)} %collective-permute-done.4.first, f32[17,32,128]{2,1,0:T(8,128)S(1)} %collective-permute-done.3.second, ...), custom_call_target="tpu_custom_call" | custom-call | tf_op jit(solution)/shard_map/half_chains/pallas_call | solution.py:275
  28.5 0.0 collective-permute-done.2.second
  28.5 0.1 collective-permute-start.6
  28.6 1.4 %collective-permute-done.1.first = f32[10,32,128]{2,1,0:T(8,128)S(1)} collective-permute-done((f32[10,32,128]{2,1,0:T(8,128)S(1)}, f32[10,32,128]{2,1,0:T(8,128)S(1)}, u32[]{:S(2)}, u32[]{:S(2)}) %collective-permute-start.1) | collective-permute-done | bytes 163872 | tf_op jit(solution)/shard_map/ppermute | solution.py:25
  30.0 0.0 collective-permute-done.6.other
  30.0 4.4 %half_chains.3.mine = f32[288,128]{1,0:T(8,128)S(1)} custom-call(s32[1]{0:T(128)} %bitcast.1.side_ref, f32[27,32,128]{2,1,0:T(8,128)S(1)} %get-tuple-element.13.own, f32[27,32,128]{2,1,0:T(8,128)S(1)} %collective-permute-done.sibling, f32[10,32,128]{2,1,0:T(8,128)S(1)} %collective-permute-done.1.first, f32[10,32,128]{2,1,0:T(8,128)S(1)} %collective-permute-done.2.second, ...), custom_call_target="tpu_custom_call" | custom-call | tf_op jit(solution)/shard_map/half_chains/pallas_call | solution.py:275
  34.4 1.7 %collective-permute-start.7 = (f32[288,128]{1,0:T(8,128)S(1)}, f32[288,128]{1,0:T(8,128)S(1)}, u32[]{:S(2)}, u32[]{:S(2)}) collective-permute-start(f32[288,128]{1,0:T(8,128)S(1)} %half_chains.3.mine), channel_id=1, source_target_pairs={{0,1},{1,0},{2,3},{3,2},{4,5},{5,4},{6,7},{7,6},{8,9},{9,8},{10,11... | collective-permute-start | bytes 442376 | tf_op jit(solution)/shard_map/ppermute | solution.py:311
  36.1 4.2 %collective-permute-done.7.theirs = f32[288,128]{1,0:T(8,128)S(1)} collective-permute-done((f32[288,128]{1,0:T(8,128)S(1)}, f32[288,128]{1,0:T(8,128)S(1)}, u32[]{:S(2)}, u32[]{:S(2)}) %collective-permute-start.7) | collective-permute-done | bytes 147488 | tf_op jit(solution)/shard_map/ppermute | solution.py:311
  40.3 0.2 meet.1.mine
  40.5 0.0 collective-permute-start.8
  40.5 1.2 %collective-permute-done.8.theirs = f32[8,128]{1,0:T(8,128)S(1)} collective-permute-done((f32[8,128]{1,0:T(8,128)S(1)}, f32[8,128]{1,0:T(8,128)S(1)}, u32[]{:S(2)}, u32[]{:S(2)}) %collective-permute-start.8) | collective-permute-done | bytes 4128 | tf_op jit(solution)/shard_map/ppermute | solution.py:25
  41.7 0.1 join.1.here
  41.7 0.2 collective-permute-start.10
  41.9 4.4 %collective-permute-start.9 = (f32[8,128]{1,0:T(8,128)S(1)}, f32[8,128]{1,0:T(8,128)S(1)}, u32[]{:S(2)}, u32[]{:S(2)}) collective-permute-start(f32[8,128]{1,0:T(8,128)S(1)} %join.1.here), channel_id=1, source_target_pairs={{4,0},{6,2},{8,4},{10,6},{12,8},{14,10},{16,12},{18,14},{20,16},{2... | collective-permute-start | bytes 12296 | tf_op jit(solution)/shard_map/ppermute | solution.py:25
  46.3 0.7 %dynamic-slice_bitcast_fusion.spot_ref = s32[8,128]{1,0:T(8,128)S(1)} fusion(s32[2,2,8,128]{3,2,1,0:T(8,128)} %constant.24.clone, s32[]{:T(128)S(6)} %select_n.14, s32[]{:T(128)S(6)} %select_n.15), kind=kLoop, calls=%fused_computation | loop fusion | bytes 8200 | tf_op jit(solution)/shard_map/squeeze | solution.py:316
  47.0 0.1 collective-permute-done.10.before
  47.2 0.5 %collective-permute-done.9.after = f32[8,128]{1,0:T(8,128)S(1)} collective-permute-done((f32[8,128]{1,0:T(8,128)S(1)}, f32[8,128]{1,0:T(8,128)S(1)}, u32[]{:S(2)}, u32[]{:S(2)}) %collective-permute-start.9) | collective-permute-done | bytes 4128 | tf_op jit(solution)/shard_map/ppermute | solution.py:25
  47.7 0.8 %pick.1 = f32[1,26]{1,0:T(1,128)} custom-call(s32[8,128]{1,0:T(8,128)S(1)} %dynamic-slice_bitcast_fusion.spot_ref, f32[8,128]{1,0:T(8,128)S(1)} %join.1.here, f32[8,128]{1,0:T(8,128)S(1)} %collective-permute-done.9.after, f32[8,128]{1,0:T(8,128)S(1)} %collective-permute-done.10.before), custom_call_target="tpu_custom_call" | custom-call | tf_op jit(solution)/shard_map/pick/pallas_call | solution.py:275
Async XLA Ops:
  0.0 1.0 %copy-start = (f32[32,32,128]{2,1,0:T(8,128)S(1)}, f32[32,32,128]{2,1,0:T(8,128)}, u32[]{:S(2)}) copy-start(f32[32,32,128]{2,1,0:T(8,128)} %sites_ref.1) | copy-start | bytes 1572868
  2.0 6.7 %collective-permute-start = (f32[27,32,128]{2,1,0:T(8,128)S(1)}, f32[27,32,128]{2,1,0:T(8,128)S(1)}, u32[]{:S(2)}, u32[]{:S(2)}) collective-permute-start(f32[27,32,128]{2,1,0:T(8,128)S(1)} %get-tuple-element.13.own), channel_id=1, source_target_pairs={{2,0},{0,2},{6,4},{4,6},{10,8},{8,10},{14,12},{12,14},{18,16},{16,... | collective-permute-start | bytes 1327112 | tf_op jit(solution)/shard_map/ppermute | solution.py:25
  2.5 12.2 %collective-permute-start.3 = (f32[17,32,128]{2,1,0:T(8,128)S(1)}, f32[17,32,128]{2,1,0:T(8,128)S(1)}, u32[]{:S(2)}, u32[]{:S(2)}) collective-permute-start(f32[17,32,128]{2,1,0:T(8,128)S(1)} %get-tuple-element.15), channel_id=1, source_target_pairs={{30,0},{8,2},{2,4},{12,6},{6,8},{16,10},{10,12},{20,14},{14,16},{2... | collective-permute-start | bytes 835592 | tf_op jit(solution)/shard_map/ppermute | solution.py:25
  7.2 14.9 %collective-permute-start.4 = (f32[17,32,128]{2,1,0:T(8,128)S(1)}, f32[17,32,128]{2,1,0:T(8,128)S(1)}, u32[]{:S(2)}, u32[]{:S(2)}) collective-permute-start(f32[17,32,128]{2,1,0:T(8,128)S(1)} %get-tuple-element.15), channel_id=1, source_target_pairs={{28,0},{10,2},{0,4},{14,6},{4,8},{18,10},{8,12},{22,14},{12,16},{2... | collective-permute-start | bytes 835592 | tf_op jit(solution)/shard_map/ppermute | solution.py:25
  14.6 7.4 %collective-permute-start.5 = (f32[17,32,128]{2,1,0:T(8,128)S(1)}, f32[17,32,128]{2,1,0:T(8,128)S(1)}, u32[]{:S(2)}, u32[]{:S(2)}) collective-permute-start(f32[17,32,128]{2,1,0:T(8,128)S(1)} %collective-permute-done.3.second), channel_id=1, source_target_pairs={{2,0},{0,2},{6,4},{4,6},{10,8},{8,10},{14,12},{12,14},{18,16},{16,... | collective-permute-start | bytes 835592 | tf_op jit(solution)/shard_map/ppermute | solution.py:25
  14.6 13.9 %collective-permute-start.2 = (f32[10,32,128]{2,1,0:T(8,128)S(1)}, f32[10,32,128]{2,1,0:T(8,128)S(1)}, u32[]{:S(2)}, u32[]{:S(2)}) collective-permute-start(f32[10,32,128]{2,1,0:T(8,128)S(1)} %get-tuple-element.14), channel_id=1, source_target_pairs={{30,0},{8,2},{2,4},{12,6},{6,8},{16,10},{10,12},{20,14},{14,16},{2... | collective-permute-start | bytes 491528 | tf_op jit(solution)/shard_map/ppermute | solution.py:25
  21.9 8.0 %collective-permute-start.1 = (f32[10,32,128]{2,1,0:T(8,128)S(1)}, f32[10,32,128]{2,1,0:T(8,128)S(1)}, u32[]{:S(2)}, u32[]{:S(2)}) collective-permute-start(f32[10,32,128]{2,1,0:T(8,128)S(1)} %get-tuple-element.14), channel_id=1, source_target_pairs={{28,0},{10,2},{0,4},{14,6},{4,8},{18,10},{8,12},{22,14},{12,16},{2... | collective-permute-start | bytes 491528 | tf_op jit(solution)/shard_map/ppermute | solution.py:25
  28.5 1.5 %collective-permute-start.6 = (f32[10,32,128]{2,1,0:T(8,128)S(1)}, f32[10,32,128]{2,1,0:T(8,128)S(1)}, u32[]{:S(2)}, u32[]{:S(2)}) collective-permute-start(f32[10,32,128]{2,1,0:T(8,128)S(1)} %collective-permute-done.2.second), channel_id=1, source_target_pairs={{2,0},{0,2},{6,4},{4,6},{10,8},{8,10},{14,12},{12,14},{18,16},{16,... | collective-permute-start | bytes 491528 | tf_op jit(solution)/shard_map/ppermute | solution.py:25
  34.4 6.0 %collective-permute-start.7 = (f32[288,128]{1,0:T(8,128)S(1)}, f32[288,128]{1,0:T(8,128)S(1)}, u32[]{:S(2)}, u32[]{:S(2)}) collective-permute-start(f32[288,128]{1,0:T(8,128)S(1)} %half_chains.3.mine), channel_id=1, source_target_pairs={{0,1},{1,0},{2,3},{3,2},{4,5},{5,4},{6,7},{7,6},{8,9},{9,8},{10,11... | collective-permute-start | bytes 442376 | tf_op jit(solution)/shard_map/ppermute | solution.py:311
  40.5 1.2 %collective-permute-start.8 = (f32[8,128]{1,0:T(8,128)S(1)}, f32[8,128]{1,0:T(8,128)S(1)}, u32[]{:S(2)}, u32[]{:S(2)}) collective-permute-start(f32[8,128]{1,0:T(8,128)S(1)} %meet.1.mine), channel_id=1, source_target_pairs={{2,0},{0,2},{6,4},{4,6},{10,8},{8,10},{14,12},{12,14},{18,16},{16,... | collective-permute-start | bytes 12296 | tf_op jit(solution)/shard_map/ppermute | solution.py:25
  41.7 5.4 %collective-permute-start.10 = (f32[8,128]{1,0:T(8,128)S(1)}, f32[8,128]{1,0:T(8,128)S(1)}, u32[]{:S(2)}, u32[]{:S(2)}) collective-permute-start(f32[8,128]{1,0:T(8,128)S(1)} %join.1.here), channel_id=1, source_target_pairs={{24,0},{26,2},{28,4},{30,6},{0,8},{2,10},{4,12},{6,14},{8,16},{10,... | collective-permute-start | bytes 12296 | tf_op jit(solution)/shard_map/ppermute | solution.py:25
  41.9 5.8 %collective-permute-start.9 = (f32[8,128]{1,0:T(8,128)S(1)}, f32[8,128]{1,0:T(8,128)S(1)}, u32[]{:S(2)}, u32[]{:S(2)}) collective-permute-start(f32[8,128]{1,0:T(8,128)S(1)} %join.1.here), channel_id=1, source_target_pairs={{4,0},{6,2},{8,4},{10,6},{12,8},{14,10},{16,12},{18,14},{20,16},{2... | collective-permute-start | bytes 12296 | tf_op jit(solution)/shard_map/ppermute | solution.py:25

commit v6 on v5

--- a/solution.py
+++ b/solution.py
@@ -120,23 +120,38 @@
     return current
 
 
-def order_kernel(side_ref, sites_ref, whole, *pieces):
-    sites = sites_ref.shape[0]
+def order_kernel(side_ref, sites_ref, whole, *rest):
+    *pieces, edges, semaphores = rest
+    sites, steps = sites_ref.shape[0], whole.shape[0]
 
     def run(flip):
-        def tile(k):
-            return sites_ref[sites - 1 - k if flip else k]
-
-        edge = edge_tile([turned(tile(k)) if flip else tile(k) for k in range(EDGE)])
+        outer = sites_ref.at[pl.ds(sites - EDGE if flip else 0, EDGE)]
+        copies = [pltpu.make_async_copy(outer, edges, semaphores.at[0])]
+        begin = 0
+        spots = []
+        for k, (array, start) in enumerate([(whole, 0)] + [(p, None) for p in pieces]):
+            start = begin if start is None else start
+            count = array.shape[0]
+            begin = 0 if k == 0 else begin + count
+            spare = 1 if start == 0 else 0
+            low = steps - start - count if flip else start
+            kept = count - spare
+            source = sites_ref.at[pl.ds(low if flip else low + spare + EDGE - 1, kept)]
+            target = array.at[pl.ds(0 if flip else spare, kept)]
+            copies.append(pltpu.make_async_copy(source, target, semaphores.at[k + 1]))
+            if spare:
+                spots.append((array, count - 1 if flip else 0))
+        for copy in copies:
+            copy.start()
+        copies[0].wait()
+        tiles = [edges[EDGE - 1 - k if flip else k] for k in range(EDGE)]
+        edge = edge_tile([turned(t) for t in tiles] if flip else tiles)
         if flip:
             edge = turned(edge)
-        at = 0
-        for piece in pieces:
-            for k in range(piece.shape[0]):
-                value = edge if at == 0 else tile(at + EDGE - 1)
-                piece[k] = value
-                whole[at] = value
-                at += 1
+        for array, at in spots:
+            array[at] = edge
+        for copy in copies[1:]:
+            copy.wait()
 
     on_each_side(side_ref, run)
 
@@ -149,16 +164,16 @@
     return jnp.concatenate([state[:192], kept], 0)
 
 
-def home_step(state, home, near, flip):
-    return advance(state, near[:2], far_weights(home, flip))
-
-
-def home_kernel(count, side_ref, own, sibling, out):
+def home_kernel(start, count, side_ref, own, sibling, *rest):
+    out = rest[-1]
+
     def run(flip):
-        state = identities(64)
-        for site in range(count):
+        state = rest[0][...] if start else identities(64)
+        for step in range(start, start + count):
+            site = own.shape[0] - 1 - step if flip else step
             home = interleave(own[site], sibling[site])
-            state = home_step(state, home, near_plain(own[site]) if flip else near_turned(home), flip)
+            near = near_plain(own[site]) if flip else near_turned(home)[:2]
+            state = advance(state, near, far_weights(home, flip))
         out[...] = state
 
     on_each_side(side_ref, run)
@@ -166,34 +181,39 @@
 
 def chain_kernel(start, side_ref, own, sibling, first, second, other, *rest):
     out = rest[-1]
-    count = first.shape[0]
-    last = start + count == own.shape[0]
+    count, steps = first.shape[0], own.shape[0]
 
     def run(flip):
-        state = rest[1][...] if start else identities(320)
-        inner = rest[0][...] if last else None
+        state = rest[-2][...] if start else identities(320)
         for index in range(count):
-            whole = start + index
-            home = interleave(own[whole], sibling[whole])
-            far = interleave(first[index], second[index])
+            whole = steps - 1 - start - index if flip else start + index
+            part = count - 1 - index if flip else index
+            far = interleave(first[part], second[part])
             if flip:
-                near = [n for t in (own[whole], sibling[whole], other[index], first[index], second[index])
+                near = [n for t in (own[whole], sibling[whole], other[part], first[part], second[part])
                         for n in near_plain(t)]
             else:
-                extra = other[index]
-                near = near_turned(home) + near_turned(interleave(extra, extra))[:2] + near_turned(far)
+                extra = other[part]
+                near = (
+                    near_turned(interleave(own[whole], sibling[whole]))
+                    + near_turned(interleave(extra, extra))[:2]
+                    + near_turned(far)
+                )
             weights = far_weights(far, flip)
             parts = [advance(state[:192], near[:6], weights), advance(state[192:], near[6:], weights)]
             state = jnp.concatenate(parts, 0)
-            if last:
-                inner = home_step(inner, home, near, flip)
-        out[...] = jnp.concatenate([norms_only(state), inner], 0) if last else state
+        out[...] = norms_only(state) if start + count == steps else state
 
     on_each_side(side_ref, run)
 
 
-def meet_kernel(mine, theirs, out):
-    units = jnp.sum((mine[...] * theirs[...]).reshape(-1, 32, 128), 1)
+def meet_kernel(*refs):
+    *states, out = refs
+    units = [
+        jnp.sum((mine[...] * theirs[...]).reshape(-1, 32, 128), 1)
+        for mine, theirs in zip(states[::2], states[1::2])
+    ]
+    units = jnp.concatenate(units, 0)
     units = jnp.concatenate([units, jnp.zeros((16 - units.shape[0], 128), F32)], 0)
     row = lax.broadcasted_iota(jnp.int32, (8, 128), 0)
     chosen = jnp.where(row == lane_slot((8, 128)), 1.0, 0.0)
@@ -207,19 +227,20 @@
     out[...] = mine[...] + pltpu.roll(theirs[...], 16, 1)
 
 
-def pick_kernel(spot_ref, here, after, before, out):
+def pick_kernel(which_ref, spots_ref, here, after, before, out):
     joined = here[...] + pltpu.roll(after[...], 32, 1) + pltpu.roll(before[...], 64, 1)
+    spots = spots_ref[which_ref[0]]
     unit = lax.broadcasted_iota(jnp.int32, (128, 128), 0)
     slot = lax.broadcasted_iota(jnp.int32, (8, 128), 0)
-    values = []
-    for k in range(3):
-        spot = spot_ref[pl.ds(k, 1), :]
-        chosen = jnp.where(unit == spot // 8, 1.0, 0.0)
-        found = jnp.dot(joined, chosen, precision=lax.Precision.HIGHEST, preferred_element_type=F32)
-        values.append(jnp.sum(jnp.where(slot == spot % 8, found, 0.0), 0, keepdims=True))
-    tile, remote, own = values
-    width = out.shape[1]
-    out[...] = (tile * tile / (own * remote))[:, :width]
+    chosen = [jnp.where(unit == spots[k : k + 1] // 8, 1.0, 0.0) for k in range(3)]
+    found = jnp.dot(
+        joined, jnp.concatenate(chosen, 1), precision=lax.Precision.HIGHEST, preferred_element_type=F32
+    )
+    tile, remote, own = [
+        jnp.sum(jnp.where(slot == spots[k : k + 1] % 8, found[:, 128 * k : 128 * k + 128], 0.0), 0, keepdims=True)
+        for k in range(3)
+    ]
+    out[...] = (tile * tile / (own * remote))[:, : out.shape[1]]
 
 
 def find(core, near, far):
@@ -269,14 +290,15 @@
     return table
 
 
-def call(kernel, shapes, *args, name):
+def call(kernel, shapes, *args, name, spaces=None, scratch=()):
     many = isinstance(shapes, list)
     shapes = [jax.ShapeDtypeStruct(shape, F32) for shape in (shapes if many else [shapes])]
     return pl.pallas_call(
         kernel,
         out_shape=shapes if many else shapes[0],
-        in_specs=[SMEM if a.ndim == 1 else VMEM for a in args],
+        in_specs=spaces or [SMEM if a.ndim == 1 else VMEM for a in args],
         out_specs=[VMEM] * len(shapes) if many else VMEM,
+        scratch_shapes=scratch,
         compiler_params=pltpu.CompilerParams(vmem_limit_bytes=40 * 2**20),
         name=name,
     )(*args)
@@ -289,32 +311,51 @@
     band = min(REACH, (blocks - 1) // 2)
     side = lax.axis_index("pair")
     flag = side[None].astype(jnp.int32)
+    core = lax.axis_index("blk") % 2
 
     steps = sites - EDGE + 1
     starts = [0, round(SHARE * steps)]
     counts = [starts[1], steps - starts[1]]
     tile = mps.shape[1:]
-    mps, *pieces = call(order_kernel, [(n, *tile) for n in (steps, *counts)], flag, mps, name="order")
+    own, *pieces = call(
+        order_kernel,
+        [(n, *tile) for n in (steps, *counts)],
+        flag,
+        mps,
+        name="order",
+        spaces=[SMEM, pl.BlockSpec(memory_space=pltpu.HBM)],
+        scratch=[pltpu.VMEM((EDGE, *tile), F32), pltpu.SemaphoreType.DMA((2 + len(counts),))],
+    )
     seconds = [move(p, lambda chip, core: (chip - 1, 1) if core == 0 else (chip + 2, 0)) for p in pieces]
     firsts = [move(p, lambda chip, core: (chip - 1, 0) if core == 0 else (chip + 2, 1)) for p in pieces]
     across = lambda chip, core: (chip, 1 - core)
-    sibling = move(mps, across)
-    inner = call(functools.partial(home_kernel, starts[-1]), (64, 128), flag, mps, sibling, name="own_chains")
-    carried = (inner,)
-    for start, first, second in zip(starts, firsts, seconds):
-        second, *carried = lax.optimization_barrier((second, *carried))
+    swap = [(0, 1), (1, 0)]
+    sibling = move(own, across)
+
+    early = steps // 2
+    home = functools.partial(home_kernel, 0, early)
+    home = call(home, (64, 128), flag, own, sibling, name="own_chains")
+    carried = (home,)
+    for k, (start, first, second) in enumerate(zip(starts, firsts, seconds)):
+        second, behind = lax.optimization_barrier((second, carried[-1]))
+        carried = (*carried[:-1], behind)
         other = move(second, across)
-        rows = 288 if start == starts[-1] else 320
-        state = call(functools.partial(chain_kernel, start), (rows, 128), flag, mps, sibling, first, second, other,
+        if k == 0:
+            home = functools.partial(home_kernel, early, steps - early)
+            home = call(home, (64, 128), flag, own, sibling, *carried, name="own_chains")
+            far_home = lax.ppermute(home, "pair", swap)
+            carried = (home,)
+        rows = 224 if k == len(starts) - 1 else 320
+        state = call(functools.partial(chain_kernel, start), (rows, 128), flag, own, sibling, first, second, other,
                      *carried, name="half_chains")
-        carried = (carried[0], state)
-    partner = lax.ppermute(state, "pair", [(0, 1), (1, 0)])
-    tile = call(meet_kernel, (8, 128), state, partner, name="meet")
+        carried = (far_home, state)
+    partner = lax.ppermute(state, "pair", swap)
+    tile = call(meet_kernel, (8, 128), state, partner, home, far_home, name="meet")
     tile = call(join_kernel, (8, 128), tile, move(tile, across), name="join")
     tiles = [tile] + [move(tile, lambda chip, core: (chip + gap, core)) for gap in (1, -2)]
-    spots = jnp.asarray([spot_table(core, samp, band) for core in range(2)], jnp.int32)
-    spot = spots[lax.axis_index("blk") % 2, side]
-    return call(pick_kernel, (1, (2 * band + 1) * samp), spot, *tiles, name="pick")
+    spots = jnp.asarray([t for k in range(2) for t in spot_table(k, samp, band)], jnp.int32)
+    which = (core * samp + side)[None].astype(jnp.int32)
+    return call(pick_kernel, (1, (2 * band + 1) * samp), which, spots, *tiles, name="pick")
 
 
 def solution(mesh):

time: 48.7 us -> 58.4 us (1.20)
  waiting for transfers between devices: 8.47 us -> 13.5 us
  Pallas kernels: 17.9 us -> 20.8 us
  starting transfers between devices: 20.4 us -> 22.9 us
  local copies, waits for them, and re-layouts: 1.73 us -> 1.04 us
    ppermute x10, waiting for transfers between devices: 4.25 us -> 8.66 us  [move(): return lax.ppermute(array, 'blk', pairs)]
    pallas_call x7 -> x8, Pallas kernels: 17.9 us -> 20.8 us  [call(): pl.pallas_call(kernel, out_shape=shapes if many else shapes[0], in_specs=...]
    ppermute x1 -> x2, starting transfers between devices: 1.74 us -> 3.94 us  [the longest x1 2.04 us: body(): partner = lax.ppermute(state, 'pair', swap)]
    squeeze x1 -> x0, local copies, waits for them, and re-layouts: 0.69 us -> none  [body(): spot = spots[lax.axis_index('blk') % 2, side]]
    ppermute x1 -> x2, waiting for transfers between devices: 4.22 us -> 4.84 us  [the longest x1 2.82 us: body(): partner = lax.ppermute(state, 'pair', swap)]
  transfers between devices with their start and end apart: 11 -> 12, of which waited for: 7 -> 6; matrix products, arithmetic and copies ran while one was open for 1% -> 0% of each run, Pallas kernels for 24% -> 25%
where the time goes in v6:
time: 58.4 us; the launch traced here: 58.3 us
  starting transfers between devices  22.9 us (39%)
  Pallas kernels  20.8 us (36%)
  waiting for transfers between devices  13.5 us (23%)
  local copies, waits for them, and re-layouts  1.04 us (2%)
    pallas_call x8, Pallas kernels, call(): pl.pallas_call(kernel, out_shape=shapes if many else shapes[0], in_specs=...  20.8 us
    ppermute x10, starting transfers between devices, move(): return lax.ppermute(array, 'blk', pairs)  18.9 us
    ppermute x10, waiting for transfers between devices, move(): return lax.ppermute(array, 'blk', pairs)  8.66 us
    ppermute x1, waiting for transfers between devices, body(): partner = lax.ppermute(state, 'pair', swap)  2.82 us
    ppermute x1, starting transfers between devices, body(): partner = lax.ppermute(state, 'pair', swap)  2.04 us
    ppermute x1, waiting for transfers between devices, body(): far_home = lax.ppermute(home, 'pair', swap)  2.02 us
    ppermute x1, starting transfers between devices, body(): far_home = lax.ppermute(home, 'pair', swap)  1.9 us
  transfers between devices with their start and end apart: 12, of which 6 were waited for; matrix products, arithmetic and copies ran while one was open for 0% of the time, Pallas kernels for 25%

profile of v6, /device:TPU:0, one launch (start us, length us, event | category | flops | bytes accessed | tf_op | source)
XLA Modules:
  0.0 58.3 jit_solution(16738151335459953019)
XLA Ops:
  0.0 1.0 %copy-done = f32[32,32,128]{2,1,0:T(8,128)S(1)} copy-done((f32[32,32,128]{2,1,0:T(8,128)S(1)}, f32[32,32,128]{2,1,0:T(8,128)}, u32[]{:S(2)}) %copy-start) | copy-done | bytes 524312
  1.0 1.6 %order.1 = (f32[27,32,128]{2,1,0:T(8,128)S(1)}, f32[17,32,128]{2,1,0:T(8,128)S(1)}, f32[10,32,128]{2,1,0:T(8,128)S(1)}) custom-call(s32[1]{0:T(128)} %bitcast.1.side_ref, f32[32,32,128]{2,1,0:T(8,128)S(1)} %copy-done), custom_call_target="tpu_custom_call" | custom-call | tf_op jit(solution)/shard_map/order/pallas_call | solution.py:296
  2.6 0.5 collective-permute-start
  3.2 4.7 %collective-permute-start.4 = (f32[17,32,128]{2,1,0:T(8,128)S(1)}, f32[17,32,128]{2,1,0:T(8,128)S(1)}, u32[]{:S(2)}, u32[]{:S(2)}) collective-permute-start(f32[17,32,128]{2,1,0:T(8,128)S(1)} %get-tuple-element.14), channel_id=1, source_target_pairs={{30,0},{8,2},{2,4},{12,6},{6,8},{16,10},{10,12},{20,14},{14,16},{2... | collective-permute-start | bytes 835592 | tf_op jit(solution)/shard_map/ppermute | solution.py:25
  7.9 1.5 %collective-permute-start.3 = (f32[17,32,128]{2,1,0:T(8,128)S(1)}, f32[17,32,128]{2,1,0:T(8,128)S(1)}, u32[]{:S(2)}, u32[]{:S(2)}) collective-permute-start(f32[17,32,128]{2,1,0:T(8,128)S(1)} %get-tuple-element.14), channel_id=1, source_target_pairs={{28,0},{10,2},{0,4},{14,6},{4,8},{18,10},{8,12},{22,14},{12,16},{2... | collective-permute-start | bytes 835592 | tf_op jit(solution)/shard_map/ppermute | solution.py:25
  9.4 0.0 collective-permute-done.sibling
  9.4 3.9 %own_chains.2.rest_0_ = f32[64,128]{1,0:T(8,128)S(1)} custom-call(s32[1]{0:T(128)} %bitcast.1.side_ref, f32[27,32,128]{2,1,0:T(8,128)S(1)} %get-tuple-element.12.own, f32[27,32,128]{2,1,0:T(8,128)S(1)} %collective-permute-done.sibling), custom_call_target="tpu_custom_call" | custom-call | tf_op jit(solution)/shard_map/own_chains/pallas_call | solution.py:296
  13.2 2.1 %collective-permute-done.4.second = f32[17,32,128]{2,1,0:T(8,128)S(1)} collective-permute-done((f32[17,32,128]{2,1,0:T(8,128)S(1)}, f32[17,32,128]{2,1,0:T(8,128)S(1)}, u32[]{:S(2)}, u32[]{:S(2)}) %collective-permute-start.4) | collective-permute-done | bytes 278560 | tf_op jit(solution)/shard_map/ppermute | solution.py:25
  15.3 0.0 collective-permute-start.5
  15.3 7.4 %collective-permute-start.2 = (f32[10,32,128]{2,1,0:T(8,128)S(1)}, f32[10,32,128]{2,1,0:T(8,128)S(1)}, u32[]{:S(2)}, u32[]{:S(2)}) collective-permute-start(f32[10,32,128]{2,1,0:T(8,128)S(1)} %get-tuple-element.13), channel_id=1, source_target_pairs={{30,0},{8,2},{2,4},{12,6},{6,8},{16,10},{10,12},{20,14},{14,16},{2... | collective-permute-start | bytes 491528 | tf_op jit(solution)/shard_map/ppermute | solution.py:25
  22.7 0.0 collective-permute-start.1
  22.7 4.2 %own_chains.3.rest_0_.refs_2_ = f32[64,128]{1,0:T(8,128)S(1)} custom-call(s32[1]{0:T(128)} %bitcast.1.side_ref, f32[27,32,128]{2,1,0:T(8,128)S(1)} %get-tuple-element.12.own, f32[27,32,128]{2,1,0:T(8,128)S(1)} %collective-permute-done.sibling, f32[64,128]{1,0:T(8,128)S(1)} %own_chains.2.rest_0_), custom_call_target="tpu_custom_call" | custom-call | tf_op jit(solution)/shard_map/own_chains/pallas_call | solution.py:296
  26.9 0.0 collective-permute-done.3.first
  26.9 0.0 collective-permute-done.5.other
  26.9 6.4 %half_chains.2.rest_1_ = f32[320,128]{1,0:T(8,128)S(1)} custom-call(s32[1]{0:T(128)} %bitcast.1.side_ref, f32[27,32,128]{2,1,0:T(8,128)S(1)} %get-tuple-element.12.own, f32[27,32,128]{2,1,0:T(8,128)S(1)} %collective-permute-done.sibling, f32[17,32,128]{2,1,0:T(8,128)S(1)} %collective-permute-done.3.first, f32[17,32,128]{2,1,0:T(8,128)S(1)} %collective-permute-done.4.second, ...), custom_call_target="tpu_custom_call" | custom-call | tf_op jit(solution)/shard_map/half_chains/pallas_call | solution.py:296
  33.3 0.0 collective-permute-done.2.second
  33.3 0.2 collective-permute-start.6
  33.5 1.9 %collective-permute-start.7 = (f32[64,128]{1,0:T(8,128)S(1)}, f32[64,128]{1,0:T(8,128)S(1)}, u32[]{:S(2)}, u32[]{:S(2)}) collective-permute-start(f32[64,128]{1,0:T(8,128)S(1)} %own_chains.3.rest_0_.refs_2_), channel_id=1, source_target_pairs={{0,1},{1,0},{2,3},{3,2},{4,5},{5,4},{6,7},{7,6},{8,9},{9,8},{10,11... | collective-permute-start | bytes 98312 | tf_op jit(solution)/shard_map/ppermute | solution.py:346
  35.4 0.0 collective-permute-done.1.first
  35.4 2.0 %collective-permute-done.7.rest_0_.refs_3_ = f32[64,128]{1,0:T(8,128)S(1)} collective-permute-done((f32[64,128]{1,0:T(8,128)S(1)}, f32[64,128]{1,0:T(8,128)S(1)}, u32[]{:S(2)}, u32[]{:S(2)}) %collective-permute-start.7) | collective-permute-done | bytes 32800 | tf_op jit(solution)/shard_map/ppermute | solution.py:346
  37.4 0.0 collective-permute-done.6.other
  37.4 3.7 %half_chains.3.refs_0_ = f32[224,128]{1,0:T(8,128)S(1)} custom-call(s32[1]{0:T(128)} %bitcast.1.side_ref, f32[27,32,128]{2,1,0:T(8,128)S(1)} %get-tuple-element.12.own, f32[27,32,128]{2,1,0:T(8,128)S(1)} %collective-permute-done.sibling, f32[10,32,128]{2,1,0:T(8,128)S(1)} %collective-permute-done.1.first, f32[10,32,128]{2,1,0:T(8,128)S(1)} %collective-permute-done.2.second, ...), custom_call_target="tpu_custom_call" | custom-call | tf_op jit(solution)/shard_map/half_chains/pallas_call | solution.py:296
  41.2 2.0 %collective-permute-start.8 = (f32[224,128]{1,0:T(8,128)S(1)}, f32[224,128]{1,0:T(8,128)S(1)}, u32[]{:S(2)}, u32[]{:S(2)}) collective-permute-start(f32[224,128]{1,0:T(8,128)S(1)} %half_chains.3.refs_0_), channel_id=1, source_target_pairs={{0,1},{1,0},{2,3},{3,2},{4,5},{5,4},{6,7},{7,6},{8,9},{9,8},{10,11... | collective-permute-start | bytes 344072 | tf_op jit(solution)/shard_map/ppermute | solution.py:352
  43.2 2.8 %collective-permute-done.8.refs_1_ = f32[224,128]{1,0:T(8,128)S(1)} collective-permute-done((f32[224,128]{1,0:T(8,128)S(1)}, f32[224,128]{1,0:T(8,128)S(1)}, u32[]{:S(2)}, u32[]{:S(2)}) %collective-permute-start.8) | collective-permute-done | bytes 114720 | tf_op jit(solution)/shard_map/ppermute | solution.py:352
  46.0 0.2 meet.1.mine
  46.2 1.2 %collective-permute-done.9.theirs = f32[8,128]{1,0:T(8,128)S(1)} collective-permute-done((f32[8,128]{1,0:T(8,128)S(1)}, f32[8,128]{1,0:T(8,128)S(1)}, u32[]{:S(2)}, u32[]{:S(2)}) %collective-permute-start.9) | collective-permute-done | bytes 4128 | tf_op jit(solution)/shard_map/ppermute | solution.py:25
  47.3 0.1 join.1.here
  47.4 4.6 %collective-permute-start.10 = (f32[8,128]{1,0:T(8,128)S(1)}, f32[8,128]{1,0:T(8,128)S(1)}, u32[]{:S(2)}, u32[]{:S(2)}) collective-permute-start(f32[8,128]{1,0:T(8,128)S(1)} %join.1.here), channel_id=1, source_target_pairs={{4,0},{6,2},{8,4},{10,6},{12,8},{14,10},{16,12},{18,14},{20,16},{2... | collective-permute-start | bytes 12296 | tf_op jit(solution)/shard_map/ppermute | solution.py:25
  52.1 0.0 collective-permute-start.11
  52.1 1.3 %collective-permute-done.10.after = f32[8,128]{1,0:T(8,128)S(1)} collective-permute-done((f32[8,128]{1,0:T(8,128)S(1)}, f32[8,128]{1,0:T(8,128)S(1)}, u32[]{:S(2)}, u32[]{:S(2)}) %collective-permute-start.10) | collective-permute-done | bytes 4128 | tf_op jit(solution)/shard_map/ppermute | solution.py:25
  53.4 4.1 %collective-permute-done.11.before = f32[8,128]{1,0:T(8,128)S(1)} collective-permute-done((f32[8,128]{1,0:T(8,128)S(1)}, f32[8,128]{1,0:T(8,128)S(1)}, u32[]{:S(2)}, u32[]{:S(2)}) %collective-permute-start.11) | collective-permute-done | bytes 4128 | tf_op jit(solution)/shard_map/ppermute | solution.py:25
  57.5 0.8 %pick.1 = f32[1,26]{1,0:T(1,128)} custom-call(s32[1]{0:T(128)} %bitcast.which_ref, s32[4,8,128]{2,1,0:T(8,128)S(1)} %copy-done.1, f32[8,128]{1,0:T(8,128)S(1)} %join.1.here, f32[8,128]{1,0:T(8,128)S(1)} %collective-permute-done.10.after, f32[8,128]{1,0:T(8,128)S(1)} %collective-permute-done.11.before), custom_call_target="tpu_custom_call" | custom-call | tf_op jit(solution)/shard_map/pick/pallas_call | solution.py:296
  (4 shorter events, 0.0 us)
Async XLA Ops:
  0.0 1.0 %copy-start = (f32[32,32,128]{2,1,0:T(8,128)S(1)}, f32[32,32,128]{2,1,0:T(8,128)}, u32[]{:S(2)}) copy-start(f32[32,32,128]{2,1,0:T(8,128)} %sites_ref.1) | copy-start | bytes 1572868
  2.6 6.7 %collective-permute-start = (f32[27,32,128]{2,1,0:T(8,128)S(1)}, f32[27,32,128]{2,1,0:T(8,128)S(1)}, u32[]{:S(2)}, u32[]{:S(2)}) collective-permute-start(f32[27,32,128]{2,1,0:T(8,128)S(1)} %get-tuple-element.12.own), channel_id=1, source_target_pairs={{2,0},{0,2},{6,4},{4,6},{10,8},{8,10},{14,12},{12,14},{18,16},{16,... | collective-permute-start | bytes 1327112 | tf_op jit(solution)/shard_map/ppermute | solution.py:25
  3.2 12.2 %collective-permute-start.4 = (f32[17,32,128]{2,1,0:T(8,128)S(1)}, f32[17,32,128]{2,1,0:T(8,128)S(1)}, u32[]{:S(2)}, u32[]{:S(2)}) collective-permute-start(f32[17,32,128]{2,1,0:T(8,128)S(1)} %get-tuple-element.14), channel_id=1, source_target_pairs={{30,0},{8,2},{2,4},{12,6},{6,8},{16,10},{10,12},{20,14},{14,16},{2... | collective-permute-start | bytes 835592 | tf_op jit(solution)/shard_map/ppermute | solution.py:25
  7.9 19.0 %collective-permute-start.3 = (f32[17,32,128]{2,1,0:T(8,128)S(1)}, f32[17,32,128]{2,1,0:T(8,128)S(1)}, u32[]{:S(2)}, u32[]{:S(2)}) collective-permute-start(f32[17,32,128]{2,1,0:T(8,128)S(1)} %get-tuple-element.14), channel_id=1, source_target_pairs={{28,0},{10,2},{0,4},{14,6},{4,8},{18,10},{8,12},{22,14},{12,16},{2... | collective-permute-start | bytes 835592 | tf_op jit(solution)/shard_map/ppermute | solution.py:25
  15.3 11.6 %collective-permute-start.5 = (f32[17,32,128]{2,1,0:T(8,128)S(1)}, f32[17,32,128]{2,1,0:T(8,128)S(1)}, u32[]{:S(2)}, u32[]{:S(2)}) collective-permute-start(f32[17,32,128]{2,1,0:T(8,128)S(1)} %collective-permute-done.4.second), channel_id=1, source_target_pairs={{2,0},{0,2},{6,4},{4,6},{10,8},{8,10},{14,12},{12,14},{18,16},{16,... | collective-permute-start | bytes 835592 | tf_op jit(solution)/shard_map/ppermute | solution.py:25
  15.3 18.0 %collective-permute-start.2 = (f32[10,32,128]{2,1,0:T(8,128)S(1)}, f32[10,32,128]{2,1,0:T(8,128)S(1)}, u32[]{:S(2)}, u32[]{:S(2)}) collective-permute-start(f32[10,32,128]{2,1,0:T(8,128)S(1)} %get-tuple-element.13), channel_id=1, source_target_pairs={{30,0},{8,2},{2,4},{12,6},{6,8},{16,10},{10,12},{20,14},{14,16},{2... | collective-permute-start | bytes 491528 | tf_op jit(solution)/shard_map/ppermute | solution.py:25
  22.7 12.7 %collective-permute-start.1 = (f32[10,32,128]{2,1,0:T(8,128)S(1)}, f32[10,32,128]{2,1,0:T(8,128)S(1)}, u32[]{:S(2)}, u32[]{:S(2)}) collective-permute-start(f32[10,32,128]{2,1,0:T(8,128)S(1)} %get-tuple-element.13), channel_id=1, source_target_pairs={{28,0},{10,2},{0,4},{14,6},{4,8},{18,10},{8,12},{22,14},{12,16},{2... | collective-permute-start | bytes 491528 | tf_op jit(solution)/shard_map/ppermute | solution.py:25
  33.3 4.1 %collective-permute-start.6 = (f32[10,32,128]{2,1,0:T(8,128)S(1)}, f32[10,32,128]{2,1,0:T(8,128)S(1)}, u32[]{:S(2)}, u32[]{:S(2)}) collective-permute-start(f32[10,32,128]{2,1,0:T(8,128)S(1)} %collective-permute-done.2.second), channel_id=1, source_target_pairs={{2,0},{0,2},{6,4},{4,6},{10,8},{8,10},{14,12},{12,14},{18,16},{16,... | collective-permute-start | bytes 491528 | tf_op jit(solution)/shard_map/ppermute | solution.py:25
  33.5 3.9 %collective-permute-start.7 = (f32[64,128]{1,0:T(8,128)S(1)}, f32[64,128]{1,0:T(8,128)S(1)}, u32[]{:S(2)}, u32[]{:S(2)}) collective-permute-start(f32[64,128]{1,0:T(8,128)S(1)} %own_chains.3.rest_0_.refs_2_), channel_id=1, source_target_pairs={{0,1},{1,0},{2,3},{3,2},{4,5},{5,4},{6,7},{7,6},{8,9},{9,8},{10,11... | collective-permute-start | bytes 98312 | tf_op jit(solution)/shard_map/ppermute | solution.py:346
  41.2 4.9 %collective-permute-start.8 = (f32[224,128]{1,0:T(8,128)S(1)}, f32[224,128]{1,0:T(8,128)S(1)}, u32[]{:S(2)}, u32[]{:S(2)}) collective-permute-start(f32[224,128]{1,0:T(8,128)S(1)} %half_chains.3.refs_0_), channel_id=1, source_target_pairs={{0,1},{1,0},{2,3},{3,2},{4,5},{5,4},{6,7},{7,6},{8,9},{9,8},{10,11... | collective-permute-start | bytes 344072 | tf_op jit(solution)/shard_map/ppermute | solution.py:352
  46.2 1.2 %collective-permute-start.9 = (f32[8,128]{1,0:T(8,128)S(1)}, f32[8,128]{1,0:T(8,128)S(1)}, u32[]{:S(2)}, u32[]{:S(2)}) collective-permute-start(f32[8,128]{1,0:T(8,128)S(1)} %meet.1.mine), channel_id=1, source_target_pairs={{2,0},{0,2},{6,4},{4,6},{10,8},{8,10},{14,12},{12,14},{18,16},{16,... | collective-permute-start | bytes 12296 | tf_op jit(solution)/shard_map/ppermute | solution.py:25
  47.4 10.1 %copy-start.1 = (s32[4,8,128]{2,1,0:T(8,128)S(1)}, s32[4,8,128]{2,1,0:T(8,128)}, u32[]{:S(2)}) copy-start(s32[4,8,128]{2,1,0:T(8,128)} %constant.23.clone.spots_ref) | copy-start | bytes 49156
  47.4 6.0 %collective-permute-start.10 = (f32[8,128]{1,0:T(8,128)S(1)}, f32[8,128]{1,0:T(8,128)S(1)}, u32[]{:S(2)}, u32[]{:S(2)}) collective-permute-start(f32[8,128]{1,0:T(8,128)S(1)} %join.1.here), channel_id=1, source_target_pairs={{4,0},{6,2},{8,4},{10,6},{12,8},{14,10},{16,12},{18,14},{20,16},{2... | collective-permute-start | bytes 12296 | tf_op jit(solution)/shard_map/ppermute | solution.py:25
  52.1 5.4 %collective-permute-start.11 = (f32[8,128]{1,0:T(8,128)S(1)}, f32[8,128]{1,0:T(8,128)S(1)}, u32[]{:S(2)}, u32[]{:S(2)}) collective-permute-start(f32[8,128]{1,0:T(8,128)S(1)} %join.1.here), channel_id=1, source_target_pairs={{24,0},{26,2},{28,4},{30,6},{0,8},{2,10},{4,12},{6,14},{8,16},{10,... | collective-permute-start | bytes 12296 | tf_op jit(solution)/shard_map/ppermute | solution.py:25

commit v7 on v6

--- a/solution.py
+++ b/solution.py
@@ -9,19 +9,20 @@
 
 REACH = 6
 EDGE = 6
-SHARE = 0.63
+SHARES = (1.0,)
 BF16, F32 = jnp.bfloat16, jnp.float32
 VMEM = pl.BlockSpec(memory_space=pltpu.VMEM)
 SMEM = pl.BlockSpec(memory_space=pltpu.SMEM)
 
 
-def move(array, source):
+def move(array, source, takes=lambda chip, core: True):
     peers = lax.axis_size("blk")
     chips = peers // 2
     pairs = []
     for d in range(peers):
-        chip, core = source(d // 2, d % 2)
-        pairs.append(((chip % chips) * 2 + core, d))
+        if takes(d // 2, d % 2):
+            chip, core = source(d // 2, d % 2)
+            pairs.append(((chip % chips) * 2 + core, d))
     return lax.ppermute(array, "blk", pairs)
 
 
@@ -120,38 +121,24 @@
     return current
 
 
-def order_kernel(side_ref, sites_ref, whole, *rest):
-    *pieces, edges, semaphores = rest
-    sites, steps = sites_ref.shape[0], whole.shape[0]
+def order_kernel(side_ref, sites_ref, whole, *pieces):
+    sites = sites_ref.shape[0]
 
     def run(flip):
-        outer = sites_ref.at[pl.ds(sites - EDGE if flip else 0, EDGE)]
-        copies = [pltpu.make_async_copy(outer, edges, semaphores.at[0])]
-        begin = 0
-        spots = []
-        for k, (array, start) in enumerate([(whole, 0)] + [(p, None) for p in pieces]):
-            start = begin if start is None else start
-            count = array.shape[0]
-            begin = 0 if k == 0 else begin + count
-            spare = 1 if start == 0 else 0
-            low = steps - start - count if flip else start
-            kept = count - spare
-            source = sites_ref.at[pl.ds(low if flip else low + spare + EDGE - 1, kept)]
-            target = array.at[pl.ds(0 if flip else spare, kept)]
-            copies.append(pltpu.make_async_copy(source, target, semaphores.at[k + 1]))
-            if spare:
-                spots.append((array, count - 1 if flip else 0))
-        for copy in copies:
-            copy.start()
-        copies[0].wait()
-        tiles = [edges[EDGE - 1 - k if flip else k] for k in range(EDGE)]
-        edge = edge_tile([turned(t) for t in tiles] if flip else tiles)
+        def tile(k):
+            return sites_ref[sites - 1 - k if flip else k]
+
+        edge = edge_tile([turned(tile(k)) if flip else tile(k) for k in range(EDGE)])
         if flip:
             edge = turned(edge)
-        for array, at in spots:
-            array[at] = edge
-        for copy in copies[1:]:
-            copy.wait()
+        tiles = [edge] + [tile(k) for k in range(EDGE, sites)]
+        for k, value in enumerate(tiles):
+            whole[k] = value
+        begin = 0
+        for piece in pieces:
+            for k in range(piece.shape[0]):
+                piece[k] = tiles[begin + k]
+            begin += piece.shape[0]
 
     on_each_side(side_ref, run)
 
@@ -170,9 +157,8 @@
     def run(flip):
         state = rest[0][...] if start else identities(64)
         for step in range(start, start + count):
-            site = own.shape[0] - 1 - step if flip else step
-            home = interleave(own[site], sibling[site])
-            near = near_plain(own[site]) if flip else near_turned(home)[:2]
+            home = interleave(own[step], sibling[step])
+            near = near_plain(own[step]) if flip else near_turned(home)[:2]
             state = advance(state, near, far_weights(home, flip))
         out[...] = state
 
@@ -186,8 +172,7 @@
     def run(flip):
         state = rest[-2][...] if start else identities(320)
         for index in range(count):
-            whole = steps - 1 - start - index if flip else start + index
-            part = count - 1 - index if flip else index
+            whole, part = start + index, index
             far = interleave(first[part], second[part])
             if flip:
                 near = [n for t in (own[whole], sibling[whole], other[part], first[part], second[part])
@@ -290,15 +275,14 @@
     return table
 
 
-def call(kernel, shapes, *args, name, spaces=None, scratch=()):
+def call(kernel, shapes, *args, name):
     many = isinstance(shapes, list)
     shapes = [jax.ShapeDtypeStruct(shape, F32) for shape in (shapes if many else [shapes])]
     return pl.pallas_call(
         kernel,
         out_shape=shapes if many else shapes[0],
-        in_specs=spaces or [SMEM if a.ndim == 1 else VMEM for a in args],
+        in_specs=[SMEM if a.ndim == 1 else VMEM for a in args],
         out_specs=[VMEM] * len(shapes) if many else VMEM,
-        scratch_shapes=scratch,
         compiler_params=pltpu.CompilerParams(vmem_limit_bytes=40 * 2**20),
         name=name,
     )(*args)
@@ -311,51 +295,51 @@
     band = min(REACH, (blocks - 1) // 2)
     side = lax.axis_index("pair")
     flag = side[None].astype(jnp.int32)
-    core = lax.axis_index("blk") % 2
+
+    place = lax.axis_index("blk")
+    core, chip = place % 2, place // 2
 
     steps = sites - EDGE + 1
-    starts = [0, round(SHARE * steps)]
-    counts = [starts[1], steps - starts[1]]
+    counts = [round(share * steps) for share in SHARES[:-1]]
+    counts.append(steps - sum(counts))
+    starts = [sum(counts[:k]) for k in range(len(counts))]
     tile = mps.shape[1:]
-    own, *pieces = call(
-        order_kernel,
-        [(n, *tile) for n in (steps, *counts)],
-        flag,
-        mps,
-        name="order",
-        spaces=[SMEM, pl.BlockSpec(memory_space=pltpu.HBM)],
-        scratch=[pltpu.VMEM((EDGE, *tile), F32), pltpu.SemaphoreType.DMA((2 + len(counts),))],
-    )
+    chunks = counts if len(counts) > 1 else []
+    own, *pieces = call(order_kernel, [(n, *tile) for n in (steps, *chunks)], flag, mps, name="order")
+    pieces = pieces or [own]
+
+    relayed = move(own, lambda chip, core: (chip - 2, core), lambda chip, core: chip % 2 == 1 and core == 0)
     seconds = [move(p, lambda chip, core: (chip - 1, 1) if core == 0 else (chip + 2, 0)) for p in pieces]
-    firsts = [move(p, lambda chip, core: (chip - 1, 0) if core == 0 else (chip + 2, 1)) for p in pieces]
     across = lambda chip, core: (chip, 1 - core)
     swap = [(0, 1), (1, 0)]
     sibling = move(own, across)
-
-    early = steps // 2
-    home = functools.partial(home_kernel, 0, early)
-    home = call(home, (64, 128), flag, own, sibling, name="own_chains")
-    carried = (home,)
+    early = steps * 5 // 8
+    home = call(functools.partial(home_kernel, 0, early), (64, 128), flag, own, sibling, name="own_chains")
+    relayed, home = lax.optimization_barrier((relayed, home))
+    passes = (chip % 2 == 1) & (core == 0)
+    firsts = [
+        move(jnp.where(passes, relayed[start : start + count], piece),
+             lambda chip, core: (chip ^ 1, 0) if core == 0 else (chip + 2, 1))
+        for start, count, piece in zip(starts, counts, pieces)
+    ]
+    behind = home
     for k, (start, first, second) in enumerate(zip(starts, firsts, seconds)):
-        second, behind = lax.optimization_barrier((second, carried[-1]))
-        carried = (*carried[:-1], behind)
+        second, behind = lax.optimization_barrier((second, behind))
         other = move(second, across)
         if k == 0:
             home = functools.partial(home_kernel, early, steps - early)
-            home = call(home, (64, 128), flag, own, sibling, *carried, name="own_chains")
-            far_home = lax.ppermute(home, "pair", swap)
-            carried = (home,)
+            home = call(home, (64, 128), flag, own, sibling, behind, name="own_chains")
+            behind = far_home = lax.ppermute(home, "pair", swap)
         rows = 224 if k == len(starts) - 1 else 320
-        state = call(functools.partial(chain_kernel, start), (rows, 128), flag, own, sibling, first, second, other,
-                     *carried, name="half_chains")
-        carried = (far_home, state)
-    partner = lax.ppermute(state, "pair", swap)
-    tile = call(meet_kernel, (8, 128), state, partner, home, far_home, name="meet")
+        behind = call(functools.partial(chain_kernel, start), (rows, 128), flag, own, sibling, first, second, other,
+                      behind, name="half_chains")
+    partner = lax.ppermute(behind, "pair", swap)
+    tile = call(meet_kernel, (8, 128), behind, partner, home, far_home, name="meet")
     tile = call(join_kernel, (8, 128), tile, move(tile, across), name="join")
-    tiles = [tile] + [move(tile, lambda chip, core: (chip + gap, core)) for gap in (1, -2)]
+    after, before = [move(tile, lambda chip, core: (chip + gap, core)) for gap in (1, -2)]
     spots = jnp.asarray([t for k in range(2) for t in spot_table(k, samp, band)], jnp.int32)
     which = (core * samp + side)[None].astype(jnp.int32)
-    return call(pick_kernel, (1, (2 * band + 1) * samp), which, spots, *tiles, name="pick")
+    return call(pick_kernel, (1, (2 * band + 1) * samp), which, spots, tile, after, before, name="pick")
 
 
 def solution(mesh):

time: 58.4 us -> 61.7 us (1.057)
  starting transfers between devices: 22.9 us -> 28.6 us
  waiting for transfers between devices: 13.5 us -> 11.8 us
  Pallas kernels: 20.8 us -> 20 us
    ppermute x10 -> x8, starting transfers between devices: 18.9 us -> 24.9 us  [move(): return lax.ppermute(array, 'blk', pairs)]
    ppermute x10 -> x8, waiting for transfers between devices: 8.66 us -> 6.58 us  [move(): return lax.ppermute(array, 'blk', pairs)]
    pallas_call x8 -> x7, Pallas kernels: 20.8 us -> 20 us  [call(): pl.pallas_call(kernel, out_shape=shapes if many else shapes[0], in_specs=...]
  transfers between devices with their start and end apart: 12 -> 10, of which waited for: 6 -> 5; matrix products, arithmetic and copies ran while one was open for 0% -> 0% of each run, Pallas kernels for 25% -> 13%
where the time goes in v7:
time: 61.7 us; the launch traced here: 61.6 us
  starting transfers between devices  28.6 us (46%)
  Pallas kernels  20 us (32%)
  waiting for transfers between devices  11.8 us (19%)
  local copies, waits for them, and re-layouts  1.04 us (2%)
    ppermute x8, starting transfers between devices, move(): return lax.ppermute(array, 'blk', pairs)  24.9 us
    pallas_call x7, Pallas kernels, call(): pl.pallas_call(kernel, out_shape=shapes if many else shapes[0], in_specs=...  20 us
    ppermute x8, waiting for transfers between devices, move(): return lax.ppermute(array, 'blk', pairs)  6.58 us
    ppermute x1, waiting for transfers between devices, body(): partner = lax.ppermute(behind, 'pair', swap)  3.15 us
    ppermute x1, waiting for transfers between devices, body(): behind = far_home = lax.ppermute(home, 'pair', swap)  2.06 us
    ppermute x1, starting transfers between devices, body(): behind = far_home = lax.ppermute(home, 'pair', swap)  1.89 us
    ppermute x1, starting transfers between devices, body(): partner = lax.ppermute(behind, 'pair', swap)  1.75 us
  transfers between devices with their start and end apart: 10, of which 5 were waited for; matrix products, arithmetic and copies ran while one was open for 0% of the time, Pallas kernels for 13%

profile of v7, /device:TPU:0, one launch (start us, length us, event | category | flops | bytes accessed | tf_op | source)
XLA Modules:
  0.0 61.6 jit_solution(17571678503860899258)
XLA Ops:
  0.0 0.0 copy-start
  0.0 1.0 %copy-done = f32[32,32,128]{2,1,0:T(8,128)S(1)} copy-done((f32[32,32,128]{2,1,0:T(8,128)S(1)}, f32[32,32,128]{2,1,0:T(8,128)}, u32[]{:S(2)}) %copy-start) | copy-done | bytes 524312
  1.0 1.0 %order.1.own = f32[27,32,128]{2,1,0:T(8,128)S(1)} custom-call(s32[1]{0:T(128)} %bitcast.1.side_ref, f32[32,32,128]{2,1,0:T(8,128)S(1)} %copy-done), custom_call_target="tpu_custom_call" | custom-call | tf_op jit(solution)/shard_map/order/pallas_call | solution.py:281
  2.0 0.5 collective-permute-start
  2.5 0.7 %collective-permute-start.1 = (f32[27,32,128]{2,1,0:T(8,128)S(1)}, f32[27,32,128]{2,1,0:T(8,128)S(1)}, u32[]{:S(2)}, u32[]{:S(2)}) collective-permute-start(f32[27,32,128]{2,1,0:T(8,128)S(1)} %order.1.own), channel_id=1, source_target_pairs={{28,4},{4,12},{12,20},{20,28},{29,5},{5,13},{13,21},{21,29}} | collective-permute-start | bytes 1327112 | tf_op jit(solution)/shard_map/ppermute | solution.py:26
  3.2 4.8 %collective-permute-start.3 = (f32[27,32,128]{2,1,0:T(8,128)S(1)}, f32[27,32,128]{2,1,0:T(8,128)S(1)}, u32[]{:S(2)}, u32[]{:S(2)}) collective-permute-start(f32[27,32,128]{2,1,0:T(8,128)S(1)} %order.1.own), channel_id=1, source_target_pairs={{30,0},{8,2},{2,4},{12,6},{6,8},{16,10},{10,12},{20,14},{14,16},{2... | collective-permute-start | bytes 1327112 | tf_op jit(solution)/shard_map/ppermute | solution.py:26
  7.9 0.0 collective-permute-done.sibling
  7.9 4.8 %own_chains.2.rest_0_ = f32[64,128]{1,0:T(8,128)S(1)} custom-call(s32[1]{0:T(128)} %bitcast.1.side_ref, f32[27,32,128]{2,1,0:T(8,128)S(1)} %order.1.own, f32[27,32,128]{2,1,0:T(8,128)S(1)} %collective-permute-done.sibling), custom_call_target="tpu_custom_call" | custom-call | tf_op jit(solution)/shard_map/own_chains/pallas_call | solution.py:281
  12.7 0.0 collective-permute-done.1
  12.7 0.1 broadcast_select_fusion
  12.8 9.1 %collective-permute-start.2 = (f32[27,32,128]{2,1,0:T(8,128)S(1)}, f32[27,32,128]{2,1,0:T(8,128)S(1)}, u32[]{:S(2)}, u32[]{:S(2)}) collective-permute-start(f32[27,32,128]{2,1,0:T(8,128)S(1)} %broadcast_select_fusion), channel_id=1, source_target_pairs={{4,0},{10,2},{0,4},{14,6},{12,8},{18,10},{8,12},{22,14},{20,16},{2... | collective-permute-start | bytes 1327112 | tf_op jit(solution)/shard_map/ppermute | solution.py:26
  21.9 0.0 collective-permute-done.3.second
  21.9 0.0 collective-permute-start.4
  21.9 3.3 %own_chains.3.refs_2_ = f32[64,128]{1,0:T(8,128)S(1)} custom-call(s32[1]{0:T(128)} %bitcast.1.side_ref, f32[27,32,128]{2,1,0:T(8,128)S(1)} %order.1.own, f32[27,32,128]{2,1,0:T(8,128)S(1)} %collective-permute-done.sibling, f32[64,128]{1,0:T(8,128)S(1)} %own_chains.2.rest_0_), custom_call_target="tpu_custom_call" | custom-call | tf_op jit(solution)/shard_map/own_chains/pallas_call | solution.py:281
  25.2 1.9 %collective-permute-start.5 = (f32[64,128]{1,0:T(8,128)S(1)}, f32[64,128]{1,0:T(8,128)S(1)}, u32[]{:S(2)}, u32[]{:S(2)}) collective-permute-start(f32[64,128]{1,0:T(8,128)S(1)} %own_chains.3.refs_2_), channel_id=1, source_target_pairs={{0,1},{1,0},{2,3},{3,2},{4,5},{5,4},{6,7},{7,6},{8,9},{9,8},{10,11... | collective-permute-start | bytes 98312 | tf_op jit(solution)/shard_map/ppermute | solution.py:332
  27.1 2.1 %collective-permute-done.5.rest_0_.refs_3_ = f32[64,128]{1,0:T(8,128)S(1)} collective-permute-done((f32[64,128]{1,0:T(8,128)S(1)}, f32[64,128]{1,0:T(8,128)S(1)}, u32[]{:S(2)}, u32[]{:S(2)}) %collective-permute-start.5) | collective-permute-done | bytes 32800 | tf_op jit(solution)/shard_map/ppermute | solution.py:332
  29.2 0.0 collective-permute-done.2.first
  29.2 0.0 collective-permute-done.4.other
  29.2 10.0 %half_chains.1.refs_0_ = f32[224,128]{1,0:T(8,128)S(1)} custom-call(s32[1]{0:T(128)} %bitcast.1.side_ref, f32[27,32,128]{2,1,0:T(8,128)S(1)} %order.1.own, f32[27,32,128]{2,1,0:T(8,128)S(1)} %collective-permute-done.sibling, f32[27,32,128]{2,1,0:T(8,128)S(1)} %collective-permute-done.2.first, f32[27,32,128]{2,1,0:T(8,128)S(1)} %collective-permute-done.3.second, ...), custom_call_target="tpu_custom_call" | custom-call | tf_op jit(solution)/shard_map/half_chains/pallas_call | solution.py:281
  39.2 1.8 %collective-permute-start.6 = (f32[224,128]{1,0:T(8,128)S(1)}, f32[224,128]{1,0:T(8,128)S(1)}, u32[]{:S(2)}, u32[]{:S(2)}) collective-permute-start(f32[224,128]{1,0:T(8,128)S(1)} %half_chains.1.refs_0_), channel_id=1, source_target_pairs={{0,1},{1,0},{2,3},{3,2},{4,5},{5,4},{6,7},{7,6},{8,9},{9,8},{10,11... | collective-permute-start | bytes 344072 | tf_op jit(solution)/shard_map/ppermute | solution.py:336
  40.9 3.2 %collective-permute-done.6.refs_1_ = f32[224,128]{1,0:T(8,128)S(1)} collective-permute-done((f32[224,128]{1,0:T(8,128)S(1)}, f32[224,128]{1,0:T(8,128)S(1)}, u32[]{:S(2)}, u32[]{:S(2)}) %collective-permute-start.6) | collective-permute-done | bytes 114720 | tf_op jit(solution)/shard_map/ppermute | solution.py:336
  44.1 0.2 meet.1.mine
  44.2 0.0 copy-start.1
  44.2 0.0 collective-permute-start.7
  44.2 1.2 %collective-permute-done.7.theirs = f32[8,128]{1,0:T(8,128)S(1)} collective-permute-done((f32[8,128]{1,0:T(8,128)S(1)}, f32[8,128]{1,0:T(8,128)S(1)}, u32[]{:S(2)}, u32[]{:S(2)}) %collective-permute-start.7) | collective-permute-done | bytes 4128 | tf_op jit(solution)/shard_map/ppermute | solution.py:26
  45.4 0.1 join.1.here
  45.5 9.9 %collective-permute-start.8 = (f32[8,128]{1,0:T(8,128)S(1)}, f32[8,128]{1,0:T(8,128)S(1)}, u32[]{:S(2)}, u32[]{:S(2)}) collective-permute-start(f32[8,128]{1,0:T(8,128)S(1)} %join.1.here), channel_id=1, source_target_pairs={{4,0},{6,2},{8,4},{10,6},{12,8},{14,10},{16,12},{18,14},{20,16},{2... | collective-permute-start | bytes 12296 | tf_op jit(solution)/shard_map/ppermute | solution.py:26
  55.3 0.0 collective-permute-start.9
  55.4 1.3 %collective-permute-done.8.after = f32[8,128]{1,0:T(8,128)S(1)} collective-permute-done((f32[8,128]{1,0:T(8,128)S(1)}, f32[8,128]{1,0:T(8,128)S(1)}, u32[]{:S(2)}, u32[]{:S(2)}) %collective-permute-start.8) | collective-permute-done | bytes 4128 | tf_op jit(solution)/shard_map/ppermute | solution.py:26
  56.7 4.1 %collective-permute-done.9.before = f32[8,128]{1,0:T(8,128)S(1)} collective-permute-done((f32[8,128]{1,0:T(8,128)S(1)}, f32[8,128]{1,0:T(8,128)S(1)}, u32[]{:S(2)}, u32[]{:S(2)}) %collective-permute-start.9) | collective-permute-done | bytes 4128 | tf_op jit(solution)/shard_map/ppermute | solution.py:26
  60.8 0.0 copy-done.1
  60.8 0.8 %pick.1 = f32[1,26]{1,0:T(1,128)} custom-call(s32[1]{0:T(128)} %bitcast.which_ref, s32[4,8,128]{2,1,0:T(8,128)S(1)} %copy-done.1, f32[8,128]{1,0:T(8,128)S(1)} %join.1.here, f32[8,128]{1,0:T(8,128)S(1)} %collective-permute-done.8.after, f32[8,128]{1,0:T(8,128)S(1)} %collective-permute-done.9.before), custom_call_target="tpu_custom_call" | custom-call | tf_op jit(solution)/shard_map/pick/pallas_call | solution.py:281
Async XLA Ops:
  0.0 1.0 %copy-start = (f32[32,32,128]{2,1,0:T(8,128)S(1)}, f32[32,32,128]{2,1,0:T(8,128)}, u32[]{:S(2)}) copy-start(f32[32,32,128]{2,1,0:T(8,128)} %sites_ref.1) | copy-start | bytes 1572868
  2.0 5.9 %collective-permute-start = (f32[27,32,128]{2,1,0:T(8,128)S(1)}, f32[27,32,128]{2,1,0:T(8,128)S(1)}, u32[]{:S(2)}, u32[]{:S(2)}) collective-permute-start(f32[27,32,128]{2,1,0:T(8,128)S(1)} %order.1.own), channel_id=1, source_target_pairs={{2,0},{0,2},{6,4},{4,6},{10,8},{8,10},{14,12},{12,14},{18,16},{16,... | collective-permute-start | bytes 1327112 | tf_op jit(solution)/shard_map/ppermute | solution.py:26
  2.5 10.2 %collective-permute-start.1 = (f32[27,32,128]{2,1,0:T(8,128)S(1)}, f32[27,32,128]{2,1,0:T(8,128)S(1)}, u32[]{:S(2)}, u32[]{:S(2)}) collective-permute-start(f32[27,32,128]{2,1,0:T(8,128)S(1)} %order.1.own), channel_id=1, source_target_pairs={{28,4},{4,12},{12,20},{20,28},{29,5},{5,13},{13,21},{21,29}} | collective-permute-start | bytes 1327112 | tf_op jit(solution)/shard_map/ppermute | solution.py:26
  3.2 18.8 %collective-permute-start.3 = (f32[27,32,128]{2,1,0:T(8,128)S(1)}, f32[27,32,128]{2,1,0:T(8,128)S(1)}, u32[]{:S(2)}, u32[]{:S(2)}) collective-permute-start(f32[27,32,128]{2,1,0:T(8,128)S(1)} %order.1.own), channel_id=1, source_target_pairs={{30,0},{8,2},{2,4},{12,6},{6,8},{16,10},{10,12},{20,14},{14,16},{2... | collective-permute-start | bytes 1327112 | tf_op jit(solution)/shard_map/ppermute | solution.py:26
  12.8 16.4 %collective-permute-start.2 = (f32[27,32,128]{2,1,0:T(8,128)S(1)}, f32[27,32,128]{2,1,0:T(8,128)S(1)}, u32[]{:S(2)}, u32[]{:S(2)}) collective-permute-start(f32[27,32,128]{2,1,0:T(8,128)S(1)} %broadcast_select_fusion), channel_id=1, source_target_pairs={{4,0},{10,2},{0,4},{14,6},{12,8},{18,10},{8,12},{22,14},{20,16},{2... | collective-permute-start | bytes 1327112 | tf_op jit(solution)/shard_map/ppermute | solution.py:26
  21.9 7.2 %collective-permute-start.4 = (f32[27,32,128]{2,1,0:T(8,128)S(1)}, f32[27,32,128]{2,1,0:T(8,128)S(1)}, u32[]{:S(2)}, u32[]{:S(2)}) collective-permute-start(f32[27,32,128]{2,1,0:T(8,128)S(1)} %collective-permute-done.3.second), channel_id=1, source_target_pairs={{2,0},{0,2},{6,4},{4,6},{10,8},{8,10},{14,12},{12,14},{18,16},{16,... | collective-permute-start | bytes 1327112 | tf_op jit(solution)/shard_map/ppermute | solution.py:26
  25.2 4.0 %collective-permute-start.5 = (f32[64,128]{1,0:T(8,128)S(1)}, f32[64,128]{1,0:T(8,128)S(1)}, u32[]{:S(2)}, u32[]{:S(2)}) collective-permute-start(f32[64,128]{1,0:T(8,128)S(1)} %own_chains.3.refs_2_), channel_id=1, source_target_pairs={{0,1},{1,0},{2,3},{3,2},{4,5},{5,4},{6,7},{7,6},{8,9},{9,8},{10,11... | collective-permute-start | bytes 98312 | tf_op jit(solution)/shard_map/ppermute | solution.py:332
  39.2 4.9 %collective-permute-start.6 = (f32[224,128]{1,0:T(8,128)S(1)}, f32[224,128]{1,0:T(8,128)S(1)}, u32[]{:S(2)}, u32[]{:S(2)}) collective-permute-start(f32[224,128]{1,0:T(8,128)S(1)} %half_chains.1.refs_0_), channel_id=1, source_target_pairs={{0,1},{1,0},{2,3},{3,2},{4,5},{5,4},{6,7},{7,6},{8,9},{9,8},{10,11... | collective-permute-start | bytes 344072 | tf_op jit(solution)/shard_map/ppermute | solution.py:336
  44.2 16.5 %copy-start.1 = (s32[4,8,128]{2,1,0:T(8,128)S(1)}, s32[4,8,128]{2,1,0:T(8,128)}, u32[]{:S(2)}) copy-start(s32[4,8,128]{2,1,0:T(8,128)} %constant.40.clone.spots_ref) | copy-start | bytes 49156
  44.2 1.2 %collective-permute-start.7 = (f32[8,128]{1,0:T(8,128)S(1)}, f32[8,128]{1,0:T(8,128)S(1)}, u32[]{:S(2)}, u32[]{:S(2)}) collective-permute-start(f32[8,128]{1,0:T(8,128)S(1)} %meet.1.mine), channel_id=1, source_target_pairs={{2,0},{0,2},{6,4},{4,6},{10,8},{8,10},{14,12},{12,14},{18,16},{16,... | collective-permute-start | bytes 12296 | tf_op jit(solution)/shard_map/ppermute | solution.py:26
  45.5 11.2 %collective-permute-start.8 = (f32[8,128]{1,0:T(8,128)S(1)}, f32[8,128]{1,0:T(8,128)S(1)}, u32[]{:S(2)}, u32[]{:S(2)}) collective-permute-start(f32[8,128]{1,0:T(8,128)S(1)} %join.1.here), channel_id=1, source_target_pairs={{4,0},{6,2},{8,4},{10,6},{12,8},{14,10},{16,12},{18,14},{20,16},{2... | collective-permute-start | bytes 12296 | tf_op jit(solution)/shard_map/ppermute | solution.py:26
  55.3 5.4 %collective-permute-start.9 = (f32[8,128]{1,0:T(8,128)S(1)}, f32[8,128]{1,0:T(8,128)S(1)}, u32[]{:S(2)}, u32[]{:S(2)}) collective-permute-start(f32[8,128]{1,0:T(8,128)S(1)} %join.1.here), channel_id=1, source_target_pairs={{24,0},{26,2},{28,4},{30,6},{0,8},{2,10},{4,12},{6,14},{8,16},{10,... | collective-permute-start | bytes 12296 | tf_op jit(solution)/shard_map/ppermute | solution.py:26

commit v8 on v5

--- a/solution.py
+++ b/solution.py
@@ -15,13 +15,14 @@
 SMEM = pl.BlockSpec(memory_space=pltpu.SMEM)
 
 
-def move(array, source):
+def move(array, source, takes=lambda chip, core: True):
     peers = lax.axis_size("blk")
     chips = peers // 2
     pairs = []
     for d in range(peers):
-        chip, core = source(d // 2, d % 2)
-        pairs.append(((chip % chips) * 2 + core, d))
+        if takes(d // 2, d % 2):
+            chip, core = source(d // 2, d % 2)
+            pairs.append(((chip % chips) * 2 + core, d))
     return lax.ppermute(array, "blk", pairs)
 
 
@@ -164,7 +165,7 @@
     on_each_side(side_ref, run)
 
 
-def chain_kernel(start, side_ref, own, sibling, first, second, other, *rest):
+def chain_kernel(start, side_ref, own, sibling, crossed, first, second, other, *rest):
     out = rest[-1]
     count = first.shape[0]
     last = start + count == own.shape[0]
@@ -175,9 +176,10 @@
         for index in range(count):
             whole = start + index
             home = interleave(own[whole], sibling[whole])
-            far = interleave(first[index], second[index])
+            one = jnp.where(side_ref[1] == 1, crossed[whole], first[index])
+            far = interleave(one, second[index])
             if flip:
-                near = [n for t in (own[whole], sibling[whole], other[index], first[index], second[index])
+                near = [n for t in (own[whole], sibling[whole], other[index], one, second[index])
                         for n in near_plain(t)]
             else:
                 extra = other[index]
@@ -288,25 +290,36 @@
     blocks = lax.axis_size("blk")
     band = min(REACH, (blocks - 1) // 2)
     side = lax.axis_index("pair")
-    flag = side[None].astype(jnp.int32)
+    place = lax.axis_index("blk")
+    chip, core = place // 2, place % 2
+    flag = jnp.stack([side, (chip % 2 == 1) & (core == 0)]).astype(jnp.int32)
 
     steps = sites - EDGE + 1
     starts = [0, round(SHARE * steps)]
     counts = [starts[1], steps - starts[1]]
     tile = mps.shape[1:]
-    mps, *pieces = call(order_kernel, [(n, *tile) for n in (steps, *counts)], flag, mps, name="order")
+    own, *pieces = call(order_kernel, [(n, *tile) for n in (steps, *counts)], flag, mps, name="order")
+
+    crossed = move(own, lambda chip, core: (chip ^ 1, core), lambda chip, core: core == 0)
     seconds = [move(p, lambda chip, core: (chip - 1, 1) if core == 0 else (chip + 2, 0)) for p in pieces]
-    firsts = [move(p, lambda chip, core: (chip - 1, 0) if core == 0 else (chip + 2, 1)) for p in pieces]
     across = lambda chip, core: (chip, 1 - core)
-    sibling = move(mps, across)
-    inner = call(functools.partial(home_kernel, starts[-1]), (64, 128), flag, mps, sibling, name="own_chains")
+    sibling = move(own, across)
+    inner = functools.partial(home_kernel, starts[-1])
+    inner = call(inner, (64, 128), flag, own, sibling, name="own_chains")
+    crossed, inner = lax.optimization_barrier((crossed, inner))
+    firsts = [
+        move(jnp.where(core == 0, crossed[start : start + count], piece),
+             lambda chip, core: (chip - 2, 0) if core == 0 else (chip + 2, 1),
+             lambda chip, core: core == 1 or chip % 2 == 0)
+        for start, count, piece in zip(starts, counts, pieces)
+    ]
     carried = (inner,)
     for start, first, second in zip(starts, firsts, seconds):
         second, *carried = lax.optimization_barrier((second, *carried))
         other = move(second, across)
         rows = 288 if start == starts[-1] else 320
-        state = call(functools.partial(chain_kernel, start), (rows, 128), flag, mps, sibling, first, second, other,
-                     *carried, name="half_chains")
+        state = call(functools.partial(chain_kernel, start), (rows, 128), flag, own, sibling, crossed, first, second,
+                     other, *carried, name="half_chains")
         carried = (carried[0], state)
     partner = lax.ppermute(state, "pair", [(0, 1), (1, 0)])
     tile = call(meet_kernel, (8, 128), state, partner, name="meet")

time: 48.7 us -> 55 us (1.13)
  waiting for transfers between devices: 8.47 us -> 13.9 us
  Pallas kernels: 17.9 us -> 20.1 us
  starting transfers between devices: 20.4 us -> 18.8 us
    ppermute x10 -> x11, waiting for transfers between devices: 4.25 us -> 9.71 us  [move(): return lax.ppermute(array, 'blk', pairs)]
    pallas_call x7, Pallas kernels: 17.9 us -> 20.1 us  [call(): pl.pallas_call(kernel, out_shape=shapes if many else shapes[0], in_specs=...]
    ppermute x10 -> x11, starting transfers between devices: 18.6 us -> 16.8 us  [move(): return lax.ppermute(array, 'blk', pairs)]
  transfers between devices with their start and end apart: 11 -> 12, of which waited for: 7 -> 7; matrix products, arithmetic and copies ran while one was open for 1% -> 1% of each run, Pallas kernels for 24% -> 23%
where the time goes in v8:
time: 55 us; the launch traced here: 54.7 us
  Pallas kernels  20.1 us (37%)
  starting transfers between devices  18.8 us (34%)
  waiting for transfers between devices  13.9 us (25%)
  local copies, waits for them, and re-layouts  1.73 us (3%)
    pallas_call x7, Pallas kernels, call(): pl.pallas_call(kernel, out_shape=shapes if many else shapes[0], in_specs=...  20.1 us
    ppermute x11, starting transfers between devices, move(): return lax.ppermute(array, 'blk', pairs)  16.8 us
    ppermute x11, waiting for transfers between devices, move(): return lax.ppermute(array, 'blk', pairs)  9.71 us
    ppermute x1, waiting for transfers between devices, body(): partner = lax.ppermute(state, 'pair', [(0, 1), (1, 0)])  4.16 us
    ppermute x1, starting transfers between devices, body(): partner = lax.ppermute(state, 'pair', [(0, 1), (1, 0)])  2.02 us
  transfers between devices with their start and end apart: 12, of which 7 were waited for; matrix products, arithmetic and copies ran while one was open for 1% of the time, Pallas kernels for 23%

profile of v8, /device:TPU:0, one launch (start us, length us, event | category | flops | bytes accessed | tf_op | source)
XLA Modules:
  0.0 54.7 jit_solution(3455738830453383187)
XLA Ops:
  0.0 0.1 pad_add_fusion.side_ref
  0.1 1.0 %copy-done = f32[32,32,128]{2,1,0:T(8,128)S(1)} copy-done((f32[32,32,128]{2,1,0:T(8,128)S(1)}, f32[32,32,128]{2,1,0:T(8,128)}, u32[]{:S(2)}) %copy-start) | copy-done | bytes 524312
  1.1 1.5 %order.1 = (f32[27,32,128]{2,1,0:T(8,128)S(1)}, f32[17,32,128]{2,1,0:T(8,128)S(1)}, f32[10,32,128]{2,1,0:T(8,128)S(1)}) custom-call(s32[2]{0:T(128)S(1)} %pad_add_fusion.side_ref, f32[32,32,128]{2,1,0:T(8,128)S(1)} %copy-done), custom_call_target="tpu_custom_call" | custom-call | tf_op jit(solution)/shard_map/order/pallas_call | solution.py:277
  2.6 0.5 collective-permute-start
  3.1 4.4 %collective-permute-start.1 = (f32[27,32,128]{2,1,0:T(8,128)S(1)}, f32[27,32,128]{2,1,0:T(8,128)S(1)}, u32[]{:S(2)}, u32[]{:S(2)}) collective-permute-start(f32[27,32,128]{2,1,0:T(8,128)S(1)} %get-tuple-element.15.own), channel_id=1, source_target_pairs={{4,0},{0,4},{12,8},{8,12},{20,16},{16,20},{28,24},{24,28},{5,1},{1... | collective-permute-start | bytes 1327112 | tf_op jit(solution)/shard_map/ppermute | solution.py:26
  7.5 1.1 %collective-permute-start.4 = (f32[17,32,128]{2,1,0:T(8,128)S(1)}, f32[17,32,128]{2,1,0:T(8,128)S(1)}, u32[]{:S(2)}, u32[]{:S(2)}) collective-permute-start(f32[17,32,128]{2,1,0:T(8,128)S(1)} %get-tuple-element.18), channel_id=1, source_target_pairs={{30,0},{8,2},{2,4},{12,6},{6,8},{16,10},{10,12},{20,14},{14,16},{2... | collective-permute-start | bytes 835592 | tf_op jit(solution)/shard_map/ppermute | solution.py:26
  8.6 5.6 %own_chains.1.rest_0_ = f32[64,128]{1,0:T(8,128)S(1)} custom-call(s32[2]{0:T(128)S(1)} %pad_add_fusion.side_ref, f32[27,32,128]{2,1,0:T(8,128)S(1)} %get-tuple-element.15.own, f32[27,32,128]{2,1,0:T(8,128)S(1)} %collective-permute-done.sibling), custom_call_target="tpu_custom_call" | custom-call | tf_op jit(solution)/shard_map/own_chains/pallas_call | solution.py:277
  14.1 1.7 %collective-permute-done.1.crossed = f32[27,32,128]{2,1,0:T(8,128)S(1)} collective-permute-done((f32[27,32,128]{2,1,0:T(8,128)S(1)}, f32[27,32,128]{2,1,0:T(8,128)S(1)}, u32[]{:S(2)}, u32[]{:S(2)}) %collective-permute-start.1) | collective-permute-done | bytes 442400 | tf_op jit(solution)/shard_map/ppermute | solution.py:26
  15.8 4.9 %collective-permute-start.5 = (f32[17,32,128]{2,1,0:T(8,128)S(1)}, f32[17,32,128]{2,1,0:T(8,128)S(1)}, u32[]{:S(2)}, u32[]{:S(2)}) collective-permute-start(f32[17,32,128]{2,1,0:T(8,128)S(1)} %slice_select_fusion), channel_id=1, source_target_pairs={{24,0},{10,2},{14,6},{0,8},{18,10},{22,14},{8,16},{26,18},{30,22},... | collective-permute-start | bytes 835592 | tf_op jit(solution)/shard_map/ppermute | solution.py:26
  20.7 0.0 collective-permute-done.4.second
  20.7 0.1 collective-permute-start.6
  20.8 2.1 %collective-permute-start.3 = (f32[10,32,128]{2,1,0:T(8,128)S(1)}, f32[10,32,128]{2,1,0:T(8,128)S(1)}, u32[]{:S(2)}, u32[]{:S(2)}) collective-permute-start(f32[10,32,128]{2,1,0:T(8,128)S(1)} %get-tuple-element.17), channel_id=1, source_target_pairs={{30,0},{8,2},{2,4},{12,6},{6,8},{16,10},{10,12},{20,14},{14,16},{2... | collective-permute-start | bytes 491528 | tf_op jit(solution)/shard_map/ppermute | solution.py:26
  22.9 1.9 %collective-permute-start.2 = (f32[10,32,128]{2,1,0:T(8,128)S(1)}, f32[10,32,128]{2,1,0:T(8,128)S(1)}, u32[]{:S(2)}, u32[]{:S(2)}) collective-permute-start(f32[10,32,128]{2,1,0:T(8,128)S(1)} %slice_select_fusion.1), channel_id=1, source_target_pairs={{24,0},{10,2},{14,6},{0,8},{18,10},{22,14},{8,16},{26,18},{30,22},... | collective-permute-start | bytes 491528 | tf_op jit(solution)/shard_map/ppermute | solution.py:26
  24.9 2.5 %collective-permute-done.5.first = f32[17,32,128]{2,1,0:T(8,128)S(1)} collective-permute-done((f32[17,32,128]{2,1,0:T(8,128)S(1)}, f32[17,32,128]{2,1,0:T(8,128)S(1)}, u32[]{:S(2)}, u32[]{:S(2)}) %collective-permute-start.5) | collective-permute-done | bytes 278560 | tf_op jit(solution)/shard_map/ppermute | solution.py:26
  27.4 6.9 %half_chains.2.rest_1_ = f32[320,128]{1,0:T(8,128)S(1)} custom-call(s32[2]{0:T(128)S(1)} %pad_add_fusion.side_ref, f32[27,32,128]{2,1,0:T(8,128)S(1)} %get-tuple-element.15.own, f32[27,32,128]{2,1,0:T(8,128)S(1)} %collective-permute-done.sibling, f32[27,32,128]{2,1,0:T(8,128)S(1)} %collective-permute-done.1.crossed, ...), custom_call_target="tpu_custom_call" | custom-call | tf_op jit(solution)/shard_map/half_chains/pallas_call | solution.py:277
  34.3 0.0 collective-permute-done.3.second
  34.3 0.1 collective-permute-start.7
  34.4 0.0 collective-permute-done.2.first
  34.4 1.4 %collective-permute-done.7.other = f32[10,32,128]{2,1,0:T(8,128)S(1)} collective-permute-done((f32[10,32,128]{2,1,0:T(8,128)S(1)}, f32[10,32,128]{2,1,0:T(8,128)S(1)}, u32[]{:S(2)}, u32[]{:S(2)}) %collective-permute-start.7) | collective-permute-done | bytes 163872 | tf_op jit(solution)/shard_map/ppermute | solution.py:26
  35.8 5.0 %half_chains.3.mine = f32[288,128]{1,0:T(8,128)S(1)} custom-call(s32[2]{0:T(128)S(1)} %pad_add_fusion.side_ref, f32[27,32,128]{2,1,0:T(8,128)S(1)} %get-tuple-element.15.own, f32[27,32,128]{2,1,0:T(8,128)S(1)} %collective-permute-done.sibling, f32[27,32,128]{2,1,0:T(8,128)S(1)} %collective-permute-done.1.crossed, ...), custom_call_target="tpu_custom_call" | custom-call | tf_op jit(solution)/shard_map/half_chains/pallas_call | solution.py:277
  40.8 2.0 %collective-permute-start.8 = (f32[288,128]{1,0:T(8,128)S(1)}, f32[288,128]{1,0:T(8,128)S(1)}, u32[]{:S(2)}, u32[]{:S(2)}) collective-permute-start(f32[288,128]{1,0:T(8,128)S(1)} %half_chains.3.mine), channel_id=1, source_target_pairs={{0,1},{1,0},{2,3},{3,2},{4,5},{5,4},{6,7},{7,6},{8,9},{9,8},{10,11... | collective-permute-start | bytes 442376 | tf_op jit(solution)/shard_map/ppermute | solution.py:324
  42.8 4.2 %collective-permute-done.8.theirs = f32[288,128]{1,0:T(8,128)S(1)} collective-permute-done((f32[288,128]{1,0:T(8,128)S(1)}, f32[288,128]{1,0:T(8,128)S(1)}, u32[]{:S(2)}, u32[]{:S(2)}) %collective-permute-start.8) | collective-permute-done | bytes 147488 | tf_op jit(solution)/shard_map/ppermute | solution.py:324
  46.9 0.2 meet.1.mine
  47.1 0.0 collective-permute-start.9
  47.1 1.2 %collective-permute-done.9.theirs = f32[8,128]{1,0:T(8,128)S(1)} collective-permute-done((f32[8,128]{1,0:T(8,128)S(1)}, f32[8,128]{1,0:T(8,128)S(1)}, u32[]{:S(2)}, u32[]{:S(2)}) %collective-permute-start.9) | collective-permute-done | bytes 4128 | tf_op jit(solution)/shard_map/ppermute | solution.py:26
  48.3 0.1 join.1.here
  48.3 0.1 collective-permute-start.10
  48.5 1.7 %collective-permute-start.11 = (f32[8,128]{1,0:T(8,128)S(1)}, f32[8,128]{1,0:T(8,128)S(1)}, u32[]{:S(2)}, u32[]{:S(2)}) collective-permute-start(f32[8,128]{1,0:T(8,128)S(1)} %join.1.here), channel_id=1, source_target_pairs={{24,0},{26,2},{28,4},{30,6},{0,8},{2,10},{4,12},{6,14},{8,16},{10,... | collective-permute-start | bytes 12296 | tf_op jit(solution)/shard_map/ppermute | solution.py:26
  50.2 0.7 %dynamic-slice_bitcast_fusion.spot_ref = s32[8,128]{1,0:T(8,128)S(1)} fusion(s32[2,2,8,128]{3,2,1,0:T(8,128)} %constant.42.clone, s32[]{:T(128)S(6)} %select_n.40, s32[]{:T(128)S(6)} %select_n.41), kind=kLoop, calls=%fused_computation.2 | loop fusion | bytes 8200 | tf_op jit(solution)/shard_map/squeeze | solution.py:329
  50.9 1.1 %collective-permute-done.10.after = f32[8,128]{1,0:T(8,128)S(1)} collective-permute-done((f32[8,128]{1,0:T(8,128)S(1)}, f32[8,128]{1,0:T(8,128)S(1)}, u32[]{:S(2)}, u32[]{:S(2)}) %collective-permute-start.10) | collective-permute-done | bytes 4128 | tf_op jit(solution)/shard_map/ppermute | solution.py:26
  51.9 1.9 %collective-permute-done.11.before = f32[8,128]{1,0:T(8,128)S(1)} collective-permute-done((f32[8,128]{1,0:T(8,128)S(1)}, f32[8,128]{1,0:T(8,128)S(1)}, u32[]{:S(2)}, u32[]{:S(2)}) %collective-permute-start.11) | collective-permute-done | bytes 4128 | tf_op jit(solution)/shard_map/ppermute | solution.py:26
  53.9 0.8 %pick.1 = f32[1,26]{1,0:T(1,128)} custom-call(s32[8,128]{1,0:T(8,128)S(1)} %dynamic-slice_bitcast_fusion.spot_ref, f32[8,128]{1,0:T(8,128)S(1)} %join.1.here, f32[8,128]{1,0:T(8,128)S(1)} %collective-permute-done.10.after, f32[8,128]{1,0:T(8,128)S(1)} %collective-permute-done.11.before), custom_call_target="tpu_custom_call" | custom-call | tf_op jit(solution)/shard_map/pick/pallas_call | solution.py:277
  (5 shorter events, 0.1 us)
Async XLA Ops:
  0.1 1.0 %copy-start = (f32[32,32,128]{2,1,0:T(8,128)S(1)}, f32[32,32,128]{2,1,0:T(8,128)}, u32[]{:S(2)}) copy-start(f32[32,32,128]{2,1,0:T(8,128)} %sites_ref.1) | copy-start | bytes 1572868
  2.6 5.9 %collective-permute-start = (f32[27,32,128]{2,1,0:T(8,128)S(1)}, f32[27,32,128]{2,1,0:T(8,128)S(1)}, u32[]{:S(2)}, u32[]{:S(2)}) collective-permute-start(f32[27,32,128]{2,1,0:T(8,128)S(1)} %get-tuple-element.15.own), channel_id=1, source_target_pairs={{2,0},{0,2},{6,4},{4,6},{10,8},{8,10},{14,12},{12,14},{18,16},{16,... | collective-permute-start | bytes 1327112 | tf_op jit(solution)/shard_map/ppermute | solution.py:26
  3.1 12.7 %collective-permute-start.1 = (f32[27,32,128]{2,1,0:T(8,128)S(1)}, f32[27,32,128]{2,1,0:T(8,128)S(1)}, u32[]{:S(2)}, u32[]{:S(2)}) collective-permute-start(f32[27,32,128]{2,1,0:T(8,128)S(1)} %get-tuple-element.15.own), channel_id=1, source_target_pairs={{4,0},{0,4},{12,8},{8,12},{20,16},{16,20},{28,24},{24,28},{5,1},{1... | collective-permute-start | bytes 1327112 | tf_op jit(solution)/shard_map/ppermute | solution.py:26
  7.5 13.2 %collective-permute-start.4 = (f32[17,32,128]{2,1,0:T(8,128)S(1)}, f32[17,32,128]{2,1,0:T(8,128)S(1)}, u32[]{:S(2)}, u32[]{:S(2)}) collective-permute-start(f32[17,32,128]{2,1,0:T(8,128)S(1)} %get-tuple-element.18), channel_id=1, source_target_pairs={{30,0},{8,2},{2,4},{12,6},{6,8},{16,10},{10,12},{20,14},{14,16},{2... | collective-permute-start | bytes 835592 | tf_op jit(solution)/shard_map/ppermute | solution.py:26
  15.8 11.5 %collective-permute-start.5 = (f32[17,32,128]{2,1,0:T(8,128)S(1)}, f32[17,32,128]{2,1,0:T(8,128)S(1)}, u32[]{:S(2)}, u32[]{:S(2)}) collective-permute-start(f32[17,32,128]{2,1,0:T(8,128)S(1)} %slice_select_fusion), channel_id=1, source_target_pairs={{24,0},{10,2},{14,6},{0,8},{18,10},{22,14},{8,16},{26,18},{30,22},... | collective-permute-start | bytes 835592 | tf_op jit(solution)/shard_map/ppermute | solution.py:26
  20.7 6.7 %collective-permute-start.6 = (f32[17,32,128]{2,1,0:T(8,128)S(1)}, f32[17,32,128]{2,1,0:T(8,128)S(1)}, u32[]{:S(2)}, u32[]{:S(2)}) collective-permute-start(f32[17,32,128]{2,1,0:T(8,128)S(1)} %collective-permute-done.4.second), channel_id=1, source_target_pairs={{2,0},{0,2},{6,4},{4,6},{10,8},{8,10},{14,12},{12,14},{18,16},{16,... | collective-permute-start | bytes 835592 | tf_op jit(solution)/shard_map/ppermute | solution.py:26
  20.8 13.5 %collective-permute-start.3 = (f32[10,32,128]{2,1,0:T(8,128)S(1)}, f32[10,32,128]{2,1,0:T(8,128)S(1)}, u32[]{:S(2)}, u32[]{:S(2)}) collective-permute-start(f32[10,32,128]{2,1,0:T(8,128)S(1)} %get-tuple-element.17), channel_id=1, source_target_pairs={{30,0},{8,2},{2,4},{12,6},{6,8},{16,10},{10,12},{20,14},{14,16},{2... | collective-permute-start | bytes 491528 | tf_op jit(solution)/shard_map/ppermute | solution.py:26
  22.9 11.5 %collective-permute-start.2 = (f32[10,32,128]{2,1,0:T(8,128)S(1)}, f32[10,32,128]{2,1,0:T(8,128)S(1)}, u32[]{:S(2)}, u32[]{:S(2)}) collective-permute-start(f32[10,32,128]{2,1,0:T(8,128)S(1)} %slice_select_fusion.1), channel_id=1, source_target_pairs={{24,0},{10,2},{14,6},{0,8},{18,10},{22,14},{8,16},{26,18},{30,22},... | collective-permute-start | bytes 491528 | tf_op jit(solution)/shard_map/ppermute | solution.py:26
  34.3 1.5 %collective-permute-start.7 = (f32[10,32,128]{2,1,0:T(8,128)S(1)}, f32[10,32,128]{2,1,0:T(8,128)S(1)}, u32[]{:S(2)}, u32[]{:S(2)}) collective-permute-start(f32[10,32,128]{2,1,0:T(8,128)S(1)} %collective-permute-done.3.second), channel_id=1, source_target_pairs={{2,0},{0,2},{6,4},{4,6},{10,8},{8,10},{14,12},{12,14},{18,16},{16,... | collective-permute-start | bytes 491528 | tf_op jit(solution)/shard_map/ppermute | solution.py:26
  40.8 6.2 %collective-permute-start.8 = (f32[288,128]{1,0:T(8,128)S(1)}, f32[288,128]{1,0:T(8,128)S(1)}, u32[]{:S(2)}, u32[]{:S(2)}) collective-permute-start(f32[288,128]{1,0:T(8,128)S(1)} %half_chains.3.mine), channel_id=1, source_target_pairs={{0,1},{1,0},{2,3},{3,2},{4,5},{5,4},{6,7},{7,6},{8,9},{9,8},{10,11... | collective-permute-start | bytes 442376 | tf_op jit(solution)/shard_map/ppermute | solution.py:324
  47.1 1.2 %collective-permute-start.9 = (f32[8,128]{1,0:T(8,128)S(1)}, f32[8,128]{1,0:T(8,128)S(1)}, u32[]{:S(2)}, u32[]{:S(2)}) collective-permute-start(f32[8,128]{1,0:T(8,128)S(1)} %meet.1.mine), channel_id=1, source_target_pairs={{2,0},{0,2},{6,4},{4,6},{10,8},{8,10},{14,12},{12,14},{18,16},{16,... | collective-permute-start | bytes 12296 | tf_op jit(solution)/shard_map/ppermute | solution.py:26
  48.3 3.6 %collective-permute-start.10 = (f32[8,128]{1,0:T(8,128)S(1)}, f32[8,128]{1,0:T(8,128)S(1)}, u32[]{:S(2)}, u32[]{:S(2)}) collective-permute-start(f32[8,128]{1,0:T(8,128)S(1)} %join.1.here), channel_id=1, source_target_pairs={{4,0},{6,2},{8,4},{10,6},{12,8},{14,10},{16,12},{18,14},{20,16},{2... | collective-permute-start | bytes 12296 | tf_op jit(solution)/shard_map/ppermute | solution.py:26
  48.5 5.4 %collective-permute-start.11 = (f32[8,128]{1,0:T(8,128)S(1)}, f32[8,128]{1,0:T(8,128)S(1)}, u32[]{:S(2)}, u32[]{:S(2)}) collective-permute-start(f32[8,128]{1,0:T(8,128)S(1)} %join.1.here), channel_id=1, source_target_pairs={{24,0},{26,2},{28,4},{30,6},{0,8},{2,10},{4,12},{6,14},{8,16},{10,... | collective-permute-start | bytes 12296 | tf_op jit(solution)/shard_map/ppermute | solution.py:26

commit v9 on v5

--- a/solution.py
+++ b/solution.py
@@ -69,12 +69,15 @@
     return [jnp.where(lower, tile, twice), jnp.where(lower, twice, tile)]
 
 
-def advance(state, near, far):
+def spread(state, far):
     double, low = far
     high, rest = split(state)
     inner = product(jnp.concatenate([high, rest], 1), double) + product(high, low)
-    h0, l0 = split(inner[:, :128])
-    h1, l1 = split(inner[:, 128:])
+    return (*split(inner[:, :128]), *split(inner[:, 128:]))
+
+
+def gather(inner, near):
+    h0, l0, h1, l1 = inner
     results = []
     for k, tile in enumerate(near):
         rows = slice(32 * k, 32 * k + 32)
@@ -149,45 +152,44 @@
     return jnp.concatenate([state[:192], kept], 0)
 
 
-def home_step(state, home, near, flip):
-    return advance(state, near[:2], far_weights(home, flip))
-
-
-def home_kernel(count, side_ref, own, sibling, out):
+def home_kernel(side_ref, own, sibling, out):
     def run(flip):
         state = identities(64)
-        for site in range(count):
+        for site in range(own.shape[0]):
             home = interleave(own[site], sibling[site])
-            state = home_step(state, home, near_plain(own[site]) if flip else near_turned(home), flip)
+            near = near_plain(own[site]) if flip else near_turned(home)[:2]
+            state = gather(spread(state, far_weights(home, flip)), near)
         out[...] = state
 
     on_each_side(side_ref, run)
 
 
-def chain_kernel(start, side_ref, own, sibling, first, second, other, *rest):
+def chain_kernel(start, side_ref, own, sibling, first, second, other, home, *rest):
     out = rest[-1]
     count = first.shape[0]
-    last = start + count == own.shape[0]
 
     def run(flip):
-        state = rest[1][...] if start else identities(320)
-        inner = rest[0][...] if last else None
+        state = rest[0][...] if start else identities(320)
+        groups = [state[:160], state[160:]]
         for index in range(count):
             whole = start + index
-            home = interleave(own[whole], sibling[whole])
             far = interleave(first[index], second[index])
             if flip:
                 near = [n for t in (own[whole], sibling[whole], other[index], first[index], second[index])
                         for n in near_plain(t)]
             else:
                 extra = other[index]
-                near = near_turned(home) + near_turned(interleave(extra, extra))[:2] + near_turned(far)
+                near = (
+                    near_turned(interleave(own[whole], sibling[whole]))
+                    + near_turned(interleave(extra, extra))[:2]
+                    + near_turned(far)
+                )
             weights = far_weights(far, flip)
-            parts = [advance(state[:192], near[:6], weights), advance(state[192:], near[6:], weights)]
-            state = jnp.concatenate(parts, 0)
-            if last:
-                inner = home_step(inner, home, near, flip)
-        out[...] = jnp.concatenate([norms_only(state), inner], 0) if last else state
+            inner = [spread(g, weights) for g in groups]
+            groups = [gather(i, near[5 * k : 5 * k + 5]) for k, i in enumerate(inner)]
+        state = jnp.concatenate(groups, 0)
+        last = start + count == own.shape[0]
+        out[...] = jnp.concatenate([norms_only(state), home[...]], 0) if last else state
 
     on_each_side(side_ref, run)
 
@@ -299,7 +301,7 @@
     firsts = [move(p, lambda chip, core: (chip - 1, 0) if core == 0 else (chip + 2, 1)) for p in pieces]
     across = lambda chip, core: (chip, 1 - core)
     sibling = move(mps, across)
-    inner = call(functools.partial(home_kernel, starts[-1]), (64, 128), flag, mps, sibling, name="own_chains")
+    inner = call(home_kernel, (64, 128), flag, mps, sibling, name="own_chains")
     carried = (inner,)
     for start, first, second in zip(starts, firsts, seconds):
         second, *carried = lax.optimization_barrier((second, *carried))

time: 48.7 us -> 47.2 us (0.969)
  starting transfers between devices: 20.4 us -> 18.7 us
  Pallas kernels: 17.9 us -> 18.9 us
  waiting for transfers between devices: 8.47 us -> 7.71 us
    ppermute x10, starting transfers between devices: 18.6 us -> 16.7 us  [move(): return lax.ppermute(array, 'blk', pairs)]
    pallas_call x7, Pallas kernels: 17.9 us -> 18.9 us  [call(): pl.pallas_call(kernel, out_shape=shapes if many else shapes[0], in_specs=...]
    ppermute x1, waiting for transfers between devices: 4.22 us -> 3.32 us  [body(): partner = lax.ppermute(state, 'pair', [(0, 1), (1, 0)])]
  transfers between devices with their start and end apart: 11 -> 11, of which waited for: 7 -> 4; matrix products, arithmetic and copies ran while one was open for 1% -> 1% of each run, Pallas kernels for 24% -> 29%
where the time goes in v9:
time: 47.2 us; the launch traced here: 47 us
  Pallas kernels  18.9 us (40%)
  starting transfers between devices  18.7 us (40%)
  waiting for transfers between devices  7.71 us (16%)
  local copies, waits for them, and re-layouts  1.73 us (4%)
    pallas_call x7, Pallas kernels, call(): pl.pallas_call(kernel, out_shape=shapes if many else shapes[0], in_specs=...  18.9 us
    ppermute x10, starting transfers between devices, move(): return lax.ppermute(array, 'blk', pairs)  16.7 us
    ppermute x10, waiting for transfers between devices, move(): return lax.ppermute(array, 'blk', pairs)  4.38 us
    ppermute x1, waiting for transfers between devices, body(): partner = lax.ppermute(state, 'pair', [(0, 1), (1, 0)])  3.32 us
    ppermute x1, starting transfers between devices, body(): partner = lax.ppermute(state, 'pair', [(0, 1), (1, 0)])  1.98 us
    unnamed x2, local copies, waits for them, and re-layouts  1.04 us
  transfers between devices with their start and end apart: 11, of which 4 were waited for; matrix products, arithmetic and copies ran while one was open for 1% of the time, Pallas kernels for 29%

profile of v9, /device:TPU:0, one launch (start us, length us, event | category | flops | bytes accessed | tf_op | source)
XLA Modules:
  0.0 47.0 jit_solution(8942509399699561373)
XLA Ops:
  0.0 0.0 copy-start
  0.0 1.0 %copy-done = f32[32,32,128]{2,1,0:T(8,128)S(1)} copy-done((f32[32,32,128]{2,1,0:T(8,128)S(1)}, f32[32,32,128]{2,1,0:T(8,128)}, u32[]{:S(2)}) %copy-start) | copy-done | bytes 524312
  1.0 1.0 %order.1 = (f32[27,32,128]{2,1,0:T(8,128)S(1)}, f32[17,32,128]{2,1,0:T(8,128)S(1)}, f32[10,32,128]{2,1,0:T(8,128)S(1)}) custom-call(s32[1]{0:T(128)} %bitcast.1.side_ref, f32[32,32,128]{2,1,0:T(8,128)S(1)} %copy-done), custom_call_target="tpu_custom_call" | custom-call | tf_op jit(solution)/shard_map/order/pallas_call | solution.py:277
  2.0 0.5 collective-permute-start
  2.5 4.7 %collective-permute-start.3 = (f32[17,32,128]{2,1,0:T(8,128)S(1)}, f32[17,32,128]{2,1,0:T(8,128)S(1)}, u32[]{:S(2)}, u32[]{:S(2)}) collective-permute-start(f32[17,32,128]{2,1,0:T(8,128)S(1)} %get-tuple-element.15), channel_id=1, source_target_pairs={{30,0},{8,2},{2,4},{12,6},{6,8},{16,10},{10,12},{20,14},{14,16},{2... | collective-permute-start | bytes 835592 | tf_op jit(solution)/shard_map/ppermute | solution.py:25
  7.2 1.5 %collective-permute-start.4 = (f32[17,32,128]{2,1,0:T(8,128)S(1)}, f32[17,32,128]{2,1,0:T(8,128)S(1)}, u32[]{:S(2)}, u32[]{:S(2)}) collective-permute-start(f32[17,32,128]{2,1,0:T(8,128)S(1)} %get-tuple-element.15), channel_id=1, source_target_pairs={{28,0},{10,2},{0,4},{14,6},{4,8},{18,10},{8,12},{22,14},{12,16},{2... | collective-permute-start | bytes 835592 | tf_op jit(solution)/shard_map/ppermute | solution.py:25
  8.7 0.0 collective-permute-done.sibling
  8.7 7.9 %own_chains.1.home = f32[64,128]{1,0:T(8,128)S(1)} custom-call(s32[1]{0:T(128)} %bitcast.1.side_ref, f32[27,32,128]{2,1,0:T(8,128)S(1)} %get-tuple-element.13.own, f32[27,32,128]{2,1,0:T(8,128)S(1)} %collective-permute-done.sibling), custom_call_target="tpu_custom_call" | custom-call | tf_op jit(solution)/shard_map/own_chains/pallas_call | solution.py:277
  16.6 0.0 collective-permute-done.3.second
  16.6 0.1 collective-permute-start.5
  16.7 5.2 %collective-permute-start.2 = (f32[10,32,128]{2,1,0:T(8,128)S(1)}, f32[10,32,128]{2,1,0:T(8,128)S(1)}, u32[]{:S(2)}, u32[]{:S(2)}) collective-permute-start(f32[10,32,128]{2,1,0:T(8,128)S(1)} %get-tuple-element.14), channel_id=1, source_target_pairs={{30,0},{8,2},{2,4},{12,6},{6,8},{16,10},{10,12},{20,14},{14,16},{2... | collective-permute-start | bytes 491528 | tf_op jit(solution)/shard_map/ppermute | solution.py:25
  21.9 0.0 collective-permute-start.1
  21.9 0.0 collective-permute-done.4.first
  21.9 0.0 collective-permute-done.5.other
  22.0 5.6 %half_chains.2.rest_0_ = f32[320,128]{1,0:T(8,128)S(1)} custom-call(s32[1]{0:T(128)} %bitcast.1.side_ref, f32[27,32,128]{2,1,0:T(8,128)S(1)} %get-tuple-element.13.own, f32[27,32,128]{2,1,0:T(8,128)S(1)} %collective-permute-done.sibling, f32[17,32,128]{2,1,0:T(8,128)S(1)} %collective-permute-done.4.first, f32[17,32,128]{2,1,0:T(8,128)S(1)} %collective-permute-done.3.second, ...), custom_call_target="tpu_custom_call" | custom-call | tf_op jit(solution)/shard_map/half_chains/pallas_call | solution.py:277
  27.6 0.0 collective-permute-done.2.second
  27.6 0.2 collective-permute-start.6
  27.8 2.2 %collective-permute-done.1.first = f32[10,32,128]{2,1,0:T(8,128)S(1)} collective-permute-done((f32[10,32,128]{2,1,0:T(8,128)S(1)}, f32[10,32,128]{2,1,0:T(8,128)S(1)}, u32[]{:S(2)}, u32[]{:S(2)}) %collective-permute-start.1) | collective-permute-done | bytes 163872 | tf_op jit(solution)/shard_map/ppermute | solution.py:25
  30.0 0.0 collective-permute-done.6.other
  30.0 3.3 %half_chains.3.mine = f32[288,128]{1,0:T(8,128)S(1)} custom-call(s32[1]{0:T(128)} %bitcast.1.side_ref, f32[27,32,128]{2,1,0:T(8,128)S(1)} %get-tuple-element.13.own, f32[27,32,128]{2,1,0:T(8,128)S(1)} %collective-permute-done.sibling, f32[10,32,128]{2,1,0:T(8,128)S(1)} %collective-permute-done.1.first, f32[10,32,128]{2,1,0:T(8,128)S(1)} %collective-permute-done.2.second, ...), custom_call_target="tpu_custom_call" | custom-call | tf_op jit(solution)/shard_map/half_chains/pallas_call | solution.py:277
  33.2 2.0 %collective-permute-start.7 = (f32[288,128]{1,0:T(8,128)S(1)}, f32[288,128]{1,0:T(8,128)S(1)}, u32[]{:S(2)}, u32[]{:S(2)}) collective-permute-start(f32[288,128]{1,0:T(8,128)S(1)} %half_chains.3.mine), channel_id=1, source_target_pairs={{0,1},{1,0},{2,3},{3,2},{4,5},{5,4},{6,7},{7,6},{8,9},{9,8},{10,11... | collective-permute-start | bytes 442376 | tf_op jit(solution)/shard_map/ppermute | solution.py:313
  35.2 3.3 %collective-permute-done.7.theirs = f32[288,128]{1,0:T(8,128)S(1)} collective-permute-done((f32[288,128]{1,0:T(8,128)S(1)}, f32[288,128]{1,0:T(8,128)S(1)}, u32[]{:S(2)}, u32[]{:S(2)}) %collective-permute-start.7) | collective-permute-done | bytes 147488 | tf_op jit(solution)/shard_map/ppermute | solution.py:313
  38.5 0.2 meet.1.mine
  38.7 0.0 collective-permute-start.8
  38.7 1.2 %collective-permute-done.8.theirs = f32[8,128]{1,0:T(8,128)S(1)} collective-permute-done((f32[8,128]{1,0:T(8,128)S(1)}, f32[8,128]{1,0:T(8,128)S(1)}, u32[]{:S(2)}, u32[]{:S(2)}) %collective-permute-start.8) | collective-permute-done | bytes 4128 | tf_op jit(solution)/shard_map/ppermute | solution.py:25
  39.9 0.1 join.1.here
  39.9 0.1 collective-permute-start.10
  40.0 4.5 %collective-permute-start.9 = (f32[8,128]{1,0:T(8,128)S(1)}, f32[8,128]{1,0:T(8,128)S(1)}, u32[]{:S(2)}, u32[]{:S(2)}) collective-permute-start(f32[8,128]{1,0:T(8,128)S(1)} %join.1.here), channel_id=1, source_target_pairs={{4,0},{6,2},{8,4},{10,6},{12,8},{14,10},{16,12},{18,14},{20,16},{2... | collective-permute-start | bytes 12296 | tf_op jit(solution)/shard_map/ppermute | solution.py:25
  44.5 0.7 %dynamic-slice_bitcast_fusion.spot_ref = s32[8,128]{1,0:T(8,128)S(1)} fusion(s32[2,2,8,128]{3,2,1,0:T(8,128)} %constant.24.clone, s32[]{:T(128)S(6)} %select_n.14, s32[]{:T(128)S(6)} %select_n.15), kind=kLoop, calls=%fused_computation | loop fusion | bytes 8200 | tf_op jit(solution)/shard_map/squeeze | solution.py:318
  45.1 1.0 %collective-permute-done.10.before = f32[8,128]{1,0:T(8,128)S(1)} collective-permute-done((f32[8,128]{1,0:T(8,128)S(1)}, f32[8,128]{1,0:T(8,128)S(1)}, u32[]{:S(2)}, u32[]{:S(2)}) %collective-permute-start.10) | collective-permute-done | bytes 4128 | tf_op jit(solution)/shard_map/ppermute | solution.py:25
  46.2 0.0 collective-permute-done.9.after
  46.2 0.8 %pick.1 = f32[1,26]{1,0:T(1,128)} custom-call(s32[8,128]{1,0:T(8,128)S(1)} %dynamic-slice_bitcast_fusion.spot_ref, f32[8,128]{1,0:T(8,128)S(1)} %join.1.here, f32[8,128]{1,0:T(8,128)S(1)} %collective-permute-done.9.after, f32[8,128]{1,0:T(8,128)S(1)} %collective-permute-done.10.before), custom_call_target="tpu_custom_call" | custom-call | tf_op jit(solution)/shard_map/pick/pallas_call | solution.py:277
Async XLA Ops:
  0.0 1.0 %copy-start = (f32[32,32,128]{2,1,0:T(8,128)S(1)}, f32[32,32,128]{2,1,0:T(8,128)}, u32[]{:S(2)}) copy-start(f32[32,32,128]{2,1,0:T(8,128)} %sites_ref.1) | copy-start | bytes 1572868
  2.0 6.7 %collective-permute-start = (f32[27,32,128]{2,1,0:T(8,128)S(1)}, f32[27,32,128]{2,1,0:T(8,128)S(1)}, u32[]{:S(2)}, u32[]{:S(2)}) collective-permute-start(f32[27,32,128]{2,1,0:T(8,128)S(1)} %get-tuple-element.13.own), channel_id=1, source_target_pairs={{2,0},{0,2},{6,4},{4,6},{10,8},{8,10},{14,12},{12,14},{18,16},{16,... | collective-permute-start | bytes 1327112 | tf_op jit(solution)/shard_map/ppermute | solution.py:25
  2.5 14.1 %collective-permute-start.3 = (f32[17,32,128]{2,1,0:T(8,128)S(1)}, f32[17,32,128]{2,1,0:T(8,128)S(1)}, u32[]{:S(2)}, u32[]{:S(2)}) collective-permute-start(f32[17,32,128]{2,1,0:T(8,128)S(1)} %get-tuple-element.15), channel_id=1, source_target_pairs={{30,0},{8,2},{2,4},{12,6},{6,8},{16,10},{10,12},{20,14},{14,16},{2... | collective-permute-start | bytes 835592 | tf_op jit(solution)/shard_map/ppermute | solution.py:25
  7.2 14.7 %collective-permute-start.4 = (f32[17,32,128]{2,1,0:T(8,128)S(1)}, f32[17,32,128]{2,1,0:T(8,128)S(1)}, u32[]{:S(2)}, u32[]{:S(2)}) collective-permute-start(f32[17,32,128]{2,1,0:T(8,128)S(1)} %get-tuple-element.15), channel_id=1, source_target_pairs={{28,0},{10,2},{0,4},{14,6},{4,8},{18,10},{8,12},{22,14},{12,16},{2... | collective-permute-start | bytes 835592 | tf_op jit(solution)/shard_map/ppermute | solution.py:25
  16.6 5.3 %collective-permute-start.5 = (f32[17,32,128]{2,1,0:T(8,128)S(1)}, f32[17,32,128]{2,1,0:T(8,128)S(1)}, u32[]{:S(2)}, u32[]{:S(2)}) collective-permute-start(f32[17,32,128]{2,1,0:T(8,128)S(1)} %collective-permute-done.3.second), channel_id=1, source_target_pairs={{2,0},{0,2},{6,4},{4,6},{10,8},{8,10},{14,12},{12,14},{18,16},{16,... | collective-permute-start | bytes 835592 | tf_op jit(solution)/shard_map/ppermute | solution.py:25
  16.7 10.8 %collective-permute-start.2 = (f32[10,32,128]{2,1,0:T(8,128)S(1)}, f32[10,32,128]{2,1,0:T(8,128)S(1)}, u32[]{:S(2)}, u32[]{:S(2)}) collective-permute-start(f32[10,32,128]{2,1,0:T(8,128)S(1)} %get-tuple-element.14), channel_id=1, source_target_pairs={{30,0},{8,2},{2,4},{12,6},{6,8},{16,10},{10,12},{20,14},{14,16},{2... | collective-permute-start | bytes 491528 | tf_op jit(solution)/shard_map/ppermute | solution.py:25
  21.9 8.0 %collective-permute-start.1 = (f32[10,32,128]{2,1,0:T(8,128)S(1)}, f32[10,32,128]{2,1,0:T(8,128)S(1)}, u32[]{:S(2)}, u32[]{:S(2)}) collective-permute-start(f32[10,32,128]{2,1,0:T(8,128)S(1)} %get-tuple-element.14), channel_id=1, source_target_pairs={{28,0},{10,2},{0,4},{14,6},{4,8},{18,10},{8,12},{22,14},{12,16},{2... | collective-permute-start | bytes 491528 | tf_op jit(solution)/shard_map/ppermute | solution.py:25
  27.6 2.4 %collective-permute-start.6 = (f32[10,32,128]{2,1,0:T(8,128)S(1)}, f32[10,32,128]{2,1,0:T(8,128)S(1)}, u32[]{:S(2)}, u32[]{:S(2)}) collective-permute-start(f32[10,32,128]{2,1,0:T(8,128)S(1)} %collective-permute-done.2.second), channel_id=1, source_target_pairs={{2,0},{0,2},{6,4},{4,6},{10,8},{8,10},{14,12},{12,14},{18,16},{16,... | collective-permute-start | bytes 491528 | tf_op jit(solution)/shard_map/ppermute | solution.py:25
  33.2 5.3 %collective-permute-start.7 = (f32[288,128]{1,0:T(8,128)S(1)}, f32[288,128]{1,0:T(8,128)S(1)}, u32[]{:S(2)}, u32[]{:S(2)}) collective-permute-start(f32[288,128]{1,0:T(8,128)S(1)} %half_chains.3.mine), channel_id=1, source_target_pairs={{0,1},{1,0},{2,3},{3,2},{4,5},{5,4},{6,7},{7,6},{8,9},{9,8},{10,11... | collective-permute-start | bytes 442376 | tf_op jit(solution)/shard_map/ppermute | solution.py:313
  38.7 1.2 %collective-permute-start.8 = (f32[8,128]{1,0:T(8,128)S(1)}, f32[8,128]{1,0:T(8,128)S(1)}, u32[]{:S(2)}, u32[]{:S(2)}) collective-permute-start(f32[8,128]{1,0:T(8,128)S(1)} %meet.1.mine), channel_id=1, source_target_pairs={{2,0},{0,2},{6,4},{4,6},{10,8},{8,10},{14,12},{12,14},{18,16},{16,... | collective-permute-start | bytes 12296 | tf_op jit(solution)/shard_map/ppermute | solution.py:25
  39.9 6.2 %collective-permute-start.10 = (f32[8,128]{1,0:T(8,128)S(1)}, f32[8,128]{1,0:T(8,128)S(1)}, u32[]{:S(2)}, u32[]{:S(2)}) collective-permute-start(f32[8,128]{1,0:T(8,128)S(1)} %join.1.here), channel_id=1, source_target_pairs={{24,0},{26,2},{28,4},{30,6},{0,8},{2,10},{4,12},{6,14},{8,16},{10,... | collective-permute-start | bytes 12296 | tf_op jit(solution)/shard_map/ppermute | solution.py:25
  40.0 6.2 %collective-permute-start.9 = (f32[8,128]{1,0:T(8,128)S(1)}, f32[8,128]{1,0:T(8,128)S(1)}, u32[]{:S(2)}, u32[]{:S(2)}) collective-permute-start(f32[8,128]{1,0:T(8,128)S(1)} %join.1.here), channel_id=1, source_target_pairs={{4,0},{6,2},{8,4},{10,6},{12,8},{14,10},{16,12},{18,14},{20,16},{2... | collective-permute-start | bytes 12296 | tf_op jit(solution)/shard_map/ppermute | solution.py:25

commit v10 on v9

--- a/solution.py
+++ b/solution.py
@@ -9,7 +9,7 @@
 
 REACH = 6
 EDGE = 6
-SHARE = 0.63
+SHARE = 0.7
 BF16, F32 = jnp.bfloat16, jnp.float32
 VMEM = pl.BlockSpec(memory_space=pltpu.VMEM)
 SMEM = pl.BlockSpec(memory_space=pltpu.SMEM)
@@ -302,6 +302,9 @@
     across = lambda chip, core: (chip, 1 - core)
     sibling = move(mps, across)
     inner = call(home_kernel, (64, 128), flag, mps, sibling, name="own_chains")
+    spots = jnp.asarray([spot_table(core, samp, band) for core in range(2)], jnp.int32)
+    spot = spots[lax.axis_index("blk") % 2, side]
+    inner, spot = lax.optimization_barrier((inner, spot))
     carried = (inner,)
     for start, first, second in zip(starts, firsts, seconds):
         second, *carried = lax.optimization_barrier((second, *carried))
@@ -314,8 +317,6 @@
     tile = call(meet_kernel, (8, 128), state, partner, name="meet")
     tile = call(join_kernel, (8, 128), tile, move(tile, across), name="join")
     tiles = [tile] + [move(tile, lambda chip, core: (chip + gap, core)) for gap in (1, -2)]
-    spots = jnp.asarray([spot_table(core, samp, band) for core in range(2)], jnp.int32)
-    spot = spots[lax.axis_index("blk") % 2, side]
     return call(pick_kernel, (1, (2 * band + 1) * samp), spot, *tiles, name="pick")
 
 

time: 47.2 us -> 48.2 us (1.021)
  starting transfers between devices: 18.7 us -> 19.5 us
    ppermute x1, waiting for transfers between devices: 3.32 us -> 4.16 us  [body(): partner = lax.ppermute(state, 'pair', [(0, 1), (1, 0)])]
    ppermute x10, starting transfers between devices: 16.7 us -> 17.4 us  [move(): return lax.ppermute(array, 'blk', pairs)]
    ppermute x10, waiting for transfers between devices: 4.38 us -> 3.72 us  [move(): return lax.ppermute(array, 'blk', pairs)]
  transfers between devices with their start and end apart: 11 -> 11, of which waited for: 4 -> 5; matrix products, arithmetic and copies ran while one was open for 1% -> 1% of each run, Pallas kernels for 29% -> 30%
where the time goes in v10:
time: 48.2 us; the launch traced here: 48 us
  starting transfers between devices  19.5 us (40%)
  Pallas kernels  18.9 us (39%)
  waiting for transfers between devices  7.88 us (16%)
  local copies, waits for them, and re-layouts  1.73 us (4%)
    pallas_call x7, Pallas kernels, call(): pl.pallas_call(kernel, out_shape=shapes if many else shapes[0], in_specs=...  18.9 us
    ppermute x10, starting transfers between devices, move(): return lax.ppermute(array, 'blk', pairs)  17.4 us
    ppermute x1, waiting for transfers between devices, body(): partner = lax.ppermute(state, 'pair', [(0, 1), (1, 0)])  4.16 us
    ppermute x10, waiting for transfers between devices, move(): return lax.ppermute(array, 'blk', pairs)  3.72 us
    ppermute x1, starting transfers between devices, body(): partner = lax.ppermute(state, 'pair', [(0, 1), (1, 0)])  2.07 us
    unnamed x2, local copies, waits for them, and re-layouts  1.04 us
  transfers between devices with their start and end apart: 11, of which 5 were waited for; matrix products, arithmetic and copies ran while one was open for 1% of the time, Pallas kernels for 30%

profile of v10, /device:TPU:0, one launch (start us, length us, event | category | flops | bytes accessed | tf_op | source)
XLA Modules:
  0.0 48.0 jit_solution(17662659529320411874)
XLA Ops:
  0.0 0.0 copy-start
  0.0 1.0 %copy-done = f32[32,32,128]{2,1,0:T(8,128)S(1)} copy-done((f32[32,32,128]{2,1,0:T(8,128)S(1)}, f32[32,32,128]{2,1,0:T(8,128)}, u32[]{:S(2)}) %copy-start) | copy-done | bytes 524312
  1.0 1.0 %order.1 = (f32[27,32,128]{2,1,0:T(8,128)S(1)}, f32[19,32,128]{2,1,0:T(8,128)S(1)}, f32[8,32,128]{2,1,0:T(8,128)S(1)}) custom-call(s32[1]{0:T(128)} %bitcast.side_ref, f32[32,32,128]{2,1,0:T(8,128)S(1)} %copy-done), custom_call_target="tpu_custom_call" | custom-call | tf_op jit(solution)/shard_map/order/pallas_call | solution.py:277
  2.0 0.5 collective-permute-start
  2.5 4.7 %collective-permute-start.3 = (f32[19,32,128]{2,1,0:T(8,128)S(1)}, f32[19,32,128]{2,1,0:T(8,128)S(1)}, u32[]{:S(2)}, u32[]{:S(2)}) collective-permute-start(f32[19,32,128]{2,1,0:T(8,128)S(1)} %get-tuple-element.18), channel_id=1, source_target_pairs={{30,0},{8,2},{2,4},{12,6},{6,8},{16,10},{10,12},{20,14},{14,16},{2... | collective-permute-start | bytes 933896 | tf_op jit(solution)/shard_map/ppermute | solution.py:25
  7.2 1.5 %collective-permute-start.4 = (f32[19,32,128]{2,1,0:T(8,128)S(1)}, f32[19,32,128]{2,1,0:T(8,128)S(1)}, u32[]{:S(2)}, u32[]{:S(2)}) collective-permute-start(f32[19,32,128]{2,1,0:T(8,128)S(1)} %get-tuple-element.18), channel_id=1, source_target_pairs={{28,0},{10,2},{0,4},{14,6},{4,8},{18,10},{8,12},{22,14},{12,16},{2... | collective-permute-start | bytes 933896 | tf_op jit(solution)/shard_map/ppermute | solution.py:25
  8.7 0.7 %dynamic-slice_bitcast_fusion.spot_ref = s32[8,128]{1,0:T(8,128)S(1)} fusion(s32[2,2,8,128]{3,2,1,0:T(8,128)} %constant.24.clone, s32[]{:T(128)S(6)} %select_n.14, s32[]{:T(128)S(6)} %select_n.15), kind=kLoop, calls=%fused_computation | loop fusion | bytes 8200 | tf_op jit(solution)/shard_map/squeeze | solution.py:306
  9.4 0.0 collective-permute-done.sibling
  9.4 7.9 %own_chains.1.home = f32[64,128]{1,0:T(8,128)S(1)} custom-call(s32[1]{0:T(128)} %bitcast.side_ref, f32[27,32,128]{2,1,0:T(8,128)S(1)} %get-tuple-element.15.own, f32[27,32,128]{2,1,0:T(8,128)S(1)} %collective-permute-done.sibling), custom_call_target="tpu_custom_call" | custom-call | tf_op jit(solution)/shard_map/own_chains/pallas_call | solution.py:277
  17.3 0.0 collective-permute-done.3.second
  17.3 0.1 collective-permute-start.5
  17.4 5.9 %collective-permute-start.2 = (f32[8,32,128]{2,1,0:T(8,128)S(1)}, f32[8,32,128]{2,1,0:T(8,128)S(1)}, u32[]{:S(2)}, u32[]{:S(2)}) collective-permute-start(f32[8,32,128]{2,1,0:T(8,128)S(1)} %get-tuple-element.17), channel_id=1, source_target_pairs={{30,0},{8,2},{2,4},{12,6},{6,8},{16,10},{10,12},{20,14},{14,16},{2... | collective-permute-start | bytes 393224 | tf_op jit(solution)/shard_map/ppermute | solution.py:25
  23.3 0.0 collective-permute-start.1
  23.4 0.0 collective-permute-done.4.first
  23.4 0.0 collective-permute-done.5.other
  23.4 6.2 %half_chains.2.rest_0_ = f32[320,128]{1,0:T(8,128)S(1)} custom-call(s32[1]{0:T(128)} %bitcast.side_ref, f32[27,32,128]{2,1,0:T(8,128)S(1)} %get-tuple-element.15.own, f32[27,32,128]{2,1,0:T(8,128)S(1)} %collective-permute-done.sibling, f32[19,32,128]{2,1,0:T(8,128)S(1)} %collective-permute-done.4.first, f32[19,32,128]{2,1,0:T(8,128)S(1)} %collective-permute-done.3.second, ...), custom_call_target="tpu_custom_call" | custom-call | tf_op jit(solution)/shard_map/half_chains/pallas_call | solution.py:277
  29.6 0.0 collective-permute-done.2.second
  29.6 0.2 collective-permute-start.6
  29.8 1.2 %collective-permute-done.1.first = f32[8,32,128]{2,1,0:T(8,128)S(1)} collective-permute-done((f32[8,32,128]{2,1,0:T(8,128)S(1)}, f32[8,32,128]{2,1,0:T(8,128)S(1)}, u32[]{:S(2)}, u32[]{:S(2)}) %collective-permute-start.1) | collective-permute-done | bytes 131104 | tf_op jit(solution)/shard_map/ppermute | solution.py:25
  31.0 0.0 collective-permute-done.6.other
  31.0 2.6 %half_chains.3.mine = f32[288,128]{1,0:T(8,128)S(1)} custom-call(s32[1]{0:T(128)} %bitcast.side_ref, f32[27,32,128]{2,1,0:T(8,128)S(1)} %get-tuple-element.15.own, f32[27,32,128]{2,1,0:T(8,128)S(1)} %collective-permute-done.sibling, f32[8,32,128]{2,1,0:T(8,128)S(1)} %collective-permute-done.1.first, f32[8,32,128]{2,1,0:T(8,128)S(1)} %collective-permute-done.2.second, ...), custom_call_target="tpu_custom_call" | custom-call | tf_op jit(solution)/shard_map/half_chains/pallas_call | solution.py:277
  33.7 2.1 %collective-permute-start.7 = (f32[288,128]{1,0:T(8,128)S(1)}, f32[288,128]{1,0:T(8,128)S(1)}, u32[]{:S(2)}, u32[]{:S(2)}) collective-permute-start(f32[288,128]{1,0:T(8,128)S(1)} %half_chains.3.mine), channel_id=1, source_target_pairs={{0,1},{1,0},{2,3},{3,2},{4,5},{5,4},{6,7},{7,6},{8,9},{9,8},{10,11... | collective-permute-start | bytes 442376 | tf_op jit(solution)/shard_map/ppermute | solution.py:316
  35.7 4.2 %collective-permute-done.7.theirs = f32[288,128]{1,0:T(8,128)S(1)} collective-permute-done((f32[288,128]{1,0:T(8,128)S(1)}, f32[288,128]{1,0:T(8,128)S(1)}, u32[]{:S(2)}, u32[]{:S(2)}) %collective-permute-start.7) | collective-permute-done | bytes 147488 | tf_op jit(solution)/shard_map/ppermute | solution.py:316
  39.9 0.2 meet.1.mine
  40.0 0.0 collective-permute-start.8
  40.1 1.2 %collective-permute-done.8.theirs = f32[8,128]{1,0:T(8,128)S(1)} collective-permute-done((f32[8,128]{1,0:T(8,128)S(1)}, f32[8,128]{1,0:T(8,128)S(1)}, u32[]{:S(2)}, u32[]{:S(2)}) %collective-permute-start.8) | collective-permute-done | bytes 4128 | tf_op jit(solution)/shard_map/ppermute | solution.py:25
  41.2 0.1 join.1.here
  41.3 0.2 collective-permute-start.10
  41.5 4.4 %collective-permute-start.9 = (f32[8,128]{1,0:T(8,128)S(1)}, f32[8,128]{1,0:T(8,128)S(1)}, u32[]{:S(2)}, u32[]{:S(2)}) collective-permute-start(f32[8,128]{1,0:T(8,128)S(1)} %join.1.here), channel_id=1, source_target_pairs={{4,0},{6,2},{8,4},{10,6},{12,8},{14,10},{16,12},{18,14},{20,16},{2... | collective-permute-start | bytes 12296 | tf_op jit(solution)/shard_map/ppermute | solution.py:25
  45.8 0.9 %collective-permute-done.10.before = f32[8,128]{1,0:T(8,128)S(1)} collective-permute-done((f32[8,128]{1,0:T(8,128)S(1)}, f32[8,128]{1,0:T(8,128)S(1)}, u32[]{:S(2)}, u32[]{:S(2)}) %collective-permute-start.10) | collective-permute-done | bytes 4128 | tf_op jit(solution)/shard_map/ppermute | solution.py:25
  46.7 0.5 collective-permute-done.9.after
  47.2 0.8 %pick.1 = f32[1,26]{1,0:T(1,128)} custom-call(s32[8,128]{1,0:T(8,128)S(1)} %dynamic-slice_bitcast_fusion.spot_ref, f32[8,128]{1,0:T(8,128)S(1)} %join.1.here, f32[8,128]{1,0:T(8,128)S(1)} %collective-permute-done.9.after, f32[8,128]{1,0:T(8,128)S(1)} %collective-permute-done.10.before), custom_call_target="tpu_custom_call" | custom-call | tf_op jit(solution)/shard_map/pick/pallas_call | solution.py:277
Async XLA Ops:
  0.0 1.0 %copy-start = (f32[32,32,128]{2,1,0:T(8,128)S(1)}, f32[32,32,128]{2,1,0:T(8,128)}, u32[]{:S(2)}) copy-start(f32[32,32,128]{2,1,0:T(8,128)} %sites_ref.1) | copy-start | bytes 1572868
  2.0 7.4 %collective-permute-start = (f32[27,32,128]{2,1,0:T(8,128)S(1)}, f32[27,32,128]{2,1,0:T(8,128)S(1)}, u32[]{:S(2)}, u32[]{:S(2)}) collective-permute-start(f32[27,32,128]{2,1,0:T(8,128)S(1)} %get-tuple-element.15.own), channel_id=1, source_target_pairs={{2,0},{0,2},{6,4},{4,6},{10,8},{8,10},{14,12},{12,14},{18,16},{16,... | collective-permute-start | bytes 1327112 | tf_op jit(solution)/shard_map/ppermute | solution.py:25
  2.5 14.8 %collective-permute-start.3 = (f32[19,32,128]{2,1,0:T(8,128)S(1)}, f32[19,32,128]{2,1,0:T(8,128)S(1)}, u32[]{:S(2)}, u32[]{:S(2)}) collective-permute-start(f32[19,32,128]{2,1,0:T(8,128)S(1)} %get-tuple-element.18), channel_id=1, source_target_pairs={{30,0},{8,2},{2,4},{12,6},{6,8},{16,10},{10,12},{20,14},{14,16},{2... | collective-permute-start | bytes 933896 | tf_op jit(solution)/shard_map/ppermute | solution.py:25
  7.2 16.1 %collective-permute-start.4 = (f32[19,32,128]{2,1,0:T(8,128)S(1)}, f32[19,32,128]{2,1,0:T(8,128)S(1)}, u32[]{:S(2)}, u32[]{:S(2)}) collective-permute-start(f32[19,32,128]{2,1,0:T(8,128)S(1)} %get-tuple-element.18), channel_id=1, source_target_pairs={{28,0},{10,2},{0,4},{14,6},{4,8},{18,10},{8,12},{22,14},{12,16},{2... | collective-permute-start | bytes 933896 | tf_op jit(solution)/shard_map/ppermute | solution.py:25
  17.3 6.0 %collective-permute-start.5 = (f32[19,32,128]{2,1,0:T(8,128)S(1)}, f32[19,32,128]{2,1,0:T(8,128)S(1)}, u32[]{:S(2)}, u32[]{:S(2)}) collective-permute-start(f32[19,32,128]{2,1,0:T(8,128)S(1)} %collective-permute-done.3.second), channel_id=1, source_target_pairs={{2,0},{0,2},{6,4},{4,6},{10,8},{8,10},{14,12},{12,14},{18,16},{16,... | collective-permute-start | bytes 933896 | tf_op jit(solution)/shard_map/ppermute | solution.py:25
  17.4 12.2 %collective-permute-start.2 = (f32[8,32,128]{2,1,0:T(8,128)S(1)}, f32[8,32,128]{2,1,0:T(8,128)S(1)}, u32[]{:S(2)}, u32[]{:S(2)}) collective-permute-start(f32[8,32,128]{2,1,0:T(8,128)S(1)} %get-tuple-element.17), channel_id=1, source_target_pairs={{30,0},{8,2},{2,4},{12,6},{6,8},{16,10},{10,12},{20,14},{14,16},{2... | collective-permute-start | bytes 393224 | tf_op jit(solution)/shard_map/ppermute | solution.py:25
  23.3 7.7 %collective-permute-start.1 = (f32[8,32,128]{2,1,0:T(8,128)S(1)}, f32[8,32,128]{2,1,0:T(8,128)S(1)}, u32[]{:S(2)}, u32[]{:S(2)}) collective-permute-start(f32[8,32,128]{2,1,0:T(8,128)S(1)} %get-tuple-element.17), channel_id=1, source_target_pairs={{28,0},{10,2},{0,4},{14,6},{4,8},{18,10},{8,12},{22,14},{12,16},{2... | collective-permute-start | bytes 393224 | tf_op jit(solution)/shard_map/ppermute | solution.py:25
  29.6 1.4 %collective-permute-start.6 = (f32[8,32,128]{2,1,0:T(8,128)S(1)}, f32[8,32,128]{2,1,0:T(8,128)S(1)}, u32[]{:S(2)}, u32[]{:S(2)}) collective-permute-start(f32[8,32,128]{2,1,0:T(8,128)S(1)} %collective-permute-done.2.second), channel_id=1, source_target_pairs={{2,0},{0,2},{6,4},{4,6},{10,8},{8,10},{14,12},{12,14},{18,16},{16,... | collective-permute-start | bytes 393224 | tf_op jit(solution)/shard_map/ppermute | solution.py:25
  33.7 6.2 %collective-permute-start.7 = (f32[288,128]{1,0:T(8,128)S(1)}, f32[288,128]{1,0:T(8,128)S(1)}, u32[]{:S(2)}, u32[]{:S(2)}) collective-permute-start(f32[288,128]{1,0:T(8,128)S(1)} %half_chains.3.mine), channel_id=1, source_target_pairs={{0,1},{1,0},{2,3},{3,2},{4,5},{5,4},{6,7},{7,6},{8,9},{9,8},{10,11... | collective-permute-start | bytes 442376 | tf_op jit(solution)/shard_map/ppermute | solution.py:316
  40.0 1.2 %collective-permute-start.8 = (f32[8,128]{1,0:T(8,128)S(1)}, f32[8,128]{1,0:T(8,128)S(1)}, u32[]{:S(2)}, u32[]{:S(2)}) collective-permute-start(f32[8,128]{1,0:T(8,128)S(1)} %meet.1.mine), channel_id=1, source_target_pairs={{2,0},{0,2},{6,4},{4,6},{10,8},{8,10},{14,12},{12,14},{18,16},{16,... | collective-permute-start | bytes 12296 | tf_op jit(solution)/shard_map/ppermute | solution.py:25
  41.3 5.4 %collective-permute-start.10 = (f32[8,128]{1,0:T(8,128)S(1)}, f32[8,128]{1,0:T(8,128)S(1)}, u32[]{:S(2)}, u32[]{:S(2)}) collective-permute-start(f32[8,128]{1,0:T(8,128)S(1)} %join.1.here), channel_id=1, source_target_pairs={{24,0},{26,2},{28,4},{30,6},{0,8},{2,10},{4,12},{6,14},{8,16},{10,... | collective-permute-start | bytes 12296 | tf_op jit(solution)/shard_map/ppermute | solution.py:25
  41.5 5.7 %collective-permute-start.9 = (f32[8,128]{1,0:T(8,128)S(1)}, f32[8,128]{1,0:T(8,128)S(1)}, u32[]{:S(2)}, u32[]{:S(2)}) collective-permute-start(f32[8,128]{1,0:T(8,128)S(1)} %join.1.here), channel_id=1, source_target_pairs={{4,0},{6,2},{8,4},{10,6},{12,8},{14,10},{16,12},{18,14},{20,16},{2... | collective-permute-start | bytes 12296 | tf_op jit(solution)/shard_map/ppermute | solution.py:25

commit v11 on v10

--- a/solution.py
+++ b/solution.py
@@ -9,7 +9,7 @@
 
 REACH = 6
 EDGE = 6
-SHARE = 0.7
+SHARE = 0.63
 BF16, F32 = jnp.bfloat16, jnp.float32
 VMEM = pl.BlockSpec(memory_space=pltpu.VMEM)
 SMEM = pl.BlockSpec(memory_space=pltpu.SMEM)
@@ -170,7 +170,8 @@
 
     def run(flip):
         state = rest[0][...] if start else identities(320)
-        groups = [state[:160], state[160:]]
+        cuts = (0, 4, 7, 10)
+        groups = [state[32 * a : 32 * b] for a, b in zip(cuts, cuts[1:])]
         for index in range(count):
             whole = start + index
             far = interleave(first[index], second[index])
@@ -186,7 +187,7 @@
                 )
             weights = far_weights(far, flip)
             inner = [spread(g, weights) for g in groups]
-            groups = [gather(i, near[5 * k : 5 * k + 5]) for k, i in enumerate(inner)]
+            groups = [gather(i, near[a:b]) for i, a, b in zip(inner, cuts, cuts[1:])]
         state = jnp.concatenate(groups, 0)
         last = start + count == own.shape[0]
         out[...] = jnp.concatenate([norms_only(state), home[...]], 0) if last else state

time: 48.2 us -> 47.3 us (0.981)
  starting transfers between devices: 19.5 us -> 18 us
  Pallas kernels: 18.9 us -> 19.4 us
    ppermute x10, starting transfers between devices: 17.4 us -> 16 us  [move(): return lax.ppermute(array, 'blk', pairs)]
    ppermute x10, waiting for transfers between devices: 3.72 us -> 4.32 us  [move(): return lax.ppermute(array, 'blk', pairs)]
    pallas_call x7, Pallas kernels: 18.9 us -> 19.4 us  [call(): pl.pallas_call(kernel, out_shape=shapes if many else shapes[0], in_specs=...]
    ppermute x1, waiting for transfers between devices: 4.16 us -> 3.64 us  [body(): partner = lax.ppermute(state, 'pair', [(0, 1), (1, 0)])]
  transfers between devices with their start and end apart: 11 -> 11, of which waited for: 5 -> 5; matrix products, arithmetic and copies ran while one was open for 1% -> 1% of each run, Pallas kernels for 30% -> 29%
where the time goes in v11:
time: 47.3 us; the launch traced here: 47.2 us
  Pallas kernels  19.4 us (41%)
  starting transfers between devices  18 us (38%)
  waiting for transfers between devices  7.96 us (17%)
  local copies, waits for them, and re-layouts  1.73 us (4%)
    pallas_call x7, Pallas kernels, call(): pl.pallas_call(kernel, out_shape=shapes if many else shapes[0], in_specs=...  19.4 us
    ppermute x10, starting transfers between devices, move(): return lax.ppermute(array, 'blk', pairs)  16 us
    ppermute x10, waiting for transfers between devices, move(): return lax.ppermute(array, 'blk', pairs)  4.32 us
    ppermute x1, waiting for transfers between devices, body(): partner = lax.ppermute(state, 'pair', [(0, 1), (1, 0)])  3.64 us
    ppermute x1, starting transfers between devices, body(): partner = lax.ppermute(state, 'pair', [(0, 1), (1, 0)])  1.97 us
    unnamed x2, local copies, waits for them, and re-layouts  1.04 us
  transfers between devices with their start and end apart: 11, of which 5 were waited for; matrix products, arithmetic and copies ran while one was open for 1% of the time, Pallas kernels for 29%

profile of v11, /device:TPU:0, one launch (start us, length us, event | category | flops | bytes accessed | tf_op | source)
XLA Modules:
  0.0 47.2 jit_solution(7921923707231929764)
XLA Ops:
  0.0 0.0 copy-start
  0.0 1.0 %copy-done = f32[32,32,128]{2,1,0:T(8,128)S(1)} copy-done((f32[32,32,128]{2,1,0:T(8,128)S(1)}, f32[32,32,128]{2,1,0:T(8,128)}, u32[]{:S(2)}) %copy-start) | copy-done | bytes 524312
  1.0 1.0 %order.1 = (f32[27,32,128]{2,1,0:T(8,128)S(1)}, f32[17,32,128]{2,1,0:T(8,128)S(1)}, f32[10,32,128]{2,1,0:T(8,128)S(1)}) custom-call(s32[1]{0:T(128)} %bitcast.side_ref, f32[32,32,128]{2,1,0:T(8,128)S(1)} %copy-done), custom_call_target="tpu_custom_call" | custom-call | tf_op jit(solution)/shard_map/order/pallas_call | solution.py:278
  2.0 0.5 collective-permute-start
  2.5 4.7 %collective-permute-start.3 = (f32[17,32,128]{2,1,0:T(8,128)S(1)}, f32[17,32,128]{2,1,0:T(8,128)S(1)}, u32[]{:S(2)}, u32[]{:S(2)}) collective-permute-start(f32[17,32,128]{2,1,0:T(8,128)S(1)} %get-tuple-element.18), channel_id=1, source_target_pairs={{30,0},{8,2},{2,4},{12,6},{6,8},{16,10},{10,12},{20,14},{14,16},{2... | collective-permute-start | bytes 835592 | tf_op jit(solution)/shard_map/ppermute | solution.py:25
  7.2 1.5 %collective-permute-start.4 = (f32[17,32,128]{2,1,0:T(8,128)S(1)}, f32[17,32,128]{2,1,0:T(8,128)S(1)}, u32[]{:S(2)}, u32[]{:S(2)}) collective-permute-start(f32[17,32,128]{2,1,0:T(8,128)S(1)} %get-tuple-element.18), channel_id=1, source_target_pairs={{28,0},{10,2},{0,4},{14,6},{4,8},{18,10},{8,12},{22,14},{12,16},{2... | collective-permute-start | bytes 835592 | tf_op jit(solution)/shard_map/ppermute | solution.py:25
  8.7 0.7 %dynamic-slice_bitcast_fusion.spot_ref = s32[8,128]{1,0:T(8,128)S(1)} fusion(s32[2,2,8,128]{3,2,1,0:T(8,128)} %constant.24.clone, s32[]{:T(128)S(6)} %select_n.14, s32[]{:T(128)S(6)} %select_n.15), kind=kLoop, calls=%fused_computation | loop fusion | bytes 8200 | tf_op jit(solution)/shard_map/squeeze | solution.py:307
  9.4 0.0 collective-permute-done.sibling
  9.4 7.9 %own_chains.1.home = f32[64,128]{1,0:T(8,128)S(1)} custom-call(s32[1]{0:T(128)} %bitcast.side_ref, f32[27,32,128]{2,1,0:T(8,128)S(1)} %get-tuple-element.15.own, f32[27,32,128]{2,1,0:T(8,128)S(1)} %collective-permute-done.sibling), custom_call_target="tpu_custom_call" | custom-call | tf_op jit(solution)/shard_map/own_chains/pallas_call | solution.py:278
  17.3 0.0 collective-permute-done.3.second
  17.3 0.1 collective-permute-start.5
  17.4 4.5 %collective-permute-start.2 = (f32[10,32,128]{2,1,0:T(8,128)S(1)}, f32[10,32,128]{2,1,0:T(8,128)S(1)}, u32[]{:S(2)}, u32[]{:S(2)}) collective-permute-start(f32[10,32,128]{2,1,0:T(8,128)S(1)} %get-tuple-element.17), channel_id=1, source_target_pairs={{30,0},{8,2},{2,4},{12,6},{6,8},{16,10},{10,12},{20,14},{14,16},{2... | collective-permute-start | bytes 491528 | tf_op jit(solution)/shard_map/ppermute | solution.py:25
  21.9 0.0 collective-permute-start.1
  21.9 0.0 collective-permute-done.4.first
  21.9 0.0 collective-permute-done.5.other
  22.0 6.0 %half_chains.2.rest_0_ = f32[320,128]{1,0:T(8,128)S(1)} custom-call(s32[1]{0:T(128)} %bitcast.side_ref, f32[27,32,128]{2,1,0:T(8,128)S(1)} %get-tuple-element.15.own, f32[27,32,128]{2,1,0:T(8,128)S(1)} %collective-permute-done.sibling, f32[17,32,128]{2,1,0:T(8,128)S(1)} %collective-permute-done.4.first, f32[17,32,128]{2,1,0:T(8,128)S(1)} %collective-permute-done.3.second, ...), custom_call_target="tpu_custom_call" | custom-call | tf_op jit(solution)/shard_map/half_chains/pallas_call | solution.py:278
  27.9 0.0 collective-permute-done.2.second
  27.9 0.2 collective-permute-start.6
  28.2 1.8 %collective-permute-done.1.first = f32[10,32,128]{2,1,0:T(8,128)S(1)} collective-permute-done((f32[10,32,128]{2,1,0:T(8,128)S(1)}, f32[10,32,128]{2,1,0:T(8,128)S(1)}, u32[]{:S(2)}, u32[]{:S(2)}) %collective-permute-start.1) | collective-permute-done | bytes 163872 | tf_op jit(solution)/shard_map/ppermute | solution.py:25
  30.0 0.0 collective-permute-done.6.other
  30.0 3.5 %half_chains.3.mine = f32[288,128]{1,0:T(8,128)S(1)} custom-call(s32[1]{0:T(128)} %bitcast.side_ref, f32[27,32,128]{2,1,0:T(8,128)S(1)} %get-tuple-element.15.own, f32[27,32,128]{2,1,0:T(8,128)S(1)} %collective-permute-done.sibling, f32[10,32,128]{2,1,0:T(8,128)S(1)} %collective-permute-done.1.first, f32[10,32,128]{2,1,0:T(8,128)S(1)} %collective-permute-done.2.second, ...), custom_call_target="tpu_custom_call" | custom-call | tf_op jit(solution)/shard_map/half_chains/pallas_call | solution.py:278
  33.4 2.0 %collective-permute-start.7 = (f32[288,128]{1,0:T(8,128)S(1)}, f32[288,128]{1,0:T(8,128)S(1)}, u32[]{:S(2)}, u32[]{:S(2)}) collective-permute-start(f32[288,128]{1,0:T(8,128)S(1)} %half_chains.3.mine), channel_id=1, source_target_pairs={{0,1},{1,0},{2,3},{3,2},{4,5},{5,4},{6,7},{7,6},{8,9},{9,8},{10,11... | collective-permute-start | bytes 442376 | tf_op jit(solution)/shard_map/ppermute | solution.py:317
  35.4 3.6 %collective-permute-done.7.theirs = f32[288,128]{1,0:T(8,128)S(1)} collective-permute-done((f32[288,128]{1,0:T(8,128)S(1)}, f32[288,128]{1,0:T(8,128)S(1)}, u32[]{:S(2)}, u32[]{:S(2)}) %collective-permute-start.7) | collective-permute-done | bytes 147488 | tf_op jit(solution)/shard_map/ppermute | solution.py:317
  39.0 0.2 meet.1.mine
  39.2 0.0 collective-permute-start.8
  39.2 1.2 %collective-permute-done.8.theirs = f32[8,128]{1,0:T(8,128)S(1)} collective-permute-done((f32[8,128]{1,0:T(8,128)S(1)}, f32[8,128]{1,0:T(8,128)S(1)}, u32[]{:S(2)}, u32[]{:S(2)}) %collective-permute-start.8) | collective-permute-done | bytes 4128 | tf_op jit(solution)/shard_map/ppermute | solution.py:25
  40.4 0.1 join.1.here
  40.4 0.0 collective-permute-start.10
  40.4 4.5 %collective-permute-start.9 = (f32[8,128]{1,0:T(8,128)S(1)}, f32[8,128]{1,0:T(8,128)S(1)}, u32[]{:S(2)}, u32[]{:S(2)}) collective-permute-start(f32[8,128]{1,0:T(8,128)S(1)} %join.1.here), channel_id=1, source_target_pairs={{4,0},{6,2},{8,4},{10,6},{12,8},{14,10},{16,12},{18,14},{20,16},{2... | collective-permute-start | bytes 12296 | tf_op jit(solution)/shard_map/ppermute | solution.py:25
  45.0 1.2 %collective-permute-done.10.before = f32[8,128]{1,0:T(8,128)S(1)} collective-permute-done((f32[8,128]{1,0:T(8,128)S(1)}, f32[8,128]{1,0:T(8,128)S(1)}, u32[]{:S(2)}, u32[]{:S(2)}) %collective-permute-start.10) | collective-permute-done | bytes 4128 | tf_op jit(solution)/shard_map/ppermute | solution.py:25
  46.2 0.2 collective-permute-done.9.after
  46.3 0.8 %pick.1 = f32[1,26]{1,0:T(1,128)} custom-call(s32[8,128]{1,0:T(8,128)S(1)} %dynamic-slice_bitcast_fusion.spot_ref, f32[8,128]{1,0:T(8,128)S(1)} %join.1.here, f32[8,128]{1,0:T(8,128)S(1)} %collective-permute-done.9.after, f32[8,128]{1,0:T(8,128)S(1)} %collective-permute-done.10.before), custom_call_target="tpu_custom_call" | custom-call | tf_op jit(solution)/shard_map/pick/pallas_call | solution.py:278
Async XLA Ops:
  0.0 1.0 %copy-start = (f32[32,32,128]{2,1,0:T(8,128)S(1)}, f32[32,32,128]{2,1,0:T(8,128)}, u32[]{:S(2)}) copy-start(f32[32,32,128]{2,1,0:T(8,128)} %sites_ref.1) | copy-start | bytes 1572868
  2.0 7.4 %collective-permute-start = (f32[27,32,128]{2,1,0:T(8,128)S(1)}, f32[27,32,128]{2,1,0:T(8,128)S(1)}, u32[]{:S(2)}, u32[]{:S(2)}) collective-permute-start(f32[27,32,128]{2,1,0:T(8,128)S(1)} %get-tuple-element.15.own), channel_id=1, source_target_pairs={{2,0},{0,2},{6,4},{4,6},{10,8},{8,10},{14,12},{12,14},{18,16},{16,... | collective-permute-start | bytes 1327112 | tf_op jit(solution)/shard_map/ppermute | solution.py:25
  2.5 14.8 %collective-permute-start.3 = (f32[17,32,128]{2,1,0:T(8,128)S(1)}, f32[17,32,128]{2,1,0:T(8,128)S(1)}, u32[]{:S(2)}, u32[]{:S(2)}) collective-permute-start(f32[17,32,128]{2,1,0:T(8,128)S(1)} %get-tuple-element.18), channel_id=1, source_target_pairs={{30,0},{8,2},{2,4},{12,6},{6,8},{16,10},{10,12},{20,14},{14,16},{2... | collective-permute-start | bytes 835592 | tf_op jit(solution)/shard_map/ppermute | solution.py:25
  7.2 14.7 %collective-permute-start.4 = (f32[17,32,128]{2,1,0:T(8,128)S(1)}, f32[17,32,128]{2,1,0:T(8,128)S(1)}, u32[]{:S(2)}, u32[]{:S(2)}) collective-permute-start(f32[17,32,128]{2,1,0:T(8,128)S(1)} %get-tuple-element.18), channel_id=1, source_target_pairs={{28,0},{10,2},{0,4},{14,6},{4,8},{18,10},{8,12},{22,14},{12,16},{2... | collective-permute-start | bytes 835592 | tf_op jit(solution)/shard_map/ppermute | solution.py:25
  17.3 4.6 %collective-permute-start.5 = (f32[17,32,128]{2,1,0:T(8,128)S(1)}, f32[17,32,128]{2,1,0:T(8,128)S(1)}, u32[]{:S(2)}, u32[]{:S(2)}) collective-permute-start(f32[17,32,128]{2,1,0:T(8,128)S(1)} %collective-permute-done.3.second), channel_id=1, source_target_pairs={{2,0},{0,2},{6,4},{4,6},{10,8},{8,10},{14,12},{12,14},{18,16},{16,... | collective-permute-start | bytes 835592 | tf_op jit(solution)/shard_map/ppermute | solution.py:25
  17.4 10.5 %collective-permute-start.2 = (f32[10,32,128]{2,1,0:T(8,128)S(1)}, f32[10,32,128]{2,1,0:T(8,128)S(1)}, u32[]{:S(2)}, u32[]{:S(2)}) collective-permute-start(f32[10,32,128]{2,1,0:T(8,128)S(1)} %get-tuple-element.17), channel_id=1, source_target_pairs={{30,0},{8,2},{2,4},{12,6},{6,8},{16,10},{10,12},{20,14},{14,16},{2... | collective-permute-start | bytes 491528 | tf_op jit(solution)/shard_map/ppermute | solution.py:25
  21.9 8.0 %collective-permute-start.1 = (f32[10,32,128]{2,1,0:T(8,128)S(1)}, f32[10,32,128]{2,1,0:T(8,128)S(1)}, u32[]{:S(2)}, u32[]{:S(2)}) collective-permute-start(f32[10,32,128]{2,1,0:T(8,128)S(1)} %get-tuple-element.17), channel_id=1, source_target_pairs={{28,0},{10,2},{0,4},{14,6},{4,8},{18,10},{8,12},{22,14},{12,16},{2... | collective-permute-start | bytes 491528 | tf_op jit(solution)/shard_map/ppermute | solution.py:25
  27.9 2.0 %collective-permute-start.6 = (f32[10,32,128]{2,1,0:T(8,128)S(1)}, f32[10,32,128]{2,1,0:T(8,128)S(1)}, u32[]{:S(2)}, u32[]{:S(2)}) collective-permute-start(f32[10,32,128]{2,1,0:T(8,128)S(1)} %collective-permute-done.2.second), channel_id=1, source_target_pairs={{2,0},{0,2},{6,4},{4,6},{10,8},{8,10},{14,12},{12,14},{18,16},{16,... | collective-permute-start | bytes 491528 | tf_op jit(solution)/shard_map/ppermute | solution.py:25
  33.4 5.6 %collective-permute-start.7 = (f32[288,128]{1,0:T(8,128)S(1)}, f32[288,128]{1,0:T(8,128)S(1)}, u32[]{:S(2)}, u32[]{:S(2)}) collective-permute-start(f32[288,128]{1,0:T(8,128)S(1)} %half_chains.3.mine), channel_id=1, source_target_pairs={{0,1},{1,0},{2,3},{3,2},{4,5},{5,4},{6,7},{7,6},{8,9},{9,8},{10,11... | collective-permute-start | bytes 442376 | tf_op jit(solution)/shard_map/ppermute | solution.py:317
  39.2 1.2 %collective-permute-start.8 = (f32[8,128]{1,0:T(8,128)S(1)}, f32[8,128]{1,0:T(8,128)S(1)}, u32[]{:S(2)}, u32[]{:S(2)}) collective-permute-start(f32[8,128]{1,0:T(8,128)S(1)} %meet.1.mine), channel_id=1, source_target_pairs={{2,0},{0,2},{6,4},{4,6},{10,8},{8,10},{14,12},{12,14},{18,16},{16,... | collective-permute-start | bytes 12296 | tf_op jit(solution)/shard_map/ppermute | solution.py:25
  40.4 5.7 %collective-permute-start.10 = (f32[8,128]{1,0:T(8,128)S(1)}, f32[8,128]{1,0:T(8,128)S(1)}, u32[]{:S(2)}, u32[]{:S(2)}) collective-permute-start(f32[8,128]{1,0:T(8,128)S(1)} %join.1.here), channel_id=1, source_target_pairs={{24,0},{26,2},{28,4},{30,6},{0,8},{2,10},{4,12},{6,14},{8,16},{10,... | collective-permute-start | bytes 12296 | tf_op jit(solution)/shard_map/ppermute | solution.py:25
  40.4 5.9 %collective-permute-start.9 = (f32[8,128]{1,0:T(8,128)S(1)}, f32[8,128]{1,0:T(8,128)S(1)}, u32[]{:S(2)}, u32[]{:S(2)}) collective-permute-start(f32[8,128]{1,0:T(8,128)S(1)} %join.1.here), channel_id=1, source_target_pairs={{4,0},{6,2},{8,4},{10,6},{12,8},{14,10},{16,12},{18,14},{20,16},{2... | collective-permute-start | bytes 12296 | tf_op jit(solution)/shard_map/ppermute | solution.py:25

commit v12 on v11

--- a/solution.py
+++ b/solution.py
@@ -170,7 +170,7 @@
 
     def run(flip):
         state = rest[0][...] if start else identities(320)
-        cuts = (0, 4, 7, 10)
+        cuts = (0, 10)
         groups = [state[32 * a : 32 * b] for a, b in zip(cuts, cuts[1:])]
         for index in range(count):
             whole = start + index

time: 47.3 us -> 49.9 us (1.055)
  Pallas kernels: 19.4 us -> 22 us
    pallas_call x7, Pallas kernels: 19.4 us -> 22 us  [call(): pl.pallas_call(kernel, out_shape=shapes if many else shapes[0], in_specs=...]
    ppermute x1, waiting for transfers between devices: 3.64 us -> 4.16 us  [body(): partner = lax.ppermute(state, 'pair', [(0, 1), (1, 0)])]
  transfers between devices with their start and end apart: 11 -> 11, of which waited for: 5 -> 6; matrix products, arithmetic and copies ran while one was open for 1% -> 1% of each run, Pallas kernels for 29% -> 31%
where the time goes in v12:
time: 49.9 us; the launch traced here: 49.7 us
  Pallas kernels  22 us (44%)
  starting transfers between devices  17.9 us (36%)
  waiting for transfers between devices  8.05 us (16%)
  local copies, waits for them, and re-layouts  1.73 us (3%)
    pallas_call x7, Pallas kernels, call(): pl.pallas_call(kernel, out_shape=shapes if many else shapes[0], in_specs=...  22 us
    ppermute x10, starting transfers between devices, move(): return lax.ppermute(array, 'blk', pairs)  15.9 us
    ppermute x1, waiting for transfers between devices, body(): partner = lax.ppermute(state, 'pair', [(0, 1), (1, 0)])  4.16 us
    ppermute x10, waiting for transfers between devices, move(): return lax.ppermute(array, 'blk', pairs)  3.89 us
    ppermute x1, starting transfers between devices, body(): partner = lax.ppermute(state, 'pair', [(0, 1), (1, 0)])  2.07 us
    unnamed x2, local copies, waits for them, and re-layouts  1.04 us
  transfers between devices with their start and end apart: 11, of which 6 were waited for; matrix products, arithmetic and copies ran while one was open for 1% of the time, Pallas kernels for 31%

profile of v12, /device:TPU:0, one launch (start us, length us, event | category | flops | bytes accessed | tf_op | source)
XLA Modules:
  0.0 49.7 jit_solution(9111968454750064158)
XLA Ops:
  0.0 0.0 copy-start
  0.0 1.0 %copy-done = f32[32,32,128]{2,1,0:T(8,128)S(1)} copy-done((f32[32,32,128]{2,1,0:T(8,128)S(1)}, f32[32,32,128]{2,1,0:T(8,128)}, u32[]{:S(2)}) %copy-start) | copy-done | bytes 524312
  1.0 1.0 %order.1 = (f32[27,32,128]{2,1,0:T(8,128)S(1)}, f32[17,32,128]{2,1,0:T(8,128)S(1)}, f32[10,32,128]{2,1,0:T(8,128)S(1)}) custom-call(s32[1]{0:T(128)} %bitcast.side_ref, f32[32,32,128]{2,1,0:T(8,128)S(1)} %copy-done), custom_call_target="tpu_custom_call" | custom-call | tf_op jit(solution)/shard_map/order/pallas_call | solution.py:278
  2.0 0.5 collective-permute-start
  2.5 4.7 %collective-permute-start.3 = (f32[17,32,128]{2,1,0:T(8,128)S(1)}, f32[17,32,128]{2,1,0:T(8,128)S(1)}, u32[]{:S(2)}, u32[]{:S(2)}) collective-permute-start(f32[17,32,128]{2,1,0:T(8,128)S(1)} %get-tuple-element.18), channel_id=1, source_target_pairs={{30,0},{8,2},{2,4},{12,6},{6,8},{16,10},{10,12},{20,14},{14,16},{2... | collective-permute-start | bytes 835592 | tf_op jit(solution)/shard_map/ppermute | solution.py:25
  7.2 1.5 %collective-permute-start.4 = (f32[17,32,128]{2,1,0:T(8,128)S(1)}, f32[17,32,128]{2,1,0:T(8,128)S(1)}, u32[]{:S(2)}, u32[]{:S(2)}) collective-permute-start(f32[17,32,128]{2,1,0:T(8,128)S(1)} %get-tuple-element.18), channel_id=1, source_target_pairs={{28,0},{10,2},{0,4},{14,6},{4,8},{18,10},{8,12},{22,14},{12,16},{2... | collective-permute-start | bytes 835592 | tf_op jit(solution)/shard_map/ppermute | solution.py:25
  8.7 0.7 %dynamic-slice_bitcast_fusion.spot_ref = s32[8,128]{1,0:T(8,128)S(1)} fusion(s32[2,2,8,128]{3,2,1,0:T(8,128)} %constant.24.clone, s32[]{:T(128)S(6)} %select_n.14, s32[]{:T(128)S(6)} %select_n.15), kind=kLoop, calls=%fused_computation | loop fusion | bytes 8200 | tf_op jit(solution)/shard_map/squeeze | solution.py:307
  9.4 0.0 collective-permute-done.sibling
  9.4 7.9 %own_chains.1.home = f32[64,128]{1,0:T(8,128)S(1)} custom-call(s32[1]{0:T(128)} %bitcast.side_ref, f32[27,32,128]{2,1,0:T(8,128)S(1)} %get-tuple-element.15.own, f32[27,32,128]{2,1,0:T(8,128)S(1)} %collective-permute-done.sibling), custom_call_target="tpu_custom_call" | custom-call | tf_op jit(solution)/shard_map/own_chains/pallas_call | solution.py:278
  17.3 0.0 collective-permute-done.3.second
  17.3 0.1 collective-permute-start.5
  17.4 4.5 %collective-permute-start.2 = (f32[10,32,128]{2,1,0:T(8,128)S(1)}, f32[10,32,128]{2,1,0:T(8,128)S(1)}, u32[]{:S(2)}, u32[]{:S(2)}) collective-permute-start(f32[10,32,128]{2,1,0:T(8,128)S(1)} %get-tuple-element.17), channel_id=1, source_target_pairs={{30,0},{8,2},{2,4},{12,6},{6,8},{16,10},{10,12},{20,14},{14,16},{2... | collective-permute-start | bytes 491528 | tf_op jit(solution)/shard_map/ppermute | solution.py:25
  21.9 0.0 collective-permute-start.1
  21.9 0.0 collective-permute-done.4.first
  21.9 0.0 collective-permute-done.5.other
  22.0 7.6 %half_chains.2.rest_0_ = f32[320,128]{1,0:T(8,128)S(1)} custom-call(s32[1]{0:T(128)} %bitcast.side_ref, f32[27,32,128]{2,1,0:T(8,128)S(1)} %get-tuple-element.15.own, f32[27,32,128]{2,1,0:T(8,128)S(1)} %collective-permute-done.sibling, f32[17,32,128]{2,1,0:T(8,128)S(1)} %collective-permute-done.4.first, f32[17,32,128]{2,1,0:T(8,128)S(1)} %collective-permute-done.3.second, ...), custom_call_target="tpu_custom_call" | custom-call | tf_op jit(solution)/shard_map/half_chains/pallas_call | solution.py:278
  29.5 0.0 collective-permute-done.2.second
  29.5 0.1 collective-permute-start.6
  29.6 0.4 collective-permute-done.1.first
  30.0 1.0 %collective-permute-done.6.other = f32[10,32,128]{2,1,0:T(8,128)S(1)} collective-permute-done((f32[10,32,128]{2,1,0:T(8,128)S(1)}, f32[10,32,128]{2,1,0:T(8,128)S(1)}, u32[]{:S(2)}, u32[]{:S(2)}) %collective-permute-start.6) | collective-permute-done | bytes 163872 | tf_op jit(solution)/shard_map/ppermute | solution.py:25
  31.0 4.4 %half_chains.3.mine = f32[288,128]{1,0:T(8,128)S(1)} custom-call(s32[1]{0:T(128)} %bitcast.side_ref, f32[27,32,128]{2,1,0:T(8,128)S(1)} %get-tuple-element.15.own, f32[27,32,128]{2,1,0:T(8,128)S(1)} %collective-permute-done.sibling, f32[10,32,128]{2,1,0:T(8,128)S(1)} %collective-permute-done.1.first, f32[10,32,128]{2,1,0:T(8,128)S(1)} %collective-permute-done.2.second, ...), custom_call_target="tpu_custom_call" | custom-call | tf_op jit(solution)/shard_map/half_chains/pallas_call | solution.py:278
  35.4 2.1 %collective-permute-start.7 = (f32[288,128]{1,0:T(8,128)S(1)}, f32[288,128]{1,0:T(8,128)S(1)}, u32[]{:S(2)}, u32[]{:S(2)}) collective-permute-start(f32[288,128]{1,0:T(8,128)S(1)} %half_chains.3.mine), channel_id=1, source_target_pairs={{0,1},{1,0},{2,3},{3,2},{4,5},{5,4},{6,7},{7,6},{8,9},{9,8},{10,11... | collective-permute-start | bytes 442376 | tf_op jit(solution)/shard_map/ppermute | solution.py:317
  37.4 4.2 %collective-permute-done.7.theirs = f32[288,128]{1,0:T(8,128)S(1)} collective-permute-done((f32[288,128]{1,0:T(8,128)S(1)}, f32[288,128]{1,0:T(8,128)S(1)}, u32[]{:S(2)}, u32[]{:S(2)}) %collective-permute-start.7) | collective-permute-done | bytes 147488 | tf_op jit(solution)/shard_map/ppermute | solution.py:317
  41.6 0.2 meet.1.mine
  41.8 0.0 collective-permute-start.8
  41.8 1.2 %collective-permute-done.8.theirs = f32[8,128]{1,0:T(8,128)S(1)} collective-permute-done((f32[8,128]{1,0:T(8,128)S(1)}, f32[8,128]{1,0:T(8,128)S(1)}, u32[]{:S(2)}, u32[]{:S(2)}) %collective-permute-start.8) | collective-permute-done | bytes 4128 | tf_op jit(solution)/shard_map/ppermute | solution.py:25
  42.9 0.1 join.1.here
  43.0 0.0 collective-permute-start.10
  43.0 4.5 %collective-permute-start.9 = (f32[8,128]{1,0:T(8,128)S(1)}, f32[8,128]{1,0:T(8,128)S(1)}, u32[]{:S(2)}, u32[]{:S(2)}) collective-permute-start(f32[8,128]{1,0:T(8,128)S(1)} %join.1.here), channel_id=1, source_target_pairs={{4,0},{6,2},{8,4},{10,6},{12,8},{14,10},{16,12},{18,14},{20,16},{2... | collective-permute-start | bytes 12296 | tf_op jit(solution)/shard_map/ppermute | solution.py:25
  47.5 0.9 %collective-permute-done.10.before = f32[8,128]{1,0:T(8,128)S(1)} collective-permute-done((f32[8,128]{1,0:T(8,128)S(1)}, f32[8,128]{1,0:T(8,128)S(1)}, u32[]{:S(2)}, u32[]{:S(2)}) %collective-permute-start.10) | collective-permute-done | bytes 4128 | tf_op jit(solution)/shard_map/ppermute | solution.py:25
  48.4 0.5 collective-permute-done.9.after
  48.9 0.8 %pick.1 = f32[1,26]{1,0:T(1,128)} custom-call(s32[8,128]{1,0:T(8,128)S(1)} %dynamic-slice_bitcast_fusion.spot_ref, f32[8,128]{1,0:T(8,128)S(1)} %join.1.here, f32[8,128]{1,0:T(8,128)S(1)} %collective-permute-done.9.after, f32[8,128]{1,0:T(8,128)S(1)} %collective-permute-done.10.before), custom_call_target="tpu_custom_call" | custom-call | tf_op jit(solution)/shard_map/pick/pallas_call | solution.py:278
Async XLA Ops:
  0.0 1.0 %copy-start = (f32[32,32,128]{2,1,0:T(8,128)S(1)}, f32[32,32,128]{2,1,0:T(8,128)}, u32[]{:S(2)}) copy-start(f32[32,32,128]{2,1,0:T(8,128)} %sites_ref.1) | copy-start | bytes 1572868
  2.0 7.4 %collective-permute-start = (f32[27,32,128]{2,1,0:T(8,128)S(1)}, f32[27,32,128]{2,1,0:T(8,128)S(1)}, u32[]{:S(2)}, u32[]{:S(2)}) collective-permute-start(f32[27,32,128]{2,1,0:T(8,128)S(1)} %get-tuple-element.15.own), channel_id=1, source_target_pairs={{2,0},{0,2},{6,4},{4,6},{10,8},{8,10},{14,12},{12,14},{18,16},{16,... | collective-permute-start | bytes 1327112 | tf_op jit(solution)/shard_map/ppermute | solution.py:25
  2.5 14.8 %collective-permute-start.3 = (f32[17,32,128]{2,1,0:T(8,128)S(1)}, f32[17,32,128]{2,1,0:T(8,128)S(1)}, u32[]{:S(2)}, u32[]{:S(2)}) collective-permute-start(f32[17,32,128]{2,1,0:T(8,128)S(1)} %get-tuple-element.18), channel_id=1, source_target_pairs={{30,0},{8,2},{2,4},{12,6},{6,8},{16,10},{10,12},{20,14},{14,16},{2... | collective-permute-start | bytes 835592 | tf_op jit(solution)/shard_map/ppermute | solution.py:25
  7.2 14.7 %collective-permute-start.4 = (f32[17,32,128]{2,1,0:T(8,128)S(1)}, f32[17,32,128]{2,1,0:T(8,128)S(1)}, u32[]{:S(2)}, u32[]{:S(2)}) collective-permute-start(f32[17,32,128]{2,1,0:T(8,128)S(1)} %get-tuple-element.18), channel_id=1, source_target_pairs={{28,0},{10,2},{0,4},{14,6},{4,8},{18,10},{8,12},{22,14},{12,16},{2... | collective-permute-start | bytes 835592 | tf_op jit(solution)/shard_map/ppermute | solution.py:25
  17.3 4.6 %collective-permute-start.5 = (f32[17,32,128]{2,1,0:T(8,128)S(1)}, f32[17,32,128]{2,1,0:T(8,128)S(1)}, u32[]{:S(2)}, u32[]{:S(2)}) collective-permute-start(f32[17,32,128]{2,1,0:T(8,128)S(1)} %collective-permute-done.3.second), channel_id=1, source_target_pairs={{2,0},{0,2},{6,4},{4,6},{10,8},{8,10},{14,12},{12,14},{18,16},{16,... | collective-permute-start | bytes 835592 | tf_op jit(solution)/shard_map/ppermute | solution.py:25
  17.4 12.1 %collective-permute-start.2 = (f32[10,32,128]{2,1,0:T(8,128)S(1)}, f32[10,32,128]{2,1,0:T(8,128)S(1)}, u32[]{:S(2)}, u32[]{:S(2)}) collective-permute-start(f32[10,32,128]{2,1,0:T(8,128)S(1)} %get-tuple-element.17), channel_id=1, source_target_pairs={{30,0},{8,2},{2,4},{12,6},{6,8},{16,10},{10,12},{20,14},{14,16},{2... | collective-permute-start | bytes 491528 | tf_op jit(solution)/shard_map/ppermute | solution.py:25
  21.9 8.0 %collective-permute-start.1 = (f32[10,32,128]{2,1,0:T(8,128)S(1)}, f32[10,32,128]{2,1,0:T(8,128)S(1)}, u32[]{:S(2)}, u32[]{:S(2)}) collective-permute-start(f32[10,32,128]{2,1,0:T(8,128)S(1)} %get-tuple-element.17), channel_id=1, source_target_pairs={{28,0},{10,2},{0,4},{14,6},{4,8},{18,10},{8,12},{22,14},{12,16},{2... | collective-permute-start | bytes 491528 | tf_op jit(solution)/shard_map/ppermute | solution.py:25
  29.5 1.4 %collective-permute-start.6 = (f32[10,32,128]{2,1,0:T(8,128)S(1)}, f32[10,32,128]{2,1,0:T(8,128)S(1)}, u32[]{:S(2)}, u32[]{:S(2)}) collective-permute-start(f32[10,32,128]{2,1,0:T(8,128)S(1)} %collective-permute-done.2.second), channel_id=1, source_target_pairs={{2,0},{0,2},{6,4},{4,6},{10,8},{8,10},{14,12},{12,14},{18,16},{16,... | collective-permute-start | bytes 491528 | tf_op jit(solution)/shard_map/ppermute | solution.py:25
  35.4 6.2 %collective-permute-start.7 = (f32[288,128]{1,0:T(8,128)S(1)}, f32[288,128]{1,0:T(8,128)S(1)}, u32[]{:S(2)}, u32[]{:S(2)}) collective-permute-start(f32[288,128]{1,0:T(8,128)S(1)} %half_chains.3.mine), channel_id=1, source_target_pairs={{0,1},{1,0},{2,3},{3,2},{4,5},{5,4},{6,7},{7,6},{8,9},{9,8},{10,11... | collective-permute-start | bytes 442376 | tf_op jit(solution)/shard_map/ppermute | solution.py:317
  41.8 1.2 %collective-permute-start.8 = (f32[8,128]{1,0:T(8,128)S(1)}, f32[8,128]{1,0:T(8,128)S(1)}, u32[]{:S(2)}, u32[]{:S(2)}) collective-permute-start(f32[8,128]{1,0:T(8,128)S(1)} %meet.1.mine), channel_id=1, source_target_pairs={{2,0},{0,2},{6,4},{4,6},{10,8},{8,10},{14,12},{12,14},{18,16},{16,... | collective-permute-start | bytes 12296 | tf_op jit(solution)/shard_map/ppermute | solution.py:25
  43.0 5.4 %collective-permute-start.10 = (f32[8,128]{1,0:T(8,128)S(1)}, f32[8,128]{1,0:T(8,128)S(1)}, u32[]{:S(2)}, u32[]{:S(2)}) collective-permute-start(f32[8,128]{1,0:T(8,128)S(1)} %join.1.here), channel_id=1, source_target_pairs={{24,0},{26,2},{28,4},{30,6},{0,8},{2,10},{4,12},{6,14},{8,16},{10,... | collective-permute-start | bytes 12296 | tf_op jit(solution)/shard_map/ppermute | solution.py:25
  43.0 5.9 %collective-permute-start.9 = (f32[8,128]{1,0:T(8,128)S(1)}, f32[8,128]{1,0:T(8,128)S(1)}, u32[]{:S(2)}, u32[]{:S(2)}) collective-permute-start(f32[8,128]{1,0:T(8,128)S(1)} %join.1.here), channel_id=1, source_target_pairs={{4,0},{6,2},{8,4},{10,6},{12,8},{14,10},{16,12},{18,14},{20,16},{2... | collective-permute-start | bytes 12296 | tf_op jit(solution)/shard_map/ppermute | solution.py:25

commit v13 on v12

--- a/solution.py
+++ b/solution.py
@@ -144,12 +144,19 @@
     on_each_side(side_ref, run)
 
 
-def norms_only(state):
-    slot = lane_slot((32, 128))
-    first = jnp.where(slot == 0, state[192:224], state[224:256])
-    second = jnp.where(slot == 1, state[256:288], state[288:320])
-    kept = jnp.where(slot % 2 == 0, first, second)
-    return jnp.concatenate([state[:192], kept], 0)
+def gather_alone(inner, near):
+    h0, l0, h1, l1 = inner
+    slot = lane_slot(h0.shape)
+    zero = jnp.zeros_like(h0)
+    high_weights, low_weights = [
+        jnp.concatenate([jnp.where(slot == k, half, zero) for k in range(4) for half in halves], 0)
+        for halves in ((h0, h1), (l0, l1))
+    ]
+    lower = lane_slot(near[0].shape) < 2
+    tensors = [jnp.where(lower, near[a], near[b]) for a, b in ((0, 2), (1, 3))]
+    high, low = split(jnp.concatenate(tensors, 1))
+    both = product(jnp.concatenate([high, low], 0), high_weights)
+    return both[:32] + both[32:] + product(high, low_weights)
 
 
 def home_kernel(side_ref, own, sibling, out):
@@ -169,9 +176,8 @@
     count = first.shape[0]
 
     def run(flip):
-        state = rest[0][...] if start else identities(320)
-        cuts = (0, 10)
-        groups = [state[32 * a : 32 * b] for a, b in zip(cuts, cuts[1:])]
+        state = rest[0][...] if start else identities(224)
+        groups = [state[:128], state[128:]]
         for index in range(count):
             whole = start + index
             far = interleave(first[index], second[index])
@@ -186,11 +192,13 @@
                     + near_turned(far)
                 )
             weights = far_weights(far, flip)
-            inner = [spread(g, weights) for g in groups]
-            groups = [gather(i, near[a:b]) for i, a, b in zip(inner, cuts, cuts[1:])]
-        state = jnp.concatenate(groups, 0)
+            pairs, rest_pairs = [spread(g, weights) for g in groups]
+            pairs = gather(pairs, near[:4])
+            others = gather([part[:64] for part in rest_pairs], near[4:6])
+            alone = gather_alone([part[64:] for part in rest_pairs], near[6:])
+            groups = [pairs, jnp.concatenate([others, alone], 0)]
         last = start + count == own.shape[0]
-        out[...] = jnp.concatenate([norms_only(state), home[...]], 0) if last else state
+        out[...] = jnp.concatenate(groups + [home[...]] if last else groups, 0)
 
     on_each_side(side_ref, run)
 
@@ -310,7 +318,7 @@
     for start, first, second in zip(starts, firsts, seconds):
         second, *carried = lax.optimization_barrier((second, *carried))
         other = move(second, across)
-        rows = 288 if start == starts[-1] else 320
+        rows = 288 if start == starts[-1] else 224
         state = call(functools.partial(chain_kernel, start), (rows, 128), flag, mps, sibling, first, second, other,
                      *carried, name="half_chains")
         carried = (carried[0], state)

time: 49.9 us -> 46.9 us (0.940)
  Pallas kernels: 22 us -> 18.7 us
    pallas_call x7, Pallas kernels: 22 us -> 18.7 us  [call(): pl.pallas_call(kernel, out_shape=shapes if many else shapes[0], in_specs=...]
    ppermute x10, waiting for transfers between devices: 3.89 us -> 5.09 us  [move(): return lax.ppermute(array, 'blk', pairs)]
    ppermute x1, waiting for transfers between devices: 4.16 us -> 3.25 us  [body(): partner = lax.ppermute(state, 'pair', [(0, 1), (1, 0)])]
  transfers between devices with their start and end apart: 11 -> 11, of which waited for: 6 -> 4; matrix products, arithmetic and copies ran while one was open for 1% -> 1% of each run, Pallas kernels for 31% -> 29%
where the time goes in v13:
time: 46.9 us; the launch traced here: 46.7 us
  Pallas kernels  18.7 us (40%)
  starting transfers between devices  17.9 us (38%)
  waiting for transfers between devices  8.34 us (18%)
  local copies, waits for them, and re-layouts  1.73 us (4%)
    pallas_call x7, Pallas kernels, call(): pl.pallas_call(kernel, out_shape=shapes if many else shapes[0], in_specs=...  18.7 us
    ppermute x10, starting transfers between devices, move(): return lax.ppermute(array, 'blk', pairs)  15.9 us
    ppermute x10, waiting for transfers between devices, move(): return lax.ppermute(array, 'blk', pairs)  5.09 us
    ppermute x1, waiting for transfers between devices, body(): partner = lax.ppermute(state, 'pair', [(0, 1), (1, 0)])  3.25 us
    ppermute x1, starting transfers between devices, body(): partner = lax.ppermute(state, 'pair', [(0, 1), (1, 0)])  1.96 us
    unnamed x2, local copies, waits for them, and re-layouts  1.04 us
  transfers between devices with their start and end apart: 11, of which 4 were waited for; matrix products, arithmetic and copies ran while one was open for 1% of the time, Pallas kernels for 29%

profile of v13, /device:TPU:0, one launch (start us, length us, event | category | flops | bytes accessed | tf_op | source)
XLA Modules:
  0.0 46.7 jit_solution(13391158539507046685)
XLA Ops:
  0.0 0.0 copy-start
  0.0 1.0 %copy-done = f32[32,32,128]{2,1,0:T(8,128)S(1)} copy-done((f32[32,32,128]{2,1,0:T(8,128)S(1)}, f32[32,32,128]{2,1,0:T(8,128)}, u32[]{:S(2)}) %copy-start) | copy-done | bytes 524312
  1.0 1.0 %order.1 = (f32[27,32,128]{2,1,0:T(8,128)S(1)}, f32[17,32,128]{2,1,0:T(8,128)S(1)}, f32[10,32,128]{2,1,0:T(8,128)S(1)}) custom-call(s32[1]{0:T(128)} %bitcast.side_ref, f32[32,32,128]{2,1,0:T(8,128)S(1)} %copy-done), custom_call_target="tpu_custom_call" | custom-call | tf_op jit(solution)/shard_map/order/pallas_call | solution.py:286
  2.0 0.5 collective-permute-start
  2.5 4.7 %collective-permute-start.3 = (f32[17,32,128]{2,1,0:T(8,128)S(1)}, f32[17,32,128]{2,1,0:T(8,128)S(1)}, u32[]{:S(2)}, u32[]{:S(2)}) collective-permute-start(f32[17,32,128]{2,1,0:T(8,128)S(1)} %get-tuple-element.18), channel_id=1, source_target_pairs={{30,0},{8,2},{2,4},{12,6},{6,8},{16,10},{10,12},{20,14},{14,16},{2... | collective-permute-start | bytes 835592 | tf_op jit(solution)/shard_map/ppermute | solution.py:25
  7.2 1.5 %collective-permute-start.4 = (f32[17,32,128]{2,1,0:T(8,128)S(1)}, f32[17,32,128]{2,1,0:T(8,128)S(1)}, u32[]{:S(2)}, u32[]{:S(2)}) collective-permute-start(f32[17,32,128]{2,1,0:T(8,128)S(1)} %get-tuple-element.18), channel_id=1, source_target_pairs={{28,0},{10,2},{0,4},{14,6},{4,8},{18,10},{8,12},{22,14},{12,16},{2... | collective-permute-start | bytes 835592 | tf_op jit(solution)/shard_map/ppermute | solution.py:25
  8.7 0.7 %dynamic-slice_bitcast_fusion.spot_ref = s32[8,128]{1,0:T(8,128)S(1)} fusion(s32[2,2,8,128]{3,2,1,0:T(8,128)} %constant.24.clone, s32[]{:T(128)S(6)} %select_n.14, s32[]{:T(128)S(6)} %select_n.15), kind=kLoop, calls=%fused_computation | loop fusion | bytes 8200 | tf_op jit(solution)/shard_map/squeeze | solution.py:315
  9.4 0.0 collective-permute-done.sibling
  9.4 7.9 %own_chains.1.home = f32[64,128]{1,0:T(8,128)S(1)} custom-call(s32[1]{0:T(128)} %bitcast.side_ref, f32[27,32,128]{2,1,0:T(8,128)S(1)} %get-tuple-element.15.own, f32[27,32,128]{2,1,0:T(8,128)S(1)} %collective-permute-done.sibling), custom_call_target="tpu_custom_call" | custom-call | tf_op jit(solution)/shard_map/own_chains/pallas_call | solution.py:286
  17.3 0.0 collective-permute-done.3.second
  17.3 0.1 collective-permute-start.5
  17.4 4.5 %collective-permute-start.2 = (f32[10,32,128]{2,1,0:T(8,128)S(1)}, f32[10,32,128]{2,1,0:T(8,128)S(1)}, u32[]{:S(2)}, u32[]{:S(2)}) collective-permute-start(f32[10,32,128]{2,1,0:T(8,128)S(1)} %get-tuple-element.17), channel_id=1, source_target_pairs={{30,0},{8,2},{2,4},{12,6},{6,8},{16,10},{10,12},{20,14},{14,16},{2... | collective-permute-start | bytes 491528 | tf_op jit(solution)/shard_map/ppermute | solution.py:25
  21.9 0.0 collective-permute-start.1
  21.9 0.0 collective-permute-done.4.first
  21.9 0.0 collective-permute-done.5.other
  22.0 5.5 %half_chains.2.rest_0_ = f32[224,128]{1,0:T(8,128)S(1)} custom-call(s32[1]{0:T(128)} %bitcast.side_ref, f32[27,32,128]{2,1,0:T(8,128)S(1)} %get-tuple-element.15.own, f32[27,32,128]{2,1,0:T(8,128)S(1)} %collective-permute-done.sibling, f32[17,32,128]{2,1,0:T(8,128)S(1)} %collective-permute-done.4.first, f32[17,32,128]{2,1,0:T(8,128)S(1)} %collective-permute-done.3.second, ...), custom_call_target="tpu_custom_call" | custom-call | tf_op jit(solution)/shard_map/half_chains/pallas_call | solution.py:286
  27.5 0.0 collective-permute-done.2.second
  27.5 0.2 collective-permute-start.6
  27.7 2.3 %collective-permute-done.1.first = f32[10,32,128]{2,1,0:T(8,128)S(1)} collective-permute-done((f32[10,32,128]{2,1,0:T(8,128)S(1)}, f32[10,32,128]{2,1,0:T(8,128)S(1)}, u32[]{:S(2)}, u32[]{:S(2)}) %collective-permute-start.1) | collective-permute-done | bytes 163872 | tf_op jit(solution)/shard_map/ppermute | solution.py:25
  30.0 0.0 collective-permute-done.6.other
  30.0 3.2 %half_chains.3.mine = f32[288,128]{1,0:T(8,128)S(1)} custom-call(s32[1]{0:T(128)} %bitcast.side_ref, f32[27,32,128]{2,1,0:T(8,128)S(1)} %get-tuple-element.15.own, f32[27,32,128]{2,1,0:T(8,128)S(1)} %collective-permute-done.sibling, f32[10,32,128]{2,1,0:T(8,128)S(1)} %collective-permute-done.1.first, f32[10,32,128]{2,1,0:T(8,128)S(1)} %collective-permute-done.2.second, ...), custom_call_target="tpu_custom_call" | custom-call | tf_op jit(solution)/shard_map/half_chains/pallas_call | solution.py:286
  33.2 2.0 %collective-permute-start.7 = (f32[288,128]{1,0:T(8,128)S(1)}, f32[288,128]{1,0:T(8,128)S(1)}, u32[]{:S(2)}, u32[]{:S(2)}) collective-permute-start(f32[288,128]{1,0:T(8,128)S(1)} %half_chains.3.mine), channel_id=1, source_target_pairs={{0,1},{1,0},{2,3},{3,2},{4,5},{5,4},{6,7},{7,6},{8,9},{9,8},{10,11... | collective-permute-start | bytes 442376 | tf_op jit(solution)/shard_map/ppermute | solution.py:325
  35.1 3.2 %collective-permute-done.7.theirs = f32[288,128]{1,0:T(8,128)S(1)} collective-permute-done((f32[288,128]{1,0:T(8,128)S(1)}, f32[288,128]{1,0:T(8,128)S(1)}, u32[]{:S(2)}, u32[]{:S(2)}) %collective-permute-start.7) | collective-permute-done | bytes 147488 | tf_op jit(solution)/shard_map/ppermute | solution.py:325
  38.4 0.2 meet.1.mine
  38.5 0.0 collective-permute-start.8
  38.5 1.2 %collective-permute-done.8.theirs = f32[8,128]{1,0:T(8,128)S(1)} collective-permute-done((f32[8,128]{1,0:T(8,128)S(1)}, f32[8,128]{1,0:T(8,128)S(1)}, u32[]{:S(2)}, u32[]{:S(2)}) %collective-permute-start.8) | collective-permute-done | bytes 4128 | tf_op jit(solution)/shard_map/ppermute | solution.py:25
  39.7 0.1 join.1.here
  39.8 0.0 collective-permute-start.10
  39.8 4.5 %collective-permute-start.9 = (f32[8,128]{1,0:T(8,128)S(1)}, f32[8,128]{1,0:T(8,128)S(1)}, u32[]{:S(2)}, u32[]{:S(2)}) collective-permute-start(f32[8,128]{1,0:T(8,128)S(1)} %join.1.here), channel_id=1, source_target_pairs={{4,0},{6,2},{8,4},{10,6},{12,8},{14,10},{16,12},{18,14},{20,16},{2... | collective-permute-start | bytes 12296 | tf_op jit(solution)/shard_map/ppermute | solution.py:25
  44.3 1.6 %collective-permute-done.10.before = f32[8,128]{1,0:T(8,128)S(1)} collective-permute-done((f32[8,128]{1,0:T(8,128)S(1)}, f32[8,128]{1,0:T(8,128)S(1)}, u32[]{:S(2)}, u32[]{:S(2)}) %collective-permute-start.10) | collective-permute-done | bytes 4128 | tf_op jit(solution)/shard_map/ppermute | solution.py:25
  45.9 0.0 collective-permute-done.9.after
  45.9 0.8 %pick.1 = f32[1,26]{1,0:T(1,128)} custom-call(s32[8,128]{1,0:T(8,128)S(1)} %dynamic-slice_bitcast_fusion.spot_ref, f32[8,128]{1,0:T(8,128)S(1)} %join.1.here, f32[8,128]{1,0:T(8,128)S(1)} %collective-permute-done.9.after, f32[8,128]{1,0:T(8,128)S(1)} %collective-permute-done.10.before), custom_call_target="tpu_custom_call" | custom-call | tf_op jit(solution)/shard_map/pick/pallas_call | solution.py:286
Async XLA Ops:
  0.0 1.0 %copy-start = (f32[32,32,128]{2,1,0:T(8,128)S(1)}, f32[32,32,128]{2,1,0:T(8,128)}, u32[]{:S(2)}) copy-start(f32[32,32,128]{2,1,0:T(8,128)} %sites_ref.1) | copy-start | bytes 1572868
  2.0 7.4 %collective-permute-start = (f32[27,32,128]{2,1,0:T(8,128)S(1)}, f32[27,32,128]{2,1,0:T(8,128)S(1)}, u32[]{:S(2)}, u32[]{:S(2)}) collective-permute-start(f32[27,32,128]{2,1,0:T(8,128)S(1)} %get-tuple-element.15.own), channel_id=1, source_target_pairs={{2,0},{0,2},{6,4},{4,6},{10,8},{8,10},{14,12},{12,14},{18,16},{16,... | collective-permute-start | bytes 1327112 | tf_op jit(solution)/shard_map/ppermute | solution.py:25
  2.5 14.8 %collective-permute-start.3 = (f32[17,32,128]{2,1,0:T(8,128)S(1)}, f32[17,32,128]{2,1,0:T(8,128)S(1)}, u32[]{:S(2)}, u32[]{:S(2)}) collective-permute-start(f32[17,32,128]{2,1,0:T(8,128)S(1)} %get-tuple-element.18), channel_id=1, source_target_pairs={{30,0},{8,2},{2,4},{12,6},{6,8},{16,10},{10,12},{20,14},{14,16},{2... | collective-permute-start | bytes 835592 | tf_op jit(solution)/shard_map/ppermute | solution.py:25
  7.2 14.7 %collective-permute-start.4 = (f32[17,32,128]{2,1,0:T(8,128)S(1)}, f32[17,32,128]{2,1,0:T(8,128)S(1)}, u32[]{:S(2)}, u32[]{:S(2)}) collective-permute-start(f32[17,32,128]{2,1,0:T(8,128)S(1)} %get-tuple-element.18), channel_id=1, source_target_pairs={{28,0},{10,2},{0,4},{14,6},{4,8},{18,10},{8,12},{22,14},{12,16},{2... | collective-permute-start | bytes 835592 | tf_op jit(solution)/shard_map/ppermute | solution.py:25
  17.3 4.6 %collective-permute-start.5 = (f32[17,32,128]{2,1,0:T(8,128)S(1)}, f32[17,32,128]{2,1,0:T(8,128)S(1)}, u32[]{:S(2)}, u32[]{:S(2)}) collective-permute-start(f32[17,32,128]{2,1,0:T(8,128)S(1)} %collective-permute-done.3.second), channel_id=1, source_target_pairs={{2,0},{0,2},{6,4},{4,6},{10,8},{8,10},{14,12},{12,14},{18,16},{16,... | collective-permute-start | bytes 835592 | tf_op jit(solution)/shard_map/ppermute | solution.py:25
  17.4 10.1 %collective-permute-start.2 = (f32[10,32,128]{2,1,0:T(8,128)S(1)}, f32[10,32,128]{2,1,0:T(8,128)S(1)}, u32[]{:S(2)}, u32[]{:S(2)}) collective-permute-start(f32[10,32,128]{2,1,0:T(8,128)S(1)} %get-tuple-element.17), channel_id=1, source_target_pairs={{30,0},{8,2},{2,4},{12,6},{6,8},{16,10},{10,12},{20,14},{14,16},{2... | collective-permute-start | bytes 491528 | tf_op jit(solution)/shard_map/ppermute | solution.py:25
  21.9 8.0 %collective-permute-start.1 = (f32[10,32,128]{2,1,0:T(8,128)S(1)}, f32[10,32,128]{2,1,0:T(8,128)S(1)}, u32[]{:S(2)}, u32[]{:S(2)}) collective-permute-start(f32[10,32,128]{2,1,0:T(8,128)S(1)} %get-tuple-element.17), channel_id=1, source_target_pairs={{28,0},{10,2},{0,4},{14,6},{4,8},{18,10},{8,12},{22,14},{12,16},{2... | collective-permute-start | bytes 491528 | tf_op jit(solution)/shard_map/ppermute | solution.py:25
  27.5 2.5 %collective-permute-start.6 = (f32[10,32,128]{2,1,0:T(8,128)S(1)}, f32[10,32,128]{2,1,0:T(8,128)S(1)}, u32[]{:S(2)}, u32[]{:S(2)}) collective-permute-start(f32[10,32,128]{2,1,0:T(8,128)S(1)} %collective-permute-done.2.second), channel_id=1, source_target_pairs={{2,0},{0,2},{6,4},{4,6},{10,8},{8,10},{14,12},{12,14},{18,16},{16,... | collective-permute-start | bytes 491528 | tf_op jit(solution)/shard_map/ppermute | solution.py:25
  33.2 5.2 %collective-permute-start.7 = (f32[288,128]{1,0:T(8,128)S(1)}, f32[288,128]{1,0:T(8,128)S(1)}, u32[]{:S(2)}, u32[]{:S(2)}) collective-permute-start(f32[288,128]{1,0:T(8,128)S(1)} %half_chains.3.mine), channel_id=1, source_target_pairs={{0,1},{1,0},{2,3},{3,2},{4,5},{5,4},{6,7},{7,6},{8,9},{9,8},{10,11... | collective-permute-start | bytes 442376 | tf_op jit(solution)/shard_map/ppermute | solution.py:325
  38.5 1.2 %collective-permute-start.8 = (f32[8,128]{1,0:T(8,128)S(1)}, f32[8,128]{1,0:T(8,128)S(1)}, u32[]{:S(2)}, u32[]{:S(2)}) collective-permute-start(f32[8,128]{1,0:T(8,128)S(1)} %meet.1.mine), channel_id=1, source_target_pairs={{2,0},{0,2},{6,4},{4,6},{10,8},{8,10},{14,12},{12,14},{18,16},{16,... | collective-permute-start | bytes 12296 | tf_op jit(solution)/shard_map/ppermute | solution.py:25
  39.8 6.1 %collective-permute-start.10 = (f32[8,128]{1,0:T(8,128)S(1)}, f32[8,128]{1,0:T(8,128)S(1)}, u32[]{:S(2)}, u32[]{:S(2)}) collective-permute-start(f32[8,128]{1,0:T(8,128)S(1)} %join.1.here), channel_id=1, source_target_pairs={{24,0},{26,2},{28,4},{30,6},{0,8},{2,10},{4,12},{6,14},{8,16},{10,... | collective-permute-start | bytes 12296 | tf_op jit(solution)/shard_map/ppermute | solution.py:25
  39.8 6.1 %collective-permute-start.9 = (f32[8,128]{1,0:T(8,128)S(1)}, f32[8,128]{1,0:T(8,128)S(1)}, u32[]{:S(2)}, u32[]{:S(2)}) collective-permute-start(f32[8,128]{1,0:T(8,128)S(1)} %join.1.here), channel_id=1, source_target_pairs={{4,0},{6,2},{8,4},{10,6},{12,8},{14,10},{16,12},{18,14},{20,16},{2... | collective-permute-start | bytes 12296 | tf_op jit(solution)/shard_map/ppermute | solution.py:25

commit v14 on v13

--- a/solution.py
+++ b/solution.py
@@ -9,7 +9,7 @@
 
 REACH = 6
 EDGE = 6
-SHARE = 0.63
+SHARE = 0.66
 BF16, F32 = jnp.bfloat16, jnp.float32
 VMEM = pl.BlockSpec(memory_space=pltpu.VMEM)
 SMEM = pl.BlockSpec(memory_space=pltpu.SMEM)
@@ -113,13 +113,9 @@
     current = jnp.broadcast_to(tiles[0][:1], (32, 128))
     for k, tile in enumerate(tiles[1:]):
         chosen = jnp.where(slot % 2 == (row >> k) % 2, current, 0.0)
-        weights = [jnp.where(slot // 2 == n, tile, 0.0) for n in (0, 0, 1, 1)]
-        current = jnp.dot(
-            chosen,
-            jnp.concatenate(weights, 0),
-            precision=lax.Precision.HIGHEST,
-            preferred_element_type=F32,
-        )
+        high, low = split(jnp.concatenate([jnp.where(slot // 2 == n, tile, 0.0) for n in (0, 0, 1, 1)], 0))
+        upper, lower = split(chosen)
+        current = product(jnp.concatenate([upper, lower], 1), jnp.concatenate([high, high], 0)) + product(upper, low)
     return current
 
 

time: 46.9 us -> 47 us (level)
  starting transfers between devices: 17.9 us -> 18.7 us
    ppermute x10, starting transfers between devices: 15.9 us -> 16.8 us  [move(): return lax.ppermute(array, 'blk', pairs)]
    ppermute x10, waiting for transfers between devices: 5.09 us -> 4.3 us  [move(): return lax.ppermute(array, 'blk', pairs)]
  transfers between devices with their start and end apart: 11 -> 11, of which waited for: 4 -> 5; matrix products, arithmetic and copies ran while one was open for 1% -> 1% of each run, Pallas kernels for 29% -> 29%
where the time goes in v14:
time: 47 us; the launch traced here: 46.8 us
  starting transfers between devices  18.7 us (40%)
  Pallas kernels  18.4 us (39%)
  waiting for transfers between devices  7.96 us (17%)
  local copies, waits for them, and re-layouts  1.73 us (4%)
    pallas_call x7, Pallas kernels, call(): pl.pallas_call(kernel, out_shape=shapes if many else shapes[0], in_specs=...  18.4 us
    ppermute x10, starting transfers between devices, move(): return lax.ppermute(array, 'blk', pairs)  16.8 us
    ppermute x10, waiting for transfers between devices, move(): return lax.ppermute(array, 'blk', pairs)  4.3 us
    ppermute x1, waiting for transfers between devices, body(): partner = lax.ppermute(state, 'pair', [(0, 1), (1, 0)])  3.65 us
    ppermute x1, starting transfers between devices, body(): partner = lax.ppermute(state, 'pair', [(0, 1), (1, 0)])  1.9 us
    unnamed x2, local copies, waits for them, and re-layouts  1.04 us
  transfers between devices with their start and end apart: 11, of which 5 were waited for; matrix products, arithmetic and copies ran while one was open for 1% of the time, Pallas kernels for 29%

profile of v14, /device:TPU:0, one launch (start us, length us, event | category | flops | bytes accessed | tf_op | source)
XLA Modules:
  0.0 46.8 jit_solution(9165390933048988584)
XLA Ops:
  0.0 0.0 copy-start
  0.0 1.0 %copy-done = f32[32,32,128]{2,1,0:T(8,128)S(1)} copy-done((f32[32,32,128]{2,1,0:T(8,128)S(1)}, f32[32,32,128]{2,1,0:T(8,128)}, u32[]{:S(2)}) %copy-start) | copy-done | bytes 524312
  1.0 0.6 %order.1 = (f32[27,32,128]{2,1,0:T(8,128)S(1)}, f32[18,32,128]{2,1,0:T(8,128)S(1)}, f32[9,32,128]{2,1,0:T(8,128)S(1)}) custom-call(s32[1]{0:T(128)} %bitcast.side_ref, f32[32,32,128]{2,1,0:T(8,128)S(1)} %copy-done), custom_call_target="tpu_custom_call" | custom-call | tf_op jit(solution)/shard_map/order/pallas_call | solution.py:282
  1.7 0.5 collective-permute-start
  2.1 4.7 %collective-permute-start.3 = (f32[18,32,128]{2,1,0:T(8,128)S(1)}, f32[18,32,128]{2,1,0:T(8,128)S(1)}, u32[]{:S(2)}, u32[]{:S(2)}) collective-permute-start(f32[18,32,128]{2,1,0:T(8,128)S(1)} %get-tuple-element.18), channel_id=1, source_target_pairs={{30,0},{8,2},{2,4},{12,6},{6,8},{16,10},{10,12},{20,14},{14,16},{2... | collective-permute-start | bytes 884744 | tf_op jit(solution)/shard_map/ppermute | solution.py:25
  6.9 1.5 %collective-permute-start.4 = (f32[18,32,128]{2,1,0:T(8,128)S(1)}, f32[18,32,128]{2,1,0:T(8,128)S(1)}, u32[]{:S(2)}, u32[]{:S(2)}) collective-permute-start(f32[18,32,128]{2,1,0:T(8,128)S(1)} %get-tuple-element.18), channel_id=1, source_target_pairs={{28,0},{10,2},{0,4},{14,6},{4,8},{18,10},{8,12},{22,14},{12,16},{2... | collective-permute-start | bytes 884744 | tf_op jit(solution)/shard_map/ppermute | solution.py:25
  8.3 0.7 %dynamic-slice_bitcast_fusion.spot_ref = s32[8,128]{1,0:T(8,128)S(1)} fusion(s32[2,2,8,128]{3,2,1,0:T(8,128)} %constant.24.clone, s32[]{:T(128)S(6)} %select_n.14, s32[]{:T(128)S(6)} %select_n.15), kind=kLoop, calls=%fused_computation | loop fusion | bytes 8200 | tf_op jit(solution)/shard_map/squeeze | solution.py:311
  9.0 0.0 collective-permute-done.sibling
  9.0 7.9 %own_chains.1.home = f32[64,128]{1,0:T(8,128)S(1)} custom-call(s32[1]{0:T(128)} %bitcast.side_ref, f32[27,32,128]{2,1,0:T(8,128)S(1)} %get-tuple-element.15.own, f32[27,32,128]{2,1,0:T(8,128)S(1)} %collective-permute-done.sibling), custom_call_target="tpu_custom_call" | custom-call | tf_op jit(solution)/shard_map/own_chains/pallas_call | solution.py:282
  17.0 0.0 collective-permute-done.3.second
  17.0 0.1 collective-permute-start.5
  17.1 5.3 %collective-permute-start.2 = (f32[9,32,128]{2,1,0:T(8,128)S(1)}, f32[9,32,128]{2,1,0:T(8,128)S(1)}, u32[]{:S(2)}, u32[]{:S(2)}) collective-permute-start(f32[9,32,128]{2,1,0:T(8,128)S(1)} %get-tuple-element.17), channel_id=1, source_target_pairs={{30,0},{8,2},{2,4},{12,6},{6,8},{16,10},{10,12},{20,14},{14,16},{2... | collective-permute-start | bytes 442376 | tf_op jit(solution)/shard_map/ppermute | solution.py:25
  22.3 0.0 collective-permute-start.1
  22.3 0.0 collective-permute-done.4.first
  22.3 0.0 collective-permute-done.5.other
  22.4 5.8 %half_chains.2.rest_0_ = f32[224,128]{1,0:T(8,128)S(1)} custom-call(s32[1]{0:T(128)} %bitcast.side_ref, f32[27,32,128]{2,1,0:T(8,128)S(1)} %get-tuple-element.15.own, f32[27,32,128]{2,1,0:T(8,128)S(1)} %collective-permute-done.sibling, f32[18,32,128]{2,1,0:T(8,128)S(1)} %collective-permute-done.4.first, f32[18,32,128]{2,1,0:T(8,128)S(1)} %collective-permute-done.3.second, ...), custom_call_target="tpu_custom_call" | custom-call | tf_op jit(solution)/shard_map/half_chains/pallas_call | solution.py:282
  28.2 0.0 collective-permute-done.2.second
  28.2 0.2 collective-permute-start.6
  28.4 1.8 %collective-permute-done.1.first = f32[9,32,128]{2,1,0:T(8,128)S(1)} collective-permute-done((f32[9,32,128]{2,1,0:T(8,128)S(1)}, f32[9,32,128]{2,1,0:T(8,128)S(1)}, u32[]{:S(2)}, u32[]{:S(2)}) %collective-permute-start.1) | collective-permute-done | bytes 147488 | tf_op jit(solution)/shard_map/ppermute | solution.py:25
  30.2 0.0 collective-permute-done.6.other
  30.2 2.9 %half_chains.3.mine = f32[288,128]{1,0:T(8,128)S(1)} custom-call(s32[1]{0:T(128)} %bitcast.side_ref, f32[27,32,128]{2,1,0:T(8,128)S(1)} %get-tuple-element.15.own, f32[27,32,128]{2,1,0:T(8,128)S(1)} %collective-permute-done.sibling, f32[9,32,128]{2,1,0:T(8,128)S(1)} %collective-permute-done.1.first, f32[9,32,128]{2,1,0:T(8,128)S(1)} %collective-permute-done.2.second, ...), custom_call_target="tpu_custom_call" | custom-call | tf_op jit(solution)/shard_map/half_chains/pallas_call | solution.py:282
  33.1 1.9 %collective-permute-start.7 = (f32[288,128]{1,0:T(8,128)S(1)}, f32[288,128]{1,0:T(8,128)S(1)}, u32[]{:S(2)}, u32[]{:S(2)}) collective-permute-start(f32[288,128]{1,0:T(8,128)S(1)} %half_chains.3.mine), channel_id=1, source_target_pairs={{0,1},{1,0},{2,3},{3,2},{4,5},{5,4},{6,7},{7,6},{8,9},{9,8},{10,11... | collective-permute-start | bytes 442376 | tf_op jit(solution)/shard_map/ppermute | solution.py:321
  35.0 3.7 %collective-permute-done.7.theirs = f32[288,128]{1,0:T(8,128)S(1)} collective-permute-done((f32[288,128]{1,0:T(8,128)S(1)}, f32[288,128]{1,0:T(8,128)S(1)}, u32[]{:S(2)}, u32[]{:S(2)}) %collective-permute-start.7) | collective-permute-done | bytes 147488 | tf_op jit(solution)/shard_map/ppermute | solution.py:321
  38.6 0.2 meet.1.mine
  38.8 0.0 collective-permute-start.8
  38.8 1.2 %collective-permute-done.8.theirs = f32[8,128]{1,0:T(8,128)S(1)} collective-permute-done((f32[8,128]{1,0:T(8,128)S(1)}, f32[8,128]{1,0:T(8,128)S(1)}, u32[]{:S(2)}, u32[]{:S(2)}) %collective-permute-start.8) | collective-permute-done | bytes 4128 | tf_op jit(solution)/shard_map/ppermute | solution.py:25
  40.0 0.1 join.1.here
  40.0 0.2 collective-permute-start.10
  40.2 4.4 %collective-permute-start.9 = (f32[8,128]{1,0:T(8,128)S(1)}, f32[8,128]{1,0:T(8,128)S(1)}, u32[]{:S(2)}, u32[]{:S(2)}) collective-permute-start(f32[8,128]{1,0:T(8,128)S(1)} %join.1.here), channel_id=1, source_target_pairs={{4,0},{6,2},{8,4},{10,6},{12,8},{14,10},{16,12},{18,14},{20,16},{2... | collective-permute-start | bytes 12296 | tf_op jit(solution)/shard_map/ppermute | solution.py:25
  44.6 0.8 %collective-permute-done.10.before = f32[8,128]{1,0:T(8,128)S(1)} collective-permute-done((f32[8,128]{1,0:T(8,128)S(1)}, f32[8,128]{1,0:T(8,128)S(1)}, u32[]{:S(2)}, u32[]{:S(2)}) %collective-permute-start.10) | collective-permute-done | bytes 4128 | tf_op jit(solution)/shard_map/ppermute | solution.py:25
  45.4 0.5 %collective-permute-done.9.after = f32[8,128]{1,0:T(8,128)S(1)} collective-permute-done((f32[8,128]{1,0:T(8,128)S(1)}, f32[8,128]{1,0:T(8,128)S(1)}, u32[]{:S(2)}, u32[]{:S(2)}) %collective-permute-start.9) | collective-permute-done | bytes 4128 | tf_op jit(solution)/shard_map/ppermute | solution.py:25
  45.9 0.8 %pick.1 = f32[1,26]{1,0:T(1,128)} custom-call(s32[8,128]{1,0:T(8,128)S(1)} %dynamic-slice_bitcast_fusion.spot_ref, f32[8,128]{1,0:T(8,128)S(1)} %join.1.here, f32[8,128]{1,0:T(8,128)S(1)} %collective-permute-done.9.after, f32[8,128]{1,0:T(8,128)S(1)} %collective-permute-done.10.before), custom_call_target="tpu_custom_call" | custom-call | tf_op jit(solution)/shard_map/pick/pallas_call | solution.py:282
Async XLA Ops:
  0.0 1.0 %copy-start = (f32[32,32,128]{2,1,0:T(8,128)S(1)}, f32[32,32,128]{2,1,0:T(8,128)}, u32[]{:S(2)}) copy-start(f32[32,32,128]{2,1,0:T(8,128)} %sites_ref.1) | copy-start | bytes 1572868
  1.7 7.4 %collective-permute-start = (f32[27,32,128]{2,1,0:T(8,128)S(1)}, f32[27,32,128]{2,1,0:T(8,128)S(1)}, u32[]{:S(2)}, u32[]{:S(2)}) collective-permute-start(f32[27,32,128]{2,1,0:T(8,128)S(1)} %get-tuple-element.15.own), channel_id=1, source_target_pairs={{2,0},{0,2},{6,4},{4,6},{10,8},{8,10},{14,12},{12,14},{18,16},{16,... | collective-permute-start | bytes 1327112 | tf_op jit(solution)/shard_map/ppermute | solution.py:25
  2.1 14.8 %collective-permute-start.3 = (f32[18,32,128]{2,1,0:T(8,128)S(1)}, f32[18,32,128]{2,1,0:T(8,128)S(1)}, u32[]{:S(2)}, u32[]{:S(2)}) collective-permute-start(f32[18,32,128]{2,1,0:T(8,128)S(1)} %get-tuple-element.18), channel_id=1, source_target_pairs={{30,0},{8,2},{2,4},{12,6},{6,8},{16,10},{10,12},{20,14},{14,16},{2... | collective-permute-start | bytes 884744 | tf_op jit(solution)/shard_map/ppermute | solution.py:25
  6.9 15.5 %collective-permute-start.4 = (f32[18,32,128]{2,1,0:T(8,128)S(1)}, f32[18,32,128]{2,1,0:T(8,128)S(1)}, u32[]{:S(2)}, u32[]{:S(2)}) collective-permute-start(f32[18,32,128]{2,1,0:T(8,128)S(1)} %get-tuple-element.18), channel_id=1, source_target_pairs={{28,0},{10,2},{0,4},{14,6},{4,8},{18,10},{8,12},{22,14},{12,16},{2... | collective-permute-start | bytes 884744 | tf_op jit(solution)/shard_map/ppermute | solution.py:25
  17.0 5.4 %collective-permute-start.5 = (f32[18,32,128]{2,1,0:T(8,128)S(1)}, f32[18,32,128]{2,1,0:T(8,128)S(1)}, u32[]{:S(2)}, u32[]{:S(2)}) collective-permute-start(f32[18,32,128]{2,1,0:T(8,128)S(1)} %collective-permute-done.3.second), channel_id=1, source_target_pairs={{2,0},{0,2},{6,4},{4,6},{10,8},{8,10},{14,12},{12,14},{18,16},{16,... | collective-permute-start | bytes 884744 | tf_op jit(solution)/shard_map/ppermute | solution.py:25
  17.1 11.1 %collective-permute-start.2 = (f32[9,32,128]{2,1,0:T(8,128)S(1)}, f32[9,32,128]{2,1,0:T(8,128)S(1)}, u32[]{:S(2)}, u32[]{:S(2)}) collective-permute-start(f32[9,32,128]{2,1,0:T(8,128)S(1)} %get-tuple-element.17), channel_id=1, source_target_pairs={{30,0},{8,2},{2,4},{12,6},{6,8},{16,10},{10,12},{20,14},{14,16},{2... | collective-permute-start | bytes 442376 | tf_op jit(solution)/shard_map/ppermute | solution.py:25
  22.3 7.8 %collective-permute-start.1 = (f32[9,32,128]{2,1,0:T(8,128)S(1)}, f32[9,32,128]{2,1,0:T(8,128)S(1)}, u32[]{:S(2)}, u32[]{:S(2)}) collective-permute-start(f32[9,32,128]{2,1,0:T(8,128)S(1)} %get-tuple-element.17), channel_id=1, source_target_pairs={{28,0},{10,2},{0,4},{14,6},{4,8},{18,10},{8,12},{22,14},{12,16},{2... | collective-permute-start | bytes 442376 | tf_op jit(solution)/shard_map/ppermute | solution.py:25
  28.2 2.0 %collective-permute-start.6 = (f32[9,32,128]{2,1,0:T(8,128)S(1)}, f32[9,32,128]{2,1,0:T(8,128)S(1)}, u32[]{:S(2)}, u32[]{:S(2)}) collective-permute-start(f32[9,32,128]{2,1,0:T(8,128)S(1)} %collective-permute-done.2.second), channel_id=1, source_target_pairs={{2,0},{0,2},{6,4},{4,6},{10,8},{8,10},{14,12},{12,14},{18,16},{16,... | collective-permute-start | bytes 442376 | tf_op jit(solution)/shard_map/ppermute | solution.py:25
  33.1 5.6 %collective-permute-start.7 = (f32[288,128]{1,0:T(8,128)S(1)}, f32[288,128]{1,0:T(8,128)S(1)}, u32[]{:S(2)}, u32[]{:S(2)}) collective-permute-start(f32[288,128]{1,0:T(8,128)S(1)} %half_chains.3.mine), channel_id=1, source_target_pairs={{0,1},{1,0},{2,3},{3,2},{4,5},{5,4},{6,7},{7,6},{8,9},{9,8},{10,11... | collective-permute-start | bytes 442376 | tf_op jit(solution)/shard_map/ppermute | solution.py:321
  38.8 1.2 %collective-permute-start.8 = (f32[8,128]{1,0:T(8,128)S(1)}, f32[8,128]{1,0:T(8,128)S(1)}, u32[]{:S(2)}, u32[]{:S(2)}) collective-permute-start(f32[8,128]{1,0:T(8,128)S(1)} %meet.1.mine), channel_id=1, source_target_pairs={{2,0},{0,2},{6,4},{4,6},{10,8},{8,10},{14,12},{12,14},{18,16},{16,... | collective-permute-start | bytes 12296 | tf_op jit(solution)/shard_map/ppermute | solution.py:25
  40.0 5.4 %collective-permute-start.10 = (f32[8,128]{1,0:T(8,128)S(1)}, f32[8,128]{1,0:T(8,128)S(1)}, u32[]{:S(2)}, u32[]{:S(2)}) collective-permute-start(f32[8,128]{1,0:T(8,128)S(1)} %join.1.here), channel_id=1, source_target_pairs={{24,0},{26,2},{28,4},{30,6},{0,8},{2,10},{4,12},{6,14},{8,16},{10,... | collective-permute-start | bytes 12296 | tf_op jit(solution)/shard_map/ppermute | solution.py:25
  40.2 5.7 %collective-permute-start.9 = (f32[8,128]{1,0:T(8,128)S(1)}, f32[8,128]{1,0:T(8,128)S(1)}, u32[]{:S(2)}, u32[]{:S(2)}) collective-permute-start(f32[8,128]{1,0:T(8,128)S(1)} %join.1.here), channel_id=1, source_target_pairs={{4,0},{6,2},{8,4},{10,6},{12,8},{14,10},{16,12},{18,14},{20,16},{2... | collective-permute-start | bytes 12296 | tf_op jit(solution)/shard_map/ppermute | solution.py:25

commit v15 on v14

--- a/solution.py
+++ b/solution.py
@@ -9,7 +9,7 @@
 
 REACH = 6
 EDGE = 6
-SHARE = 0.66
+SHARE = 0.63
 BF16, F32 = jnp.bfloat16, jnp.float32
 VMEM = pl.BlockSpec(memory_space=pltpu.VMEM)
 SMEM = pl.BlockSpec(memory_space=pltpu.SMEM)

time: 47 us -> 46.6 us (level)
  starting transfers between devices: 18.7 us -> 17.9 us
    ppermute x10, starting transfers between devices: 16.8 us -> 16 us  [move(): return lax.ppermute(array, 'blk', pairs)]
    ppermute x10, waiting for transfers between devices: 4.3 us -> 5.07 us  [move(): return lax.ppermute(array, 'blk', pairs)]
  transfers between devices with their start and end apart: 11 -> 11, of which waited for: 5 -> 4; matrix products, arithmetic and copies ran while one was open for 1% -> 1% of each run, Pallas kernels for 29% -> 29%
where the time goes in v15:
time: 46.6 us; the launch traced here: 46.4 us
  Pallas kernels  18.4 us (39%)
  starting transfers between devices  17.9 us (38%)
  waiting for transfers between devices  8.36 us (18%)
  local copies, waits for them, and re-layouts  1.73 us (4%)
    pallas_call x7, Pallas kernels, call(): pl.pallas_call(kernel, out_shape=shapes if many else shapes[0], in_specs=...  18.4 us
    ppermute x10, starting transfers between devices, move(): return lax.ppermute(array, 'blk', pairs)  16 us
    ppermute x10, waiting for transfers between devices, move(): return lax.ppermute(array, 'blk', pairs)  5.07 us
    ppermute x1, waiting for transfers between devices, body(): partner = lax.ppermute(state, 'pair', [(0, 1), (1, 0)])  3.29 us
    ppermute x1, starting transfers between devices, body(): partner = lax.ppermute(state, 'pair', [(0, 1), (1, 0)])  1.92 us
    unnamed x2, local copies, waits for them, and re-layouts  1.04 us
  transfers between devices with their start and end apart: 11, of which 4 were waited for; matrix products, arithmetic and copies ran while one was open for 1% of the time, Pallas kernels for 29%

profile of v15, /device:TPU:0, one launch (start us, length us, event | category | flops | bytes accessed | tf_op | source)
XLA Modules:
  0.0 46.4 jit_solution(9608555231828142371)
XLA Ops:
  0.0 0.0 copy-start
  0.0 1.0 %copy-done = f32[32,32,128]{2,1,0:T(8,128)S(1)} copy-done((f32[32,32,128]{2,1,0:T(8,128)S(1)}, f32[32,32,128]{2,1,0:T(8,128)}, u32[]{:S(2)}) %copy-start) | copy-done | bytes 524312
  1.0 0.6 %order.1 = (f32[27,32,128]{2,1,0:T(8,128)S(1)}, f32[17,32,128]{2,1,0:T(8,128)S(1)}, f32[10,32,128]{2,1,0:T(8,128)S(1)}) custom-call(s32[1]{0:T(128)} %bitcast.side_ref, f32[32,32,128]{2,1,0:T(8,128)S(1)} %copy-done), custom_call_target="tpu_custom_call" | custom-call | tf_op jit(solution)/shard_map/order/pallas_call | solution.py:282
  1.7 0.5 collective-permute-start
  2.1 4.7 %collective-permute-start.3 = (f32[17,32,128]{2,1,0:T(8,128)S(1)}, f32[17,32,128]{2,1,0:T(8,128)S(1)}, u32[]{:S(2)}, u32[]{:S(2)}) collective-permute-start(f32[17,32,128]{2,1,0:T(8,128)S(1)} %get-tuple-element.18), channel_id=1, source_target_pairs={{30,0},{8,2},{2,4},{12,6},{6,8},{16,10},{10,12},{20,14},{14,16},{2... | collective-permute-start | bytes 835592 | tf_op jit(solution)/shard_map/ppermute | solution.py:25
  6.9 1.5 %collective-permute-start.4 = (f32[17,32,128]{2,1,0:T(8,128)S(1)}, f32[17,32,128]{2,1,0:T(8,128)S(1)}, u32[]{:S(2)}, u32[]{:S(2)}) collective-permute-start(f32[17,32,128]{2,1,0:T(8,128)S(1)} %get-tuple-element.18), channel_id=1, source_target_pairs={{28,0},{10,2},{0,4},{14,6},{4,8},{18,10},{8,12},{22,14},{12,16},{2... | collective-permute-start | bytes 835592 | tf_op jit(solution)/shard_map/ppermute | solution.py:25
  8.3 0.7 %dynamic-slice_bitcast_fusion.spot_ref = s32[8,128]{1,0:T(8,128)S(1)} fusion(s32[2,2,8,128]{3,2,1,0:T(8,128)} %constant.24.clone, s32[]{:T(128)S(6)} %select_n.14, s32[]{:T(128)S(6)} %select_n.15), kind=kLoop, calls=%fused_computation | loop fusion | bytes 8200 | tf_op jit(solution)/shard_map/squeeze | solution.py:311
  9.0 0.0 collective-permute-done.sibling
  9.0 7.9 %own_chains.1.home = f32[64,128]{1,0:T(8,128)S(1)} custom-call(s32[1]{0:T(128)} %bitcast.side_ref, f32[27,32,128]{2,1,0:T(8,128)S(1)} %get-tuple-element.15.own, f32[27,32,128]{2,1,0:T(8,128)S(1)} %collective-permute-done.sibling), custom_call_target="tpu_custom_call" | custom-call | tf_op jit(solution)/shard_map/own_chains/pallas_call | solution.py:282
  17.0 0.0 collective-permute-done.3.second
  17.0 0.1 collective-permute-start.5
  17.1 4.6 %collective-permute-start.2 = (f32[10,32,128]{2,1,0:T(8,128)S(1)}, f32[10,32,128]{2,1,0:T(8,128)S(1)}, u32[]{:S(2)}, u32[]{:S(2)}) collective-permute-start(f32[10,32,128]{2,1,0:T(8,128)S(1)} %get-tuple-element.17), channel_id=1, source_target_pairs={{30,0},{8,2},{2,4},{12,6},{6,8},{16,10},{10,12},{20,14},{14,16},{2... | collective-permute-start | bytes 491528 | tf_op jit(solution)/shard_map/ppermute | solution.py:25
  21.6 0.0 collective-permute-start.1
  21.6 0.0 collective-permute-done.4.first
  21.6 0.0 collective-permute-done.5.other
  21.6 5.5 %half_chains.2.rest_0_ = f32[224,128]{1,0:T(8,128)S(1)} custom-call(s32[1]{0:T(128)} %bitcast.side_ref, f32[27,32,128]{2,1,0:T(8,128)S(1)} %get-tuple-element.15.own, f32[27,32,128]{2,1,0:T(8,128)S(1)} %collective-permute-done.sibling, f32[17,32,128]{2,1,0:T(8,128)S(1)} %collective-permute-done.4.first, f32[17,32,128]{2,1,0:T(8,128)S(1)} %collective-permute-done.3.second, ...), custom_call_target="tpu_custom_call" | custom-call | tf_op jit(solution)/shard_map/half_chains/pallas_call | solution.py:282
  27.2 0.0 collective-permute-done.2.second
  27.2 0.2 collective-permute-start.6
  27.4 2.3 %collective-permute-done.1.first = f32[10,32,128]{2,1,0:T(8,128)S(1)} collective-permute-done((f32[10,32,128]{2,1,0:T(8,128)S(1)}, f32[10,32,128]{2,1,0:T(8,128)S(1)}, u32[]{:S(2)}, u32[]{:S(2)}) %collective-permute-start.1) | collective-permute-done | bytes 163872 | tf_op jit(solution)/shard_map/ppermute | solution.py:25
  29.7 0.0 collective-permute-done.6.other
  29.7 3.2 %half_chains.3.mine = f32[288,128]{1,0:T(8,128)S(1)} custom-call(s32[1]{0:T(128)} %bitcast.side_ref, f32[27,32,128]{2,1,0:T(8,128)S(1)} %get-tuple-element.15.own, f32[27,32,128]{2,1,0:T(8,128)S(1)} %collective-permute-done.sibling, f32[10,32,128]{2,1,0:T(8,128)S(1)} %collective-permute-done.1.first, f32[10,32,128]{2,1,0:T(8,128)S(1)} %collective-permute-done.2.second, ...), custom_call_target="tpu_custom_call" | custom-call | tf_op jit(solution)/shard_map/half_chains/pallas_call | solution.py:282
  32.9 1.9 %collective-permute-start.7 = (f32[288,128]{1,0:T(8,128)S(1)}, f32[288,128]{1,0:T(8,128)S(1)}, u32[]{:S(2)}, u32[]{:S(2)}) collective-permute-start(f32[288,128]{1,0:T(8,128)S(1)} %half_chains.3.mine), channel_id=1, source_target_pairs={{0,1},{1,0},{2,3},{3,2},{4,5},{5,4},{6,7},{7,6},{8,9},{9,8},{10,11... | collective-permute-start | bytes 442376 | tf_op jit(solution)/shard_map/ppermute | solution.py:321
  34.8 3.3 %collective-permute-done.7.theirs = f32[288,128]{1,0:T(8,128)S(1)} collective-permute-done((f32[288,128]{1,0:T(8,128)S(1)}, f32[288,128]{1,0:T(8,128)S(1)}, u32[]{:S(2)}, u32[]{:S(2)}) %collective-permute-start.7) | collective-permute-done | bytes 147488 | tf_op jit(solution)/shard_map/ppermute | solution.py:321
  38.1 0.2 meet.1.mine
  38.2 0.0 collective-permute-start.8
  38.2 1.2 %collective-permute-done.8.theirs = f32[8,128]{1,0:T(8,128)S(1)} collective-permute-done((f32[8,128]{1,0:T(8,128)S(1)}, f32[8,128]{1,0:T(8,128)S(1)}, u32[]{:S(2)}, u32[]{:S(2)}) %collective-permute-start.8) | collective-permute-done | bytes 4128 | tf_op jit(solution)/shard_map/ppermute | solution.py:25
  39.4 0.1 join.1.here
  39.5 0.0 collective-permute-start.10
  39.5 4.4 %collective-permute-start.9 = (f32[8,128]{1,0:T(8,128)S(1)}, f32[8,128]{1,0:T(8,128)S(1)}, u32[]{:S(2)}, u32[]{:S(2)}) collective-permute-start(f32[8,128]{1,0:T(8,128)S(1)} %join.1.here), channel_id=1, source_target_pairs={{4,0},{6,2},{8,4},{10,6},{12,8},{14,10},{16,12},{18,14},{20,16},{2... | collective-permute-start | bytes 12296 | tf_op jit(solution)/shard_map/ppermute | solution.py:25
  43.9 1.6 %collective-permute-done.10.before = f32[8,128]{1,0:T(8,128)S(1)} collective-permute-done((f32[8,128]{1,0:T(8,128)S(1)}, f32[8,128]{1,0:T(8,128)S(1)}, u32[]{:S(2)}, u32[]{:S(2)}) %collective-permute-start.10) | collective-permute-done | bytes 4128 | tf_op jit(solution)/shard_map/ppermute | solution.py:25
  45.5 0.0 collective-permute-done.9.after
  45.5 0.8 %pick.1 = f32[1,26]{1,0:T(1,128)} custom-call(s32[8,128]{1,0:T(8,128)S(1)} %dynamic-slice_bitcast_fusion.spot_ref, f32[8,128]{1,0:T(8,128)S(1)} %join.1.here, f32[8,128]{1,0:T(8,128)S(1)} %collective-permute-done.9.after, f32[8,128]{1,0:T(8,128)S(1)} %collective-permute-done.10.before), custom_call_target="tpu_custom_call" | custom-call | tf_op jit(solution)/shard_map/pick/pallas_call | solution.py:282
Async XLA Ops:
  0.0 1.0 %copy-start = (f32[32,32,128]{2,1,0:T(8,128)S(1)}, f32[32,32,128]{2,1,0:T(8,128)}, u32[]{:S(2)}) copy-start(f32[32,32,128]{2,1,0:T(8,128)} %sites_ref.1) | copy-start | bytes 1572868
  1.7 7.4 %collective-permute-start = (f32[27,32,128]{2,1,0:T(8,128)S(1)}, f32[27,32,128]{2,1,0:T(8,128)S(1)}, u32[]{:S(2)}, u32[]{:S(2)}) collective-permute-start(f32[27,32,128]{2,1,0:T(8,128)S(1)} %get-tuple-element.15.own), channel_id=1, source_target_pairs={{2,0},{0,2},{6,4},{4,6},{10,8},{8,10},{14,12},{12,14},{18,16},{16,... | collective-permute-start | bytes 1327112 | tf_op jit(solution)/shard_map/ppermute | solution.py:25
  2.1 14.8 %collective-permute-start.3 = (f32[17,32,128]{2,1,0:T(8,128)S(1)}, f32[17,32,128]{2,1,0:T(8,128)S(1)}, u32[]{:S(2)}, u32[]{:S(2)}) collective-permute-start(f32[17,32,128]{2,1,0:T(8,128)S(1)} %get-tuple-element.18), channel_id=1, source_target_pairs={{30,0},{8,2},{2,4},{12,6},{6,8},{16,10},{10,12},{20,14},{14,16},{2... | collective-permute-start | bytes 835592 | tf_op jit(solution)/shard_map/ppermute | solution.py:25
  6.9 14.8 %collective-permute-start.4 = (f32[17,32,128]{2,1,0:T(8,128)S(1)}, f32[17,32,128]{2,1,0:T(8,128)S(1)}, u32[]{:S(2)}, u32[]{:S(2)}) collective-permute-start(f32[17,32,128]{2,1,0:T(8,128)S(1)} %get-tuple-element.18), channel_id=1, source_target_pairs={{28,0},{10,2},{0,4},{14,6},{4,8},{18,10},{8,12},{22,14},{12,16},{2... | collective-permute-start | bytes 835592 | tf_op jit(solution)/shard_map/ppermute | solution.py:25
  17.0 4.7 %collective-permute-start.5 = (f32[17,32,128]{2,1,0:T(8,128)S(1)}, f32[17,32,128]{2,1,0:T(8,128)S(1)}, u32[]{:S(2)}, u32[]{:S(2)}) collective-permute-start(f32[17,32,128]{2,1,0:T(8,128)S(1)} %collective-permute-done.3.second), channel_id=1, source_target_pairs={{2,0},{0,2},{6,4},{4,6},{10,8},{8,10},{14,12},{12,14},{18,16},{16,... | collective-permute-start | bytes 835592 | tf_op jit(solution)/shard_map/ppermute | solution.py:25
  17.1 10.1 %collective-permute-start.2 = (f32[10,32,128]{2,1,0:T(8,128)S(1)}, f32[10,32,128]{2,1,0:T(8,128)S(1)}, u32[]{:S(2)}, u32[]{:S(2)}) collective-permute-start(f32[10,32,128]{2,1,0:T(8,128)S(1)} %get-tuple-element.17), channel_id=1, source_target_pairs={{30,0},{8,2},{2,4},{12,6},{6,8},{16,10},{10,12},{20,14},{14,16},{2... | collective-permute-start | bytes 491528 | tf_op jit(solution)/shard_map/ppermute | solution.py:25
  21.6 8.0 %collective-permute-start.1 = (f32[10,32,128]{2,1,0:T(8,128)S(1)}, f32[10,32,128]{2,1,0:T(8,128)S(1)}, u32[]{:S(2)}, u32[]{:S(2)}) collective-permute-start(f32[10,32,128]{2,1,0:T(8,128)S(1)} %get-tuple-element.17), channel_id=1, source_target_pairs={{28,0},{10,2},{0,4},{14,6},{4,8},{18,10},{8,12},{22,14},{12,16},{2... | collective-permute-start | bytes 491528 | tf_op jit(solution)/shard_map/ppermute | solution.py:25
  27.2 2.5 %collective-permute-start.6 = (f32[10,32,128]{2,1,0:T(8,128)S(1)}, f32[10,32,128]{2,1,0:T(8,128)S(1)}, u32[]{:S(2)}, u32[]{:S(2)}) collective-permute-start(f32[10,32,128]{2,1,0:T(8,128)S(1)} %collective-permute-done.2.second), channel_id=1, source_target_pairs={{2,0},{0,2},{6,4},{4,6},{10,8},{8,10},{14,12},{12,14},{18,16},{16,... | collective-permute-start | bytes 491528 | tf_op jit(solution)/shard_map/ppermute | solution.py:25
  32.9 5.2 %collective-permute-start.7 = (f32[288,128]{1,0:T(8,128)S(1)}, f32[288,128]{1,0:T(8,128)S(1)}, u32[]{:S(2)}, u32[]{:S(2)}) collective-permute-start(f32[288,128]{1,0:T(8,128)S(1)} %half_chains.3.mine), channel_id=1, source_target_pairs={{0,1},{1,0},{2,3},{3,2},{4,5},{5,4},{6,7},{7,6},{8,9},{9,8},{10,11... | collective-permute-start | bytes 442376 | tf_op jit(solution)/shard_map/ppermute | solution.py:321
  38.2 1.2 %collective-permute-start.8 = (f32[8,128]{1,0:T(8,128)S(1)}, f32[8,128]{1,0:T(8,128)S(1)}, u32[]{:S(2)}, u32[]{:S(2)}) collective-permute-start(f32[8,128]{1,0:T(8,128)S(1)} %meet.1.mine), channel_id=1, source_target_pairs={{2,0},{0,2},{6,4},{4,6},{10,8},{8,10},{14,12},{12,14},{18,16},{16,... | collective-permute-start | bytes 12296 | tf_op jit(solution)/shard_map/ppermute | solution.py:25
  39.5 6.1 %collective-permute-start.10 = (f32[8,128]{1,0:T(8,128)S(1)}, f32[8,128]{1,0:T(8,128)S(1)}, u32[]{:S(2)}, u32[]{:S(2)}) collective-permute-start(f32[8,128]{1,0:T(8,128)S(1)} %join.1.here), channel_id=1, source_target_pairs={{24,0},{26,2},{28,4},{30,6},{0,8},{2,10},{4,12},{6,14},{8,16},{10,... | collective-permute-start | bytes 12296 | tf_op jit(solution)/shard_map/ppermute | solution.py:25
  39.5 6.1 %collective-permute-start.9 = (f32[8,128]{1,0:T(8,128)S(1)}, f32[8,128]{1,0:T(8,128)S(1)}, u32[]{:S(2)}, u32[]{:S(2)}) collective-permute-start(f32[8,128]{1,0:T(8,128)S(1)} %join.1.here), channel_id=1, source_target_pairs={{4,0},{6,2},{8,4},{10,6},{12,8},{14,10},{16,12},{18,14},{20,16},{2... | collective-permute-start | bytes 12296 | tf_op jit(solution)/shard_map/ppermute | solution.py:25

commit v16 on v15

--- a/solution.py
+++ b/solution.py
@@ -9,7 +9,7 @@
 
 REACH = 6
 EDGE = 6
-SHARE = 0.63
+SHARE = 0.6
 BF16, F32 = jnp.bfloat16, jnp.float32
 VMEM = pl.BlockSpec(memory_space=pltpu.VMEM)
 SMEM = pl.BlockSpec(memory_space=pltpu.SMEM)

time: 46.6 us -> 46.3 us (level)
  starting transfers between devices: 17.9 us -> 16.3 us
  waiting for transfers between devices: 8.36 us -> 9.67 us
    ppermute x10, starting transfers between devices: 16 us -> 14.3 us  [move(): return lax.ppermute(array, 'blk', pairs)]
    ppermute x10, waiting for transfers between devices: 5.07 us -> 6.45 us  [move(): return lax.ppermute(array, 'blk', pairs)]
  transfers between devices with their start and end apart: 11 -> 11, of which waited for: 4 -> 4; matrix products, arithmetic and copies ran while one was open for 1% -> 1% of each run, Pallas kernels for 29% -> 28%
where the time goes in v16:
time: 46.3 us; the launch traced here: 46.1 us
  Pallas kernels  18.4 us (40%)
  starting transfers between devices  16.3 us (35%)
  waiting for transfers between devices  9.67 us (21%)
  local copies, waits for them, and re-layouts  1.73 us (4%)
    pallas_call x7, Pallas kernels, call(): pl.pallas_call(kernel, out_shape=shapes if many else shapes[0], in_specs=...  18.4 us
    ppermute x10, starting transfers between devices, move(): return lax.ppermute(array, 'blk', pairs)  14.3 us
    ppermute x10, waiting for transfers between devices, move(): return lax.ppermute(array, 'blk', pairs)  6.45 us
    ppermute x1, waiting for transfers between devices, body(): partner = lax.ppermute(state, 'pair', [(0, 1), (1, 0)])  3.22 us
    ppermute x1, starting transfers between devices, body(): partner = lax.ppermute(state, 'pair', [(0, 1), (1, 0)])  1.99 us
    unnamed x2, local copies, waits for them, and re-layouts  1.04 us
  transfers between devices with their start and end apart: 11, of which 4 were waited for; matrix products, arithmetic and copies ran while one was open for 1% of the time, Pallas kernels for 28%

profile of v16, /device:TPU:0, one launch (start us, length us, event | category | flops | bytes accessed | tf_op | source)
XLA Modules:
  0.0 46.1 jit_solution(13433709211218470365)
XLA Ops:
  0.0 0.0 copy-start
  0.0 1.0 %copy-done = f32[32,32,128]{2,1,0:T(8,128)S(1)} copy-done((f32[32,32,128]{2,1,0:T(8,128)S(1)}, f32[32,32,128]{2,1,0:T(8,128)}, u32[]{:S(2)}) %copy-start) | copy-done | bytes 524312
  1.0 0.6 %order.1 = (f32[27,32,128]{2,1,0:T(8,128)S(1)}, f32[16,32,128]{2,1,0:T(8,128)S(1)}, f32[11,32,128]{2,1,0:T(8,128)S(1)}) custom-call(s32[1]{0:T(128)} %bitcast.side_ref, f32[32,32,128]{2,1,0:T(8,128)S(1)} %copy-done), custom_call_target="tpu_custom_call" | custom-call | tf_op jit(solution)/shard_map/order/pallas_call | solution.py:282
  1.7 0.5 collective-permute-start
  2.1 4.7 %collective-permute-start.3 = (f32[16,32,128]{2,1,0:T(8,128)S(1)}, f32[16,32,128]{2,1,0:T(8,128)S(1)}, u32[]{:S(2)}, u32[]{:S(2)}) collective-permute-start(f32[16,32,128]{2,1,0:T(8,128)S(1)} %get-tuple-element.18), channel_id=1, source_target_pairs={{30,0},{8,2},{2,4},{12,6},{6,8},{16,10},{10,12},{20,14},{14,16},{2... | collective-permute-start | bytes 786440 | tf_op jit(solution)/shard_map/ppermute | solution.py:25
  6.9 1.5 %collective-permute-start.4 = (f32[16,32,128]{2,1,0:T(8,128)S(1)}, f32[16,32,128]{2,1,0:T(8,128)S(1)}, u32[]{:S(2)}, u32[]{:S(2)}) collective-permute-start(f32[16,32,128]{2,1,0:T(8,128)S(1)} %get-tuple-element.18), channel_id=1, source_target_pairs={{28,0},{10,2},{0,4},{14,6},{4,8},{18,10},{8,12},{22,14},{12,16},{2... | collective-permute-start | bytes 786440 | tf_op jit(solution)/shard_map/ppermute | solution.py:25
  8.3 0.7 %dynamic-slice_bitcast_fusion.spot_ref = s32[8,128]{1,0:T(8,128)S(1)} fusion(s32[2,2,8,128]{3,2,1,0:T(8,128)} %constant.24.clone, s32[]{:T(128)S(6)} %select_n.14, s32[]{:T(128)S(6)} %select_n.15), kind=kLoop, calls=%fused_computation | loop fusion | bytes 8200 | tf_op jit(solution)/shard_map/squeeze | solution.py:311
  9.0 0.0 collective-permute-done.sibling
  9.0 7.9 %own_chains.1.home = f32[64,128]{1,0:T(8,128)S(1)} custom-call(s32[1]{0:T(128)} %bitcast.side_ref, f32[27,32,128]{2,1,0:T(8,128)S(1)} %get-tuple-element.15.own, f32[27,32,128]{2,1,0:T(8,128)S(1)} %collective-permute-done.sibling), custom_call_target="tpu_custom_call" | custom-call | tf_op jit(solution)/shard_map/own_chains/pallas_call | solution.py:282
  17.0 0.0 collective-permute-done.3.second
  17.0 0.1 collective-permute-start.5
  17.1 3.9 %collective-permute-start.2 = (f32[11,32,128]{2,1,0:T(8,128)S(1)}, f32[11,32,128]{2,1,0:T(8,128)S(1)}, u32[]{:S(2)}, u32[]{:S(2)}) collective-permute-start(f32[11,32,128]{2,1,0:T(8,128)S(1)} %get-tuple-element.17), channel_id=1, source_target_pairs={{30,0},{8,2},{2,4},{12,6},{6,8},{16,10},{10,12},{20,14},{14,16},{2... | collective-permute-start | bytes 540680 | tf_op jit(solution)/shard_map/ppermute | solution.py:25
  20.9 0.0 collective-permute-start.1
  21.0 0.0 collective-permute-done.4.first
  21.0 0.0 collective-permute-done.5.other
  21.0 5.2 %half_chains.2.rest_0_ = f32[224,128]{1,0:T(8,128)S(1)} custom-call(s32[1]{0:T(128)} %bitcast.side_ref, f32[27,32,128]{2,1,0:T(8,128)S(1)} %get-tuple-element.15.own, f32[27,32,128]{2,1,0:T(8,128)S(1)} %collective-permute-done.sibling, f32[16,32,128]{2,1,0:T(8,128)S(1)} %collective-permute-done.4.first, f32[16,32,128]{2,1,0:T(8,128)S(1)} %collective-permute-done.3.second, ...), custom_call_target="tpu_custom_call" | custom-call | tf_op jit(solution)/shard_map/half_chains/pallas_call | solution.py:282
  26.2 0.0 collective-permute-done.2.second
  26.2 0.2 collective-permute-start.6
  26.4 3.2 %collective-permute-done.1.first = f32[11,32,128]{2,1,0:T(8,128)S(1)} collective-permute-done((f32[11,32,128]{2,1,0:T(8,128)S(1)}, f32[11,32,128]{2,1,0:T(8,128)S(1)}, u32[]{:S(2)}, u32[]{:S(2)}) %collective-permute-start.1) | collective-permute-done | bytes 180256 | tf_op jit(solution)/shard_map/ppermute | solution.py:25
  29.6 0.0 collective-permute-done.6.other
  29.6 3.5 %half_chains.3.mine = f32[288,128]{1,0:T(8,128)S(1)} custom-call(s32[1]{0:T(128)} %bitcast.side_ref, f32[27,32,128]{2,1,0:T(8,128)S(1)} %get-tuple-element.15.own, f32[27,32,128]{2,1,0:T(8,128)S(1)} %collective-permute-done.sibling, f32[11,32,128]{2,1,0:T(8,128)S(1)} %collective-permute-done.1.first, f32[11,32,128]{2,1,0:T(8,128)S(1)} %collective-permute-done.2.second, ...), custom_call_target="tpu_custom_call" | custom-call | tf_op jit(solution)/shard_map/half_chains/pallas_call | solution.py:282
  33.1 2.0 %collective-permute-start.7 = (f32[288,128]{1,0:T(8,128)S(1)}, f32[288,128]{1,0:T(8,128)S(1)}, u32[]{:S(2)}, u32[]{:S(2)}) collective-permute-start(f32[288,128]{1,0:T(8,128)S(1)} %half_chains.3.mine), channel_id=1, source_target_pairs={{0,1},{1,0},{2,3},{3,2},{4,5},{5,4},{6,7},{7,6},{8,9},{9,8},{10,11... | collective-permute-start | bytes 442376 | tf_op jit(solution)/shard_map/ppermute | solution.py:321
  35.1 3.2 %collective-permute-done.7.theirs = f32[288,128]{1,0:T(8,128)S(1)} collective-permute-done((f32[288,128]{1,0:T(8,128)S(1)}, f32[288,128]{1,0:T(8,128)S(1)}, u32[]{:S(2)}, u32[]{:S(2)}) %collective-permute-start.7) | collective-permute-done | bytes 147488 | tf_op jit(solution)/shard_map/ppermute | solution.py:321
  38.3 0.2 meet.1.mine
  38.5 0.0 collective-permute-start.8
  38.5 1.2 %collective-permute-done.8.theirs = f32[8,128]{1,0:T(8,128)S(1)} collective-permute-done((f32[8,128]{1,0:T(8,128)S(1)}, f32[8,128]{1,0:T(8,128)S(1)}, u32[]{:S(2)}, u32[]{:S(2)}) %collective-permute-start.8) | collective-permute-done | bytes 4128 | tf_op jit(solution)/shard_map/ppermute | solution.py:25
  39.7 0.1 join.1.here
  39.7 0.2 collective-permute-start.10
  39.9 3.3 %collective-permute-start.9 = (f32[8,128]{1,0:T(8,128)S(1)}, f32[8,128]{1,0:T(8,128)S(1)}, u32[]{:S(2)}, u32[]{:S(2)}) collective-permute-start(f32[8,128]{1,0:T(8,128)S(1)} %join.1.here), channel_id=1, source_target_pairs={{4,0},{6,2},{8,4},{10,6},{12,8},{14,10},{16,12},{18,14},{20,16},{2... | collective-permute-start | bytes 12296 | tf_op jit(solution)/shard_map/ppermute | solution.py:25
  43.2 2.0 %collective-permute-done.10.before = f32[8,128]{1,0:T(8,128)S(1)} collective-permute-done((f32[8,128]{1,0:T(8,128)S(1)}, f32[8,128]{1,0:T(8,128)S(1)}, u32[]{:S(2)}, u32[]{:S(2)}) %collective-permute-start.10) | collective-permute-done | bytes 4128 | tf_op jit(solution)/shard_map/ppermute | solution.py:25
  45.3 0.0 collective-permute-done.9.after
  45.3 0.8 %pick.1 = f32[1,26]{1,0:T(1,128)} custom-call(s32[8,128]{1,0:T(8,128)S(1)} %dynamic-slice_bitcast_fusion.spot_ref, f32[8,128]{1,0:T(8,128)S(1)} %join.1.here, f32[8,128]{1,0:T(8,128)S(1)} %collective-permute-done.9.after, f32[8,128]{1,0:T(8,128)S(1)} %collective-permute-done.10.before), custom_call_target="tpu_custom_call" | custom-call | tf_op jit(solution)/shard_map/pick/pallas_call | solution.py:282
Async XLA Ops:
  0.0 1.0 %copy-start = (f32[32,32,128]{2,1,0:T(8,128)S(1)}, f32[32,32,128]{2,1,0:T(8,128)}, u32[]{:S(2)}) copy-start(f32[32,32,128]{2,1,0:T(8,128)} %sites_ref.1) | copy-start | bytes 1572868
  1.7 7.4 %collective-permute-start = (f32[27,32,128]{2,1,0:T(8,128)S(1)}, f32[27,32,128]{2,1,0:T(8,128)S(1)}, u32[]{:S(2)}, u32[]{:S(2)}) collective-permute-start(f32[27,32,128]{2,1,0:T(8,128)S(1)} %get-tuple-element.15.own), channel_id=1, source_target_pairs={{2,0},{0,2},{6,4},{4,6},{10,8},{8,10},{14,12},{12,14},{18,16},{16,... | collective-permute-start | bytes 1327112 | tf_op jit(solution)/shard_map/ppermute | solution.py:25
  2.1 14.8 %collective-permute-start.3 = (f32[16,32,128]{2,1,0:T(8,128)S(1)}, f32[16,32,128]{2,1,0:T(8,128)S(1)}, u32[]{:S(2)}, u32[]{:S(2)}) collective-permute-start(f32[16,32,128]{2,1,0:T(8,128)S(1)} %get-tuple-element.18), channel_id=1, source_target_pairs={{30,0},{8,2},{2,4},{12,6},{6,8},{16,10},{10,12},{20,14},{14,16},{2... | collective-permute-start | bytes 786440 | tf_op jit(solution)/shard_map/ppermute | solution.py:25
  6.9 14.1 %collective-permute-start.4 = (f32[16,32,128]{2,1,0:T(8,128)S(1)}, f32[16,32,128]{2,1,0:T(8,128)S(1)}, u32[]{:S(2)}, u32[]{:S(2)}) collective-permute-start(f32[16,32,128]{2,1,0:T(8,128)S(1)} %get-tuple-element.18), channel_id=1, source_target_pairs={{28,0},{10,2},{0,4},{14,6},{4,8},{18,10},{8,12},{22,14},{12,16},{2... | collective-permute-start | bytes 786440 | tf_op jit(solution)/shard_map/ppermute | solution.py:25
  17.0 4.0 %collective-permute-start.5 = (f32[16,32,128]{2,1,0:T(8,128)S(1)}, f32[16,32,128]{2,1,0:T(8,128)S(1)}, u32[]{:S(2)}, u32[]{:S(2)}) collective-permute-start(f32[16,32,128]{2,1,0:T(8,128)S(1)} %collective-permute-done.3.second), channel_id=1, source_target_pairs={{2,0},{0,2},{6,4},{4,6},{10,8},{8,10},{14,12},{12,14},{18,16},{16,... | collective-permute-start | bytes 786440 | tf_op jit(solution)/shard_map/ppermute | solution.py:25
  17.1 9.1 %collective-permute-start.2 = (f32[11,32,128]{2,1,0:T(8,128)S(1)}, f32[11,32,128]{2,1,0:T(8,128)S(1)}, u32[]{:S(2)}, u32[]{:S(2)}) collective-permute-start(f32[11,32,128]{2,1,0:T(8,128)S(1)} %get-tuple-element.17), channel_id=1, source_target_pairs={{30,0},{8,2},{2,4},{12,6},{6,8},{16,10},{10,12},{20,14},{14,16},{2... | collective-permute-start | bytes 540680 | tf_op jit(solution)/shard_map/ppermute | solution.py:25
  20.9 8.7 %collective-permute-start.1 = (f32[11,32,128]{2,1,0:T(8,128)S(1)}, f32[11,32,128]{2,1,0:T(8,128)S(1)}, u32[]{:S(2)}, u32[]{:S(2)}) collective-permute-start(f32[11,32,128]{2,1,0:T(8,128)S(1)} %get-tuple-element.17), channel_id=1, source_target_pairs={{28,0},{10,2},{0,4},{14,6},{4,8},{18,10},{8,12},{22,14},{12,16},{2... | collective-permute-start | bytes 540680 | tf_op jit(solution)/shard_map/ppermute | solution.py:25
  26.2 3.4 %collective-permute-start.6 = (f32[11,32,128]{2,1,0:T(8,128)S(1)}, f32[11,32,128]{2,1,0:T(8,128)S(1)}, u32[]{:S(2)}, u32[]{:S(2)}) collective-permute-start(f32[11,32,128]{2,1,0:T(8,128)S(1)} %collective-permute-done.2.second), channel_id=1, source_target_pairs={{2,0},{0,2},{6,4},{4,6},{10,8},{8,10},{14,12},{12,14},{18,16},{16,... | collective-permute-start | bytes 540680 | tf_op jit(solution)/shard_map/ppermute | solution.py:25
  33.1 5.2 %collective-permute-start.7 = (f32[288,128]{1,0:T(8,128)S(1)}, f32[288,128]{1,0:T(8,128)S(1)}, u32[]{:S(2)}, u32[]{:S(2)}) collective-permute-start(f32[288,128]{1,0:T(8,128)S(1)} %half_chains.3.mine), channel_id=1, source_target_pairs={{0,1},{1,0},{2,3},{3,2},{4,5},{5,4},{6,7},{7,6},{8,9},{9,8},{10,11... | collective-permute-start | bytes 442376 | tf_op jit(solution)/shard_map/ppermute | solution.py:321
  38.5 1.2 %collective-permute-start.8 = (f32[8,128]{1,0:T(8,128)S(1)}, f32[8,128]{1,0:T(8,128)S(1)}, u32[]{:S(2)}, u32[]{:S(2)}) collective-permute-start(f32[8,128]{1,0:T(8,128)S(1)} %meet.1.mine), channel_id=1, source_target_pairs={{2,0},{0,2},{6,4},{4,6},{10,8},{8,10},{14,12},{12,14},{18,16},{16,... | collective-permute-start | bytes 12296 | tf_op jit(solution)/shard_map/ppermute | solution.py:25
  39.7 5.5 %collective-permute-start.10 = (f32[8,128]{1,0:T(8,128)S(1)}, f32[8,128]{1,0:T(8,128)S(1)}, u32[]{:S(2)}, u32[]{:S(2)}) collective-permute-start(f32[8,128]{1,0:T(8,128)S(1)} %join.1.here), channel_id=1, source_target_pairs={{24,0},{26,2},{28,4},{30,6},{0,8},{2,10},{4,12},{6,14},{8,16},{10,... | collective-permute-start | bytes 12296 | tf_op jit(solution)/shard_map/ppermute | solution.py:25
  39.9 5.3 %collective-permute-start.9 = (f32[8,128]{1,0:T(8,128)S(1)}, f32[8,128]{1,0:T(8,128)S(1)}, u32[]{:S(2)}, u32[]{:S(2)}) collective-permute-start(f32[8,128]{1,0:T(8,128)S(1)} %join.1.here), channel_id=1, source_target_pairs={{4,0},{6,2},{8,4},{10,6},{12,8},{14,10},{16,12},{18,14},{20,16},{2... | collective-permute-start | bytes 12296 | tf_op jit(solution)/shard_map/ppermute | solution.py:25

commit v17 on v15

--- a/solution.py
+++ b/solution.py
@@ -309,10 +309,12 @@
     inner = call(home_kernel, (64, 128), flag, mps, sibling, name="own_chains")
     spots = jnp.asarray([spot_table(core, samp, band) for core in range(2)], jnp.int32)
     spot = spots[lax.axis_index("blk") % 2, side]
-    inner, spot = lax.optimization_barrier((inner, spot))
     carried = (inner,)
     for start, first, second in zip(starts, firsts, seconds):
         second, *carried = lax.optimization_barrier((second, *carried))
+        if start:
+            spot, state = lax.optimization_barrier((spot, carried[-1]))
+            carried = (carried[0], state)
         other = move(second, across)
         rows = 288 if start == starts[-1] else 224
         state = call(functools.partial(chain_kernel, start), (rows, 128), flag, mps, sibling, first, second, other,

time: 46.6 us -> 46.8 us (level)
  starting transfers between devices: 17.9 us -> 18.6 us
  waiting for transfers between devices: 8.36 us -> 7.88 us
    ppermute x10, starting transfers between devices: 16 us -> 16.6 us  [move(): return lax.ppermute(array, 'blk', pairs)]
    ppermute x10, waiting for transfers between devices: 5.07 us -> 4.58 us  [move(): return lax.ppermute(array, 'blk', pairs)]
where the time goes in v17:
time: 46.8 us; the launch traced here: 46.6 us
  starting transfers between devices  18.6 us (40%)
  Pallas kernels  18.4 us (39%)
  waiting for transfers between devices  7.88 us (17%)
  local copies, waits for them, and re-layouts  1.73 us (4%)
    pallas_call x7, Pallas kernels, call(): pl.pallas_call(kernel, out_shape=shapes if many else shapes[0], in_specs=...  18.4 us
    ppermute x10, starting transfers between devices, move(): return lax.ppermute(array, 'blk', pairs)  16.6 us
    ppermute x10, waiting for transfers between devices, move(): return lax.ppermute(array, 'blk', pairs)  4.58 us
    ppermute x1, waiting for transfers between devices, body(): partner = lax.ppermute(state, 'pair', [(0, 1), (1, 0)])  3.3 us
    ppermute x1, starting transfers between devices, body(): partner = lax.ppermute(state, 'pair', [(0, 1), (1, 0)])  1.91 us
    unnamed x2, local copies, waits for them, and re-layouts  1.04 us
  transfers between devices with their start and end apart: 11, of which 4 were waited for; matrix products, arithmetic and copies ran while one was open for 1% of the time, Pallas kernels for 29%

profile of v17, /device:TPU:0, one launch (start us, length us, event | category | flops | bytes accessed | tf_op | source)
XLA Modules:
  0.0 46.6 jit_solution(5014852835085220622)
XLA Ops:
  0.0 0.0 copy-start
  0.0 1.0 %copy-done = f32[32,32,128]{2,1,0:T(8,128)S(1)} copy-done((f32[32,32,128]{2,1,0:T(8,128)S(1)}, f32[32,32,128]{2,1,0:T(8,128)}, u32[]{:S(2)}) %copy-start) | copy-done | bytes 524312
  1.0 0.6 %order.1 = (f32[27,32,128]{2,1,0:T(8,128)S(1)}, f32[17,32,128]{2,1,0:T(8,128)S(1)}, f32[10,32,128]{2,1,0:T(8,128)S(1)}) custom-call(s32[1]{0:T(128)} %bitcast.1.side_ref, f32[32,32,128]{2,1,0:T(8,128)S(1)} %copy-done), custom_call_target="tpu_custom_call" | custom-call | tf_op jit(solution)/shard_map/order/pallas_call | solution.py:282
  1.7 0.5 collective-permute-start.2
  2.1 4.7 %collective-permute-start.1 = (f32[17,32,128]{2,1,0:T(8,128)S(1)}, f32[17,32,128]{2,1,0:T(8,128)S(1)}, u32[]{:S(2)}, u32[]{:S(2)}) collective-permute-start(f32[17,32,128]{2,1,0:T(8,128)S(1)} %get-tuple-element.16), channel_id=1, source_target_pairs={{30,0},{8,2},{2,4},{12,6},{6,8},{16,10},{10,12},{20,14},{14,16},{2... | collective-permute-start | bytes 835592 | tf_op jit(solution)/shard_map/ppermute | solution.py:25
  6.9 1.5 %collective-permute-start.3 = (f32[17,32,128]{2,1,0:T(8,128)S(1)}, f32[17,32,128]{2,1,0:T(8,128)S(1)}, u32[]{:S(2)}, u32[]{:S(2)}) collective-permute-start(f32[17,32,128]{2,1,0:T(8,128)S(1)} %get-tuple-element.16), channel_id=1, source_target_pairs={{28,0},{10,2},{0,4},{14,6},{4,8},{18,10},{8,12},{22,14},{12,16},{2... | collective-permute-start | bytes 835592 | tf_op jit(solution)/shard_map/ppermute | solution.py:25
  8.3 0.0 collective-permute-done.2.sibling
  8.3 7.9 %own_chains.1.home = f32[64,128]{1,0:T(8,128)S(1)} custom-call(s32[1]{0:T(128)} %bitcast.1.side_ref, f32[27,32,128]{2,1,0:T(8,128)S(1)} %get-tuple-element.17.own, f32[27,32,128]{2,1,0:T(8,128)S(1)} %collective-permute-done.2.sibling), custom_call_target="tpu_custom_call" | custom-call | tf_op jit(solution)/shard_map/own_chains/pallas_call | solution.py:282
  16.3 0.0 collective-permute-done.1.second
  16.3 0.1 collective-permute-start.4
  16.4 5.3 %collective-permute-start = (f32[10,32,128]{2,1,0:T(8,128)S(1)}, f32[10,32,128]{2,1,0:T(8,128)S(1)}, u32[]{:S(2)}, u32[]{:S(2)}) collective-permute-start(f32[10,32,128]{2,1,0:T(8,128)S(1)} %get-tuple-element.15), channel_id=1, source_target_pairs={{30,0},{8,2},{2,4},{12,6},{6,8},{16,10},{10,12},{20,14},{14,16},{2... | collective-permute-start | bytes 491528 | tf_op jit(solution)/shard_map/ppermute | solution.py:25
  21.6 0.0 collective-permute-start.5
  21.6 0.0 collective-permute-done.3.first
  21.6 0.0 collective-permute-done.4.other
  21.6 5.5 %half_chains.2.rest_0_ = f32[224,128]{1,0:T(8,128)S(1)} custom-call(s32[1]{0:T(128)} %bitcast.1.side_ref, f32[27,32,128]{2,1,0:T(8,128)S(1)} %get-tuple-element.17.own, f32[27,32,128]{2,1,0:T(8,128)S(1)} %collective-permute-done.2.sibling, f32[17,32,128]{2,1,0:T(8,128)S(1)} %collective-permute-done.3.first, ...), custom_call_target="tpu_custom_call" | custom-call | tf_op jit(solution)/shard_map/half_chains/pallas_call | solution.py:282
  27.2 0.0 collective-permute-done.second
  27.2 0.2 collective-permute-start.6
  27.4 0.7 %dynamic-slice_bitcast_fusion.spot_ref = s32[8,128]{1,0:T(8,128)S(1)} fusion(s32[2,2,8,128]{3,2,1,0:T(8,128)} %constant.24.clone, s32[]{:T(128)S(6)} %select_n.14, s32[]{:T(128)S(6)} %select_n.15), kind=kLoop, calls=%fused_computation | loop fusion | bytes 8200 | tf_op jit(solution)/shard_map/squeeze | solution.py:311
  28.1 1.6 %collective-permute-done.5.first = f32[10,32,128]{2,1,0:T(8,128)S(1)} collective-permute-done((f32[10,32,128]{2,1,0:T(8,128)S(1)}, f32[10,32,128]{2,1,0:T(8,128)S(1)}, u32[]{:S(2)}, u32[]{:S(2)}) %collective-permute-start.5) | collective-permute-done | bytes 163872 | tf_op jit(solution)/shard_map/ppermute | solution.py:25
  29.7 0.0 collective-permute-done.6.other
  29.7 3.2 %half_chains.3.mine = f32[288,128]{1,0:T(8,128)S(1)} custom-call(s32[1]{0:T(128)} %bitcast.1.side_ref, f32[27,32,128]{2,1,0:T(8,128)S(1)} %get-tuple-element.17.own, f32[27,32,128]{2,1,0:T(8,128)S(1)} %collective-permute-done.2.sibling, f32[10,32,128]{2,1,0:T(8,128)S(1)} %collective-permute-done.5.first, f32[10,32,128]{2,1,0:T(8,128)S(1)} %collective-permute-done.second, ...), custom_call_target="tpu_custom_call" | custom-call | tf_op jit(solution)/shard_map/half_chains/pallas_call | solution.py:282
  32.9 1.9 %collective-permute-start.7 = (f32[288,128]{1,0:T(8,128)S(1)}, f32[288,128]{1,0:T(8,128)S(1)}, u32[]{:S(2)}, u32[]{:S(2)}) collective-permute-start(f32[288,128]{1,0:T(8,128)S(1)} %half_chains.3.mine), channel_id=1, source_target_pairs={{0,1},{1,0},{2,3},{3,2},{4,5},{5,4},{6,7},{7,6},{8,9},{9,8},{10,11... | collective-permute-start | bytes 442376 | tf_op jit(solution)/shard_map/ppermute | solution.py:323
  34.8 3.3 %collective-permute-done.7.theirs = f32[288,128]{1,0:T(8,128)S(1)} collective-permute-done((f32[288,128]{1,0:T(8,128)S(1)}, f32[288,128]{1,0:T(8,128)S(1)}, u32[]{:S(2)}, u32[]{:S(2)}) %collective-permute-start.7) | collective-permute-done | bytes 147488 | tf_op jit(solution)/shard_map/ppermute | solution.py:323
  38.1 0.2 meet.1.mine
  38.2 0.0 collective-permute-start.8
  38.2 1.2 %collective-permute-done.8.theirs = f32[8,128]{1,0:T(8,128)S(1)} collective-permute-done((f32[8,128]{1,0:T(8,128)S(1)}, f32[8,128]{1,0:T(8,128)S(1)}, u32[]{:S(2)}, u32[]{:S(2)}) %collective-permute-start.8) | collective-permute-done | bytes 4128 | tf_op jit(solution)/shard_map/ppermute | solution.py:25
  39.4 0.1 join.1.here
  39.5 0.1 collective-permute-start.10
  39.6 4.4 %collective-permute-start.9 = (f32[8,128]{1,0:T(8,128)S(1)}, f32[8,128]{1,0:T(8,128)S(1)}, u32[]{:S(2)}, u32[]{:S(2)}) collective-permute-start(f32[8,128]{1,0:T(8,128)S(1)} %join.1.here), channel_id=1, source_target_pairs={{4,0},{6,2},{8,4},{10,6},{12,8},{14,10},{16,12},{18,14},{20,16},{2... | collective-permute-start | bytes 12296 | tf_op jit(solution)/shard_map/ppermute | solution.py:25
  43.9 1.8 %collective-permute-done.10.before = f32[8,128]{1,0:T(8,128)S(1)} collective-permute-done((f32[8,128]{1,0:T(8,128)S(1)}, f32[8,128]{1,0:T(8,128)S(1)}, u32[]{:S(2)}, u32[]{:S(2)}) %collective-permute-start.10) | collective-permute-done | bytes 4128 | tf_op jit(solution)/shard_map/ppermute | solution.py:25
  45.7 0.0 collective-permute-done.9.after
  45.7 0.8 %pick.1 = f32[1,26]{1,0:T(1,128)} custom-call(s32[8,128]{1,0:T(8,128)S(1)} %dynamic-slice_bitcast_fusion.spot_ref, f32[8,128]{1,0:T(8,128)S(1)} %join.1.here, f32[8,128]{1,0:T(8,128)S(1)} %collective-permute-done.9.after, f32[8,128]{1,0:T(8,128)S(1)} %collective-permute-done.10.before), custom_call_target="tpu_custom_call" | custom-call | tf_op jit(solution)/shard_map/pick/pallas_call | solution.py:282
Async XLA Ops:
  0.0 1.0 %copy-start = (f32[32,32,128]{2,1,0:T(8,128)S(1)}, f32[32,32,128]{2,1,0:T(8,128)}, u32[]{:S(2)}) copy-start(f32[32,32,128]{2,1,0:T(8,128)} %sites_ref.1) | copy-start | bytes 1572868
  1.7 6.7 %collective-permute-start.2 = (f32[27,32,128]{2,1,0:T(8,128)S(1)}, f32[27,32,128]{2,1,0:T(8,128)S(1)}, u32[]{:S(2)}, u32[]{:S(2)}) collective-permute-start(f32[27,32,128]{2,1,0:T(8,128)S(1)} %get-tuple-element.17.own), channel_id=1, source_target_pairs={{2,0},{0,2},{6,4},{4,6},{10,8},{8,10},{14,12},{12,14},{18,16},{16,... | collective-permute-start | bytes 1327112 | tf_op jit(solution)/shard_map/ppermute | solution.py:25
  2.1 14.1 %collective-permute-start.1 = (f32[17,32,128]{2,1,0:T(8,128)S(1)}, f32[17,32,128]{2,1,0:T(8,128)S(1)}, u32[]{:S(2)}, u32[]{:S(2)}) collective-permute-start(f32[17,32,128]{2,1,0:T(8,128)S(1)} %get-tuple-element.16), channel_id=1, source_target_pairs={{30,0},{8,2},{2,4},{12,6},{6,8},{16,10},{10,12},{20,14},{14,16},{2... | collective-permute-start | bytes 835592 | tf_op jit(solution)/shard_map/ppermute | solution.py:25
  6.9 14.8 %collective-permute-start.3 = (f32[17,32,128]{2,1,0:T(8,128)S(1)}, f32[17,32,128]{2,1,0:T(8,128)S(1)}, u32[]{:S(2)}, u32[]{:S(2)}) collective-permute-start(f32[17,32,128]{2,1,0:T(8,128)S(1)} %get-tuple-element.16), channel_id=1, source_target_pairs={{28,0},{10,2},{0,4},{14,6},{4,8},{18,10},{8,12},{22,14},{12,16},{2... | collective-permute-start | bytes 835592 | tf_op jit(solution)/shard_map/ppermute | solution.py:25
  16.3 5.3 %collective-permute-start.4 = (f32[17,32,128]{2,1,0:T(8,128)S(1)}, f32[17,32,128]{2,1,0:T(8,128)S(1)}, u32[]{:S(2)}, u32[]{:S(2)}) collective-permute-start(f32[17,32,128]{2,1,0:T(8,128)S(1)} %collective-permute-done.1.second), channel_id=1, source_target_pairs={{2,0},{0,2},{6,4},{4,6},{10,8},{8,10},{14,12},{12,14},{18,16},{16,... | collective-permute-start | bytes 835592 | tf_op jit(solution)/shard_map/ppermute | solution.py:25
  16.4 10.8 %collective-permute-start = (f32[10,32,128]{2,1,0:T(8,128)S(1)}, f32[10,32,128]{2,1,0:T(8,128)S(1)}, u32[]{:S(2)}, u32[]{:S(2)}) collective-permute-start(f32[10,32,128]{2,1,0:T(8,128)S(1)} %get-tuple-element.15), channel_id=1, source_target_pairs={{30,0},{8,2},{2,4},{12,6},{6,8},{16,10},{10,12},{20,14},{14,16},{2... | collective-permute-start | bytes 491528 | tf_op jit(solution)/shard_map/ppermute | solution.py:25
  21.6 8.0 %collective-permute-start.5 = (f32[10,32,128]{2,1,0:T(8,128)S(1)}, f32[10,32,128]{2,1,0:T(8,128)S(1)}, u32[]{:S(2)}, u32[]{:S(2)}) collective-permute-start(f32[10,32,128]{2,1,0:T(8,128)S(1)} %get-tuple-element.15), channel_id=1, source_target_pairs={{28,0},{10,2},{0,4},{14,6},{4,8},{18,10},{8,12},{22,14},{12,16},{2... | collective-permute-start | bytes 491528 | tf_op jit(solution)/shard_map/ppermute | solution.py:25
  27.2 2.5 %collective-permute-start.6 = (f32[10,32,128]{2,1,0:T(8,128)S(1)}, f32[10,32,128]{2,1,0:T(8,128)S(1)}, u32[]{:S(2)}, u32[]{:S(2)}) collective-permute-start(f32[10,32,128]{2,1,0:T(8,128)S(1)} %collective-permute-done.second), channel_id=1, source_target_pairs={{2,0},{0,2},{6,4},{4,6},{10,8},{8,10},{14,12},{12,14},{18,16},{16,... | collective-permute-start | bytes 491528 | tf_op jit(solution)/shard_map/ppermute | solution.py:25
  32.9 5.2 %collective-permute-start.7 = (f32[288,128]{1,0:T(8,128)S(1)}, f32[288,128]{1,0:T(8,128)S(1)}, u32[]{:S(2)}, u32[]{:S(2)}) collective-permute-start(f32[288,128]{1,0:T(8,128)S(1)} %half_chains.3.mine), channel_id=1, source_target_pairs={{0,1},{1,0},{2,3},{3,2},{4,5},{5,4},{6,7},{7,6},{8,9},{9,8},{10,11... | collective-permute-start | bytes 442376 | tf_op jit(solution)/shard_map/ppermute | solution.py:323
  38.2 1.2 %collective-permute-start.8 = (f32[8,128]{1,0:T(8,128)S(1)}, f32[8,128]{1,0:T(8,128)S(1)}, u32[]{:S(2)}, u32[]{:S(2)}) collective-permute-start(f32[8,128]{1,0:T(8,128)S(1)} %meet.1.mine), channel_id=1, source_target_pairs={{2,0},{0,2},{6,4},{4,6},{10,8},{8,10},{14,12},{12,14},{18,16},{16,... | collective-permute-start | bytes 12296 | tf_op jit(solution)/shard_map/ppermute | solution.py:25
  39.5 6.3 %collective-permute-start.10 = (f32[8,128]{1,0:T(8,128)S(1)}, f32[8,128]{1,0:T(8,128)S(1)}, u32[]{:S(2)}, u32[]{:S(2)}) collective-permute-start(f32[8,128]{1,0:T(8,128)S(1)} %join.1.here), channel_id=1, source_target_pairs={{24,0},{26,2},{28,4},{30,6},{0,8},{2,10},{4,12},{6,14},{8,16},{10,... | collective-permute-start | bytes 12296 | tf_op jit(solution)/shard_map/ppermute | solution.py:25
  39.6 6.2 %collective-permute-start.9 = (f32[8,128]{1,0:T(8,128)S(1)}, f32[8,128]{1,0:T(8,128)S(1)}, u32[]{:S(2)}, u32[]{:S(2)}) collective-permute-start(f32[8,128]{1,0:T(8,128)S(1)} %join.1.here), channel_id=1, source_target_pairs={{4,0},{6,2},{8,4},{10,6},{12,8},{14,10},{16,12},{18,14},{20,16},{2... | collective-permute-start | bytes 12296 | tf_op jit(solution)/shard_map/ppermute | solution.py:25
